TPU v7x, 32 devices: a whole 2x2x4 slice. The times are simulated.
32 devices in a mesh: blk: 2 (over core), smp: 16 (over z, y, x).
Axes of the slice: x: 2, y: 2, z: 4, core: 2. Of those that a mesh axis runs over, the one named last changes fastest.
Arguments:
- genotypes: bfloat16 [2, 16384, 2048], P('blk', 'smp'), may hold values from -2 to 10, as said below
- sizes: int32 [2], P('blk'), may hold values from 1024 to 2048, as said below
- start: float32 [2, 2048, 256], P('blk', 'smp'), may hold values from -6 to 6
Outputs:
- basis: float32 [2, 2048, 256], P('blk', 'smp')
- scaled: float32 [2, 256, 256], P('blk')
Inputs may be any that keep to these rules, and one draw needn't show every extreme that they name: `sizes`: at least one block has exactly 2048 SNPs. `genotypes`: each column is a standardized count of 0, 1 or 2 alleles; columns at or past a block's size hold values that the block does not use.
All inputs are finite; a program needn't handle non-finite values.
Results may differ from a plain program's by a relative error of at most 0.0003.
Values may be sent and summed in bfloat16 or wider, within the bound.
No kernel may reach another device: no remote copies, remote signals or barrier semaphores. Data moves between devices by JAX's collectives and lax.ppermute only.
A program may use at most 128 MiB of HBM per device.

v0:
```python
import math

import jax
import jax.numpy as jnp
from jax import lax
from jax.sharding import PartitionSpec as P

CAP = 2048
K = 256


def column_inner(left, right):
    return lax.dot_general(
        left,
        right,
        (((0,), (0,)), ((), ())),
        precision=lax.Precision.HIGHEST,
        preferred_element_type=jnp.float32,
    )


def form_gram(masked, samples_total):
    product = lax.dot_general(
        masked, masked, (((0,), (0,)), ((), ())), preferred_element_type=jnp.float32
    )
    return lax.psum_scatter(product / samples_total, "smp", scatter_dimension=0, tiled=True)


def apply_gram(gram, vectors):
    return jnp.dot(
        gram,
        lax.all_gather(vectors, "smp", axis=0, tiled=True),
        precision=lax.Precision.HIGHEST,
        preferred_element_type=jnp.float32,
    )


def orthonormal(image):
    inner = lax.psum(column_inner(image, image), "smp")
    lower = jnp.linalg.cholesky(inner)
    return lax.linalg.triangular_solve(lower, image, left_side=False, lower=True, transpose_a=True)


def iterate(gram, vectors):
    vectors = orthonormal(apply_gram(gram, vectors))
    image = apply_gram(gram, vectors)
    second = apply_gram(gram, image)
    inner, cross = lax.psum((column_inner(image, image), column_inner(image, second)), "smp")
    lower = jnp.linalg.cholesky(inner)
    vectors = lax.linalg.triangular_solve(
        lower, image, left_side=False, lower=True, transpose_a=True
    )
    halfway = lax.linalg.triangular_solve(lower, cross, left_side=True, lower=True)
    rayleigh = lax.linalg.triangular_solve(
        lower, halfway, left_side=False, lower=True, transpose_a=True
    )
    return (vectors, rayleigh)


def body(genotypes, sizes, start):
    groups = lax.axis_size("smp")
    samples_total = genotypes.shape[1] * groups
    live = (lax.iota(jnp.int32, CAP) < sizes[0]).astype(jnp.bfloat16)
    masked = genotypes[0] * live[None, :]
    gram = form_gram(masked, samples_total)
    vectors, rayleigh = iterate(gram, start[0])
    bases = [vectors]
    projected = [rayleigh]
    stacked = jnp.stack(projected)
    partial_trace = jnp.sum(jnp.trace(stacked, axis1=1, axis2=2))
    total = lax.psum(partial_trace, "blk")
    blocks_all = genotypes.shape[0] * lax.axis_size("blk")
    scaled = stacked * (blocks_all * K) / total
    basis = jnp.stack(bases) * math.sqrt(CAP)
    return (basis, scaled)


def solution(mesh):
    return jax.shard_map(
        body,
        mesh=mesh,
        in_specs=(P("blk", "smp", None), P("blk"), P("blk", "smp", None)),
        out_specs=(P("blk", "smp", None), P("blk", None, None)),
        check_vma=False,
    )
```

profile of v0, /device:TPU:0, one launch (start us, length us, event | category | flops | bytes accessed | tf_op | source)
XLA Modules:
  0.0 924.3 jit_solution(6817076381870417102)
XLA Ops:
  7.2 0.7 all-gather.9.cloned.1.call-update
  8.6 15.2 %convolution_multiply_fusion = f32[2048,2048]{1,0:T(8,128)} fusion(bf16[1,1024,2048]{2,1,0:T(8,128)(2,1)} %param.6, bf16[2048]{0:T(1024)(128)(2,1)S(1)} %fusion.37), kind=kOutput, calls=%fused_computation.4 | convolution fusion | flops 8596226048 | bytes 20975616 | tf_op jit(solution)/shard_map/dot_general | solution.py:23
  23.9 50.3 %all-gather.9.cloned.1.call-done = f32[1,2048,256]{2,1,0:T(8,128)} async-done(((f32[1,128,256]{2,1,0:T(8,128)}), f32[1,2048,256]{2,1,0:T(8,128)}) %all-gather.9.cloned.1.call-update) | async-done | bytes 2097168 | tf_op jit(solution)/shard_map/all_gather | solution.py:32
  74.2 347.3 %reduce-scatter.2.cloned.1.call-done = f32[128,2048]{1,0:T(8,128)} async-done(((f32[2048,2048]{1,0:T(8,128)}), f32[128,2048]{1,0:T(8,128)}) %reduce-scatter.2.cloned.1.call-update) | async-done | bytes 1048592 | tf_op jit(solution)/shard_map/reduce_scatter | solution.py:26
  421.6 3.0 fusion.2
  424.6 1.1 fusion.41
  426.0 113.8 %all-reduce.5.cloned.1.call-done = f32[256,256]{0,1:T(8,128)} async-done(((f32[256,256]{0,1:T(8,128)}), f32[256,256]{0,1:T(8,128)}) %all-reduce.5.cloned.1.call-update) | async-done | bytes 262160 | tf_op jit(solution)/shard_map/psum | solution.py:39
  539.8 1.1 copy.6
  540.9 1.0 fusion.8
  541.9 11.7 %cholesky.130 = f32[128,128]{1,0:T(8,128)S(1)} custom-call(f32[128,128]{1,0:T(8,128)S(1)} %cholesky.194), custom_call_target="Cholesky" | custom-call | tf_op jit(solution)/shard_map/jit(cholesky)/cholesky | solution.py:40
  553.7 9.8 %custom-call.19 = f32[1,128,128]{1,2,0:T(8,128)S(1)} custom-call(f32[1,128,128]{2,1,0:T(8,128)S(1)} %get-tuple-element.59), custom_call_target="InvertDiagBlocksLowerTriangular" | custom-call | tf_op jit(solution)/shard_map/jit(cholesky)/cholesky | solution.py:40
  564.0 11.7 %cholesky.147 = f32[128,128]{1,0:T(8,128)S(1)} custom-call(f32[128,128]{1,0:T(8,128)S(1)} %convolution_subtract_fusion.5), custom_call_target="Cholesky" | custom-call | tf_op jit(solution)/shard_map/jit(cholesky)/cholesky | solution.py:40
  575.8 0.7 compare_reduce_fusion.2
  577.9 4.3 while.5
  578.2 0.6 fusion.71
  578.8 1.4 bitcast_dynamic-update-slice_fusion.4
  580.2 0.6 fusion.71
  580.8 1.4 bitcast_dynamic-update-slice_fusion.4
  582.3 19.7 %custom-call.20 = f32[2,128,128]{1,2,0:T(8,128)S(1)} custom-call(f32[2,128,128]{2,1,0:T(8,128)S(1)} %get-tuple-element.26), custom_call_target="InvertDiagBlocksLowerTriangular" | custom-call | tf_op jit(solution)/shard_map/triangular_solve/custom-call.0 | solution.py:41
  602.8 0.7 pad_maximum_fusion.1
  603.6 64.2 %all-gather.5.cloned.1.call-done = f32[2048,256]{0,1:T(8,128)} async-done(((f32[128,256]{0,1:T(8,128)}), f32[2048,256]{0,1:T(8,128)}) %all-gather.5.cloned.1.call-update) | async-done | bytes 2097168 | tf_op jit(solution)/shard_map/all_gather | solution.py:32
  667.8 4.5 fusion.42
  672.4 2.1 fusion.43
  674.5 57.1 %all-gather.7.cloned.1.call-done = f32[2048,256]{1,0:T(8,128)} async-done(((f32[128,256]{1,0:T(8,128)}), f32[2048,256]{1,0:T(8,128)}) %all-gather.7.cloned.1.call-update) | async-done | bytes 2097168 | tf_op jit(solution)/shard_map/all_gather | solution.py:32
  731.6 2.7 fusion.44
  734.3 1.1 fusion.45
  735.4 110.0 %all-reduce.7.cloned.1.call-done = (f32[256,256]{0,1:T(8,128)}, f32[256,256]{1,0:T(8,128)}) async-done(((f32[256,256]{0,1:T(8,128)}, f32[256,256]{1,0:T(8,128)}), (f32[256,256]{0,1:T(8,128)}, f32[256,256]{1,0:T(8,128)})) %all-reduce.7.cloned.1.call-update) | async-done | bytes 524304 | tf_op jit(solution)/shard_map/psum | solution.py:48
  845.4 1.1 copy.8
  846.5 1.0 fusion.7
  847.6 11.7 %cholesky.164 = f32[128,128]{1,0:T(8,128)S(1)} custom-call(f32[128,128]{1,0:T(8,128)S(1)} %cholesky.197), custom_call_target="Cholesky" | custom-call | tf_op jit(solution)/shard_map/jit(cholesky)/cholesky | solution.py:49
  859.3 9.8 %custom-call.21 = f32[1,128,128]{1,2,0:T(8,128)S(1)} custom-call(f32[1,128,128]{2,1,0:T(8,128)S(1)} %get-tuple-element.55), custom_call_target="InvertDiagBlocksLowerTriangular" | custom-call | tf_op jit(solution)/shard_map/jit(cholesky)/cholesky | solution.py:49
  869.6 11.7 %cholesky.181 = f32[128,128]{1,0:T(8,128)S(1)} custom-call(f32[128,128]{1,0:T(8,128)S(1)} %convolution_subtract_fusion.3), custom_call_target="Cholesky" | custom-call | tf_op jit(solution)/shard_map/jit(cholesky)/cholesky | solution.py:49
  881.6 0.6 compare_reduce_fusion
  882.3 0.6 compare_reduce_fusion.1
  884.2 4.0 while.6
  884.3 0.6 fusion.72
  884.9 1.4 bitcast_dynamic-update-slice_fusion.5
  886.3 0.6 fusion.72
  886.9 1.4 bitcast_dynamic-update-slice_fusion.5
  888.3 19.7 %custom-call.22 = f32[2,128,128]{1,2,0:T(8,128)S(1)} custom-call(f32[2,128,128]{2,1,0:T(8,128)S(1)} %get-tuple-element.27), custom_call_target="InvertDiagBlocksLowerTriangular" | custom-call | tf_op jit(solution)/shard_map/triangular_solve/custom-call.0 | solution.py:50
  908.9 0.3 fusion.10
  909.2 0.4 convolution_subtract_fusion
  909.7 0.3 fusion.31
  910.1 0.6 fusion.6
  911.0 3.1 psum.31
  914.1 0.7 fusion.5
  914.8 0.8 copy.12
  916.3 0.8 copy.11
  (52 shorter events, 4.9 us)
Async XLA Ops:
  7.2 67.0 %all-gather.9.cloned.1.call-start = ((), (), s32[]{:S(2)}) async-start(), calls=%async_computation.5 | async-start | bytes 2228224 | tf_op jit(solution)/shard_map/all_gather | solution.py:32
  7.9 413.7 %reduce-scatter.2.cloned.1.call-start = ((), (), s32[]{:S(2)}) async-start(), calls=%async_computation.1 | async-start | bytes 17825792 | tf_op jit(solution)/shard_map/reduce_scatter | solution.py:26
  23.8 516.0 %all-reduce.5.cloned.1.call-start = ((), (), s32[]{:S(2)}) async-start(), calls=%async_computation.2 | async-start | bytes 524288 | tf_op jit(solution)/shard_map/psum | solution.py:39
  425.7 242.1 %all-gather.5.cloned.1.call-start = ((), (), s32[]{:S(2)}) async-start(), calls=%async_computation.3 | async-start | bytes 2228224 | tf_op jit(solution)/shard_map/all_gather | solution.py:32
  541.9 125.9 %copy-start = (f32[128,2048]{1,0:T(8,128)S(1)}, f32[128,2048]{1,0:T(8,128)}, u32[]{:S(2)}) copy-start(f32[128,2048]{1,0:T(8,128)} %reduce-scatter.2.cloned.1.call-done) | copy-start | bytes 3145732
  603.5 128.0 %all-gather.7.cloned.1.call-start = ((), (), s32[]{:S(2)}) async-start(), calls=%async_computation.4 | async-start | bytes 2228224 | tf_op jit(solution)/shard_map/all_gather | solution.py:32
  672.3 62.0 %copy-start.1 = (f32[128,256]{1,0:T(8,128)S(1)}, f32[128,256]{1,0:T(8,128)}, u32[]{:S(2)}) copy-start(f32[128,256]{1,0:T(8,128)} %fusion.42) | copy-start | bytes 393220
  672.3 173.1 %all-reduce.7.cloned.1.call-start = ((), (), s32[]{:S(2)}) async-start(), calls=%async_computation.6 | async-start | bytes 1048576 | tf_op jit(solution)/shard_map/psum | solution.py:48
  845.4 62.5 %copy-start.2 = (f32[256,256]{1,0:T(8,128)S(1)}, f32[256,256]{1,0:T(8,128)}, u32[]{:S(2)}) copy-start(f32[256,256]{1,0:T(8,128)} %get-tuple-element.47) | copy-start | bytes 786436
Sparse Core Ops, SparseCore 0:
  10.8 63.3 all-gather.8
  76.5 345.0 reduce-scatter.1
  427.4 112.4 all-reduce.4
  603.6 64.1 all-gather.4
  672.4 59.0 all-gather.6
  738.0 107.3 all-reduce.6
where the time goes:
time: 935 us; the launch traced here: 924 us
  waiting for transfers between devices  744 us (80%)
  other arithmetic  112 us (12%)
  matrix products  34.3 us (4%)
  between operations  18.2 us (2%)
  local copies, waits for them, and re-layouts  12.1 us (1%)
    reduce_scatter x1, waiting for transfers between devices, form_gram(): lax.psum_scatter(product / samples_total, 'smp', scatter_dimension=0, til...  347 us
    all_gather x3, waiting for transfers between devices, apply_gram(): lax.all_gather(vectors, 'smp', axis=0, tiled=True)  172 us
    psum x1, waiting for transfers between devices, orthonormal(): inner = lax.psum(column_inner(image, image), 'smp')  114 us
    psum x1, waiting for transfers between devices, iterate(): lax.psum((column_inner(image, image), column_inner(image, second)), 'smp')  110 us
    another operation x7, other arithmetic, iterate(): lower = jnp.linalg.cholesky(inner)  34.8 us
    another operation x6, other arithmetic, orthonormal(): lower = jnp.linalg.cholesky(inner)  34 us
    another operation x4, other arithmetic, orthonormal(): lax.linalg.triangular_solve(lower, image, left_side=False, lower=True, tr...  20.4 us
    another operation x2, other arithmetic, iterate(): lax.linalg.triangular_solve(lower, image, left_side=False, lower=True, tr...  19.7 us
  transfers between devices with their start and end apart: 6, of which 6 were waited for; matrix products, arithmetic and copies ran while one was open for 2% of the time, Pallas kernels for 0%

commit v1 on v0

v1 whole, which is shorter than its diff:
```python
import functools
import math

import jax
import jax.numpy as jnp
from jax import lax
from jax.experimental import pallas as pl
from jax.experimental.pallas import tpu as pltpu
from jax.sharding import PartitionSpec as P

LANES = 128
SUBLANES = 8
VMEM_LIMIT = 48 * 1024 * 1024
HIGHEST = lax.Precision.HIGHEST


def stage_bits(groups, flip):
    count = groups.bit_length() - 1
    bits = list(range(count))
    if flip and count >= 2:
        bits[0], bits[1] = bits[1], bits[0]
    stages = [[bit] for bit in bits[:2]]
    rest = bits[2:]
    while rest:
        stages.append(rest[:2])
        rest = rest[2:]
    return stages


def offsets(bits):
    found = [0]
    for bit in bits:
        found = found + [value ^ (1 << bit) for value in found]
    return found


def relative_order(stages):
    order = [0]
    for bits in reversed(stages):
        order = [high ^ low for high in offsets(bits) for low in order]
    return order


def exchange(value, groups, offset):
    return lax.ppermute(value, "smp", [(device, device ^ offset) for device in range(groups)])


def reduce_chunks(keep, send, groups, stages):
    total = keep + exchange(send, groups, 1 << stages[0][0])
    for bits in stages[1:]:
        spans = offsets(bits)
        width = total.shape[0] // len(spans)
        arrived = [
            exchange(total[place * width : (place + 1) * width], groups, span)
            for place, span in enumerate(spans)
            if place > 0
        ]
        total = total[:width]
        for part in arrived:
            total = total + part
    return total


def gather_chunks(chunk, groups, stages):
    held = chunk
    for bits in reversed(stages[1:]):
        held = jnp.concatenate([held] + [exchange(held, groups, span) for span in offsets(bits)[1:]], axis=0)
    return held, exchange(held, groups, 1 << stages[0][0])


def split_pieces(value, pieces):
    parts = []
    rest = value
    for piece in range(pieces):
        part = rest.astype(jnp.bfloat16)
        parts.append(part)
        if piece + 1 < pieces:
            rest = rest - part.astype(jnp.float32)
    return parts


def apply_kernel(
    order, pieces, scale, place_ref, size_ref, near_ref, far_ref, rows_ref, keep_ref, send_ref, split_ref, total_ref
):
    step = pl.program_id(0)
    half, width = near_ref.shape[1:]
    me = place_ref[0]

    def columns(offset):
        return pl.ds(pl.multiple_of(jnp.bitwise_xor(me, offset) * width, width), width)

    middle = len(order) // 2

    @pl.when(step == 0)
    def _():
        for place, offset in enumerate(order):
            value = near_ref[place] if place < middle else far_ref[place - middle]
            for piece, part in enumerate(split_pieces(value, pieces)):
                split_ref[pl.ds(piece * half, half), columns(offset)] = part

    rows = rows_ref[...]
    image = lax.dot_general(
        split_ref[...], rows, (((1,), (1,)), ((), ())), preferred_element_type=jnp.float32
    )
    image = sum(image[piece * half : (piece + 1) * half] for piece in range(pieces))
    back = jnp.dot(
        jnp.concatenate(split_pieces(image, pieces), axis=0), rows, preferred_element_type=jnp.float32
    )
    back = sum(back[piece * half : (piece + 1) * half] for piece in range(pieces))

    @pl.when(step == 0)
    def _():
        total_ref[...] = back

    @pl.when(step > 0)
    def _():
        total_ref[...] += back

    @pl.when(step == pl.num_programs(0) - 1)
    def _():
        for place, offset in enumerate(order):
            first = jnp.bitwise_xor(me, offset) * width
            live = first + lax.broadcasted_iota(jnp.int32, (half, width), 1) < size_ref[0]
            value = jnp.where(live, total_ref[:, columns(offset)] * scale, 0.0)
            if place < middle:
                keep_ref[place] = value
            else:
                send_ref[place - middle] = value


def apply_samples(genotypes, size, me, near, far, order, pieces, scale):
    samples, cap = genotypes.shape
    count, half, width = near.shape
    block = min(256, samples)
    whole = pl.BlockSpec((count, half, width), lambda step: (0, 0, 0))
    scalar = pl.BlockSpec(memory_space=pltpu.SMEM)
    out = jax.ShapeDtypeStruct(near.shape, jnp.float32)
    return pl.pallas_call(
        functools.partial(apply_kernel, order, pieces, scale),
        grid=(samples // block,),
        in_specs=[scalar, scalar, whole, whole, pl.BlockSpec((block, cap), lambda step: (step, 0))],
        out_specs=[whole, whole],
        out_shape=[out, out],
        scratch_shapes=[
            pltpu.VMEM((pieces * half, cap), jnp.bfloat16),
            pltpu.VMEM((half, cap), jnp.float32),
        ],
        compiler_params=pltpu.CompilerParams(vmem_limit_bytes=VMEM_LIMIT),
        cost_estimate=pl.CostEstimate(
            flops=4 * samples * cap * half * pieces,
            bytes_accessed=2 * samples * cap + 16 * half * cap,
            transcendentals=0,
        ),
    )(me, size, near, far, genotypes)


def full_rows(place_ref, orders, pairs, target_ref):
    me = place_ref[0]
    for chain, (order, (near_ref, far_ref)) in enumerate(zip(orders, pairs)):
        half, width = near_ref.shape[1:]
        middle = len(order) // 2
        for place, offset in enumerate(order):
            first = pl.multiple_of(jnp.bitwise_xor(me, offset) * width, width)
            value = near_ref[place] if place < middle else far_ref[place - middle]
            target_ref[pl.ds(chain * half, half), pl.ds(first, width)] = value


def lane_splat(tile, lane):
    return jnp.broadcast_to(tile[:, lane : lane + 1], (SUBLANES, LANES))


def row_splat(tile, row):
    return jnp.broadcast_to(tile[row : row + 1, :], (SUBLANES, LANES))


def inverse_factor(work_ref, size, panel):
    tiles = 2 * size // LANES
    below = lax.broadcasted_iota(jnp.int32, (SUBLANES, LANES), 0)
    groups = panel // SUBLANES
    for top in range(0, size, panel):
        active = [
            tile
            for tile in range(tiles)
            if (top // LANES <= tile < size // LANES)
            or (size // LANES <= tile <= size // LANES + (top + panel - 1) // LANES)
        ]
        rows = [
            {
                tile: work_ref[top + SUBLANES * group : top + SUBLANES * (group + 1), tile * LANES : (tile + 1) * LANES]
                for tile in active
            }
            for group in range(groups)
        ]
        for block in range(groups):
            base = top + SUBLANES * block
            columns = {
                group: [lane_splat(rows[group][base // LANES], base % LANES + lane) for lane in range(SUBLANES)]
                for group in range(block, groups)
            }
            for step in range(SUBLANES):
                pivot = row_splat(columns[block][step], step)
                root = lax.rsqrt(pivot)
                root = root * (1.5 - 0.5 * pivot * root * root)
                factor = {group: columns[group][step] * root for group in range(block, groups)}
                for later in range(step + 1, SUBLANES):
                    weight = row_splat(factor[block], later)
                    for group in range(block, groups):
                        columns[group][later] = columns[group][later] - factor[group] * weight
                lower = jnp.where(below > step, factor[block], 0.0)
                for tile in active:
                    line = row_splat(rows[block][tile], step) * root
                    rows[block][tile] = jnp.where(
                        below == step, line, rows[block][tile] - lower * line
                    )
                    for group in range(block + 1, groups):
                        rows[group][tile] = rows[group][tile] - factor[group] * line
        for group in range(groups):
            for tile in active:
                work_ref[top + SUBLANES * group : top + SUBLANES * (group + 1), tile * LANES : (tile + 1) * LANES] = rows[
                    group
                ][tile]
        rest = top + panel
        if rest < size:
            first, last = active[0] * LANES, (active[-1] + 1) * LANES
            lines = work_ref[top:rest, first:last]
            weights = work_ref[top:rest, rest // LANES * LANES : size].T[rest % LANES :, :]
            work_ref[rest:, first:last] -= jnp.dot(
                weights, lines, precision=HIGHEST, preferred_element_type=jnp.float32
            )


def start_factor(work_ref, inner):
    size = inner.shape[0]
    work_ref[:, :size] = inner
    row = lax.broadcasted_iota(jnp.int32, (size, size), 0)
    column = lax.broadcasted_iota(jnp.int32, (size, size), 1)
    work_ref[:, size:] = jnp.where(row == column, 1.0, 0.0)


def finish_factor(work_ref):
    size = work_ref.shape[0]
    row = lax.broadcasted_iota(jnp.int32, (size, size), 0)
    column = lax.broadcasted_iota(jnp.int32, (size, size), 1)
    return jnp.where(row >= column, work_ref[:, size:], 0.0)


def rows_inner(value):
    return lax.dot_general(
        value, value, (((1,), (1,)), ((), ())), precision=HIGHEST, preferred_element_type=jnp.float32
    )


def factor_kernel(orders, place_ref, *refs):
    pairs = list(zip(refs[: 2 * len(orders) : 2], refs[1 : 2 * len(orders) : 2]))
    out_ref, full_ref, work_ref = refs[2 * len(orders) :]
    full_rows(place_ref, orders, pairs, full_ref)
    start_factor(work_ref, rows_inner(full_ref[...]))
    inverse_factor(work_ref, work_ref.shape[0], 32)
    out_ref[...] = finish_factor(work_ref)


def first_factor(me, pairs, orders, cap):
    size = sum(near.shape[1] for near, far in pairs)
    return pl.pallas_call(
        functools.partial(factor_kernel, orders),
        in_specs=[pl.BlockSpec(memory_space=pltpu.SMEM)]
        + [pl.BlockSpec(memory_space=pltpu.VMEM)] * (2 * len(pairs)),
        out_specs=pl.BlockSpec(memory_space=pltpu.VMEM),
        out_shape=jax.ShapeDtypeStruct((size, size), jnp.float32),
        scratch_shapes=[pltpu.VMEM((size, cap), jnp.float32), pltpu.VMEM((size, 2 * size), jnp.float32)],
        compiler_params=pltpu.CompilerParams(vmem_limit_bytes=VMEM_LIMIT),
    )(me, *[ref for pair in pairs for ref in pair])


def project_kernel(
    orders, out_orders, pieces, place_ref, *refs
):
    count = 2 * len(orders)
    pairs = list(zip(refs[:count:2], refs[1:count:2]))
    first_ref, rows_ref, image_ref, inner_ref = refs[count : count + 4]
    outs = refs[count + 4 : count + 8]
    full_ref, split_ref, cross_ref = refs[count + 8 :]
    step = pl.program_id(0)
    size = first_ref.shape[0]

    @pl.when(step == 0)
    def _():
        full_rows(place_ref, orders, pairs, full_ref)
        image = jnp.dot(
            first_ref[...], full_ref[...], precision=HIGHEST, preferred_element_type=jnp.float32
        )
        image_ref[...] = image
        inner_ref[...] = rows_inner(image)
        for piece, part in enumerate(split_pieces(image, pieces)):
            split_ref[pl.ds(piece * size, size), :] = part
        cross_ref[...] = jnp.zeros_like(cross_ref)

    sampled = lax.dot_general(
        split_ref[...], rows_ref[...], (((1,), (1,)), ((), ())), preferred_element_type=jnp.float32
    )
    sampled = sum(sampled[piece * size : (piece + 1) * size] for piece in range(pieces))
    cross_ref[...] += rows_inner(sampled)

    @pl.when(step == pl.num_programs(0) - 1)
    def _():
        me = place_ref[0]
        for chain, order in enumerate(out_orders):
            keep_ref, send_ref = outs[2 * chain : 2 * chain + 2]
            height, width = keep_ref.shape[1:]
            middle = len(order) // 2
            for place, offset in enumerate(order):
                first = pl.multiple_of(jnp.bitwise_xor(me, offset) * height, height)
                value = cross_ref[pl.ds(first, height), chain * width : (chain + 1) * width]
                if place < middle:
                    keep_ref[place] = value
                else:
                    send_ref[place - middle] = value


def project(genotypes, me, pairs, orders, out_orders, first, pieces):
    samples, cap = genotypes.shape
    size = first.shape[0]
    block = min(256, samples)
    scalar = pl.BlockSpec(memory_space=pltpu.SMEM)

    def whole(shape):
        return pl.BlockSpec(shape, lambda step: (0,) * len(shape))

    height, width = size // len(out_orders[0]), size // len(out_orders)
    part = (len(out_orders[0]) // 2, height, width)
    return pl.pallas_call(
        functools.partial(project_kernel, orders, out_orders, pieces),
        grid=(samples // block,),
        in_specs=[scalar]
        + [whole(near.shape) for near, far in pairs for _ in range(2)]
        + [whole((size, size)), pl.BlockSpec((block, cap), lambda step: (step, 0))],
        out_specs=[whole((size, cap)), whole((size, size))] + [whole(part)] * (2 * len(out_orders)),
        out_shape=[
            jax.ShapeDtypeStruct((size, cap), jnp.float32),
            jax.ShapeDtypeStruct((size, size), jnp.float32),
        ]
        + [jax.ShapeDtypeStruct(part, jnp.float32)] * (2 * len(out_orders)),
        scratch_shapes=[
            pltpu.VMEM((size, cap), jnp.float32),
            pltpu.VMEM((pieces * size, cap), jnp.bfloat16),
            pltpu.VMEM((size, size), jnp.float32),
        ],
        compiler_params=pltpu.CompilerParams(vmem_limit_bytes=VMEM_LIMIT),
    )(me, *[ref for pair in pairs for ref in pair], first, genotypes)


def second_kernel(inner_ref, out_ref, work_ref):
    start_factor(work_ref, inner_ref[...])
    inverse_factor(work_ref, work_ref.shape[0], 32)
    out_ref[...] = finish_factor(work_ref)


def second_factor(inner):
    size = inner.shape[0]
    return pl.pallas_call(
        second_kernel,
        in_specs=[pl.BlockSpec(memory_space=pltpu.VMEM)],
        out_specs=pl.BlockSpec(memory_space=pltpu.VMEM),
        out_shape=jax.ShapeDtypeStruct((size, size), jnp.float32),
        scratch_shapes=[pltpu.VMEM((size, 2 * size), jnp.float32)],
        compiler_params=pltpu.CompilerParams(vmem_limit_bytes=VMEM_LIMIT),
    )(inner)


def to_natural(pair, order, me):
    places = jnp.argsort(jnp.array(order, jnp.int32))
    mine = jnp.bitwise_xor(jnp.arange(len(order), dtype=jnp.int32), me)
    stacked = jnp.concatenate(pair, axis=0)[places][mine]
    rows = jnp.transpose(stacked, (1, 0, 2)).reshape(1, stacked.shape[1], -1)
    return tuple(jnp.split(rows, 2, axis=2))


def to_relative(pair, order, me, width):
    rows = jnp.concatenate(pair, axis=2)[0]
    chunks = jnp.transpose(rows.reshape(rows.shape[0], -1, width), (1, 0, 2))
    chunks = chunks[jnp.bitwise_xor(jnp.array(order, jnp.int32), me)]
    return tuple(jnp.split(chunks, 2, axis=0))


def stacked_rows(pair, order, me):
    places = jnp.argsort(jnp.array(order, jnp.int32))
    mine = jnp.bitwise_xor(jnp.arange(len(order), dtype=jnp.int32), me)
    stacked = jnp.concatenate(pair, axis=0)[places][mine]
    return stacked.reshape(-1, stacked.shape[2])


def cut_rows(pair, order, me, height):
    rows = jnp.concatenate(pair, axis=0).reshape(-1, height, pair[0].shape[2])
    return tuple(jnp.split(rows[jnp.bitwise_xor(jnp.array(order, jnp.int32), me)], 2, axis=0))


def body(genotypes, sizes, start):
    groups = lax.axis_size("smp")
    dosages = genotypes[0]
    samples, cap = dosages.shape
    width, size = start.shape[1:]
    half = size // 2
    scale = 1.0 / (samples * groups)
    me = lax.axis_index("smp")
    where = me.reshape(1).astype(jnp.int32)
    chains = [stage_bits(groups, flip) for flip in (False, True)]
    orders = [relative_order(stages) for stages in chains]

    first_row = me * width
    live = first_row + lax.broadcasted_iota(jnp.int32, (width, size), 0) < sizes[0]
    columns = jnp.where(live, start[0], 0.0).T
    chunks = [columns[chain * half : (chain + 1) * half][None] for chain in range(2)]

    aligned = width % LANES == 0 and (size // groups) % SUBLANES == 0
    plain = [[0, 1]] * 2

    def gather(chunk, chain):
        pair = gather_chunks(chunk, groups, chains[chain])
        return pair if aligned else to_natural(pair, orders[chain], me)

    place = where if aligned else jnp.zeros_like(where)
    laid = orders if aligned else plain

    def apply(chunk, chain):
        pair = gather(chunk, chain)
        out = apply_samples(dosages, sizes, place, *pair, laid[chain], 3, scale)
        if not aligned:
            out = to_relative(out, orders[chain], me, width)
        return pair, reduce_chunks(*out, groups, chains[chain])

    images = [apply(chunks[chain], chain)[1] for chain in range(2)]
    done = [apply(images[chain], chain) for chain in range(2)]
    first = first_factor(place, [pair for pair, _ in done], laid, cap)
    pairs = [gather(done[chain][1], chain) for chain in range(2)]
    image, inner, *cross = project(dosages, place, pairs, laid, laid, first, 3)
    crossed = []
    for chain in range(2):
        part = tuple(cross[2 * chain : 2 * chain + 2])
        if not aligned:
            part = cut_rows(part, orders[chain], me, size // groups)
        part = gather_chunks(reduce_chunks(*part, groups, chains[chain]), groups, chains[chain])
        crossed.append(stacked_rows(part, orders[chain], me))
    crossed = jnp.concatenate(crossed, axis=1)
    second = second_factor(inner)
    own = lax.dynamic_slice(image, (0, first_row), (size, width))
    basis = jnp.dot(second, own, precision=HIGHEST, preferred_element_type=jnp.float32).T * math.sqrt(cap)
    rayleigh = jnp.dot(
        jnp.dot(second, crossed, precision=HIGHEST, preferred_element_type=jnp.float32),
        second.T,
        precision=HIGHEST,
        preferred_element_type=jnp.float32,
    ) * scale
    blocks = lax.axis_size("blk")
    partial = jnp.broadcast_to(jnp.trace(rayleigh), (SUBLANES, LANES))
    total = partial
    for shift in range(1, blocks):
        total = total + lax.ppermute(partial, "blk", [(block, (block + shift) % blocks) for block in range(blocks)])
    scaled = rayleigh * (genotypes.shape[0] * blocks * size) / total[0, 0]
    return basis[None], scaled[None]


def solution(mesh):
    return jax.shard_map(
        body,
        mesh=mesh,
        in_specs=(P("blk", "smp", None), P("blk"), P("blk", "smp", None)),
        out_specs=(P("blk", "smp", None), P("blk", None, None)),
        check_vma=False,
    )
```

time: 935 us -> 261 us (0.28); the launches traced: 924 us -> 261 us
  waiting for transfers between devices: 744 us -> 70.6 us
  other arithmetic: 112 us -> 2.62 us
  starting transfers between devices: 0.42 us -> 102 us
  Pallas kernels: 0 us -> 75.6 us
  matrix products: 34.3 us -> 2.45 us
  between operations: 18.2 us -> 1.96 us
    reduce_scatter x1 -> x0, waiting for transfers between devices: 347 us -> none  [form_gram(): lax.psum_scatter(product / samples_total, 'smp', scatter_dimension=0, til...]
    psum x2 -> x0, waiting for transfers between devices: 224 us -> none  [the longest x1 114 us: orthonormal(): inner = lax.psum(column_inner(image, image), 'smp')]
    all_gather x3 -> x0, waiting for transfers between devices: 172 us -> none  [apply_gram(): lax.all_gather(vectors, 'smp', axis=0, tiled=True)]
    another operation x19 -> x0, other arithmetic: 109 us -> none  [the longest x7 34.8 us: iterate(): lower = jnp.linalg.cholesky(inner)]
    ppermute x0 -> x71, starting transfers between devices: none -> 102 us  [the longest x70 102 us: exchange(): lax.ppermute(value, 'smp', [(device, device ^ offset) for device in range...]
    pallas_call x0 -> x7, Pallas kernels: none -> 75.6 us  [the longest x4 39.3 us: apply_samples(): pl.pallas_call(functools.partial(apply_kernel, order, pieces, scale), gri...]
    ppermute x0 -> x71, waiting for transfers between devices: none -> 70.6 us  [the longest x70 70.5 us: exchange(): lax.ppermute(value, 'smp', [(device, device ^ offset) for device in range...]
    dot_general x7 -> x3, matrix products: 29.8 us -> 2.45 us  [the longest x1 1.06 us: body(): jnp.dot(second, own, precision=HIGHEST, preferred_element_type=jnp.float32)]
  transfers between devices with their start and end apart: 6 -> 71, of which waited for: 6 -> 25; matrix products, arithmetic and copies ran while one was open for 2% -> 1% of each run, Pallas kernels for 0% -> 24%
where the time goes in v1:
time: 261 us
  starting transfers between devices  102 us (39%)
  Pallas kernels  75.6 us (29%)
  waiting for transfers between devices  70.6 us (27%)
  local copies, waits for them, and re-layouts  4.93 us (2%)
  other arithmetic  2.62 us (1%)
    ppermute x70, starting transfers between devices, exchange(): lax.ppermute(value, 'smp', [(device, device ^ offset) for device in range...  102 us
    ppermute x70, waiting for transfers between devices, exchange(): lax.ppermute(value, 'smp', [(device, device ^ offset) for device in range...  70.5 us
    pallas_call x4, Pallas kernels, apply_samples(): pl.pallas_call(functools.partial(apply_kernel, order, pieces, scale), gri...  39.3 us
    pallas_call x1, Pallas kernels, first_factor(): pl.pallas_call(functools.partial(factor_kernel, orders), in_specs=[pl.Blo...  13.2 us
    pallas_call x1, Pallas kernels, project(): pl.pallas_call(functools.partial(project_kernel, orders, out_orders, piec...  13 us
    pallas_call x1, Pallas kernels, second_factor(): pl.pallas_call(second_kernel, in_specs=[pl.BlockSpec(memory_space=pltpu.V...  10.2 us
  transfers between devices with their start and end apart: 71, of which 25 were waited for; matrix products, arithmetic and copies ran while one was open for 1% of the time, Pallas kernels for 24%

profile of v1, /device:TPU:0, one launch (start us, length us, event | category | flops | bytes accessed | tf_op | source)
XLA Modules:
  0.0 260.6 jit_solution(6300721935841324066)
XLA Ops:
  2.3 3.1 %collective-permute-start.25 = (f32[1,128,128]{2,1,0:T(8,128)S(1)}, f32[1,128,128]{2,1,0:T(8,128)S(1)}, u32[]{:S(2)}, u32[]{:S(2)}) collective-permute-start(f32[1,128,128]{2,1,0:T(8,128)S(1)} %get-tuple-element.58), channel_id=1, source_target_pairs={{0,4},{1,5},{2,6},{3,7},{4,0},{5,1},{6,2},{7,3},{8,12},{9,13},{10,... | collective-permute-start | bytes 196616 | tf_op jit(solution)/shard_map/ppermute | solution.py:45
  5.4 2.6 collective-permute-start.26
  8.9 3.5 %collective-permute-start.1 = (f32[1,128,128]{2,1,0:T(8,128)S(1)}, f32[1,128,128]{2,1,0:T(8,128)S(1)}, u32[]{:S(2)}, u32[]{:S(2)}) collective-permute-start(f32[1,128,128]{2,1,0:T(8,128)S(1)} %get-tuple-element.59), channel_id=1, source_target_pairs={{0,8},{1,9},{2,10},{3,11},{4,12},{5,13},{6,14},{7,15},{8,0},{9,1},... | collective-permute-start | bytes 196616 | tf_op jit(solution)/shard_map/ppermute | solution.py:45
  12.8 1.8 collective-permute-done.27
  16.2 2.8 %collective-permute-done.1 = f32[1,128,128]{2,1,0:T(8,128)S(1)} collective-permute-done((f32[1,128,128]{2,1,0:T(8,128)S(1)}, f32[1,128,128]{2,1,0:T(8,128)S(1)}, u32[]{:S(2)}, u32[]{:S(2)}) %collective-permute-start.1) | collective-permute-done | bytes 65568 | tf_op jit(solution)/shard_map/ppermute | solution.py:45
  19.0 1.6 collective-permute-start.3
  22.7 5.7 %collective-permute-done.3 = f32[4,128,128]{2,1,0:T(8,128)S(1)} collective-permute-done((f32[4,128,128]{2,1,0:T(8,128)S(1)}, f32[4,128,128]{2,1,0:T(8,128)S(1)}, u32[]{:S(2)}, u32[]{:S(2)}) %collective-permute-start.3) | collective-permute-done | bytes 262176 | tf_op jit(solution)/shard_map/ppermute | solution.py:45
  29.9 6.2 %collective-permute-done.29.far_ref = f32[8,128,128]{2,1,0:T(8,128)S(1)} collective-permute-done((f32[8,128,128]{2,1,0:T(8,128)S(1)}, f32[8,128,128]{2,1,0:T(8,128)S(1)}, u32[]{:S(2)}, u32[]{:S(2)}) %collective-permute-start.29) | collective-permute-done | bytes 524320 | tf_op jit(solution)/shard_map/ppermute | solution.py:45
  36.2 9.8 %shard_map.70 = (f32[8,128,128]{2,1,0:T(8,128)S(1)}, f32[8,128,128]{2,1,0:T(8,128)S(1)}) custom-call(s32[1]{0:T(128)} %bitcast.place_ref, s32[1]{0:T(128)} %copy.50.size_ref, f32[8,128,128]{2,1,0:T(8,128)S(1)} %constant_dynamic-update-slice_fusion.15.near_ref, f32[8,128,128]{2,1,0:T(8,128)S(1)} %collective-permute-done.29.far_ref, bf16[1024,2048]{1,0:T(8,128)(2,1)} %bitcast.31), custom_call_target="tpu_custom_call" | custom-call | flops 3221225472 | bytes 8388608 | tf_op jit(solution)/shard_map/pallas_call | solution.py:138
  47.5 9.8 %shard_map.68 = (f32[8,128,128]{2,1,0:T(8,128)S(1)}, f32[8,128,128]{2,1,0:T(8,128)S(1)}) custom-call(s32[1]{0:T(128)} %bitcast.place_ref, s32[1]{0:T(128)} %copy.50.size_ref, f32[8,128,128]{2,1,0:T(8,128)S(1)} %constant_dynamic-update-slice_fusion.near_ref, f32[8,128,128]{2,1,0:T(8,128)S(1)} %collective-permute-done.4.far_ref, bf16[1024,2048]{1,0:T(8,128)(2,1)} %bitcast.32), custom_call_target="tpu_custom_call" | custom-call | flops 3221225472 | bytes 8388608 | tf_op jit(solution)/shard_map/pallas_call | solution.py:138
  59.5 10.9 %collective-permute-done.5 = f32[8,128,128]{2,1,0:T(8,128)S(1)} collective-permute-done((f32[8,128,128]{2,1,0:T(8,128)S(1)}, f32[8,128,128]{2,1,0:T(8,128)S(1)}, u32[]{:S(2)}, u32[]{:S(2)}) %collective-permute-start.5) | collective-permute-done | bytes 524320 | tf_op jit(solution)/shard_map/ppermute | solution.py:45
  71.1 2.2 collective-permute-done.31
  73.3 4.1 %collective-permute-start.32 = (f32[1,128,128]{2,1,0:T(8,128)S(1)}, f32[1,128,128]{2,1,0:T(8,128)S(1)}, u32[]{:S(2)}, u32[]{:S(2)}) collective-permute-start(f32[1,128,128]{2,1,0:T(8,128)S(1)} %get-tuple-element.49), channel_id=1, source_target_pairs={{0,4},{1,5},{2,6},{3,7},{4,0},{5,1},{6,2},{7,3},{8,12},{9,13},{10,... | collective-permute-start | bytes 196616 | tf_op jit(solution)/shard_map/ppermute | solution.py:45
  77.8 2.1 collective-permute-start.34
  82.3 2.1 collective-permute-start.9
  84.4 1.8 collective-permute-done.33
  86.2 5.8 %collective-permute-start.35 = (f32[1,128,128]{2,1,0:T(8,128)S(1)}, f32[1,128,128]{2,1,0:T(8,128)S(1)}, u32[]{:S(2)}, u32[]{:S(2)}) collective-permute-start(f32[1,128,128]{2,1,0:T(8,128)S(1)} %get-tuple-element.41), channel_id=1, source_target_pairs={{0,4},{1,5},{2,6},{3,7},{4,0},{5,1},{6,2},{7,3},{8,12},{9,13},{10,... | collective-permute-start | bytes 196616 | tf_op jit(solution)/shard_map/ppermute | solution.py:45
  92.0 2.4 collective-permute-start.37
  96.5 2.4 collective-permute-start.12
  103.3 4.9 %collective-permute-done.38 = f32[4,128,128]{2,1,0:T(8,128)S(1)} collective-permute-done((f32[4,128,128]{2,1,0:T(8,128)S(1)}, f32[4,128,128]{2,1,0:T(8,128)S(1)}, u32[]{:S(2)}, u32[]{:S(2)}) %collective-permute-start.38) | collective-permute-done | bytes 262176 | tf_op jit(solution)/shard_map/ppermute | solution.py:45
  110.7 7.7 %collective-permute-done.39.far_ref.refs_3_ = f32[8,128,128]{2,1,0:T(8,128)S(1)} collective-permute-done((f32[8,128,128]{2,1,0:T(8,128)S(1)}, f32[8,128,128]{2,1,0:T(8,128)S(1)}, u32[]{:S(2)}, u32[]{:S(2)}) %collective-permute-start.39) | collective-permute-done | bytes 524320 | tf_op jit(solution)/shard_map/ppermute | solution.py:45
  118.4 9.8 %shard_map.71 = (f32[8,128,128]{2,1,0:T(8,128)S(1)}, f32[8,128,128]{2,1,0:T(8,128)S(1)}) custom-call(s32[1]{0:T(128)} %bitcast.place_ref, s32[1]{0:T(128)} %copy.50.size_ref, f32[8,128,128]{2,1,0:T(8,128)S(1)} %constant_dynamic-update-slice_fusion.20.near_ref.refs_2_, f32[8,128,128]{2,1,0:T(8,128)S(1)} %collective-permute-done.39.far_ref.refs_3_, ...), custom_call_target="tpu_custom_call" | custom-call | flops 3221225472 | bytes 8388608 | tf_op jit(solution)/shard_map/pallas_call | solution.py:138
  128.8 10.0 %shard_map.69 = (f32[8,128,128]{2,1,0:T(8,128)S(1)}, f32[8,128,128]{2,1,0:T(8,128)S(1)}) custom-call(s32[1]{0:T(128)} %bitcast.place_ref, s32[1]{0:T(128)} %copy.50.size_ref, f32[8,128,128]{2,1,0:T(8,128)S(1)} %constant_dynamic-update-slice_fusion.5.near_ref.refs_0_, f32[8,128,128]{2,1,0:T(8,128)S(1)} %collective-permute-done.14.far_ref.refs_1_, ...), custom_call_target="tpu_custom_call" | custom-call | flops 3221225472 | bytes 8388608 | tf_op jit(solution)/shard_map/pallas_call | solution.py:138
  141.0 7.0 %collective-permute-done.15 = f32[8,128,128]{2,1,0:T(8,128)S(1)} collective-permute-done((f32[8,128,128]{2,1,0:T(8,128)S(1)}, f32[8,128,128]{2,1,0:T(8,128)S(1)}, u32[]{:S(2)}, u32[]{:S(2)}) %collective-permute-start.15) | collective-permute-done | bytes 524320 | tf_op jit(solution)/shard_map/ppermute | solution.py:45
  150.9 2.3 collective-permute-start.43
  153.3 2.0 collective-permute-start.44
  155.5 2.3 collective-permute-start.18
  157.8 2.0 collective-permute-start.19
  159.9 2.3 collective-permute-start.46
  162.3 2.0 collective-permute-start.47
  164.4 2.3 collective-permute-start.21
  166.8 2.0 collective-permute-start.22
  170.3 2.5 collective-permute-done.22
  176.8 2.5 collective-permute-done.23
  180.9 13.2 %shard_map.72.refs_4_ = f32[256,256]{1,0:T(8,128)S(1)} custom-call(s32[1]{0:T(128)} %bitcast.place_ref, f32[8,128,128]{2,1,0:T(8,128)S(1)} %constant_dynamic-update-slice_fusion.5.near_ref.refs_0_, f32[8,128,128]{2,1,0:T(8,128)S(1)} %collective-permute-done.14.far_ref.refs_1_, f32[8,128,128]{2,1,0:T(8,128)S(1)} %constant_dynamic-update-slice_fusion.20.near_ref.refs_2_, ...), custom_call_target="tpu_custom_call" | custom-call | tf_op jit(solution)/shard_map/pallas_call | solution.py:264
  194.1 13.0 %shard_map.73 = (f32[256,2048]{1,0:T(8,128)S(1)}, f32[256,256]{1,0:T(8,128)S(1)}, f32[8,16,128]{2,1,0:T(8,128)S(1)}, f32[8,16,128]{2,1,0:T(8,128)S(1)}, f32[8,16...) custom-call(s32[1]{0:T(128)} %bitcast.place_ref, f32[8,128,128]{2,1,0:T(8,128)S(1)} %constant_dynamic-update-slice_fusion.10.refs_0_, ...), custom_call_target="tpu_custom_call" | custom-call | tf_op jit(solution)/shard_map/pallas_call | solution.py:331
  209.2 2.2 collective-permute-done.50
  213.0 10.2 %shard_map.74 = f32[256,256]{1,0:T(8,128)S(1)} custom-call(f32[256,256]{1,0:T(8,128)S(1)} %get-tuple-element.27.inner_ref), custom_call_target="tpu_custom_call" | custom-call | tf_op jit(solution)/shard_map/pallas_call | solution.py:360
  223.9 2.5 collective-permute-start.53
  226.5 1.8 collective-permute-start.54
  228.4 2.5 collective-permute-start.63
  231.0 1.8 collective-permute-start.64
  232.9 2.5 collective-permute-start.56
  235.4 1.8 collective-permute-start.57
  237.4 2.5 collective-permute-start.66
  239.9 1.8 collective-permute-start.67
  242.4 3.0 %collective-permute-done.67 = f32[1,16,128]{2,1,0:T(8,128)S(1)} collective-permute-done((f32[1,16,128]{2,1,0:T(8,128)S(1)}, f32[1,16,128]{2,1,0:T(8,128)S(1)}, u32[]{:S(2)}, u32[]{:S(2)}) %collective-permute-start.67) | collective-permute-done | bytes 8224 | tf_op jit(solution)/shard_map/ppermute | solution.py:45
  247.5 1.8 collective-permute-done.68
  (199 shorter events, 55.5 us)
Async XLA Ops:
  2.3 10.1 %collective-permute-start.25 = (f32[1,128,128]{2,1,0:T(8,128)S(1)}, f32[1,128,128]{2,1,0:T(8,128)S(1)}, u32[]{:S(2)}, u32[]{:S(2)}) collective-permute-start(f32[1,128,128]{2,1,0:T(8,128)S(1)} %get-tuple-element.58), channel_id=1, source_target_pairs={{0,4},{1,5},{2,6},{3,7},{4,0},{5,1},{6,2},{7,3},{8,12},{9,13},{10,... | collective-permute-start | bytes 196616 | tf_op jit(solution)/shard_map/ppermute | solution.py:45
  5.4 7.4 %collective-permute-start.26 = (f32[1,128,128]{2,1,0:T(8,128)S(1)}, f32[1,128,128]{2,1,0:T(8,128)S(1)}, u32[]{:S(2)}, u32[]{:S(2)}) collective-permute-start(f32[1,128,128]{2,1,0:T(8,128)S(1)} %get-tuple-element.58), channel_id=1, source_target_pairs={{0,8},{1,9},{2,10},{3,11},{4,12},{5,13},{6,14},{7,15},{8,0},{9,1},... | collective-permute-start | bytes 196616 | tf_op jit(solution)/shard_map/ppermute | solution.py:45
  8.0 6.6 %collective-permute-start.27 = (f32[1,128,128]{2,1,0:T(8,128)S(1)}, f32[1,128,128]{2,1,0:T(8,128)S(1)}, u32[]{:S(2)}, u32[]{:S(2)}) collective-permute-start(f32[1,128,128]{2,1,0:T(8,128)S(1)} %get-tuple-element.58), channel_id=1, source_target_pairs={{0,12},{1,13},{2,14},{3,15},{4,8},{5,9},{6,10},{7,11},{8,4},{9,5},... | collective-permute-start | bytes 196616 | tf_op jit(solution)/shard_map/ppermute | solution.py:45
  8.0 8.2 %collective-permute-start = (f32[1,128,128]{2,1,0:T(8,128)S(1)}, f32[1,128,128]{2,1,0:T(8,128)S(1)}, u32[]{:S(2)}, u32[]{:S(2)}) collective-permute-start(f32[1,128,128]{2,1,0:T(8,128)S(1)} %get-tuple-element.59), channel_id=1, source_target_pairs={{0,4},{1,5},{2,6},{3,7},{4,0},{5,1},{6,2},{7,3},{8,12},{9,13},{10,... | collective-permute-start | bytes 196616 | tf_op jit(solution)/shard_map/ppermute | solution.py:45
  8.9 10.1 %collective-permute-start.1 = (f32[1,128,128]{2,1,0:T(8,128)S(1)}, f32[1,128,128]{2,1,0:T(8,128)S(1)}, u32[]{:S(2)}, u32[]{:S(2)}) collective-permute-start(f32[1,128,128]{2,1,0:T(8,128)S(1)} %get-tuple-element.59), channel_id=1, source_target_pairs={{0,8},{1,9},{2,10},{3,11},{4,12},{5,13},{6,14},{7,15},{8,0},{9,1},... | collective-permute-start | bytes 196616 | tf_op jit(solution)/shard_map/ppermute | solution.py:45
  12.4 6.6 %collective-permute-start.2 = (f32[1,128,128]{2,1,0:T(8,128)S(1)}, f32[1,128,128]{2,1,0:T(8,128)S(1)}, u32[]{:S(2)}, u32[]{:S(2)}) collective-permute-start(f32[1,128,128]{2,1,0:T(8,128)S(1)} %get-tuple-element.59), channel_id=1, source_target_pairs={{0,12},{1,13},{2,14},{3,15},{4,8},{5,9},{6,10},{7,11},{8,4},{9,5},... | collective-permute-start | bytes 196616 | tf_op jit(solution)/shard_map/ppermute | solution.py:45
  19.0 9.3 %collective-permute-start.3 = (f32[4,128,128]{2,1,0:T(8,128)S(1)}, f32[4,128,128]{2,1,0:T(8,128)S(1)}, u32[]{:S(2)}, u32[]{:S(2)}) collective-permute-start(f32[4,128,128]{2,1,0:T(8,128)S(1)} %pad_maximum_fusion), channel_id=1, source_target_pairs={{0,2},{1,3},{2,0},{3,1},{4,6},{5,7},{6,4},{7,5},{8,10},{9,11},{10,... | collective-permute-start | bytes 786440 | tf_op jit(solution)/shard_map/ppermute | solution.py:45
  21.1 15.1 %collective-permute-start.29 = (f32[8,128,128]{2,1,0:T(8,128)S(1)}, f32[8,128,128]{2,1,0:T(8,128)S(1)}, u32[]{:S(2)}, u32[]{:S(2)}) collective-permute-start(f32[8,128,128]{2,1,0:T(8,128)S(1)} %constant_dynamic-update-slice_fusion.15.near_ref), channel_id=1, source_target_pairs={{0,2},{1,3},{2,0},{3,1},{4,6},{5,7},{6,4},{7,5},{8,10},{9,11},{10,... | collective-permute-start | bytes 1572872 | tf_op jit(solution)/shard_map/ppermute | solution.py:45
  28.4 19.2 %collective-permute-start.4 = (f32[8,128,128]{2,1,0:T(8,128)S(1)}, f32[8,128,128]{2,1,0:T(8,128)S(1)}, u32[]{:S(2)}, u32[]{:S(2)}) collective-permute-start(f32[8,128,128]{2,1,0:T(8,128)S(1)} %constant_dynamic-update-slice_fusion.near_ref), channel_id=1, source_target_pairs={{0,1},{1,0},{2,3},{3,2},{4,5},{5,4},{6,7},{7,6},{8,9},{9,8},{10,11... | collective-permute-start | bytes 1572872 | tf_op jit(solution)/shard_map/ppermute | solution.py:45
  45.9 12.9 %collective-permute-start.30 = (f32[8,128,128]{2,1,0:T(8,128)S(1)}, f32[8,128,128]{2,1,0:T(8,128)S(1)}, u32[]{:S(2)}, u32[]{:S(2)}) collective-permute-start(f32[8,128,128]{2,1,0:T(8,128)S(1)} %get-tuple-element.23), channel_id=1, source_target_pairs={{0,2},{1,3},{2,0},{3,1},{4,6},{5,7},{6,4},{7,5},{8,10},{9,11},{10,... | collective-permute-start | bytes 1572872 | tf_op jit(solution)/shard_map/ppermute | solution.py:45
  57.3 13.1 %collective-permute-start.5 = (f32[8,128,128]{2,1,0:T(8,128)S(1)}, f32[8,128,128]{2,1,0:T(8,128)S(1)}, u32[]{:S(2)}, u32[]{:S(2)}) collective-permute-start(f32[8,128,128]{2,1,0:T(8,128)S(1)} %get-tuple-element.19), channel_id=1, source_target_pairs={{0,1},{1,0},{2,3},{3,2},{4,5},{5,4},{6,7},{7,6},{8,9},{9,8},{10,11... | collective-permute-start | bytes 1572872 | tf_op jit(solution)/shard_map/ppermute | solution.py:45
  58.9 14.3 %collective-permute-start.31 = (f32[4,128,128]{2,1,0:T(8,128)S(1)}, f32[4,128,128]{2,1,0:T(8,128)S(1)}, u32[]{:S(2)}, u32[]{:S(2)}) collective-permute-start(f32[4,128,128]{2,1,0:T(8,128)S(1)} %slice.179), channel_id=1, source_target_pairs={{0,1},{1,0},{2,3},{3,2},{4,5},{5,4},{6,7},{7,6},{8,9},{9,8},{10,11... | collective-permute-start | bytes 786440 | tf_op jit(solution)/shard_map/ppermute | solution.py:45
  70.5 9.4 %collective-permute-start.6 = (f32[4,128,128]{2,1,0:T(8,128)S(1)}, f32[4,128,128]{2,1,0:T(8,128)S(1)}, u32[]{:S(2)}, u32[]{:S(2)}) collective-permute-start(f32[4,128,128]{2,1,0:T(8,128)S(1)} %slice.166), channel_id=1, source_target_pairs={{0,2},{1,3},{2,0},{3,1},{4,6},{5,7},{6,4},{7,5},{8,10},{9,11},{10,... | collective-permute-start | bytes 786440 | tf_op jit(solution)/shard_map/ppermute | solution.py:45
  73.3 9.0 %collective-permute-start.32 = (f32[1,128,128]{2,1,0:T(8,128)S(1)}, f32[1,128,128]{2,1,0:T(8,128)S(1)}, u32[]{:S(2)}, u32[]{:S(2)}) collective-permute-start(f32[1,128,128]{2,1,0:T(8,128)S(1)} %get-tuple-element.49), channel_id=1, source_target_pairs={{0,4},{1,5},{2,6},{3,7},{4,0},{5,1},{6,2},{7,3},{8,12},{9,13},{10,... | collective-permute-start | bytes 196616 | tf_op jit(solution)/shard_map/ppermute | solution.py:45
  77.4 8.7 %collective-permute-start.33 = (f32[1,128,128]{2,1,0:T(8,128)S(1)}, f32[1,128,128]{2,1,0:T(8,128)S(1)}, u32[]{:S(2)}, u32[]{:S(2)}) collective-permute-start(f32[1,128,128]{2,1,0:T(8,128)S(1)} %get-tuple-element.51), channel_id=1, source_target_pairs={{0,8},{1,9},{2,10},{3,11},{4,12},{5,13},{6,14},{7,15},{8,0},{9,1},... | collective-permute-start | bytes 196616 | tf_op jit(solution)/shard_map/ppermute | solution.py:45
  77.8 8.4 %collective-permute-start.34 = (f32[1,128,128]{2,1,0:T(8,128)S(1)}, f32[1,128,128]{2,1,0:T(8,128)S(1)}, u32[]{:S(2)}, u32[]{:S(2)}) collective-permute-start(f32[1,128,128]{2,1,0:T(8,128)S(1)} %get-tuple-element.50), channel_id=1, source_target_pairs={{0,12},{1,13},{2,14},{3,15},{4,8},{5,9},{6,10},{7,11},{8,4},{9,5},... | collective-permute-start | bytes 196616 | tf_op jit(solution)/shard_map/ppermute | solution.py:45
  79.9 12.1 %collective-permute-start.7 = (f32[1,128,128]{2,1,0:T(8,128)S(1)}, f32[1,128,128]{2,1,0:T(8,128)S(1)}, u32[]{:S(2)}, u32[]{:S(2)}) collective-permute-start(f32[1,128,128]{2,1,0:T(8,128)S(1)} %get-tuple-element.55), channel_id=1, source_target_pairs={{0,4},{1,5},{2,6},{3,7},{4,0},{5,1},{6,2},{7,3},{8,12},{9,13},{10,... | collective-permute-start | bytes 196616 | tf_op jit(solution)/shard_map/ppermute | solution.py:45
  81.1 13.3 %collective-permute-start.8 = (f32[1,128,128]{2,1,0:T(8,128)S(1)}, f32[1,128,128]{2,1,0:T(8,128)S(1)}, u32[]{:S(2)}, u32[]{:S(2)}) collective-permute-start(f32[1,128,128]{2,1,0:T(8,128)S(1)} %get-tuple-element.57), channel_id=1, source_target_pairs={{0,8},{1,9},{2,10},{3,11},{4,12},{5,13},{6,14},{7,15},{8,0},{9,1},... | collective-permute-start | bytes 196616 | tf_op jit(solution)/shard_map/ppermute | solution.py:45
  82.3 12.1 %collective-permute-start.9 = (f32[1,128,128]{2,1,0:T(8,128)S(1)}, f32[1,128,128]{2,1,0:T(8,128)S(1)}, u32[]{:S(2)}, u32[]{:S(2)}) collective-permute-start(f32[1,128,128]{2,1,0:T(8,128)S(1)} %get-tuple-element.56), channel_id=1, source_target_pairs={{0,12},{1,13},{2,14},{3,15},{4,8},{5,9},{6,10},{7,11},{8,4},{9,5},... | collective-permute-start | bytes 196616 | tf_op jit(solution)/shard_map/ppermute | solution.py:45
  86.2 10.3 %collective-permute-start.35 = (f32[1,128,128]{2,1,0:T(8,128)S(1)}, f32[1,128,128]{2,1,0:T(8,128)S(1)}, u32[]{:S(2)}, u32[]{:S(2)}) collective-permute-start(f32[1,128,128]{2,1,0:T(8,128)S(1)} %get-tuple-element.41), channel_id=1, source_target_pairs={{0,4},{1,5},{2,6},{3,7},{4,0},{5,1},{6,2},{7,3},{8,12},{9,13},{10,... | collective-permute-start | bytes 196616 | tf_op jit(solution)/shard_map/ppermute | solution.py:45
  92.0 6.9 %collective-permute-start.36 = (f32[1,128,128]{2,1,0:T(8,128)S(1)}, f32[1,128,128]{2,1,0:T(8,128)S(1)}, u32[]{:S(2)}, u32[]{:S(2)}) collective-permute-start(f32[1,128,128]{2,1,0:T(8,128)S(1)} %get-tuple-element.41), channel_id=1, source_target_pairs={{0,8},{1,9},{2,10},{3,11},{4,12},{5,13},{6,14},{7,15},{8,0},{9,1},... | collective-permute-start | bytes 196616 | tf_op jit(solution)/shard_map/ppermute | solution.py:45
  92.0 6.9 %collective-permute-start.37 = (f32[1,128,128]{2,1,0:T(8,128)S(1)}, f32[1,128,128]{2,1,0:T(8,128)S(1)}, u32[]{:S(2)}, u32[]{:S(2)}) collective-permute-start(f32[1,128,128]{2,1,0:T(8,128)S(1)} %get-tuple-element.41), channel_id=1, source_target_pairs={{0,12},{1,13},{2,14},{3,15},{4,8},{5,9},{6,10},{7,11},{8,4},{9,5},... | collective-permute-start | bytes 196616 | tf_op jit(solution)/shard_map/ppermute | solution.py:45
  99.0 9.3 %collective-permute-start.38 = (f32[4,128,128]{2,1,0:T(8,128)S(1)}, f32[4,128,128]{2,1,0:T(8,128)S(1)}, u32[]{:S(2)}, u32[]{:S(2)}) collective-permute-start(f32[4,128,128]{2,1,0:T(8,128)S(1)} %pad_maximum_fusion.4), channel_id=1, source_target_pairs={{0,1},{1,0},{2,3},{3,2},{4,5},{5,4},{6,7},{7,6},{8,9},{9,8},{10,11... | collective-permute-start | bytes 786440 | tf_op jit(solution)/shard_map/ppermute | solution.py:45
  108.3 10.1 %collective-permute-start.39 = (f32[8,128,128]{2,1,0:T(8,128)S(1)}, f32[8,128,128]{2,1,0:T(8,128)S(1)}, u32[]{:S(2)}, u32[]{:S(2)}) collective-permute-start(f32[8,128,128]{2,1,0:T(8,128)S(1)} %constant_dynamic-update-slice_fusion.20.near_ref.refs_2_), channel_id=1, source_target_pairs={{0,2},{1,3},{2,0},{3,1},{4,6},{5,7},{6,4},{7,5},{8,10},{9,11},{10,... | collective-permute-start | bytes 1572872 | tf_op jit(solution)/shard_map/ppermute | solution.py:45
  109.1 19.6 %collective-permute-start.14 = (f32[8,128,128]{2,1,0:T(8,128)S(1)}, f32[8,128,128]{2,1,0:T(8,128)S(1)}, u32[]{:S(2)}, u32[]{:S(2)}) collective-permute-start(f32[8,128,128]{2,1,0:T(8,128)S(1)} %constant_dynamic-update-slice_fusion.5.near_ref.refs_0_), channel_id=1, source_target_pairs={{0,1},{1,0},{2,3},{3,2},{4,5},{5,4},{6,7},{7,6},{8,9},{9,8},{10,11... | collective-permute-start | bytes 1572872 | tf_op jit(solution)/shard_map/ppermute | solution.py:45
  128.1 12.1 %collective-permute-start.40 = (f32[8,128,128]{2,1,0:T(8,128)S(1)}, f32[8,128,128]{2,1,0:T(8,128)S(1)}, u32[]{:S(2)}, u32[]{:S(2)}) collective-permute-start(f32[8,128,128]{2,1,0:T(8,128)S(1)} %get-tuple-element.25), channel_id=1, source_target_pairs={{0,2},{1,3},{2,0},{3,1},{4,6},{5,7},{6,4},{7,5},{8,10},{9,11},{10,... | collective-permute-start | bytes 1572872 | tf_op jit(solution)/shard_map/ppermute | solution.py:45
  138.7 9.2 %collective-permute-start.15 = (f32[8,128,128]{2,1,0:T(8,128)S(1)}, f32[8,128,128]{2,1,0:T(8,128)S(1)}, u32[]{:S(2)}, u32[]{:S(2)}) collective-permute-start(f32[8,128,128]{2,1,0:T(8,128)S(1)} %get-tuple-element.21), channel_id=1, source_target_pairs={{0,1},{1,0},{2,3},{3,2},{4,5},{5,4},{6,7},{7,6},{8,9},{9,8},{10,11... | collective-permute-start | bytes 1572872 | tf_op jit(solution)/shard_map/ppermute | solution.py:45
  140.3 10.5 %collective-permute-start.41 = (f32[4,128,128]{2,1,0:T(8,128)S(1)}, f32[4,128,128]{2,1,0:T(8,128)S(1)}, u32[]{:S(2)}, u32[]{:S(2)}) collective-permute-start(f32[4,128,128]{2,1,0:T(8,128)S(1)} %slice.185), channel_id=1, source_target_pairs={{0,1},{1,0},{2,3},{3,2},{4,5},{5,4},{6,7},{7,6},{8,9},{9,8},{10,11... | collective-permute-start | bytes 786440 | tf_op jit(solution)/shard_map/ppermute | solution.py:45
  148.1 7.2 %collective-permute-start.16 = (f32[4,128,128]{2,1,0:T(8,128)S(1)}, f32[4,128,128]{2,1,0:T(8,128)S(1)}, u32[]{:S(2)}, u32[]{:S(2)}) collective-permute-start(f32[4,128,128]{2,1,0:T(8,128)S(1)} %slice.172), channel_id=1, source_target_pairs={{0,2},{1,3},{2,0},{3,1},{4,6},{5,7},{6,4},{7,5},{8,10},{9,11},{10,... | collective-permute-start | bytes 786440 | tf_op jit(solution)/shard_map/ppermute | solution.py:45
  150.9 7.0 %collective-permute-start.42 = (f32[1,128,128]{2,1,0:T(8,128)S(1)}, f32[1,128,128]{2,1,0:T(8,128)S(1)}, u32[]{:S(2)}, u32[]{:S(2)}) collective-permute-start(f32[1,128,128]{2,1,0:T(8,128)S(1)} %get-tuple-element.46), channel_id=1, source_target_pairs={{0,4},{1,5},{2,6},{3,7},{4,0},{5,1},{6,2},{7,3},{8,12},{9,13},{10,... | collective-permute-start | bytes 196616 | tf_op jit(solution)/shard_map/ppermute | solution.py:45
  150.9 8.9 %collective-permute-start.43 = (f32[1,128,128]{2,1,0:T(8,128)S(1)}, f32[1,128,128]{2,1,0:T(8,128)S(1)}, u32[]{:S(2)}, u32[]{:S(2)}) collective-permute-start(f32[1,128,128]{2,1,0:T(8,128)S(1)} %get-tuple-element.48), channel_id=1, source_target_pairs={{0,8},{1,9},{2,10},{3,11},{4,12},{5,13},{6,14},{7,15},{8,0},{9,1},... | collective-permute-start | bytes 196616 | tf_op jit(solution)/shard_map/ppermute | solution.py:45
  153.3 6.6 %collective-permute-start.44 = (f32[1,128,128]{2,1,0:T(8,128)S(1)}, f32[1,128,128]{2,1,0:T(8,128)S(1)}, u32[]{:S(2)}, u32[]{:S(2)}) collective-permute-start(f32[1,128,128]{2,1,0:T(8,128)S(1)} %get-tuple-element.47), channel_id=1, source_target_pairs={{0,12},{1,13},{2,14},{3,15},{4,8},{5,9},{6,10},{7,11},{8,4},{9,5},... | collective-permute-start | bytes 196616 | tf_op jit(solution)/shard_map/ppermute | solution.py:45
  155.4 6.9 %collective-permute-start.17 = (f32[1,128,128]{2,1,0:T(8,128)S(1)}, f32[1,128,128]{2,1,0:T(8,128)S(1)}, u32[]{:S(2)}, u32[]{:S(2)}) collective-permute-start(f32[1,128,128]{2,1,0:T(8,128)S(1)} %get-tuple-element.52), channel_id=1, source_target_pairs={{0,4},{1,5},{2,6},{3,7},{4,0},{5,1},{6,2},{7,3},{8,12},{9,13},{10,... | collective-permute-start | bytes 196616 | tf_op jit(solution)/shard_map/ppermute | solution.py:45
  155.5 8.9 %collective-permute-start.18 = (f32[1,128,128]{2,1,0:T(8,128)S(1)}, f32[1,128,128]{2,1,0:T(8,128)S(1)}, u32[]{:S(2)}, u32[]{:S(2)}) collective-permute-start(f32[1,128,128]{2,1,0:T(8,128)S(1)} %get-tuple-element.54), channel_id=1, source_target_pairs={{0,8},{1,9},{2,10},{3,11},{4,12},{5,13},{6,14},{7,15},{8,0},{9,1},... | collective-permute-start | bytes 196616 | tf_op jit(solution)/shard_map/ppermute | solution.py:45
  157.8 6.5 %collective-permute-start.19 = (f32[1,128,128]{2,1,0:T(8,128)S(1)}, f32[1,128,128]{2,1,0:T(8,128)S(1)}, u32[]{:S(2)}, u32[]{:S(2)}) collective-permute-start(f32[1,128,128]{2,1,0:T(8,128)S(1)} %get-tuple-element.53), channel_id=1, source_target_pairs={{0,12},{1,13},{2,14},{3,15},{4,8},{5,9},{6,10},{7,11},{8,4},{9,5},... | collective-permute-start | bytes 196616 | tf_op jit(solution)/shard_map/ppermute | solution.py:45
  159.9 6.9 %collective-permute-start.45 = (f32[1,128,128]{2,1,0:T(8,128)S(1)}, f32[1,128,128]{2,1,0:T(8,128)S(1)}, u32[]{:S(2)}, u32[]{:S(2)}) collective-permute-start(f32[1,128,128]{2,1,0:T(8,128)S(1)} %get-tuple-element.39), channel_id=1, source_target_pairs={{0,4},{1,5},{2,6},{3,7},{4,0},{5,1},{6,2},{7,3},{8,12},{9,13},{10,... | collective-permute-start | bytes 196616 | tf_op jit(solution)/shard_map/ppermute | solution.py:45
  159.9 8.9 %collective-permute-start.46 = (f32[1,128,128]{2,1,0:T(8,128)S(1)}, f32[1,128,128]{2,1,0:T(8,128)S(1)}, u32[]{:S(2)}, u32[]{:S(2)}) collective-permute-start(f32[1,128,128]{2,1,0:T(8,128)S(1)} %get-tuple-element.39), channel_id=1, source_target_pairs={{0,8},{1,9},{2,10},{3,11},{4,12},{5,13},{6,14},{7,15},{8,0},{9,1},... | collective-permute-start | bytes 196616 | tf_op jit(solution)/shard_map/ppermute | solution.py:45
  162.3 6.5 %collective-permute-start.47 = (f32[1,128,128]{2,1,0:T(8,128)S(1)}, f32[1,128,128]{2,1,0:T(8,128)S(1)}, u32[]{:S(2)}, u32[]{:S(2)}) collective-permute-start(f32[1,128,128]{2,1,0:T(8,128)S(1)} %get-tuple-element.39), channel_id=1, source_target_pairs={{0,12},{1,13},{2,14},{3,15},{4,8},{5,9},{6,10},{7,11},{8,4},{9,5},... | collective-permute-start | bytes 196616 | tf_op jit(solution)/shard_map/ppermute | solution.py:45
  175.3 18.8 %collective-permute-start.49 = (f32[8,128,128]{2,1,0:T(8,128)S(1)}, f32[8,128,128]{2,1,0:T(8,128)S(1)}, u32[]{:S(2)}, u32[]{:S(2)}) collective-permute-start(f32[8,128,128]{2,1,0:T(8,128)S(1)} %constant_dynamic-update-slice_fusion.25.refs_2_), channel_id=1, source_target_pairs={{0,2},{1,3},{2,0},{3,1},{4,6},{5,7},{6,4},{7,5},{8,10},{9,11},{10,... | collective-permute-start | bytes 1572872 | tf_op jit(solution)/shard_map/ppermute | solution.py:45
  179.3 14.8 %collective-permute-start.24 = (f32[8,128,128]{2,1,0:T(8,128)S(1)}, f32[8,128,128]{2,1,0:T(8,128)S(1)}, u32[]{:S(2)}, u32[]{:S(2)}) collective-permute-start(f32[8,128,128]{2,1,0:T(8,128)S(1)} %constant_dynamic-update-slice_fusion.10.refs_0_), channel_id=1, source_target_pairs={{0,1},{1,0},{2,3},{3,2},{4,5},{5,4},{6,7},{7,6},{8,9},{9,8},{10,11... | collective-permute-start | bytes 1572872 | tf_op jit(solution)/shard_map/ppermute | solution.py:45
  207.7 15.5 %collective-permute-start.60 = (f32[8,16,128]{2,1,0:T(8,128)S(1)}, f32[8,16,128]{2,1,0:T(8,128)S(1)}, u32[]{:S(2)}, u32[]{:S(2)}) collective-permute-start(f32[8,16,128]{2,1,0:T(8,128)S(1)} %get-tuple-element.32), channel_id=1, source_target_pairs={{0,2},{1,3},{2,0},{3,1},{4,6},{5,7},{6,4},{7,5},{8,10},{9,11},{10,... | collective-permute-start | bytes 196616 | tf_op jit(solution)/shard_map/ppermute | solution.py:45
  211.4 12.4 %collective-permute-start.51 = (f32[4,16,128]{2,1,0:T(8,128)S(1)}, f32[4,16,128]{2,1,0:T(8,128)S(1)}, u32[]{:S(2)}, u32[]{:S(2)}) collective-permute-start(f32[4,16,128]{2,1,0:T(8,128)S(1)} %slice.191), channel_id=1, source_target_pairs={{0,2},{1,3},{2,0},{3,1},{4,6},{5,7},{6,4},{7,5},{8,10},{9,11},{10,... | collective-permute-start | bytes 98312 | tf_op jit(solution)/shard_map/ppermute | solution.py:45
  223.9 7.1 %collective-permute-start.52 = (f32[1,16,128]{2,1,0:T(8,128)S(1)}, f32[1,16,128]{2,1,0:T(8,128)S(1)}, u32[]{:S(2)}, u32[]{:S(2)}) collective-permute-start(f32[1,16,128]{2,1,0:T(8,128)S(1)} %get-tuple-element.64), channel_id=1, source_target_pairs={{0,4},{1,5},{2,6},{3,7},{4,0},{5,1},{6,2},{7,3},{8,12},{9,13},{10,... | collective-permute-start | bytes 24584 | tf_op jit(solution)/shard_map/ppermute | solution.py:45
  223.9 8.9 %collective-permute-start.53 = (f32[1,16,128]{2,1,0:T(8,128)S(1)}, f32[1,16,128]{2,1,0:T(8,128)S(1)}, u32[]{:S(2)}, u32[]{:S(2)}) collective-permute-start(f32[1,16,128]{2,1,0:T(8,128)S(1)} %get-tuple-element.66), channel_id=1, source_target_pairs={{0,8},{1,9},{2,10},{3,11},{4,12},{5,13},{6,14},{7,15},{8,0},{9,1},... | collective-permute-start | bytes 24584 | tf_op jit(solution)/shard_map/ppermute | solution.py:45
  228.3 7.1 %collective-permute-start.62 = (f32[1,16,128]{2,1,0:T(8,128)S(1)}, f32[1,16,128]{2,1,0:T(8,128)S(1)}, u32[]{:S(2)}, u32[]{:S(2)}) collective-permute-start(f32[1,16,128]{2,1,0:T(8,128)S(1)} %get-tuple-element.69), channel_id=1, source_target_pairs={{0,4},{1,5},{2,6},{3,7},{4,0},{5,1},{6,2},{7,3},{8,12},{9,13},{10,... | collective-permute-start | bytes 24584 | tf_op jit(solution)/shard_map/ppermute | solution.py:45
  228.4 8.9 %collective-permute-start.63 = (f32[1,16,128]{2,1,0:T(8,128)S(1)}, f32[1,16,128]{2,1,0:T(8,128)S(1)}, u32[]{:S(2)}, u32[]{:S(2)}) collective-permute-start(f32[1,16,128]{2,1,0:T(8,128)S(1)} %get-tuple-element.71), channel_id=1, source_target_pairs={{0,8},{1,9},{2,10},{3,11},{4,12},{5,13},{6,14},{7,15},{8,0},{9,1},... | collective-permute-start | bytes 24584 | tf_op jit(solution)/shard_map/ppermute | solution.py:45
  232.8 7.1 %collective-permute-start.55 = (f32[1,16,128]{2,1,0:T(8,128)S(1)}, f32[1,16,128]{2,1,0:T(8,128)S(1)}, u32[]{:S(2)}, u32[]{:S(2)}) collective-permute-start(f32[1,16,128]{2,1,0:T(8,128)S(1)} %get-tuple-element.35), channel_id=1, source_target_pairs={{0,4},{1,5},{2,6},{3,7},{4,0},{5,1},{6,2},{7,3},{8,12},{9,13},{10,... | collective-permute-start | bytes 24584 | tf_op jit(solution)/shard_map/ppermute | solution.py:45
  232.9 8.9 %collective-permute-start.56 = (f32[1,16,128]{2,1,0:T(8,128)S(1)}, f32[1,16,128]{2,1,0:T(8,128)S(1)}, u32[]{:S(2)}, u32[]{:S(2)}) collective-permute-start(f32[1,16,128]{2,1,0:T(8,128)S(1)} %get-tuple-element.35), channel_id=1, source_target_pairs={{0,8},{1,9},{2,10},{3,11},{4,12},{5,13},{6,14},{7,15},{8,0},{9,1},... | collective-permute-start | bytes 24584 | tf_op jit(solution)/shard_map/ppermute | solution.py:45
  (25 other events, 169.0 us)

commit v2 on v1

--- a/solution.py
+++ b/solution.py
@@ -10,8 +10,11 @@
 
 LANES = 128
 SUBLANES = 8
+BLOCK = 1024
+PIECES = 2
 VMEM_LIMIT = 48 * 1024 * 1024
 HIGHEST = lax.Precision.HIGHEST
+FACTOR_COST = pl.CostEstimate(flops=12_000_000_000, bytes_accessed=4 << 20, transcendentals=0)
 
 
 def stage_bits(groups, flip):
@@ -45,27 +48,56 @@
     return lax.ppermute(value, "smp", [(device, device ^ offset) for device in range(groups)])
 
 
-def reduce_chunks(keep, send, groups, stages):
-    total = keep + exchange(send, groups, 1 << stages[0][0])
+def reduce_chunks(pairs, groups, chains):
+    totals = [
+        keep + exchange(send, groups, 1 << stages[0][0]) for (keep, send), stages in zip(pairs, chains)
+    ]
+    for depth in range(1, len(chains[0])):
+        choices = [offsets(stages[depth]) for stages in chains]
+        width = totals[0].shape[0] // len(choices[0])
+        kept = [total[:width] for total in totals]
+        for place in range(1, len(choices[0])):
+            parts = [total[place * width : (place + 1) * width] for total in totals]
+            spans = [spans[place] for spans in choices]
+            if len(set(spans)) == 1:
+                arrived = jnp.split(exchange(jnp.concatenate(parts, axis=0), groups, spans[0]), len(parts), axis=0)
+            else:
+                arrived = [exchange(part, groups, span) for part, span in zip(parts, spans)]
+            kept = [total + part for total, part in zip(kept, arrived)]
+        totals = kept
+    return jnp.concatenate(totals, axis=0)
+
+
+def gather_chunks(chunks, groups, chains):
+    held = jnp.split(chunks, len(chains), axis=0)
+    for depth in reversed(range(1, len(chains[0]))):
+        choices = [offsets(stages[depth]) for stages in chains]
+        if all(spans == choices[0] for spans in choices):
+            whole = jnp.concatenate(held, axis=0) if depth + 1 < len(chains[0]) else chunks
+            arrived = [jnp.split(exchange(whole, groups, span), len(chains), axis=0) for span in choices[0][1:]]
+            held = [jnp.concatenate([own] + [part[chain] for part in arrived], axis=0) for chain, own in enumerate(held)]
+        else:
+            held = [
+                jnp.concatenate([own] + [exchange(own, groups, span) for span in spans[1:]], axis=0)
+                for own, spans in zip(held, choices)
+            ]
+    return [(own, exchange(own, groups, 1 << stages[0][0])) for own, stages in zip(held, chains)]
+
+
+def pair_sum(parts):
+    while len(parts) > 1:
+        parts = [left + right for left, right in zip(parts[::2], parts[1::2])]
+    return parts[0]
+
+
+def sum_quarters(quarters, groups):
+    count = groups.bit_length() - 1
+    stages = [list(range(count))[place : place + 2] for place in range(0, count, 2)]
+    spans = offsets(stages[0])
+    total = pair_sum([quarters[0]] + [exchange(part, groups, span) for part, span in zip(quarters[1:], spans[1:])])
     for bits in stages[1:]:
-        spans = offsets(bits)
-        width = total.shape[0] // len(spans)
-        arrived = [
-            exchange(total[place * width : (place + 1) * width], groups, span)
-            for place, span in enumerate(spans)
-            if place > 0
-        ]
-        total = total[:width]
-        for part in arrived:
-            total = total + part
-    return total
-
-
-def gather_chunks(chunk, groups, stages):
-    held = chunk
-    for bits in reversed(stages[1:]):
-        held = jnp.concatenate([held] + [exchange(held, groups, span) for span in offsets(bits)[1:]], axis=0)
-    return held, exchange(held, groups, 1 << stages[0][0])
+        total = pair_sum([total] + [exchange(total, groups, span) for span in offsets(bits)[1:]])
+    return [total] + [exchange(total, groups, span) for span in spans[1:]]
 
 
 def split_pieces(value, pieces):
@@ -131,7 +163,7 @@
 def apply_samples(genotypes, size, me, near, far, order, pieces, scale):
     samples, cap = genotypes.shape
     count, half, width = near.shape
-    block = min(256, samples)
+    block = min(BLOCK, samples)
     whole = pl.BlockSpec((count, half, width), lambda step: (0, 0, 0))
     scalar = pl.BlockSpec(memory_space=pltpu.SMEM)
     out = jax.ShapeDtypeStruct(near.shape, jnp.float32)
@@ -269,17 +301,43 @@
         out_shape=jax.ShapeDtypeStruct((size, size), jnp.float32),
         scratch_shapes=[pltpu.VMEM((size, cap), jnp.float32), pltpu.VMEM((size, 2 * size), jnp.float32)],
         compiler_params=pltpu.CompilerParams(vmem_limit_bytes=VMEM_LIMIT),
+        cost_estimate=FACTOR_COST,
     )(me, *[ref for pair in pairs for ref in pair])
 
 
-def project_kernel(
-    orders, out_orders, pieces, place_ref, *refs
-):
+def fold_symmetric(value, folded_ref, height):
+    half = value.shape[0] // 2
+    row = lax.broadcasted_iota(jnp.int32, (half, half), 0)
+    column = lax.broadcasted_iota(jnp.int32, (half, half), 1)
+    corner = value[half:, half:]
+    both = jnp.where(row >= column, value[:half, :half], corner)
+    diagonal = jnp.sum(jnp.where(row == column, corner, 0.0), axis=0, keepdims=True)
+    quarter = half // 2
+    for place in range(4):
+        source = value[half:, :half] if place < 2 else both
+        folded_ref[place, :quarter] = source[place % 2 * quarter : (place % 2 + 1) * quarter]
+        folded_ref[place, quarter:] = jnp.broadcast_to(diagonal, (SUBLANES, half))
+
+
+def unfold_symmetric(parts):
+    quarter = parts[0].shape[0] - SUBLANES
+    half = 2 * quarter
+    row = lax.broadcasted_iota(jnp.int32, (half, half), 0)
+    column = lax.broadcasted_iota(jnp.int32, (half, half), 1)
+    left = jnp.concatenate([parts[0][:quarter], parts[1][:quarter]], axis=0)
+    both = jnp.concatenate([parts[2][:quarter], parts[3][:quarter]], axis=0)
+    turned = both.T
+    corner = jnp.where(row == column, parts[3][quarter : quarter + 1], jnp.where(row < column, both, turned))
+    upper = jnp.concatenate([jnp.where(row >= column, both, turned), left.T], axis=1)
+    return jnp.concatenate([upper, jnp.concatenate([left, corner], axis=1)], axis=0)
+
+
+def project_kernel(orders, pieces, aligned, quarter_ref, place_ref, *refs):
     count = 2 * len(orders)
     pairs = list(zip(refs[:count:2], refs[1:count:2]))
     first_ref, rows_ref, image_ref, inner_ref = refs[count : count + 4]
     outs = refs[count + 4 : count + 8]
-    full_ref, split_ref, cross_ref = refs[count + 8 :]
+    full_ref, split_ref, cross_ref, folded_ref = refs[count + 8 :]
     step = pl.program_id(0)
     size = first_ref.shape[0]
 
@@ -289,8 +347,13 @@
         image = jnp.dot(
             first_ref[...], full_ref[...], precision=HIGHEST, preferred_element_type=jnp.float32
         )
-        image_ref[...] = image
         inner_ref[...] = rows_inner(image)
+        full_ref[...] = image
+        if aligned:
+            width = image_ref.shape[1]
+            image_ref[...] = full_ref[:, pl.ds(pl.multiple_of(place_ref[0] * width, width), width)]
+        else:
+            image_ref[...] = image
         for piece, part in enumerate(split_pieces(image, pieces)):
             split_ref[pl.ds(piece * size, size), :] = part
         cross_ref[...] = jnp.zeros_like(cross_ref)
@@ -303,68 +366,96 @@
 
     @pl.when(step == pl.num_programs(0) - 1)
     def _():
-        me = place_ref[0]
-        for chain, order in enumerate(out_orders):
-            keep_ref, send_ref = outs[2 * chain : 2 * chain + 2]
-            height, width = keep_ref.shape[1:]
-            middle = len(order) // 2
-            for place, offset in enumerate(order):
-                first = pl.multiple_of(jnp.bitwise_xor(me, offset) * height, height)
-                value = cross_ref[pl.ds(first, height), chain * width : (chain + 1) * width]
-                if place < middle:
-                    keep_ref[place] = value
-                else:
-                    send_ref[place - middle] = value
-
-
-def project(genotypes, me, pairs, orders, out_orders, first, pieces):
+        fold_symmetric(cross_ref[...], folded_ref, size)
+        for offset in range(4):
+            outs[offset][...] = folded_ref[jnp.bitwise_xor(quarter_ref[0], offset)]
+
+
+def project(genotypes, quarter, place, pairs, orders, first, pieces, aligned, width):
     samples, cap = genotypes.shape
     size = first.shape[0]
-    block = min(256, samples)
+    block = min(BLOCK, samples)
     scalar = pl.BlockSpec(memory_space=pltpu.SMEM)
 
     def whole(shape):
         return pl.BlockSpec(shape, lambda step: (0,) * len(shape))
 
-    height, width = size // len(out_orders[0]), size // len(out_orders)
-    part = (len(out_orders[0]) // 2, height, width)
+    own = (size, width if aligned else cap)
+    part = (size // 4 + SUBLANES, size // 2)
+    outs = [own, (size, size)] + [part] * 4
     return pl.pallas_call(
-        functools.partial(project_kernel, orders, out_orders, pieces),
+        functools.partial(project_kernel, orders, pieces, aligned),
         grid=(samples // block,),
-        in_specs=[scalar]
+        in_specs=[scalar, scalar]
         + [whole(near.shape) for near, far in pairs for _ in range(2)]
         + [whole((size, size)), pl.BlockSpec((block, cap), lambda step: (step, 0))],
-        out_specs=[whole((size, cap)), whole((size, size))] + [whole(part)] * (2 * len(out_orders)),
-        out_shape=[
-            jax.ShapeDtypeStruct((size, cap), jnp.float32),
-            jax.ShapeDtypeStruct((size, size), jnp.float32),
-        ]
-        + [jax.ShapeDtypeStruct(part, jnp.float32)] * (2 * len(out_orders)),
+        out_specs=[whole(shape) for shape in outs],
+        out_shape=[jax.ShapeDtypeStruct(shape, jnp.float32) for shape in outs],
         scratch_shapes=[
             pltpu.VMEM((size, cap), jnp.float32),
             pltpu.VMEM((pieces * size, cap), jnp.bfloat16),
             pltpu.VMEM((size, size), jnp.float32),
+            pltpu.VMEM((4,) + part, jnp.float32),
         ],
         compiler_params=pltpu.CompilerParams(vmem_limit_bytes=VMEM_LIMIT),
-    )(me, *[ref for pair in pairs for ref in pair], first, genotypes)
-
-
-def second_kernel(inner_ref, out_ref, work_ref):
+        cost_estimate=FACTOR_COST,
+    )(quarter, place, *[ref for pair in pairs for ref in pair], first, genotypes)
+
+
+def second_kernel(gain, inner_ref, own_ref, out_ref, basis_ref, work_ref):
     start_factor(work_ref, inner_ref[...])
     inverse_factor(work_ref, work_ref.shape[0], 32)
-    out_ref[...] = finish_factor(work_ref)
-
-
-def second_factor(inner):
-    size = inner.shape[0]
+    factor = finish_factor(work_ref)
+    out_ref[...] = factor
+    own = jnp.dot(factor, own_ref[...], precision=HIGHEST, preferred_element_type=jnp.float32)
+    basis_ref[...] = own.T * gain
+
+
+def second_factor(inner, own, gain):
+    size, width = own.shape
     return pl.pallas_call(
-        second_kernel,
-        in_specs=[pl.BlockSpec(memory_space=pltpu.VMEM)],
-        out_specs=pl.BlockSpec(memory_space=pltpu.VMEM),
-        out_shape=jax.ShapeDtypeStruct((size, size), jnp.float32),
+        functools.partial(second_kernel, gain),
+        in_specs=[pl.BlockSpec(memory_space=pltpu.VMEM)] * 2,
+        out_specs=[pl.BlockSpec(memory_space=pltpu.VMEM)] * 2,
+        out_shape=[
+            jax.ShapeDtypeStruct((size, size), jnp.float32),
+            jax.ShapeDtypeStruct((width, size), jnp.float32),
+        ],
         scratch_shapes=[pltpu.VMEM((size, 2 * size), jnp.float32)],
         compiler_params=pltpu.CompilerParams(vmem_limit_bytes=VMEM_LIMIT),
-    )(inner)
+        cost_estimate=FACTOR_COST,
+    )(inner, own)
+
+
+def finish_kernel(scale, quarter_ref, factor_ref, *refs):
+    parts, (out_ref, trace_ref, folded_ref) = refs[:4], refs[4:]
+    for offset in range(4):
+        folded_ref[jnp.bitwise_xor(quarter_ref[0], offset)] = parts[offset][...]
+    cross = unfold_symmetric([folded_ref[place] for place in range(4)])
+    factor = factor_ref[...]
+    half = jnp.dot(factor, cross, precision=HIGHEST, preferred_element_type=jnp.float32)
+    result = scale * lax.dot_general(
+        half, factor, (((1,), (1,)), ((), ())), precision=HIGHEST, preferred_element_type=jnp.float32
+    )
+    out_ref[...] = result
+    row = lax.broadcasted_iota(jnp.int32, result.shape, 0)
+    column = lax.broadcasted_iota(jnp.int32, result.shape, 1)
+    trace_ref[...] = jnp.broadcast_to(jnp.sum(jnp.where(row == column, result, 0.0)), trace_ref.shape)
+
+
+def finish(quarter, factor, parts, scale):
+    vmem = pl.BlockSpec(memory_space=pltpu.VMEM)
+    return pl.pallas_call(
+        functools.partial(finish_kernel, scale),
+        in_specs=[pl.BlockSpec(memory_space=pltpu.SMEM)] + [vmem] * 5,
+        out_specs=[vmem] * 2,
+        out_shape=[
+            jax.ShapeDtypeStruct(factor.shape, jnp.float32),
+            jax.ShapeDtypeStruct((SUBLANES, LANES), jnp.float32),
+        ],
+        scratch_shapes=[pltpu.VMEM((4,) + parts[0].shape, jnp.float32)],
+        compiler_params=pltpu.CompilerParams(vmem_limit_bytes=VMEM_LIMIT),
+    )(quarter, factor, *parts)
 
 
 def to_natural(pair, order, me):
@@ -380,18 +471,6 @@
     chunks = jnp.transpose(rows.reshape(rows.shape[0], -1, width), (1, 0, 2))
     chunks = chunks[jnp.bitwise_xor(jnp.array(order, jnp.int32), me)]
     return tuple(jnp.split(chunks, 2, axis=0))
-
-
-def stacked_rows(pair, order, me):
-    places = jnp.argsort(jnp.array(order, jnp.int32))
-    mine = jnp.bitwise_xor(jnp.arange(len(order), dtype=jnp.int32), me)
-    stacked = jnp.concatenate(pair, axis=0)[places][mine]
-    return stacked.reshape(-1, stacked.shape[2])
-
-
-def cut_rows(pair, order, me, height):
-    rows = jnp.concatenate(pair, axis=0).reshape(-1, height, pair[0].shape[2])
-    return tuple(jnp.split(rows[jnp.bitwise_xor(jnp.array(order, jnp.int32), me)], 2, axis=0))
 
 
 def body(genotypes, sizes, start):
@@ -409,53 +488,40 @@
     first_row = me * width
     live = first_row + lax.broadcasted_iota(jnp.int32, (width, size), 0) < sizes[0]
     columns = jnp.where(live, start[0], 0.0).T
-    chunks = [columns[chain * half : (chain + 1) * half][None] for chain in range(2)]
-
-    aligned = width % LANES == 0 and (size // groups) % SUBLANES == 0
-    plain = [[0, 1]] * 2
-
-    def gather(chunk, chain):
-        pair = gather_chunks(chunk, groups, chains[chain])
-        return pair if aligned else to_natural(pair, orders[chain], me)
-
+    chunks = columns.reshape(2, half, width)
+    aligned = width % LANES == 0
     place = where if aligned else jnp.zeros_like(where)
-    laid = orders if aligned else plain
-
-    def apply(chunk, chain):
-        pair = gather(chunk, chain)
-        out = apply_samples(dosages, sizes, place, *pair, laid[chain], 3, scale)
+    laid = orders if aligned else [[0, 1]] * 2
+
+    def gather(chunks):
+        pairs = gather_chunks(chunks, groups, chains)
+        if aligned:
+            return pairs
+        return [to_natural(pair, order, me) for pair, order in zip(pairs, orders)]
+
+    def apply(pairs):
+        outs = [
+            apply_samples(dosages, sizes, place, *pair, order, PIECES, scale) for pair, order in zip(pairs, laid)
+        ]
         if not aligned:
-            out = to_relative(out, orders[chain], me, width)
-        return pair, reduce_chunks(*out, groups, chains[chain])
-
-    images = [apply(chunks[chain], chain)[1] for chain in range(2)]
-    done = [apply(images[chain], chain) for chain in range(2)]
-    first = first_factor(place, [pair for pair, _ in done], laid, cap)
-    pairs = [gather(done[chain][1], chain) for chain in range(2)]
-    image, inner, *cross = project(dosages, place, pairs, laid, laid, first, 3)
-    crossed = []
-    for chain in range(2):
-        part = tuple(cross[2 * chain : 2 * chain + 2])
-        if not aligned:
-            part = cut_rows(part, orders[chain], me, size // groups)
-        part = gather_chunks(reduce_chunks(*part, groups, chains[chain]), groups, chains[chain])
-        crossed.append(stacked_rows(part, orders[chain], me))
-    crossed = jnp.concatenate(crossed, axis=1)
-    second = second_factor(inner)
-    own = lax.dynamic_slice(image, (0, first_row), (size, width))
-    basis = jnp.dot(second, own, precision=HIGHEST, preferred_element_type=jnp.float32).T * math.sqrt(cap)
-    rayleigh = jnp.dot(
-        jnp.dot(second, crossed, precision=HIGHEST, preferred_element_type=jnp.float32),
-        second.T,
-        precision=HIGHEST,
-        preferred_element_type=jnp.float32,
-    ) * scale
+            outs = [to_relative(out, order, me, width) for out, order in zip(outs, orders)]
+        return reduce_chunks(outs, groups, chains)
+
+    pairs = gather(apply(gather(chunks)))
+    first = first_factor(place, pairs, laid, cap)
+    pairs = gather(apply(pairs))
+    quarter = jnp.bitwise_and(where, 3)
+    own, inner, *quarters = project(dosages, quarter, place, pairs, laid, first, PIECES, aligned, width)
+    if not aligned:
+        own = lax.dynamic_slice(own, (0, first_row), (size, width))
+    quarters = sum_quarters(quarters, groups)
+    second, basis = second_factor(inner, own, math.sqrt(cap))
+    rayleigh, trace = finish(quarter, second, quarters, scale)
     blocks = lax.axis_size("blk")
-    partial = jnp.broadcast_to(jnp.trace(rayleigh), (SUBLANES, LANES))
-    total = partial
+    total = trace
     for shift in range(1, blocks):
-        total = total + lax.ppermute(partial, "blk", [(block, (block + shift) % blocks) for block in range(blocks)])
-    scaled = rayleigh * (genotypes.shape[0] * blocks * size) / total[0, 0]
+        total = total + lax.ppermute(trace, "blk", [(block, (block + shift) % blocks) for block in range(blocks)])
+    scaled = rayleigh * (genotypes.shape[0] * blocks * size / total[0, 0])
     return basis[None], scaled[None]
 
 

time: 261 us -> 234 us (0.90)
  starting transfers between devices: 102 us -> 57.8 us
  waiting for transfers between devices: 70.6 us -> 114 us
  Pallas kernels: 75.6 us -> 55.6 us
  local copies, waits for them, and re-layouts: 4.93 us -> 1.94 us
    ppermute x70 -> x44, starting transfers between devices: 102 us -> 57.7 us  [exchange(): lax.ppermute(value, 'smp', [(device, device ^ offset) for device in range...]
    ppermute x70 -> x44, waiting for transfers between devices: 70.5 us -> 113 us  [exchange(): lax.ppermute(value, 'smp', [(device, device ^ offset) for device in range...]
    pallas_call x4, Pallas kernels: 39.3 us -> 19.8 us  [apply_samples(): pl.pallas_call(functools.partial(apply_kernel, order, pieces, scale), gri...]
    pallas_call x2 -> x3, Pallas kernels: 23.1 us -> 22.4 us  [the longest x1 11.2 us: second_factor(): pl.pallas_call(functools.partial(second_kernel, gain), in_specs=[pl.Block...]
  transfers between devices with their start and end apart: 71 -> 45, of which waited for: 25 -> 30; matrix products, arithmetic and copies ran while one was open for 1% -> 0% of each run, Pallas kernels for 24% -> 19%
where the time goes in v2:
time: 234 us
  waiting for transfers between devices  114 us (49%)
  starting transfers between devices  57.8 us (25%)
  Pallas kernels  55.6 us (24%)
  between operations  2.41 us (1%)
    ppermute x44, waiting for transfers between devices, exchange(): lax.ppermute(value, 'smp', [(device, device ^ offset) for device in range...  113 us
    ppermute x44, starting transfers between devices, exchange(): lax.ppermute(value, 'smp', [(device, device ^ offset) for device in range...  57.7 us
    pallas_call x4, Pallas kernels, apply_samples(): pl.pallas_call(functools.partial(apply_kernel, order, pieces, scale), gri...  19.8 us
    pallas_call x1, Pallas kernels, first_factor(): pl.pallas_call(functools.partial(factor_kernel, orders), in_specs=[pl.Blo...  13.3 us
    pallas_call x1, Pallas kernels, second_factor(): pl.pallas_call(functools.partial(second_kernel, gain), in_specs=[pl.Block...  11.2 us
    pallas_call x1, Pallas kernels, project(): pl.pallas_call(functools.partial(project_kernel, orders, pieces, aligned)...  9.95 us
  transfers between devices with their start and end apart: 45, of which 30 were waited for; matrix products, arithmetic and copies ran while one was open for 0% of the time, Pallas kernels for 19%

profile of v2, /device:TPU:0, one launch (start us, length us, event | category | flops | bytes accessed | tf_op | source)
XLA Modules:
  0.0 233.5 jit_solution(7506729785863831473)
XLA Ops:
  2.3 3.1 %collective-permute-start = (f32[2,128,128]{2,1,0:T(8,128)S(1)}, f32[2,128,128]{2,1,0:T(8,128)S(1)}, u32[]{:S(2)}, u32[]{:S(2)}) collective-permute-start(f32[2,128,128]{2,1,0:T(8,128)S(1)} %bitcast.24), channel_id=1, source_target_pairs={{0,4},{1,5},{2,6},{3,7},{4,0},{5,1},{6,2},{7,3},{8,12},{9,13},{10,... | collective-permute-start | bytes 393224 | tf_op jit(solution)/shard_map/ppermute | solution.py:48
  5.4 2.6 %collective-permute-start.1 = (f32[2,128,128]{2,1,0:T(8,128)S(1)}, f32[2,128,128]{2,1,0:T(8,128)S(1)}, u32[]{:S(2)}, u32[]{:S(2)}) collective-permute-start(f32[2,128,128]{2,1,0:T(8,128)S(1)} %bitcast.25), channel_id=1, source_target_pairs={{0,8},{1,9},{2,10},{3,11},{4,12},{5,13},{6,14},{7,15},{8,0},{9,1},... | collective-permute-start | bytes 393224 | tf_op jit(solution)/shard_map/ppermute | solution.py:48
  8.1 2.4 %collective-permute-done = f32[2,128,128]{2,1,0:T(8,128)S(1)} collective-permute-done((f32[2,128,128]{2,1,0:T(8,128)S(1)}, f32[2,128,128]{2,1,0:T(8,128)S(1)}, u32[]{:S(2)}, u32[]{:S(2)}) %collective-permute-start) | collective-permute-done | bytes 131104 | tf_op jit(solution)/shard_map/ppermute | solution.py:48
  10.5 7.9 %collective-permute-done.1 = f32[2,128,128]{2,1,0:T(8,128)S(1)} collective-permute-done((f32[2,128,128]{2,1,0:T(8,128)S(1)}, f32[2,128,128]{2,1,0:T(8,128)S(1)}, u32[]{:S(2)}, u32[]{:S(2)}) %collective-permute-start.1) | collective-permute-done | bytes 131104 | tf_op jit(solution)/shard_map/ppermute | solution.py:48
  18.4 1.6 collective-permute-start.3
  20.0 1.6 collective-permute-start.7
  21.6 3.3 %collective-permute-done.3 = f32[4,128,128]{2,1,0:T(8,128)S(1)} collective-permute-done((f32[4,128,128]{2,1,0:T(8,128)S(1)}, f32[4,128,128]{2,1,0:T(8,128)S(1)}, u32[]{:S(2)}, u32[]{:S(2)}) %collective-permute-start.3) | collective-permute-done | bytes 262176 | tf_op jit(solution)/shard_map/ppermute | solution.py:48
  24.9 1.6 collective-permute-start.4
  26.4 2.7 %collective-permute-done.7 = f32[4,128,128]{2,1,0:T(8,128)S(1)} collective-permute-done((f32[4,128,128]{2,1,0:T(8,128)S(1)}, f32[4,128,128]{2,1,0:T(8,128)S(1)}, u32[]{:S(2)}, u32[]{:S(2)}) %collective-permute-start.7) | collective-permute-done | bytes 262176 | tf_op jit(solution)/shard_map/ppermute | solution.py:48
  29.3 8.4 %collective-permute-done.4.far_ref = f32[8,128,128]{2,1,0:T(8,128)S(1)} collective-permute-done((f32[8,128,128]{2,1,0:T(8,128)S(1)}, f32[8,128,128]{2,1,0:T(8,128)S(1)}, u32[]{:S(2)}, u32[]{:S(2)}) %collective-permute-start.4) | collective-permute-done | bytes 524320 | tf_op jit(solution)/shard_map/ppermute | solution.py:48
  37.7 5.0 %shard_map.50 = (f32[8,128,128]{2,1,0:T(8,128)S(1)}, f32[8,128,128]{2,1,0:T(8,128)S(1)}) custom-call(s32[1]{0:T(128)} %bitcast.place_ref, s32[1]{0:T(128)} %copy.30.size_ref, f32[8,128,128]{2,1,0:T(8,128)S(1)} %constant_dynamic-update-slice_fusion.near_ref, f32[8,128,128]{2,1,0:T(8,128)S(1)} %collective-permute-done.4.far_ref, bf16[1024,2048]{1,0:T(8,128)(2,1)} %bitcast.27), custom_call_target="tpu_custom_call" | custom-call | flops 2147483648 | bytes 8388608 | tf_op jit(solution)/shard_map/pallas_call | solution.py:170
  44.2 5.0 %shard_map.51 = (f32[8,128,128]{2,1,0:T(8,128)S(1)}, f32[8,128,128]{2,1,0:T(8,128)S(1)}) custom-call(s32[1]{0:T(128)} %bitcast.place_ref, s32[1]{0:T(128)} %copy.30.size_ref, f32[8,128,128]{2,1,0:T(8,128)S(1)} %constant_dynamic-update-slice_fusion.5.near_ref, f32[8,128,128]{2,1,0:T(8,128)S(1)} %collective-permute-done.8.far_ref, bf16[1024,2048]{1,0:T(8,128)(2,1)} %bitcast.28), custom_call_target="tpu_custom_call" | custom-call | flops 2147483648 | bytes 8388608 | tf_op jit(solution)/shard_map/pallas_call | solution.py:170
  49.8 4.2 %collective-permute-done.5 = f32[8,128,128]{2,1,0:T(8,128)S(1)} collective-permute-done((f32[8,128,128]{2,1,0:T(8,128)S(1)}, f32[8,128,128]{2,1,0:T(8,128)S(1)}, u32[]{:S(2)}, u32[]{:S(2)}) %collective-permute-start.5) | collective-permute-done | bytes 524320 | tf_op jit(solution)/shard_map/ppermute | solution.py:48
  54.1 8.9 %collective-permute-done.9 = f32[8,128,128]{2,1,0:T(8,128)S(1)} collective-permute-done((f32[8,128,128]{2,1,0:T(8,128)S(1)}, f32[8,128,128]{2,1,0:T(8,128)S(1)}, u32[]{:S(2)}, u32[]{:S(2)}) %collective-permute-start.9) | collective-permute-done | bytes 524320 | tf_op jit(solution)/shard_map/ppermute | solution.py:48
  63.7 2.1 collective-permute-done.6
  65.9 3.7 %collective-permute-done.10 = f32[4,128,128]{2,1,0:T(8,128)S(1)} collective-permute-done((f32[4,128,128]{2,1,0:T(8,128)S(1)}, f32[4,128,128]{2,1,0:T(8,128)S(1)}, u32[]{:S(2)}, u32[]{:S(2)}) %collective-permute-start.10) | collective-permute-done | bytes 262176 | tf_op jit(solution)/shard_map/ppermute | solution.py:48
  69.6 2.4 %collective-permute-start.11 = (f32[2,128,128]{2,1,0:T(8,128)S(1)}, f32[2,128,128]{2,1,0:T(8,128)S(1)}, u32[]{:S(2)}, u32[]{:S(2)}) collective-permute-start(f32[2,128,128]{2,1,0:T(8,128)S(1)} %pad_maximum_fusion.6), channel_id=1, source_target_pairs={{0,4},{1,5},{2,6},{3,7},{4,0},{5,1},{6,2},{7,3},{8,12},{9,13},{10,... | collective-permute-start | bytes 393224 | tf_op jit(solution)/shard_map/ppermute | solution.py:48
  75.0 3.4 %collective-permute-done.12 = f32[2,128,128]{2,1,0:T(8,128)S(1)} collective-permute-done((f32[2,128,128]{2,1,0:T(8,128)S(1)}, f32[2,128,128]{2,1,0:T(8,128)S(1)}, u32[]{:S(2)}, u32[]{:S(2)}) %collective-permute-start.12) | collective-permute-done | bytes 131104 | tf_op jit(solution)/shard_map/ppermute | solution.py:48
  78.4 5.4 %collective-permute-done.13 = f32[2,128,128]{2,1,0:T(8,128)S(1)} collective-permute-done((f32[2,128,128]{2,1,0:T(8,128)S(1)}, f32[2,128,128]{2,1,0:T(8,128)S(1)}, u32[]{:S(2)}, u32[]{:S(2)}) %collective-permute-start.13) | collective-permute-done | bytes 131104 | tf_op jit(solution)/shard_map/ppermute | solution.py:48
  83.9 3.5 %collective-permute-start.14 = (f32[2,128,128]{2,1,0:T(8,128)S(1)}, f32[2,128,128]{2,1,0:T(8,128)S(1)}, u32[]{:S(2)}, u32[]{:S(2)}) collective-permute-start(f32[2,128,128]{2,1,0:T(8,128)S(1)} %pad_maximum_fusion.9), channel_id=1, source_target_pairs={{0,4},{1,5},{2,6},{3,7},{4,0},{5,1},{6,2},{7,3},{8,12},{9,13},{10,... | collective-permute-start | bytes 393224 | tf_op jit(solution)/shard_map/ppermute | solution.py:48
  87.5 1.9 collective-permute-start.15
  90.7 2.6 %collective-permute-done.15 = f32[2,128,128]{2,1,0:T(8,128)S(1)} collective-permute-done((f32[2,128,128]{2,1,0:T(8,128)S(1)}, f32[2,128,128]{2,1,0:T(8,128)S(1)}, u32[]{:S(2)}, u32[]{:S(2)}) %collective-permute-start.15) | collective-permute-done | bytes 131104 | tf_op jit(solution)/shard_map/ppermute | solution.py:48
  93.3 3.2 %collective-permute-done.16 = f32[2,128,128]{2,1,0:T(8,128)S(1)} collective-permute-done((f32[2,128,128]{2,1,0:T(8,128)S(1)}, f32[2,128,128]{2,1,0:T(8,128)S(1)}, u32[]{:S(2)}, u32[]{:S(2)}) %collective-permute-start.16) | collective-permute-done | bytes 131104 | tf_op jit(solution)/shard_map/ppermute | solution.py:48
  97.8 5.3 %collective-permute-done.17 = f32[4,128,128]{2,1,0:T(8,128)S(1)} collective-permute-done((f32[4,128,128]{2,1,0:T(8,128)S(1)}, f32[4,128,128]{2,1,0:T(8,128)S(1)}, u32[]{:S(2)}, u32[]{:S(2)}) %collective-permute-start.17) | collective-permute-done | bytes 262176 | tf_op jit(solution)/shard_map/ppermute | solution.py:48
  105.2 12.4 %collective-permute-done.18.far_ref.refs_1_ = f32[8,128,128]{2,1,0:T(8,128)S(1)} collective-permute-done((f32[8,128,128]{2,1,0:T(8,128)S(1)}, f32[8,128,128]{2,1,0:T(8,128)S(1)}, u32[]{:S(2)}, u32[]{:S(2)}) %collective-permute-start.18) | collective-permute-done | bytes 524320 | tf_op jit(solution)/shard_map/ppermute | solution.py:48
  117.7 5.0 %shard_map.52 = (f32[8,128,128]{2,1,0:T(8,128)S(1)}, f32[8,128,128]{2,1,0:T(8,128)S(1)}) custom-call(s32[1]{0:T(128)} %bitcast.place_ref, s32[1]{0:T(128)} %copy.30.size_ref, f32[8,128,128]{2,1,0:T(8,128)S(1)} %constant_dynamic-update-slice_fusion.10.near_ref.refs_0_, f32[8,128,128]{2,1,0:T(8,128)S(1)} %collective-permute-done.18.far_ref.refs_1_, ...), custom_call_target="tpu_custom_call" | custom-call | flops 2147483648 | bytes 8388608 | tf_op jit(solution)/shard_map/pallas_call | solution.py:170
  123.8 5.0 %shard_map.53 = (f32[8,128,128]{2,1,0:T(8,128)S(1)}, f32[8,128,128]{2,1,0:T(8,128)S(1)}) custom-call(s32[1]{0:T(128)} %bitcast.place_ref, s32[1]{0:T(128)} %copy.30.size_ref, f32[8,128,128]{2,1,0:T(8,128)S(1)} %constant_dynamic-update-slice_fusion.15.near_ref.refs_2_, f32[8,128,128]{2,1,0:T(8,128)S(1)} %collective-permute-done.22.far_ref.refs_3_, ...), custom_call_target="tpu_custom_call" | custom-call | flops 2147483648 | bytes 8388608 | tf_op jit(solution)/shard_map/pallas_call | solution.py:170
  129.1 2.8 %collective-permute-done.19 = f32[8,128,128]{2,1,0:T(8,128)S(1)} collective-permute-done((f32[8,128,128]{2,1,0:T(8,128)S(1)}, f32[8,128,128]{2,1,0:T(8,128)S(1)}, u32[]{:S(2)}, u32[]{:S(2)}) %collective-permute-start.19) | collective-permute-done | bytes 524320 | tf_op jit(solution)/shard_map/ppermute | solution.py:48
  132.9 5.2 %collective-permute-done.23 = f32[8,128,128]{2,1,0:T(8,128)S(1)} collective-permute-done((f32[8,128,128]{2,1,0:T(8,128)S(1)}, f32[8,128,128]{2,1,0:T(8,128)S(1)}, u32[]{:S(2)}, u32[]{:S(2)}) %collective-permute-start.23) | collective-permute-done | bytes 524320 | tf_op jit(solution)/shard_map/ppermute | solution.py:48
  139.1 1.7 collective-permute-done.20
  140.9 3.7 %collective-permute-done.24 = f32[4,128,128]{2,1,0:T(8,128)S(1)} collective-permute-done((f32[4,128,128]{2,1,0:T(8,128)S(1)}, f32[4,128,128]{2,1,0:T(8,128)S(1)}, u32[]{:S(2)}, u32[]{:S(2)}) %collective-permute-start.24) | collective-permute-done | bytes 262176 | tf_op jit(solution)/shard_map/ppermute | solution.py:48
  144.6 2.3 %collective-permute-start.25 = (f32[2,128,128]{2,1,0:T(8,128)S(1)}, f32[2,128,128]{2,1,0:T(8,128)S(1)}, u32[]{:S(2)}, u32[]{:S(2)}) collective-permute-start(f32[2,128,128]{2,1,0:T(8,128)S(1)} %pad_maximum_fusion.10), channel_id=1, source_target_pairs={{0,4},{1,5},{2,6},{3,7},{4,0},{5,1},{6,2},{7,3},{8,12},{9,13},{10,... | collective-permute-start | bytes 393224 | tf_op jit(solution)/shard_map/ppermute | solution.py:48
  147.0 1.8 collective-permute-start.26
  150.3 2.6 %collective-permute-done.26 = f32[2,128,128]{2,1,0:T(8,128)S(1)} collective-permute-done((f32[2,128,128]{2,1,0:T(8,128)S(1)}, f32[2,128,128]{2,1,0:T(8,128)S(1)}, u32[]{:S(2)}, u32[]{:S(2)}) %collective-permute-start.26) | collective-permute-done | bytes 131104 | tf_op jit(solution)/shard_map/ppermute | solution.py:48
  152.9 3.0 %collective-permute-done.27 = f32[2,128,128]{2,1,0:T(8,128)S(1)} collective-permute-done((f32[2,128,128]{2,1,0:T(8,128)S(1)}, f32[2,128,128]{2,1,0:T(8,128)S(1)}, u32[]{:S(2)}, u32[]{:S(2)}) %collective-permute-start.27) | collective-permute-done | bytes 131104 | tf_op jit(solution)/shard_map/ppermute | solution.py:48
  156.0 1.9 collective-permute-start.28
  161.1 5.5 %collective-permute-done.29 = f32[2,128,128]{2,1,0:T(8,128)S(1)} collective-permute-done((f32[2,128,128]{2,1,0:T(8,128)S(1)}, f32[2,128,128]{2,1,0:T(8,128)S(1)}, u32[]{:S(2)}, u32[]{:S(2)}) %collective-permute-start.29) | collective-permute-done | bytes 131104 | tf_op jit(solution)/shard_map/ppermute | solution.py:48
  168.5 4.6 %collective-permute-done.33 = f32[4,128,128]{2,1,0:T(8,128)S(1)} collective-permute-done((f32[4,128,128]{2,1,0:T(8,128)S(1)}, f32[4,128,128]{2,1,0:T(8,128)S(1)}, u32[]{:S(2)}, u32[]{:S(2)}) %collective-permute-start.33) | collective-permute-done | bytes 262176 | tf_op jit(solution)/shard_map/ppermute | solution.py:48
  173.7 1.6 collective-permute-start.32
  175.3 13.3 %shard_map.54.refs_4_ = f32[256,256]{1,0:T(8,128)S(1)} custom-call(s32[1]{0:T(128)} %bitcast.place_ref, f32[8,128,128]{2,1,0:T(8,128)S(1)} %constant_dynamic-update-slice_fusion.10.near_ref.refs_0_, f32[8,128,128]{2,1,0:T(8,128)S(1)} %collective-permute-done.18.far_ref.refs_1_, f32[8,128,128]{2,1,0:T(8,128)S(1)} %constant_dynamic-update-slice_fusion.15.near_ref.refs_2_, ...), custom_call_target="tpu_custom_call" | custom-call | flops 12000000000 | bytes 4194304 | tf_op jit(solution)/shard_map/pallas_call | solution.py:296
  188.7 10.0 %shard_map.55 = (f32[256,128]{1,0:T(8,128)S(1)}, f32[256,256]{1,0:T(8,128)S(1)}, f32[72,128]{1,0:T(8,128)S(1)}, f32[72,128]{1,0:T(8,128)S(1)}, f32[72,128]{1,0:T(8,128)S(1)}, /*index=5*/f32[72,128]{1,0:T(8,128)S(1)}) custom-call(s32[1]{0:T(128)S(6)} %and.4.quarter_ref, s32[1]{0:T(128)} %bitcast.place_ref, ...), custom_call_target="tpu_custom_call" | custom-call | flops 12000000000 | bytes 4194304 | tf_op jit(solution)/shard_map/pallas_call | solution.py:386
  199.2 1.6 collective-permute-start.36
  203.2 2.5 %collective-permute-done.37 = f32[72,128]{1,0:T(8,128)S(1)} collective-permute-done((f32[72,128]{1,0:T(8,128)S(1)}, f32[72,128]{1,0:T(8,128)S(1)}, u32[]{:S(2)}, u32[]{:S(2)}) %collective-permute-start.37) | collective-permute-done | bytes 36896 | tf_op jit(solution)/shard_map/ppermute | solution.py:48
  205.6 2.0 collective-permute-start.38
  210.1 2.6 %collective-permute-done.39 = f32[72,128]{1,0:T(8,128)S(1)} collective-permute-done((f32[72,128]{1,0:T(8,128)S(1)}, f32[72,128]{1,0:T(8,128)S(1)}, u32[]{:S(2)}, u32[]{:S(2)}) %collective-permute-start.39) | collective-permute-done | bytes 36896 | tf_op jit(solution)/shard_map/ppermute | solution.py:48
  212.7 1.7 collective-permute-done.40
  214.9 1.6 collective-permute-start.42
  217.9 11.2 %shard_map.56 = (f32[256,256]{1,0:T(8,128)S(1)}, f32[128,256]{1,0:T(8,128)}) custom-call(f32[256,256]{1,0:T(8,128)S(1)} %get-tuple-element.28.inner_ref, f32[256,128]{1,0:T(8,128)S(1)} %get-tuple-element.29.own_ref), custom_call_target="tpu_custom_call" | custom-call | flops 12000000000 | bytes 4194304 | tf_op jit(solution)/shard_map/pallas_call | solution.py:416
  (108 shorter events, 34.1 us)
Async XLA Ops:
  2.3 8.1 %collective-permute-start = (f32[2,128,128]{2,1,0:T(8,128)S(1)}, f32[2,128,128]{2,1,0:T(8,128)S(1)}, u32[]{:S(2)}, u32[]{:S(2)}) collective-permute-start(f32[2,128,128]{2,1,0:T(8,128)S(1)} %bitcast.24), channel_id=1, source_target_pairs={{0,4},{1,5},{2,6},{3,7},{4,0},{5,1},{6,2},{7,3},{8,12},{9,13},{10,... | collective-permute-start | bytes 393224 | tf_op jit(solution)/shard_map/ppermute | solution.py:48
  5.4 12.9 %collective-permute-start.1 = (f32[2,128,128]{2,1,0:T(8,128)S(1)}, f32[2,128,128]{2,1,0:T(8,128)S(1)}, u32[]{:S(2)}, u32[]{:S(2)}) collective-permute-start(f32[2,128,128]{2,1,0:T(8,128)S(1)} %bitcast.25), channel_id=1, source_target_pairs={{0,8},{1,9},{2,10},{3,11},{4,12},{5,13},{6,14},{7,15},{8,0},{9,1},... | collective-permute-start | bytes 393224 | tf_op jit(solution)/shard_map/ppermute | solution.py:48
  8.0 10.4 %collective-permute-start.2 = (f32[2,128,128]{2,1,0:T(8,128)S(1)}, f32[2,128,128]{2,1,0:T(8,128)S(1)}, u32[]{:S(2)}, u32[]{:S(2)}) collective-permute-start(f32[2,128,128]{2,1,0:T(8,128)S(1)} %bitcast.26), channel_id=1, source_target_pairs={{0,12},{1,13},{2,14},{3,15},{4,8},{5,9},{6,10},{7,11},{8,4},{9,5},... | collective-permute-start | bytes 393224 | tf_op jit(solution)/shard_map/ppermute | solution.py:48
  18.4 6.4 %collective-permute-start.3 = (f32[4,128,128]{2,1,0:T(8,128)S(1)}, f32[4,128,128]{2,1,0:T(8,128)S(1)}, u32[]{:S(2)}, u32[]{:S(2)}) collective-permute-start(f32[4,128,128]{2,1,0:T(8,128)S(1)} %pad_maximum_fusion), channel_id=1, source_target_pairs={{0,2},{1,3},{2,0},{3,1},{4,6},{5,7},{6,4},{7,5},{8,10},{9,11},{10,... | collective-permute-start | bytes 786440 | tf_op jit(solution)/shard_map/ppermute | solution.py:48
  20.0 9.2 %collective-permute-start.7 = (f32[4,128,128]{2,1,0:T(8,128)S(1)}, f32[4,128,128]{2,1,0:T(8,128)S(1)}, u32[]{:S(2)}, u32[]{:S(2)}) collective-permute-start(f32[4,128,128]{2,1,0:T(8,128)S(1)} %pad_maximum_fusion.1), channel_id=1, source_target_pairs={{0,1},{1,0},{2,3},{3,2},{4,5},{5,4},{6,7},{7,6},{8,9},{9,8},{10,11... | collective-permute-start | bytes 786440 | tf_op jit(solution)/shard_map/ppermute | solution.py:48
  24.9 12.8 %collective-permute-start.4 = (f32[8,128,128]{2,1,0:T(8,128)S(1)}, f32[8,128,128]{2,1,0:T(8,128)S(1)}, u32[]{:S(2)}, u32[]{:S(2)}) collective-permute-start(f32[8,128,128]{2,1,0:T(8,128)S(1)} %constant_dynamic-update-slice_fusion.near_ref), channel_id=1, source_target_pairs={{0,1},{1,0},{2,3},{3,2},{4,5},{5,4},{6,7},{7,6},{8,9},{9,8},{10,11... | collective-permute-start | bytes 1572872 | tf_op jit(solution)/shard_map/ppermute | solution.py:48
  29.2 15.0 %collective-permute-start.8 = (f32[8,128,128]{2,1,0:T(8,128)S(1)}, f32[8,128,128]{2,1,0:T(8,128)S(1)}, u32[]{:S(2)}, u32[]{:S(2)}) collective-permute-start(f32[8,128,128]{2,1,0:T(8,128)S(1)} %constant_dynamic-update-slice_fusion.5.near_ref), channel_id=1, source_target_pairs={{0,2},{1,3},{2,0},{3,1},{4,6},{5,7},{6,4},{7,5},{8,10},{9,11},{10,... | collective-permute-start | bytes 1572872 | tf_op jit(solution)/shard_map/ppermute | solution.py:48
  42.7 11.3 %collective-permute-start.5 = (f32[8,128,128]{2,1,0:T(8,128)S(1)}, f32[8,128,128]{2,1,0:T(8,128)S(1)}, u32[]{:S(2)}, u32[]{:S(2)}) collective-permute-start(f32[8,128,128]{2,1,0:T(8,128)S(1)} %get-tuple-element.21), channel_id=1, source_target_pairs={{0,1},{1,0},{2,3},{3,2},{4,5},{5,4},{6,7},{7,6},{8,9},{9,8},{10,11... | collective-permute-start | bytes 1572872 | tf_op jit(solution)/shard_map/ppermute | solution.py:48
  49.2 13.8 %collective-permute-start.9 = (f32[8,128,128]{2,1,0:T(8,128)S(1)}, f32[8,128,128]{2,1,0:T(8,128)S(1)}, u32[]{:S(2)}, u32[]{:S(2)}) collective-permute-start(f32[8,128,128]{2,1,0:T(8,128)S(1)} %get-tuple-element.23), channel_id=1, source_target_pairs={{0,2},{1,3},{2,0},{3,1},{4,6},{5,7},{6,4},{7,5},{8,10},{9,11},{10,... | collective-permute-start | bytes 1572872 | tf_op jit(solution)/shard_map/ppermute | solution.py:48
  54.0 11.8 %collective-permute-start.6 = (f32[4,128,128]{2,1,0:T(8,128)S(1)}, f32[4,128,128]{2,1,0:T(8,128)S(1)}, u32[]{:S(2)}, u32[]{:S(2)}) collective-permute-start(f32[4,128,128]{2,1,0:T(8,128)S(1)} %slice.103), channel_id=1, source_target_pairs={{0,2},{1,3},{2,0},{3,1},{4,6},{5,7},{6,4},{7,5},{8,10},{9,11},{10,... | collective-permute-start | bytes 786440 | tf_op jit(solution)/shard_map/ppermute | solution.py:48
  63.1 6.4 %collective-permute-start.10 = (f32[4,128,128]{2,1,0:T(8,128)S(1)}, f32[4,128,128]{2,1,0:T(8,128)S(1)}, u32[]{:S(2)}, u32[]{:S(2)}) collective-permute-start(f32[4,128,128]{2,1,0:T(8,128)S(1)} %slice.107), channel_id=1, source_target_pairs={{0,1},{1,0},{2,3},{3,2},{4,5},{5,4},{6,7},{7,6},{8,9},{9,8},{10,11... | collective-permute-start | bytes 786440 | tf_op jit(solution)/shard_map/ppermute | solution.py:48
  69.6 5.4 %collective-permute-start.11 = (f32[2,128,128]{2,1,0:T(8,128)S(1)}, f32[2,128,128]{2,1,0:T(8,128)S(1)}, u32[]{:S(2)}, u32[]{:S(2)}) collective-permute-start(f32[2,128,128]{2,1,0:T(8,128)S(1)} %pad_maximum_fusion.6), channel_id=1, source_target_pairs={{0,4},{1,5},{2,6},{3,7},{4,0},{5,1},{6,2},{7,3},{8,12},{9,13},{10,... | collective-permute-start | bytes 393224 | tf_op jit(solution)/shard_map/ppermute | solution.py:48
  72.0 6.4 %collective-permute-start.12 = (f32[2,128,128]{2,1,0:T(8,128)S(1)}, f32[2,128,128]{2,1,0:T(8,128)S(1)}, u32[]{:S(2)}, u32[]{:S(2)}) collective-permute-start(f32[2,128,128]{2,1,0:T(8,128)S(1)} %pad_maximum_fusion.7), channel_id=1, source_target_pairs={{0,8},{1,9},{2,10},{3,11},{4,12},{5,13},{6,14},{7,15},{8,0},{9,1},... | collective-permute-start | bytes 393224 | tf_op jit(solution)/shard_map/ppermute | solution.py:48
  73.5 10.4 %collective-permute-start.13 = (f32[2,128,128]{2,1,0:T(8,128)S(1)}, f32[2,128,128]{2,1,0:T(8,128)S(1)}, u32[]{:S(2)}, u32[]{:S(2)}) collective-permute-start(f32[2,128,128]{2,1,0:T(8,128)S(1)} %pad_maximum_fusion.8), channel_id=1, source_target_pairs={{0,12},{1,13},{2,14},{3,15},{4,8},{5,9},{6,10},{7,11},{8,4},{9,5},... | collective-permute-start | bytes 393224 | tf_op jit(solution)/shard_map/ppermute | solution.py:48
  83.9 6.8 %collective-permute-start.14 = (f32[2,128,128]{2,1,0:T(8,128)S(1)}, f32[2,128,128]{2,1,0:T(8,128)S(1)}, u32[]{:S(2)}, u32[]{:S(2)}) collective-permute-start(f32[2,128,128]{2,1,0:T(8,128)S(1)} %pad_maximum_fusion.9), channel_id=1, source_target_pairs={{0,4},{1,5},{2,6},{3,7},{4,0},{5,1},{6,2},{7,3},{8,12},{9,13},{10,... | collective-permute-start | bytes 393224 | tf_op jit(solution)/shard_map/ppermute | solution.py:48
  87.5 5.9 %collective-permute-start.15 = (f32[2,128,128]{2,1,0:T(8,128)S(1)}, f32[2,128,128]{2,1,0:T(8,128)S(1)}, u32[]{:S(2)}, u32[]{:S(2)}) collective-permute-start(f32[2,128,128]{2,1,0:T(8,128)S(1)} %pad_maximum_fusion.9), channel_id=1, source_target_pairs={{0,8},{1,9},{2,10},{3,11},{4,12},{5,13},{6,14},{7,15},{8,0},{9,1},... | collective-permute-start | bytes 393224 | tf_op jit(solution)/shard_map/ppermute | solution.py:48
  89.3 7.2 %collective-permute-start.16 = (f32[2,128,128]{2,1,0:T(8,128)S(1)}, f32[2,128,128]{2,1,0:T(8,128)S(1)}, u32[]{:S(2)}, u32[]{:S(2)}) collective-permute-start(f32[2,128,128]{2,1,0:T(8,128)S(1)} %pad_maximum_fusion.9), channel_id=1, source_target_pairs={{0,12},{1,13},{2,14},{3,15},{4,8},{5,9},{6,10},{7,11},{8,4},{9,5},... | collective-permute-start | bytes 393224 | tf_op jit(solution)/shard_map/ppermute | solution.py:48
  96.6 6.4 %collective-permute-start.17 = (f32[4,128,128]{2,1,0:T(8,128)S(1)}, f32[4,128,128]{2,1,0:T(8,128)S(1)}, u32[]{:S(2)}, u32[]{:S(2)}) collective-permute-start(f32[4,128,128]{2,1,0:T(8,128)S(1)} %pad_maximum_fusion.2), channel_id=1, source_target_pairs={{0,2},{1,3},{2,0},{3,1},{4,6},{5,7},{6,4},{7,5},{8,10},{9,11},{10,... | collective-permute-start | bytes 786440 | tf_op jit(solution)/shard_map/ppermute | solution.py:48
  97.2 7.1 %collective-permute-start.21 = (f32[4,128,128]{2,1,0:T(8,128)S(1)}, f32[4,128,128]{2,1,0:T(8,128)S(1)}, u32[]{:S(2)}, u32[]{:S(2)}) collective-permute-start(f32[4,128,128]{2,1,0:T(8,128)S(1)} %pad_maximum_fusion.3), channel_id=1, source_target_pairs={{0,1},{1,0},{2,3},{3,2},{4,5},{5,4},{6,7},{7,6},{8,9},{9,8},{10,11... | collective-permute-start | bytes 786440 | tf_op jit(solution)/shard_map/ppermute | solution.py:48
  103.1 14.6 %collective-permute-start.18 = (f32[8,128,128]{2,1,0:T(8,128)S(1)}, f32[8,128,128]{2,1,0:T(8,128)S(1)}, u32[]{:S(2)}, u32[]{:S(2)}) collective-permute-start(f32[8,128,128]{2,1,0:T(8,128)S(1)} %constant_dynamic-update-slice_fusion.10.near_ref.refs_0_), channel_id=1, source_target_pairs={{0,1},{1,0},{2,3},{3,2},{4,5},{5,4},{6,7},{7,6},{8,9},{9,8},{10,11... | collective-permute-start | bytes 1572872 | tf_op jit(solution)/shard_map/ppermute | solution.py:48
  104.3 19.5 %collective-permute-start.22 = (f32[8,128,128]{2,1,0:T(8,128)S(1)}, f32[8,128,128]{2,1,0:T(8,128)S(1)}, u32[]{:S(2)}, u32[]{:S(2)}) collective-permute-start(f32[8,128,128]{2,1,0:T(8,128)S(1)} %constant_dynamic-update-slice_fusion.15.near_ref.refs_2_), channel_id=1, source_target_pairs={{0,2},{1,3},{2,0},{3,1},{4,6},{5,7},{6,4},{7,5},{8,10},{9,11},{10,... | collective-permute-start | bytes 1572872 | tf_op jit(solution)/shard_map/ppermute | solution.py:48
  122.6 9.2 %collective-permute-start.19 = (f32[8,128,128]{2,1,0:T(8,128)S(1)}, f32[8,128,128]{2,1,0:T(8,128)S(1)}, u32[]{:S(2)}, u32[]{:S(2)}) collective-permute-start(f32[8,128,128]{2,1,0:T(8,128)S(1)} %get-tuple-element.25), channel_id=1, source_target_pairs={{0,1},{1,0},{2,3},{3,2},{4,5},{5,4},{6,7},{7,6},{8,9},{9,8},{10,11... | collective-permute-start | bytes 1572872 | tf_op jit(solution)/shard_map/ppermute | solution.py:48
  128.8 9.2 %collective-permute-start.23 = (f32[8,128,128]{2,1,0:T(8,128)S(1)}, f32[8,128,128]{2,1,0:T(8,128)S(1)}, u32[]{:S(2)}, u32[]{:S(2)}) collective-permute-start(f32[8,128,128]{2,1,0:T(8,128)S(1)} %get-tuple-element.27), channel_id=1, source_target_pairs={{0,2},{1,3},{2,0},{3,1},{4,6},{5,7},{6,4},{7,5},{8,10},{9,11},{10,... | collective-permute-start | bytes 1572872 | tf_op jit(solution)/shard_map/ppermute | solution.py:48
  132.0 8.9 %collective-permute-start.20 = (f32[4,128,128]{2,1,0:T(8,128)S(1)}, f32[4,128,128]{2,1,0:T(8,128)S(1)}, u32[]{:S(2)}, u32[]{:S(2)}) collective-permute-start(f32[4,128,128]{2,1,0:T(8,128)S(1)} %slice.115), channel_id=1, source_target_pairs={{0,2},{1,3},{2,0},{3,1},{4,6},{5,7},{6,4},{7,5},{8,10},{9,11},{10,... | collective-permute-start | bytes 786440 | tf_op jit(solution)/shard_map/ppermute | solution.py:48
  138.1 6.4 %collective-permute-start.24 = (f32[4,128,128]{2,1,0:T(8,128)S(1)}, f32[4,128,128]{2,1,0:T(8,128)S(1)}, u32[]{:S(2)}, u32[]{:S(2)}) collective-permute-start(f32[4,128,128]{2,1,0:T(8,128)S(1)} %slice.119), channel_id=1, source_target_pairs={{0,1},{1,0},{2,3},{3,2},{4,5},{5,4},{6,7},{7,6},{8,9},{9,8},{10,11... | collective-permute-start | bytes 786440 | tf_op jit(solution)/shard_map/ppermute | solution.py:48
  144.6 5.7 %collective-permute-start.25 = (f32[2,128,128]{2,1,0:T(8,128)S(1)}, f32[2,128,128]{2,1,0:T(8,128)S(1)}, u32[]{:S(2)}, u32[]{:S(2)}) collective-permute-start(f32[2,128,128]{2,1,0:T(8,128)S(1)} %pad_maximum_fusion.10), channel_id=1, source_target_pairs={{0,4},{1,5},{2,6},{3,7},{4,0},{5,1},{6,2},{7,3},{8,12},{9,13},{10,... | collective-permute-start | bytes 393224 | tf_op jit(solution)/shard_map/ppermute | solution.py:48
  147.0 5.9 %collective-permute-start.26 = (f32[2,128,128]{2,1,0:T(8,128)S(1)}, f32[2,128,128]{2,1,0:T(8,128)S(1)}, u32[]{:S(2)}, u32[]{:S(2)}) collective-permute-start(f32[2,128,128]{2,1,0:T(8,128)S(1)} %pad_maximum_fusion.11), channel_id=1, source_target_pairs={{0,8},{1,9},{2,10},{3,11},{4,12},{5,13},{6,14},{7,15},{8,0},{9,1},... | collective-permute-start | bytes 393224 | tf_op jit(solution)/shard_map/ppermute | solution.py:48
  148.8 7.2 %collective-permute-start.27 = (f32[2,128,128]{2,1,0:T(8,128)S(1)}, f32[2,128,128]{2,1,0:T(8,128)S(1)}, u32[]{:S(2)}, u32[]{:S(2)}) collective-permute-start(f32[2,128,128]{2,1,0:T(8,128)S(1)} %pad_maximum_fusion.12), channel_id=1, source_target_pairs={{0,12},{1,13},{2,14},{3,15},{4,8},{5,9},{6,10},{7,11},{8,4},{9,5},... | collective-permute-start | bytes 393224 | tf_op jit(solution)/shard_map/ppermute | solution.py:48
  156.0 5.0 %collective-permute-start.28 = (f32[2,128,128]{2,1,0:T(8,128)S(1)}, f32[2,128,128]{2,1,0:T(8,128)S(1)}, u32[]{:S(2)}, u32[]{:S(2)}) collective-permute-start(f32[2,128,128]{2,1,0:T(8,128)S(1)} %pad_maximum_fusion.13), channel_id=1, source_target_pairs={{0,4},{1,5},{2,6},{3,7},{4,0},{5,1},{6,2},{7,3},{8,12},{9,13},{10,... | collective-permute-start | bytes 393224 | tf_op jit(solution)/shard_map/ppermute | solution.py:48
  157.9 8.7 %collective-permute-start.29 = (f32[2,128,128]{2,1,0:T(8,128)S(1)}, f32[2,128,128]{2,1,0:T(8,128)S(1)}, u32[]{:S(2)}, u32[]{:S(2)}) collective-permute-start(f32[2,128,128]{2,1,0:T(8,128)S(1)} %pad_maximum_fusion.13), channel_id=1, source_target_pairs={{0,8},{1,9},{2,10},{3,11},{4,12},{5,13},{6,14},{7,15},{8,0},{9,1},... | collective-permute-start | bytes 393224 | tf_op jit(solution)/shard_map/ppermute | solution.py:48
  159.0 7.6 %collective-permute-start.30 = (f32[2,128,128]{2,1,0:T(8,128)S(1)}, f32[2,128,128]{2,1,0:T(8,128)S(1)}, u32[]{:S(2)}, u32[]{:S(2)}) collective-permute-start(f32[2,128,128]{2,1,0:T(8,128)S(1)} %pad_maximum_fusion.13), channel_id=1, source_target_pairs={{0,12},{1,13},{2,14},{3,15},{4,8},{5,9},{6,10},{7,11},{8,4},{9,5},... | collective-permute-start | bytes 393224 | tf_op jit(solution)/shard_map/ppermute | solution.py:48
  166.7 6.4 %collective-permute-start.33 = (f32[4,128,128]{2,1,0:T(8,128)S(1)}, f32[4,128,128]{2,1,0:T(8,128)S(1)}, u32[]{:S(2)}, u32[]{:S(2)}) collective-permute-start(f32[4,128,128]{2,1,0:T(8,128)S(1)} %pad_maximum_fusion.5), channel_id=1, source_target_pairs={{0,1},{1,0},{2,3},{3,2},{4,5},{5,4},{6,7},{7,6},{8,9},{9,8},{10,11... | collective-permute-start | bytes 786440 | tf_op jit(solution)/shard_map/ppermute | solution.py:48
  167.0 6.7 %collective-permute-start.31 = (f32[4,128,128]{2,1,0:T(8,128)S(1)}, f32[4,128,128]{2,1,0:T(8,128)S(1)}, u32[]{:S(2)}, u32[]{:S(2)}) collective-permute-start(f32[4,128,128]{2,1,0:T(8,128)S(1)} %pad_maximum_fusion.4), channel_id=1, source_target_pairs={{0,2},{1,3},{2,0},{3,1},{4,6},{5,7},{6,4},{7,5},{8,10},{9,11},{10,... | collective-permute-start | bytes 786440 | tf_op jit(solution)/shard_map/ppermute | solution.py:48
  173.2 15.5 %collective-permute-start.34 = (f32[8,128,128]{2,1,0:T(8,128)S(1)}, f32[8,128,128]{2,1,0:T(8,128)S(1)}, u32[]{:S(2)}, u32[]{:S(2)}) collective-permute-start(f32[8,128,128]{2,1,0:T(8,128)S(1)} %constant_dynamic-update-slice_fusion.25.refs_2_), channel_id=1, source_target_pairs={{0,2},{1,3},{2,0},{3,1},{4,6},{5,7},{6,4},{7,5},{8,10},{9,11},{10,... | collective-permute-start | bytes 1572872 | tf_op jit(solution)/shard_map/ppermute | solution.py:48
  173.7 15.0 %collective-permute-start.32 = (f32[8,128,128]{2,1,0:T(8,128)S(1)}, f32[8,128,128]{2,1,0:T(8,128)S(1)}, u32[]{:S(2)}, u32[]{:S(2)}) collective-permute-start(f32[8,128,128]{2,1,0:T(8,128)S(1)} %constant_dynamic-update-slice_fusion.20.refs_0_), channel_id=1, source_target_pairs={{0,1},{1,0},{2,3},{3,2},{4,5},{5,4},{6,7},{7,6},{8,9},{9,8},{10,11... | collective-permute-start | bytes 1572872 | tf_op jit(solution)/shard_map/ppermute | solution.py:48
  198.7 4.0 %collective-permute-start.35 = (f32[72,128]{1,0:T(8,128)S(1)}, f32[72,128]{1,0:T(8,128)S(1)}, u32[]{:S(2)}, u32[]{:S(2)}) collective-permute-start(f32[72,128]{1,0:T(8,128)S(1)} %get-tuple-element.33), channel_id=1, source_target_pairs={{0,1},{1,0},{2,3},{3,2},{4,5},{5,4},{6,7},{7,6},{8,9},{9,8},{10,11... | collective-permute-start | bytes 110600 | tf_op jit(solution)/shard_map/ppermute | solution.py:48
  199.2 4.0 %collective-permute-start.36 = (f32[72,128]{1,0:T(8,128)S(1)}, f32[72,128]{1,0:T(8,128)S(1)}, u32[]{:S(2)}, u32[]{:S(2)}) collective-permute-start(f32[72,128]{1,0:T(8,128)S(1)} %get-tuple-element.34), channel_id=1, source_target_pairs={{0,2},{1,3},{2,0},{3,1},{4,6},{5,7},{6,4},{7,5},{8,10},{9,11},{10,... | collective-permute-start | bytes 110600 | tf_op jit(solution)/shard_map/ppermute | solution.py:48
  200.8 4.9 %collective-permute-start.37 = (f32[72,128]{1,0:T(8,128)S(1)}, f32[72,128]{1,0:T(8,128)S(1)}, u32[]{:S(2)}, u32[]{:S(2)}) collective-permute-start(f32[72,128]{1,0:T(8,128)S(1)} %get-tuple-element.35), channel_id=1, source_target_pairs={{0,3},{1,2},{2,1},{3,0},{4,7},{5,6},{6,5},{7,4},{8,11},{9,10},{10,... | collective-permute-start | bytes 110600 | tf_op jit(solution)/shard_map/ppermute | solution.py:48
  205.6 4.5 %collective-permute-start.38 = (f32[72,128]{1,0:T(8,128)S(1)}, f32[72,128]{1,0:T(8,128)S(1)}, u32[]{:S(2)}, u32[]{:S(2)}) collective-permute-start(f32[72,128]{1,0:T(8,128)S(1)} %add_add_fusion.1), channel_id=1, source_target_pairs={{0,4},{1,5},{2,6},{3,7},{4,0},{5,1},{6,2},{7,3},{8,12},{9,13},{10,... | collective-permute-start | bytes 110600 | tf_op jit(solution)/shard_map/ppermute | solution.py:48
  207.6 5.0 %collective-permute-start.39 = (f32[72,128]{1,0:T(8,128)S(1)}, f32[72,128]{1,0:T(8,128)S(1)}, u32[]{:S(2)}, u32[]{:S(2)}) collective-permute-start(f32[72,128]{1,0:T(8,128)S(1)} %add_add_fusion.1), channel_id=1, source_target_pairs={{0,8},{1,9},{2,10},{3,11},{4,12},{5,13},{6,14},{7,15},{8,0},{9,1},... | collective-permute-start | bytes 110600 | tf_op jit(solution)/shard_map/ppermute | solution.py:48
  208.6 5.8 %collective-permute-start.40 = (f32[72,128]{1,0:T(8,128)S(1)}, f32[72,128]{1,0:T(8,128)S(1)}, u32[]{:S(2)}, u32[]{:S(2)}) collective-permute-start(f32[72,128]{1,0:T(8,128)S(1)} %add_add_fusion.1), channel_id=1, source_target_pairs={{0,12},{1,13},{2,14},{3,15},{4,8},{5,9},{6,10},{7,11},{8,4},{9,5},... | collective-permute-start | bytes 110600 | tf_op jit(solution)/shard_map/ppermute | solution.py:48
  214.4 14.7 %collective-permute-start.41 = (f32[72,128]{1,0:T(8,128)S(1)}, f32[72,128]{1,0:T(8,128)S(1)}, u32[]{:S(2)}, u32[]{:S(2)}) collective-permute-start(f32[72,128]{1,0:T(8,128)S(1)} %add_add_fusion.refs_0_), channel_id=1, source_target_pairs={{0,1},{1,0},{2,3},{3,2},{4,5},{5,4},{6,7},{7,6},{8,9},{9,8},{10,11... | collective-permute-start | bytes 110600 | tf_op jit(solution)/shard_map/ppermute | solution.py:48
  214.9 14.2 %collective-permute-start.42 = (f32[72,128]{1,0:T(8,128)S(1)}, f32[72,128]{1,0:T(8,128)S(1)}, u32[]{:S(2)}, u32[]{:S(2)}) collective-permute-start(f32[72,128]{1,0:T(8,128)S(1)} %add_add_fusion.refs_0_), channel_id=1, source_target_pairs={{0,2},{1,3},{2,0},{3,1},{4,6},{5,7},{6,4},{7,5},{8,10},{9,11},{10,... | collective-permute-start | bytes 110600 | tf_op jit(solution)/shard_map/ppermute | solution.py:48
  216.4 12.7 %collective-permute-start.43 = (f32[72,128]{1,0:T(8,128)S(1)}, f32[72,128]{1,0:T(8,128)S(1)}, u32[]{:S(2)}, u32[]{:S(2)}) collective-permute-start(f32[72,128]{1,0:T(8,128)S(1)} %add_add_fusion.refs_0_), channel_id=1, source_target_pairs={{0,3},{1,2},{2,1},{3,0},{4,7},{5,6},{6,5},{7,4},{8,11},{9,10},{10,... | collective-permute-start | bytes 110600 | tf_op jit(solution)/shard_map/ppermute | solution.py:48
  230.4 1.2 collective-permute-start.44

commit v3 on v2

v3 whole, which is shorter than its diff:
```python
import functools
import math

import jax
import jax.numpy as jnp
from jax import lax
from jax.experimental import pallas as pl
from jax.experimental.pallas import tpu as pltpu
from jax.sharding import PartitionSpec as P

LANES = 128
SUBLANES = 8
BLOCK = 1024
PANEL = 32
PIECES = 2
CODES = 128
STEPS = 65535.0
LEAST = 2.0**-90
VMEM_LIMIT = 48 * 1024 * 1024
HIGHEST = lax.Precision.HIGHEST
FACTOR_COST = pl.CostEstimate(flops=12_000_000_000, bytes_accessed=4 << 20, transcendentals=0)


def stage_bits(groups):
    count = groups.bit_length() - 1
    return [list(range(count))[place : place + 2] for place in range(0, count, 2)]


def offsets(bits):
    found = [0]
    for bit in bits:
        found = found + [value ^ (1 << bit) for value in found]
    return found


def relative_order(stages):
    order = [0]
    for bits in reversed(stages):
        order = [high ^ low for high in offsets(bits) for low in order]
    return order


def exchange(value, groups, offset):
    return lax.ppermute(value, "smp", [(device, device ^ offset) for device in range(groups)])


def reduce_chunks(keep, sends, groups, packed):
    stages = stage_bits(groups)
    for depth, bits in enumerate(stages):
        arrived = [exchange(send, groups, span) for send, span in zip(sends, offsets(bits)[1:])]
        parts = len(offsets(stages[depth + 1])) if depth + 1 < len(stages) else 1
        if packed:
            keep, *sends = combine(keep, arrived, parts)
        else:
            keep, *sends = jnp.split(keep + sum(arrived), parts, axis=0)
    return keep, sends[0] if packed else keep


def gather_chunks(message, groups):
    stages = stage_bits(groups)
    for bits in reversed(stages[1:]):
        message = jnp.concatenate([message] + [exchange(message, groups, span) for span in offsets(bits)[1:]], axis=0)
    return [message] + [exchange(message, groups, span) for span in offsets(stages[0])[1:]]


def pair_sum(parts):
    while len(parts) > 1:
        parts = [left + right for left, right in zip(parts[::2], parts[1::2])]
    return parts[0]


def sum_quarters(quarters, groups):
    stages = stage_bits(groups)
    spans = offsets(stages[0])
    total = pair_sum([quarters[0]] + [exchange(part, groups, span) for part, span in zip(quarters[1:], spans[1:])])
    for bits in stages[1:]:
        total = pair_sum([total] + [exchange(total, groups, span) for span in offsets(bits)[1:]])
    return [total] + [exchange(total, groups, span) for span in spans[1:]]


def row_scales(peaks):
    codes = jnp.ceil(jnp.log2(jnp.maximum(peaks, LEAST)) * CODES) + 1.0
    return codes, jnp.exp2(codes * (1.0 / CODES))


def gather_columns(columns):
    lane = lax.broadcasted_iota(jnp.int32, (LANES, LANES), 1)
    matrix = jnp.zeros((LANES, LANES), jnp.float32)
    for place, column in enumerate(columns):
        matrix = jnp.where(lane == place, column, matrix)
    return matrix


def pack_tiles(tiles):
    peaks = gather_columns([jnp.max(jnp.abs(tile), axis=1, keepdims=True) for tile in tiles])
    codes, scales = row_scales(peaks)
    factors = STEPS / scales
    lines = codes.T
    half = LANES // 2
    messages = []
    for place, tile in enumerate(tiles):
        value = jnp.round(tile * factors[:, place : place + 1]).astype(jnp.int32)
        high = jnp.right_shift(value, 1)
        low = jnp.bitwise_and(value, 1)
        words = jnp.bitwise_or(jnp.left_shift(high[:half], 16), jnp.bitwise_and(high[half:], 0xFFFF))
        code = jnp.broadcast_to(lines[place : place + 1, :], (SUBLANES, LANES)).astype(jnp.int32)
        extra = jnp.left_shift(code, 16)
        for group in range(LANES // SUBLANES):
            bits = low[group * SUBLANES : (group + 1) * SUBLANES]
            extra = jnp.bitwise_or(extra, jnp.left_shift(bits, group))
        messages.append(jnp.concatenate([words, extra], axis=0))
    return messages


def unpack_tiles(messages):
    half = LANES // 2
    lines = [jnp.right_shift(message[half : half + 1], 16).astype(jnp.float32) for message in messages]
    lines.append(jnp.zeros((LANES - len(messages), LANES), jnp.float32))
    scales = (jnp.exp2(jnp.concatenate(lines, axis=0) * (1.0 / CODES)) * (1.0 / STEPS)).T

    def tile(place):
        words, extra = messages[place][:half], messages[place][half:]
        high = jnp.concatenate([jnp.right_shift(words, 16), jnp.right_shift(jnp.left_shift(words, 16), 16)], axis=0)
        low = jnp.concatenate(
            [jnp.bitwise_and(jnp.right_shift(extra, group), 1) for group in range(LANES // SUBLANES)], axis=0
        )
        value = jnp.bitwise_or(jnp.left_shift(high, 1), low)
        return value.astype(jnp.float32) * scales[:, place : place + 1]

    return [functools.partial(tile, place) for place in range(len(messages))]


PACKED = LANES // 2 + SUBLANES


def pack_chunks(chunks):
    parts = chunks[0].shape[0] // LANES
    messages = pack_tiles([chunk[part * LANES : (part + 1) * LANES] for chunk in chunks for part in range(parts)])
    return [jnp.concatenate(messages[place * parts : (place + 1) * parts], axis=0) for place in range(len(chunks))]


def unpack_chunks(messages):
    parts = messages[0].shape[0] // PACKED
    tiles = unpack_tiles(
        [message[part * PACKED : (part + 1) * PACKED] for message in messages for part in range(parts)]
    )
    return [tiles[place * parts : (place + 1) * parts] for place in range(len(messages))]


def encode_kernel(place_ref, size_ref, start_ref, out_ref):
    width, size = start_ref.shape
    row = place_ref[0] * width + lax.broadcasted_iota(jnp.int32, (width, size), 0)
    value = jnp.where(row < size_ref[0], start_ref[...], 0.0)
    out_ref[0] = pack_chunks([value.T])[0]


def encode(place, sizes, start):
    width, size = start.shape
    scalar, vmem = pl.BlockSpec(memory_space=pltpu.SMEM), pl.BlockSpec(memory_space=pltpu.VMEM)
    return pl.pallas_call(
        encode_kernel,
        in_specs=[scalar, scalar, vmem],
        out_specs=vmem,
        out_shape=jax.ShapeDtypeStruct((1, size // LANES * PACKED, width), jnp.int32),
    )(place, sizes, start)


def combine_kernel(count, parts, keep_ref, *refs):
    arrived, own_ref, sends = refs[:count], refs[count], refs[count + 1 :]
    chunks = keep_ref.shape[0]
    tiles = unpack_chunks([part[place] for place in range(chunks) for part in arrived])
    totals = []
    for place in range(chunks):
        total = keep_ref[place]
        for source in range(count):
            total = total + jnp.concatenate([tile() for tile in tiles[place * count + source]], axis=0)
        totals.append(total)
    width = chunks // parts
    for place in range(width):
        own_ref[place] = totals[place]
    first = 0 if parts == 1 else width
    for place, message in enumerate(pack_chunks(totals[first:])):
        sends[place // width][place % width] = message


def combine(keep, arrived, parts):
    chunks, rows, lanes = keep.shape
    width = chunks // parts
    vmem = pl.BlockSpec(memory_space=pltpu.VMEM)
    outs = [jax.ShapeDtypeStruct((width, rows, lanes), jnp.float32)]
    outs += [jax.ShapeDtypeStruct((width, rows // LANES * PACKED, lanes), jnp.int32)] * max(parts - 1, 1)
    return pl.pallas_call(
        functools.partial(combine_kernel, len(arrived), parts),
        in_specs=[vmem] * (1 + len(arrived)),
        out_specs=[vmem] * len(outs),
        out_shape=outs,
        compiler_params=pltpu.CompilerParams(vmem_limit_bytes=VMEM_LIMIT),
    )(keep, *arrived)


def split_pieces(value, pieces):
    parts = []
    rest = value
    for piece in range(pieces):
        part = rest.astype(jnp.bfloat16)
        parts.append(part)
        if piece + 1 < pieces:
            rest = rest - part.astype(jnp.float32)
    return parts


def load_all(order, place_ref, refs, full_ref):
    if len(refs) == 1:
        full_ref[...] = refs[0][...]
        return
    width = refs[0].shape[2]
    each = refs[0].shape[0]
    tiles = unpack_chunks([ref[place] for ref in refs for place in range(each)])
    for offset, chunk in zip(order, tiles):
        first = pl.multiple_of(jnp.bitwise_xor(place_ref[0], offset) * width, width)
        for part, tile in enumerate(chunk):
            full_ref[pl.ds(part * LANES, LANES), pl.ds(first, width)] = tile()


def apply_kernel(order, normalise, scale, sources, place_ref, size_ref, rows_ref, *refs):
    refs, outs, (full_ref, split_ref, work_ref) = refs[:sources], refs[sources:-3], refs[-3:]
    step = pl.program_id(0)
    size, cap = full_ref.shape

    @pl.when(step == 0)
    def _():
        load_all(order, place_ref, refs, full_ref)
        value = full_ref[...]
        if normalise:
            start_factor(work_ref, rows_inner(value))
            inverse_factor(work_ref, size, PANEL)
            value = jnp.dot(
                finish_factor(work_ref), value, precision=HIGHEST, preferred_element_type=jnp.float32
            )
        for piece, part in enumerate(split_pieces(value, PIECES)):
            split_ref[pl.ds(piece * size, size), :] = part

    rows = rows_ref[...]
    image = lax.dot_general(
        split_ref[...], rows, (((1,), (1,)), ((), ())), preferred_element_type=jnp.float32
    )
    image = sum(image[piece * size : (piece + 1) * size] for piece in range(PIECES)) * scale
    back = jnp.dot(
        jnp.concatenate(split_pieces(image, PIECES), axis=0), rows, preferred_element_type=jnp.float32
    )
    back = sum(back[piece * size : (piece + 1) * size] for piece in range(PIECES))

    @pl.when(step == 0)
    def _():
        full_ref[...] = back

    @pl.when(step > 0)
    def _():
        full_ref[...] += back

    @pl.when(step == pl.num_programs(0) - 1)
    def _():
        live = lax.broadcasted_iota(jnp.int32, (1, cap), 1) < size_ref[0]
        full_ref[...] = jnp.where(live, full_ref[...], 0.0)
        if len(outs) == 1:
            outs[0][...] = full_ref[...]
            return
        each, _, width = outs[0].shape
        chunks = []
        for offset in order:
            first = pl.multiple_of(jnp.bitwise_xor(place_ref[0], offset) * width, width)
            chunks.append(full_ref[:, pl.ds(first, width)])
        for place in range(each):
            outs[0][place] = chunks[place]
        for place, message in enumerate(pack_chunks(chunks[each:])):
            outs[1 + place // each][place % each] = message


def apply_samples(genotypes, sizes, place, gathered, order, normalise, scale, groups):
    samples, cap = genotypes.shape
    block = min(BLOCK, samples)
    packed = len(gathered) > 1
    if packed:
        each, rows, width = gathered[0].shape
        size = rows // PACKED * LANES
        outs = [jax.ShapeDtypeStruct((each, size, width), jnp.float32)]
        outs += [jax.ShapeDtypeStruct((each, rows, width), jnp.int32)] * (len(gathered) - 1)
    else:
        size = gathered[0].shape[0]
        outs = [jax.ShapeDtypeStruct((size, cap), jnp.float32)]
    scalar = pl.BlockSpec(memory_space=pltpu.SMEM)

    def whole(value):
        return pl.BlockSpec(value.shape, lambda step: (0,) * len(value.shape))

    return pl.pallas_call(
        functools.partial(apply_kernel, order, normalise, scale, len(gathered)),
        grid=(samples // block,),
        in_specs=[scalar, scalar, pl.BlockSpec((block, cap), lambda step: (step, 0))]
        + [whole(part) for part in gathered],
        out_specs=[whole(out) for out in outs],
        out_shape=outs,
        scratch_shapes=[
            pltpu.VMEM((size, cap), jnp.float32),
            pltpu.VMEM((PIECES * size, cap), jnp.bfloat16),
            pltpu.VMEM((size, 2 * size), jnp.float32),
        ],
        compiler_params=pltpu.CompilerParams(vmem_limit_bytes=VMEM_LIMIT),
    )(place, sizes, genotypes, *gathered)


def lane_splat(tile, lane):
    return jnp.broadcast_to(tile[:, lane : lane + 1], (SUBLANES, LANES))


def row_splat(tile, row):
    return jnp.broadcast_to(tile[row : row + 1, :], (SUBLANES, LANES))


def inverse_factor(work_ref, size, panel):
    tiles = 2 * size // LANES
    below = lax.broadcasted_iota(jnp.int32, (SUBLANES, LANES), 0)
    groups = panel // SUBLANES
    for top in range(0, size, panel):
        active = [
            tile
            for tile in range(tiles)
            if (top // LANES <= tile < size // LANES)
            or (size // LANES <= tile <= size // LANES + (top + panel - 1) // LANES)
        ]
        rows = [
            {
                tile: work_ref[top + SUBLANES * group : top + SUBLANES * (group + 1), tile * LANES : (tile + 1) * LANES]
                for tile in active
            }
            for group in range(groups)
        ]
        for block in range(groups):
            base = top + SUBLANES * block
            columns = {
                group: [lane_splat(rows[group][base // LANES], base % LANES + lane) for lane in range(SUBLANES)]
                for group in range(block, groups)
            }
            for step in range(SUBLANES):
                pivot = row_splat(columns[block][step], step)
                root = lax.rsqrt(pivot)
                root = root * (1.5 - 0.5 * pivot * root * root)
                factor = {group: columns[group][step] * root for group in range(block, groups)}
                for later in range(step + 1, SUBLANES):
                    weight = row_splat(factor[block], later)
                    for group in range(block, groups):
                        columns[group][later] = columns[group][later] - factor[group] * weight
                lower = jnp.where(below > step, factor[block], 0.0)
                for tile in active:
                    line = row_splat(rows[block][tile], step) * root
                    rows[block][tile] = jnp.where(
                        below == step, line, rows[block][tile] - lower * line
                    )
                    for group in range(block + 1, groups):
                        rows[group][tile] = rows[group][tile] - factor[group] * line
        for group in range(groups):
            for tile in active:
                work_ref[top + SUBLANES * group : top + SUBLANES * (group + 1), tile * LANES : (tile + 1) * LANES] = rows[
                    group
                ][tile]
        rest = top + panel
        if rest < size:
            first, last = active[0] * LANES, (active[-1] + 1) * LANES
            lines = work_ref[top:rest, first:last]
            weights = work_ref[top:rest, rest // LANES * LANES : size].T[rest % LANES :, :]
            work_ref[rest:, first:last] -= jnp.dot(
                weights, lines, precision=HIGHEST, preferred_element_type=jnp.float32
            )


def start_factor(work_ref, inner):
    size = inner.shape[0]
    work_ref[:, :size] = inner
    row = lax.broadcasted_iota(jnp.int32, (size, size), 0)
    column = lax.broadcasted_iota(jnp.int32, (size, size), 1)
    work_ref[:, size:] = jnp.where(row == column, 1.0, 0.0)


def finish_factor(work_ref):
    size = work_ref.shape[0]
    row = lax.broadcasted_iota(jnp.int32, (size, size), 0)
    column = lax.broadcasted_iota(jnp.int32, (size, size), 1)
    return jnp.where(row >= column, work_ref[:, size:], 0.0)


def rows_inner(value):
    return lax.dot_general(
        value, value, (((1,), (1,)), ((), ())), precision=HIGHEST, preferred_element_type=jnp.float32
    )


def fold_symmetric(value, folded_ref, height):
    half = value.shape[0] // 2
    row = lax.broadcasted_iota(jnp.int32, (half, half), 0)
    column = lax.broadcasted_iota(jnp.int32, (half, half), 1)
    corner = value[half:, half:]
    both = jnp.where(row >= column, value[:half, :half], corner)
    diagonal = jnp.sum(jnp.where(row == column, corner, 0.0), axis=0, keepdims=True)
    quarter = half // 2
    for place in range(4):
        source = value[half:, :half] if place < 2 else both
        folded_ref[place, :quarter] = source[place % 2 * quarter : (place % 2 + 1) * quarter]
        folded_ref[place, quarter:] = jnp.broadcast_to(diagonal, (SUBLANES, half))


def unfold_symmetric(parts):
    quarter = parts[0].shape[0] - SUBLANES
    half = 2 * quarter
    row = lax.broadcasted_iota(jnp.int32, (half, half), 0)
    column = lax.broadcasted_iota(jnp.int32, (half, half), 1)
    left = jnp.concatenate([parts[0][:quarter], parts[1][:quarter]], axis=0)
    both = jnp.concatenate([parts[2][:quarter], parts[3][:quarter]], axis=0)
    turned = both.T
    corner = jnp.where(row == column, parts[3][quarter : quarter + 1], jnp.where(row < column, both, turned))
    upper = jnp.concatenate([jnp.where(row >= column, both, turned), left.T], axis=1)
    return jnp.concatenate([upper, jnp.concatenate([left, corner], axis=1)], axis=0)


def project_kernel(order, sources, quarter_ref, place_ref, rows_ref, *refs):
    refs, (inner_ref, *outs), (full_ref, split_ref, cross_ref, folded_ref) = refs[:sources], refs[sources:-4], refs[-4:]
    step = pl.program_id(0)
    size = full_ref.shape[0]

    @pl.when(step == 0)
    def _():
        load_all(order, place_ref, refs, full_ref)
        image = full_ref[...]
        inner_ref[...] = rows_inner(image)
        for piece, part in enumerate(split_pieces(image, PIECES)):
            split_ref[pl.ds(piece * size, size), :] = part
        cross_ref[...] = jnp.zeros_like(cross_ref)

    sampled = lax.dot_general(
        split_ref[...], rows_ref[...], (((1,), (1,)), ((), ())), preferred_element_type=jnp.float32
    )
    sampled = sum(sampled[piece * size : (piece + 1) * size] for piece in range(PIECES))
    cross_ref[...] += rows_inner(sampled)

    @pl.when(step == pl.num_programs(0) - 1)
    def _():
        fold_symmetric(cross_ref[...], folded_ref, size)
        for offset, out_ref in enumerate(outs):
            out_ref[...] = folded_ref[jnp.bitwise_xor(quarter_ref[0], offset)]


def project(genotypes, quarter, place, gathered, order, size):
    samples, cap = genotypes.shape
    block = min(BLOCK, samples)
    scalar = pl.BlockSpec(memory_space=pltpu.SMEM)

    def whole(shape):
        return pl.BlockSpec(shape, lambda step: (0,) * len(shape))

    part = (size // 4 + SUBLANES, size // 2)
    outs = [(size, size)] + [part] * 4
    return pl.pallas_call(
        functools.partial(project_kernel, order, len(gathered)),
        grid=(samples // block,),
        in_specs=[scalar, scalar, pl.BlockSpec((block, cap), lambda step: (step, 0))]
        + [whole(part.shape) for part in gathered],
        out_specs=[whole(shape) for shape in outs],
        out_shape=[jax.ShapeDtypeStruct(shape, jnp.float32) for shape in outs],
        scratch_shapes=[
            pltpu.VMEM((size, cap), jnp.float32),
            pltpu.VMEM((PIECES * size, cap), jnp.bfloat16),
            pltpu.VMEM((size, size), jnp.float32),
            pltpu.VMEM((4,) + part, jnp.float32),
        ],
        compiler_params=pltpu.CompilerParams(vmem_limit_bytes=VMEM_LIMIT),
    )(quarter, place, genotypes, *gathered)


def second_kernel(gain, inner_ref, own_ref, out_ref, basis_ref, work_ref):
    start_factor(work_ref, inner_ref[...])
    inverse_factor(work_ref, work_ref.shape[0], PANEL)
    factor = finish_factor(work_ref)
    out_ref[...] = factor
    own = jnp.dot(factor, own_ref[...], precision=HIGHEST, preferred_element_type=jnp.float32)
    basis_ref[...] = own.T * gain


def second_factor(inner, own, gain):
    size, width = own.shape
    return pl.pallas_call(
        functools.partial(second_kernel, gain),
        in_specs=[pl.BlockSpec(memory_space=pltpu.VMEM)] * 2,
        out_specs=[pl.BlockSpec(memory_space=pltpu.VMEM)] * 2,
        out_shape=[
            jax.ShapeDtypeStruct((size, size), jnp.float32),
            jax.ShapeDtypeStruct((width, size), jnp.float32),
        ],
        scratch_shapes=[pltpu.VMEM((size, 2 * size), jnp.float32)],
        compiler_params=pltpu.CompilerParams(vmem_limit_bytes=VMEM_LIMIT),
        cost_estimate=FACTOR_COST,
    )(inner, own)


def finish_kernel(scale, quarter_ref, factor_ref, *refs):
    parts, (out_ref, trace_ref, folded_ref) = refs[:4], refs[4:]
    for offset in range(4):
        folded_ref[jnp.bitwise_xor(quarter_ref[0], offset)] = parts[offset][...]
    cross = unfold_symmetric([folded_ref[place] for place in range(4)])
    factor = factor_ref[...]
    half = jnp.dot(factor, cross, precision=HIGHEST, preferred_element_type=jnp.float32)
    result = scale * lax.dot_general(
        half, factor, (((1,), (1,)), ((), ())), precision=HIGHEST, preferred_element_type=jnp.float32
    )
    out_ref[...] = result
    row = lax.broadcasted_iota(jnp.int32, result.shape, 0)
    column = lax.broadcasted_iota(jnp.int32, result.shape, 1)
    trace_ref[...] = jnp.broadcast_to(jnp.sum(jnp.where(row == column, result, 0.0)), trace_ref.shape)


def finish(quarter, factor, parts, scale):
    vmem = pl.BlockSpec(memory_space=pltpu.VMEM)
    return pl.pallas_call(
        functools.partial(finish_kernel, scale),
        in_specs=[pl.BlockSpec(memory_space=pltpu.SMEM)] + [vmem] * 5,
        out_specs=[vmem] * 2,
        out_shape=[
            jax.ShapeDtypeStruct(factor.shape, jnp.float32),
            jax.ShapeDtypeStruct((SUBLANES, LANES), jnp.float32),
        ],
        scratch_shapes=[pltpu.VMEM((4,) + parts[0].shape, jnp.float32)],
        compiler_params=pltpu.CompilerParams(vmem_limit_bytes=VMEM_LIMIT),
    )(quarter, factor, *parts)


def to_natural(gathered, order, me):
    places = jnp.argsort(jnp.array(order, jnp.int32))
    mine = jnp.bitwise_xor(jnp.arange(len(order), dtype=jnp.int32), me)
    stacked = jnp.concatenate(gathered, axis=0)[places][mine]
    return jnp.transpose(stacked, (1, 0, 2)).reshape(stacked.shape[1], -1)


def to_relative(rows, order, me, width, parts):
    chunks = jnp.transpose(rows.reshape(rows.shape[0], -1, width), (1, 0, 2))
    return jnp.split(chunks[jnp.bitwise_xor(jnp.array(order, jnp.int32), me)], parts, axis=0)


def body(genotypes, sizes, start):
    groups = lax.axis_size("smp")
    dosages = genotypes[0]
    samples, cap = dosages.shape
    width, size = start.shape[1:]
    scale = 1.0 / (samples * groups)
    me = lax.axis_index("smp")
    place = me.reshape(1).astype(jnp.int32)
    stages = stage_bits(groups)
    order = relative_order(stages)
    packed = width == LANES

    def gather(message):
        gathered = gather_chunks(message, groups)
        return gathered if packed else [to_natural(gathered, order, me)]

    def apply(message, normalise):
        outs = apply_samples(dosages, sizes, place, gather(message), order, normalise, scale, groups)
        if not packed:
            outs = to_relative(outs[0], order, me, width, len(offsets(stages[0])))
        return reduce_chunks(outs[0], outs[1:], groups, packed)

    if packed:
        message = encode(place, sizes, start[0])
    else:
        row = me * width + lax.broadcasted_iota(jnp.int32, (width, size), 0)
        message = jnp.where(row < sizes[0], start[0], 0.0).T[None]
    _, message = apply(message, False)
    own, message = apply(message, True)
    quarter = jnp.bitwise_and(place, 3)
    inner, *quarters = project(dosages, quarter, place, gather(message), order, size)
    quarters = sum_quarters(quarters, groups)
    second, basis = second_factor(inner, own[0], math.sqrt(cap))
    rayleigh, trace = finish(quarter, second, quarters, scale)
    blocks = lax.axis_size("blk")
    total = trace
    for shift in range(1, blocks):
        total = total + lax.ppermute(trace, "blk", [(block, (block + shift) % blocks) for block in range(blocks)])
    scaled = rayleigh * (genotypes.shape[0] * blocks * size / total[0, 0])
    return basis[None], scaled[None]


def solution(mesh):
    return jax.shard_map(
        body,
        mesh=mesh,
        in_specs=(P("blk", "smp", None), P("blk"), P("blk", "smp", None)),
        out_specs=(P("blk", "smp", None), P("blk", None, None)),
        check_vma=False,
    )
```

time: 234 us -> 205 us (0.88); the launches traced: 234 us -> 201 us
  waiting for transfers between devices: 114 us -> 77.4 us
  Pallas kernels: 55.6 us -> 67.2 us
  starting transfers between devices: 57.8 us -> 52.2 us
    ppermute x44 -> x39, waiting for transfers between devices: 113 us -> 76.2 us  [exchange(): lax.ppermute(value, 'smp', [(device, device ^ offset) for device in range...]
    pallas_call x6 -> x8, Pallas kernels: 43.1 us -> 54.8 us  [the longest x2 33.1 us: apply_samples(): pl.pallas_call(functools.partial(apply_kernel, order, normalise, scale, l...]
    ppermute x44 -> x39, starting transfers between devices: 57.7 us -> 52.1 us  [exchange(): lax.ppermute(value, 'smp', [(device, device ^ offset) for device in range...]
  transfers between devices with their start and end apart: 45 -> 40, of which waited for: 30 -> 27; matrix products, arithmetic and copies ran while one was open for 0% -> 0% of each run, Pallas kernels for 19% -> 6%
where the time goes in v3:
time: 205 us; the launch traced here: 201 us
  waiting for transfers between devices  77.4 us (38%)
  Pallas kernels  67.2 us (33%)
  starting transfers between devices  52.2 us (25%)
  between operations  2.3 us (1%)
    ppermute x39, waiting for transfers between devices, exchange(): lax.ppermute(value, 'smp', [(device, device ^ offset) for device in range...  76.2 us
    ppermute x39, starting transfers between devices, exchange(): lax.ppermute(value, 'smp', [(device, device ^ offset) for device in range...  52.1 us
    pallas_call x2, Pallas kernels, apply_samples(): pl.pallas_call(functools.partial(apply_kernel, order, normalise, scale, l...  33.1 us
    pallas_call x4, Pallas kernels, combine(): pl.pallas_call(functools.partial(combine_kernel, len(arrived), parts), in...  13.4 us
    pallas_call x1, Pallas kernels, second_factor(): pl.pallas_call(functools.partial(second_kernel, gain), in_specs=[pl.Block...  11.2 us
    pallas_call x1, Pallas kernels, project(): pl.pallas_call(functools.partial(project_kernel, order, len(gathered)), g...  6.32 us
  transfers between devices with their start and end apart: 40, of which 27 were waited for; matrix products, arithmetic and copies ran while one was open for 0% of the time, Pallas kernels for 6%

profile of v3, /device:TPU:0, one launch (start us, length us, event | category | flops | bytes accessed | tf_op | source)
XLA Modules:
  0.0 201.3 jit_solution(6327547448851813510)
XLA Ops:
  1.3 1.9 shard_map.50
  3.2 3.0 %collective-permute-start = (s32[1,144,128]{2,1,0:T(8,128)}, s32[1,144,128]{2,1,0:T(8,128)S(1)}, u32[]{:S(2)}, u32[]{:S(2)}) collective-permute-start(s32[1,144,128]{2,1,0:T(8,128)} %shard_map.50), channel_id=1, source_target_pairs={{0,4},{1,5},{2,6},{3,7},{4,0},{5,1},{6,2},{7,3},{8,12},{9,13},{10,... | collective-permute-start | bytes 221192 | tf_op jit(solution)/shard_map/ppermute | solution.py:44
  6.2 2.6 %collective-permute-start.1 = (s32[1,144,128]{2,1,0:T(8,128)}, s32[1,144,128]{2,1,0:T(8,128)S(1)}, u32[]{:S(2)}, u32[]{:S(2)}) collective-permute-start(s32[1,144,128]{2,1,0:T(8,128)} %shard_map.50), channel_id=1, source_target_pairs={{0,8},{1,9},{2,10},{3,11},{4,12},{5,13},{6,14},{7,15},{8,0},{9,1},... | collective-permute-start | bytes 221192 | tf_op jit(solution)/shard_map/ppermute | solution.py:44
  8.8 5.4 %collective-permute-done.1 = s32[1,144,128]{2,1,0:T(8,128)S(1)} collective-permute-done((s32[1,144,128]{2,1,0:T(8,128)}, s32[1,144,128]{2,1,0:T(8,128)S(1)}, u32[]{:S(2)}, u32[]{:S(2)}) %collective-permute-start.1) | collective-permute-done | bytes 73760 | tf_op jit(solution)/shard_map/ppermute | solution.py:44
  16.2 1.6 collective-permute-start.3
  17.7 1.5 collective-permute-start.4
  19.7 6.5 %collective-permute-done.3.refs_1_ = s32[4,144,128]{2,1,0:T(8,128)S(1)} collective-permute-done((s32[4,144,128]{2,1,0:T(8,128)S(1)}, s32[4,144,128]{2,1,0:T(8,128)S(1)}, u32[]{:S(2)}, u32[]{:S(2)}) %collective-permute-start.3) | collective-permute-done | bytes 294944 | tf_op jit(solution)/shard_map/ppermute | solution.py:44
  26.2 4.5 %collective-permute-done.4.refs_2_ = s32[4,144,128]{2,1,0:T(8,128)S(1)} collective-permute-done((s32[4,144,128]{2,1,0:T(8,128)S(1)}, s32[4,144,128]{2,1,0:T(8,128)S(1)}, u32[]{:S(2)}, u32[]{:S(2)}) %collective-permute-start.4) | collective-permute-done | bytes 294944 | tf_op jit(solution)/shard_map/ppermute | solution.py:44
  30.7 8.6 %shard_map.51 = (f32[4,256,128]{2,1,0:T(8,128)S(1)}, s32[4,144,128]{2,1,0:T(8,128)S(1)}, s32[4,144,128]{2,1,0:T(8,128)S(1)}, s32[4,144,128]{2,1,0:T(8,128)S(1)}) custom-call(s32[1]{0:T(128)} %bitcast.place_ref, s32[1]{0:T(128)S(6)} %copy.11.size_ref, bf16[1024,2048]{1,0:T(8,128)(2,1)} %bitcast.8, s32[4,144,128]{2,1,0:T(8,128)S(1)} %pad_add_fusion.refs_0_, ...), custom_call_target="tpu_custom_call" | custom-call | tf_op jit(solution)/shard_map/pallas_call | solution.py:296
  41.5 1.4 collective-permute-start.8
  42.9 5.5 %collective-permute-done.6.refs_0_ = s32[4,144,128]{2,1,0:T(8,128)S(1)} collective-permute-done((s32[4,144,128]{2,1,0:T(8,128)S(1)}, s32[4,144,128]{2,1,0:T(8,128)S(1)}, u32[]{:S(2)}, u32[]{:S(2)}) %collective-permute-start.6) | collective-permute-done | bytes 294944 | tf_op jit(solution)/shard_map/ppermute | solution.py:44
  48.4 4.3 %collective-permute-done.7.refs_1_ = s32[4,144,128]{2,1,0:T(8,128)S(1)} collective-permute-done((s32[4,144,128]{2,1,0:T(8,128)S(1)}, s32[4,144,128]{2,1,0:T(8,128)S(1)}, u32[]{:S(2)}, u32[]{:S(2)}) %collective-permute-start.7) | collective-permute-done | bytes 294944 | tf_op jit(solution)/shard_map/ppermute | solution.py:44
  53.7 3.4 %collective-permute-start.10 = (s32[1,144,128]{2,1,0:T(8,128)S(1)}, s32[1,144,128]{2,1,0:T(8,128)S(1)}, u32[]{:S(2)}, u32[]{:S(2)}) collective-permute-start(s32[1,144,128]{2,1,0:T(8,128)S(1)} %get-tuple-element.36), channel_id=1, source_target_pairs={{0,8},{1,9},{2,10},{3,11},{4,12},{5,13},{6,14},{7,15},{8,0},{9,1},... | collective-permute-start | bytes 221192 | tf_op jit(solution)/shard_map/ppermute | solution.py:44
  57.8 2.5 %collective-permute-done.10.refs_1_ = s32[1,144,128]{2,1,0:T(8,128)S(1)} collective-permute-done((s32[1,144,128]{2,1,0:T(8,128)S(1)}, s32[1,144,128]{2,1,0:T(8,128)S(1)}, u32[]{:S(2)}, u32[]{:S(2)}) %collective-permute-start.10) | collective-permute-done | bytes 73760 | tf_op jit(solution)/shard_map/ppermute | solution.py:44
  60.3 3.7 %collective-permute-done.11.refs_2_ = s32[1,144,128]{2,1,0:T(8,128)S(1)} collective-permute-done((s32[1,144,128]{2,1,0:T(8,128)S(1)}, s32[1,144,128]{2,1,0:T(8,128)S(1)}, u32[]{:S(2)}, u32[]{:S(2)}) %collective-permute-start.11) | collective-permute-done | bytes 73760 | tf_op jit(solution)/shard_map/ppermute | solution.py:44
  65.9 1.6 collective-permute-start.13
  67.5 1.9 collective-permute-start.14
  69.4 2.5 %collective-permute-done.13 = s32[1,144,128]{2,1,0:T(8,128)S(1)} collective-permute-done((s32[1,144,128]{2,1,0:T(8,128)S(1)}, s32[1,144,128]{2,1,0:T(8,128)S(1)}, u32[]{:S(2)}, u32[]{:S(2)}) %collective-permute-start.13) | collective-permute-done | bytes 73760 | tf_op jit(solution)/shard_map/ppermute | solution.py:44
  71.9 1.7 collective-permute-done.14
  73.6 1.4 collective-permute-start.15
  75.0 1.5 collective-permute-start.16
  77.1 3.2 %collective-permute-done.15.refs_1_ = s32[4,144,128]{2,1,0:T(8,128)S(1)} collective-permute-done((s32[4,144,128]{2,1,0:T(8,128)S(1)}, s32[4,144,128]{2,1,0:T(8,128)S(1)}, u32[]{:S(2)}, u32[]{:S(2)}) %collective-permute-start.15) | collective-permute-done | bytes 294944 | tf_op jit(solution)/shard_map/ppermute | solution.py:44
  80.4 4.5 %collective-permute-done.16.refs_2_ = s32[4,144,128]{2,1,0:T(8,128)S(1)} collective-permute-done((s32[4,144,128]{2,1,0:T(8,128)S(1)}, s32[4,144,128]{2,1,0:T(8,128)S(1)}, u32[]{:S(2)}, u32[]{:S(2)}) %collective-permute-start.16) | collective-permute-done | bytes 294944 | tf_op jit(solution)/shard_map/ppermute | solution.py:44
  84.9 24.5 %shard_map.54 = (f32[4,256,128]{2,1,0:T(8,128)S(1)}, s32[4,144,128]{2,1,0:T(8,128)S(1)}, s32[4,144,128]{2,1,0:T(8,128)S(1)}, s32[4,144,128]{2,1,0:T(8,128)S(1)}) custom-call(s32[1]{0:T(128)} %bitcast.place_ref, s32[1]{0:T(128)S(6)} %copy.11.size_ref, bf16[1024,2048]{1,0:T(8,128)(2,1)} %bitcast.9, ...), custom_call_target="tpu_custom_call" | custom-call | tf_op jit(solution)/shard_map/pallas_call | solution.py:296
  111.5 1.5 collective-permute-start.20
  112.9 3.2 %collective-permute-done.18.refs_0_ = s32[4,144,128]{2,1,0:T(8,128)S(1)} collective-permute-done((s32[4,144,128]{2,1,0:T(8,128)S(1)}, s32[4,144,128]{2,1,0:T(8,128)S(1)}, u32[]{:S(2)}, u32[]{:S(2)}) %collective-permute-start.18) | collective-permute-done | bytes 294944 | tf_op jit(solution)/shard_map/ppermute | solution.py:44
  116.2 2.7 %collective-permute-done.19.refs_1_ = s32[4,144,128]{2,1,0:T(8,128)S(1)} collective-permute-done((s32[4,144,128]{2,1,0:T(8,128)S(1)}, s32[4,144,128]{2,1,0:T(8,128)S(1)}, u32[]{:S(2)}, u32[]{:S(2)}) %collective-permute-start.19) | collective-permute-done | bytes 294944 | tf_op jit(solution)/shard_map/ppermute | solution.py:44
  118.9 1.4 collective-permute-done.20.refs_2_
  120.3 10.9 %shard_map.55 = (f32[1,256,128]{2,1,0:T(8,128)S(1)}, s32[1,144,128]{2,1,0:T(8,128)S(1)}, s32[1,144,128]{2,1,0:T(8,128)S(1)}, s32[1,144,128]{2,1,0:T(8,128)S(1)}) custom-call(f32[4,256,128]{2,1,0:T(8,128)S(1)} %get-tuple-element.39.keep_ref, s32[4,144,128]{2,1,0:T(8,128)S(1)} %collective-permute-done.18.refs_0_, ...), custom_call_target="tpu_custom_call" | custom-call | tf_op jit(solution)/shard_map/pallas_call | solution.py:192
  131.3 2.2 %collective-permute-start.22 = (s32[1,144,128]{2,1,0:T(8,128)S(1)}, s32[1,144,128]{2,1,0:T(8,128)S(1)}, u32[]{:S(2)}, u32[]{:S(2)}) collective-permute-start(s32[1,144,128]{2,1,0:T(8,128)S(1)} %get-tuple-element.45), channel_id=1, source_target_pairs={{0,8},{1,9},{2,10},{3,11},{4,12},{5,13},{6,14},{7,15},{8,0},{9,1},... | collective-permute-start | bytes 221192 | tf_op jit(solution)/shard_map/ppermute | solution.py:44
  133.5 2.2 %collective-permute-start.23 = (s32[1,144,128]{2,1,0:T(8,128)S(1)}, s32[1,144,128]{2,1,0:T(8,128)S(1)}, u32[]{:S(2)}, u32[]{:S(2)}) collective-permute-start(s32[1,144,128]{2,1,0:T(8,128)S(1)} %get-tuple-element.46), channel_id=1, source_target_pairs={{0,12},{1,13},{2,14},{3,15},{4,8},{5,9},{6,10},{7,11},{8,4},{9,5},... | collective-permute-start | bytes 221192 | tf_op jit(solution)/shard_map/ppermute | solution.py:44
  135.7 1.4 collective-permute-done.21.refs_0_
  137.1 2.6 %collective-permute-done.23.refs_2_ = s32[1,144,128]{2,1,0:T(8,128)S(1)} collective-permute-done((s32[1,144,128]{2,1,0:T(8,128)S(1)}, s32[1,144,128]{2,1,0:T(8,128)S(1)}, u32[]{:S(2)}, u32[]{:S(2)}) %collective-permute-start.23) | collective-permute-done | bytes 73760 | tf_op jit(solution)/shard_map/ppermute | solution.py:44
  140.3 2.7 %collective-permute-start.25 = (s32[1,144,128]{2,1,0:T(8,128)S(1)}, s32[1,144,128]{2,1,0:T(8,128)S(1)}, u32[]{:S(2)}, u32[]{:S(2)}) collective-permute-start(s32[1,144,128]{2,1,0:T(8,128)S(1)} %get-tuple-element.47), channel_id=1, source_target_pairs={{0,8},{1,9},{2,10},{3,11},{4,12},{5,13},{6,14},{7,15},{8,0},{9,1},... | collective-permute-start | bytes 221192 | tf_op jit(solution)/shard_map/ppermute | solution.py:44
  143.0 1.7 collective-permute-start.26
  145.6 3.5 %collective-permute-done.26 = s32[1,144,128]{2,1,0:T(8,128)S(1)} collective-permute-done((s32[1,144,128]{2,1,0:T(8,128)S(1)}, s32[1,144,128]{2,1,0:T(8,128)S(1)}, u32[]{:S(2)}, u32[]{:S(2)}) %collective-permute-start.26) | collective-permute-done | bytes 73760 | tf_op jit(solution)/shard_map/ppermute | solution.py:44
  150.2 1.5 collective-permute-start.28
  152.7 3.7 %collective-permute-done.27.refs_1_ = s32[4,144,128]{2,1,0:T(8,128)S(1)} collective-permute-done((s32[4,144,128]{2,1,0:T(8,128)S(1)}, s32[4,144,128]{2,1,0:T(8,128)S(1)}, u32[]{:S(2)}, u32[]{:S(2)}) %collective-permute-start.27) | collective-permute-done | bytes 294944 | tf_op jit(solution)/shard_map/ppermute | solution.py:44
  156.4 4.5 %collective-permute-done.28.refs_2_ = s32[4,144,128]{2,1,0:T(8,128)S(1)} collective-permute-done((s32[4,144,128]{2,1,0:T(8,128)S(1)}, s32[4,144,128]{2,1,0:T(8,128)S(1)}, u32[]{:S(2)}, u32[]{:S(2)}) %collective-permute-start.28) | collective-permute-done | bytes 294944 | tf_op jit(solution)/shard_map/ppermute | solution.py:44
  160.9 6.3 %shard_map.57 = (f32[256,256]{1,0:T(8,128)S(1)}, f32[72,128]{1,0:T(8,128)S(1)}, f32[72,128]{1,0:T(8,128)S(1)}, f32[72,128]{1,0:T(8,128)S(1)}, f32[72,128]{1,0:T(8,128)S(1)}) custom-call(s32[1]{0:T(128)S(6)} %and.4.quarter_ref, s32[1]{0:T(128)} %bitcast.place_ref, bf16[1024,2048]{1,0:T(8,128)(2,1)S(1)} %bitcast.10, ...), custom_call_target="tpu_custom_call" | custom-call | tf_op jit(solution)/shard_map/pallas_call | solution.py:461
  169.3 1.5 collective-permute-start.32
  172.2 1.9 collective-permute-done.32
  174.2 1.9 collective-permute-start.34
  176.2 2.4 %collective-permute-start.35 = (f32[72,128]{1,0:T(8,128)S(1)}, f32[72,128]{1,0:T(8,128)S(1)}, u32[]{:S(2)}, u32[]{:S(2)}) collective-permute-start(f32[72,128]{1,0:T(8,128)S(1)} %add_add_fusion.1), channel_id=1, source_target_pairs={{0,12},{1,13},{2,14},{3,15},{4,8},{5,9},{6,10},{7,11},{8,4},{9,5},... | collective-permute-start | bytes 110600 | tf_op jit(solution)/shard_map/ppermute | solution.py:44
  179.2 2.8 %collective-permute-done.35 = f32[72,128]{1,0:T(8,128)S(1)} collective-permute-done((f32[72,128]{1,0:T(8,128)S(1)}, f32[72,128]{1,0:T(8,128)S(1)}, u32[]{:S(2)}, u32[]{:S(2)}) %collective-permute-start.35) | collective-permute-done | bytes 36896 | tf_op jit(solution)/shard_map/ppermute | solution.py:44
  181.9 1.7 collective-permute-start.36
  184.1 1.5 collective-permute-start.38
  185.5 11.2 %shard_map.58 = (f32[256,256]{1,0:T(8,128)S(1)}, f32[128,256]{1,0:T(8,128)}) custom-call(f32[256,256]{1,0:T(8,128)S(1)} %get-tuple-element.48.inner_ref, f32[256,128]{1,0:T(8,128)S(1)} %bitcast.11), custom_call_target="tpu_custom_call" | custom-call | flops 12000000000 | bytes 4194304 | tf_op jit(solution)/shard_map/pallas_call | solution.py:489
  (58 shorter events, 22.6 us)
Async XLA Ops:
  3.2 5.6 %collective-permute-start = (s32[1,144,128]{2,1,0:T(8,128)}, s32[1,144,128]{2,1,0:T(8,128)S(1)}, u32[]{:S(2)}, u32[]{:S(2)}) collective-permute-start(s32[1,144,128]{2,1,0:T(8,128)} %shard_map.50), channel_id=1, source_target_pairs={{0,4},{1,5},{2,6},{3,7},{4,0},{5,1},{6,2},{7,3},{8,12},{9,13},{10,... | collective-permute-start | bytes 221192 | tf_op jit(solution)/shard_map/ppermute | solution.py:44
  6.2 8.0 %collective-permute-start.1 = (s32[1,144,128]{2,1,0:T(8,128)}, s32[1,144,128]{2,1,0:T(8,128)S(1)}, u32[]{:S(2)}, u32[]{:S(2)}) collective-permute-start(s32[1,144,128]{2,1,0:T(8,128)} %shard_map.50), channel_id=1, source_target_pairs={{0,8},{1,9},{2,10},{3,11},{4,12},{5,13},{6,14},{7,15},{8,0},{9,1},... | collective-permute-start | bytes 221192 | tf_op jit(solution)/shard_map/ppermute | solution.py:44
  8.8 6.5 %collective-permute-start.2 = (s32[1,144,128]{2,1,0:T(8,128)}, s32[1,144,128]{2,1,0:T(8,128)S(1)}, u32[]{:S(2)}, u32[]{:S(2)}) collective-permute-start(s32[1,144,128]{2,1,0:T(8,128)} %shard_map.50), channel_id=1, source_target_pairs={{0,12},{1,13},{2,14},{3,15},{4,8},{5,9},{6,10},{7,11},{8,4},{9,5},... | collective-permute-start | bytes 221192 | tf_op jit(solution)/shard_map/ppermute | solution.py:44
  16.2 10.0 %collective-permute-start.3 = (s32[4,144,128]{2,1,0:T(8,128)S(1)}, s32[4,144,128]{2,1,0:T(8,128)S(1)}, u32[]{:S(2)}, u32[]{:S(2)}) collective-permute-start(s32[4,144,128]{2,1,0:T(8,128)S(1)} %pad_add_fusion.refs_0_), channel_id=1, source_target_pairs={{0,1},{1,0},{2,3},{3,2},{4,5},{5,4},{6,7},{7,6},{8,9},{9,8},{10,11... | collective-permute-start | bytes 884744 | tf_op jit(solution)/shard_map/ppermute | solution.py:44
  17.7 13.0 %collective-permute-start.4 = (s32[4,144,128]{2,1,0:T(8,128)S(1)}, s32[4,144,128]{2,1,0:T(8,128)S(1)}, u32[]{:S(2)}, u32[]{:S(2)}) collective-permute-start(s32[4,144,128]{2,1,0:T(8,128)S(1)} %pad_add_fusion.refs_0_), channel_id=1, source_target_pairs={{0,2},{1,3},{2,0},{3,1},{4,6},{5,7},{6,4},{7,5},{8,10},{9,11},{10,... | collective-permute-start | bytes 884744 | tf_op jit(solution)/shard_map/ppermute | solution.py:44
  19.2 11.5 %collective-permute-start.5 = (s32[4,144,128]{2,1,0:T(8,128)S(1)}, s32[4,144,128]{2,1,0:T(8,128)S(1)}, u32[]{:S(2)}, u32[]{:S(2)}) collective-permute-start(s32[4,144,128]{2,1,0:T(8,128)S(1)} %pad_add_fusion.refs_0_), channel_id=1, source_target_pairs={{0,3},{1,2},{2,1},{3,0},{4,7},{5,6},{6,5},{7,4},{8,11},{9,10},{10,... | collective-permute-start | bytes 884744 | tf_op jit(solution)/shard_map/ppermute | solution.py:44
  39.3 9.0 %collective-permute-start.6 = (s32[4,144,128]{2,1,0:T(8,128)S(1)}, s32[4,144,128]{2,1,0:T(8,128)S(1)}, u32[]{:S(2)}, u32[]{:S(2)}) collective-permute-start(s32[4,144,128]{2,1,0:T(8,128)S(1)} %get-tuple-element.31), channel_id=1, source_target_pairs={{0,1},{1,0},{2,3},{3,2},{4,5},{5,4},{6,7},{7,6},{8,9},{9,8},{10,11... | collective-permute-start | bytes 884744 | tf_op jit(solution)/shard_map/ppermute | solution.py:44
  40.6 12.1 %collective-permute-start.7 = (s32[4,144,128]{2,1,0:T(8,128)S(1)}, s32[4,144,128]{2,1,0:T(8,128)S(1)}, u32[]{:S(2)}, u32[]{:S(2)}) collective-permute-start(s32[4,144,128]{2,1,0:T(8,128)S(1)} %get-tuple-element.32), channel_id=1, source_target_pairs={{0,2},{1,3},{2,0},{3,1},{4,6},{5,7},{6,4},{7,5},{8,10},{9,11},{10,... | collective-permute-start | bytes 884744 | tf_op jit(solution)/shard_map/ppermute | solution.py:44
  41.5 11.2 %collective-permute-start.8 = (s32[4,144,128]{2,1,0:T(8,128)S(1)}, s32[4,144,128]{2,1,0:T(8,128)S(1)}, u32[]{:S(2)}, u32[]{:S(2)}) collective-permute-start(s32[4,144,128]{2,1,0:T(8,128)S(1)} %get-tuple-element.33), channel_id=1, source_target_pairs={{0,3},{1,2},{2,1},{3,0},{4,7},{5,6},{6,5},{7,4},{8,11},{9,10},{10,... | collective-permute-start | bytes 884744 | tf_op jit(solution)/shard_map/ppermute | solution.py:44
  53.7 6.5 %collective-permute-start.10 = (s32[1,144,128]{2,1,0:T(8,128)S(1)}, s32[1,144,128]{2,1,0:T(8,128)S(1)}, u32[]{:S(2)}, u32[]{:S(2)}) collective-permute-start(s32[1,144,128]{2,1,0:T(8,128)S(1)} %get-tuple-element.36), channel_id=1, source_target_pairs={{0,8},{1,9},{2,10},{3,11},{4,12},{5,13},{6,14},{7,15},{8,0},{9,1},... | collective-permute-start | bytes 221192 | tf_op jit(solution)/shard_map/ppermute | solution.py:44
  57.1 6.9 %collective-permute-start.11 = (s32[1,144,128]{2,1,0:T(8,128)S(1)}, s32[1,144,128]{2,1,0:T(8,128)S(1)}, u32[]{:S(2)}, u32[]{:S(2)}) collective-permute-start(s32[1,144,128]{2,1,0:T(8,128)S(1)} %get-tuple-element.37), channel_id=1, source_target_pairs={{0,12},{1,13},{2,14},{3,15},{4,8},{5,9},{6,10},{7,11},{8,4},{9,5},... | collective-permute-start | bytes 221192 | tf_op jit(solution)/shard_map/ppermute | solution.py:44
  57.5 6.5 %collective-permute-start.9 = (s32[1,144,128]{2,1,0:T(8,128)S(1)}, s32[1,144,128]{2,1,0:T(8,128)S(1)}, u32[]{:S(2)}, u32[]{:S(2)}) collective-permute-start(s32[1,144,128]{2,1,0:T(8,128)S(1)} %get-tuple-element.35), channel_id=1, source_target_pairs={{0,4},{1,5},{2,6},{3,7},{4,0},{5,1},{6,2},{7,3},{8,12},{9,13},{10,... | collective-permute-start | bytes 221192 | tf_op jit(solution)/shard_map/ppermute | solution.py:44
  65.0 95.9 %copy-start = (bf16[1,1024,2048]{2,1,0:T(8,128)(2,1)S(1)}, bf16[1,1024,2048]{2,1,0:T(8,128)(2,1)}, u32[]{:S(2)}) copy-start(bf16[1,1024,2048]{2,1,0:T(8,128)(2,1)} %param.3) | copy-start | bytes 12582916
  65.0 4.4 %collective-permute-start.12 = (s32[1,144,128]{2,1,0:T(8,128)S(1)}, s32[1,144,128]{2,1,0:T(8,128)S(1)}, u32[]{:S(2)}, u32[]{:S(2)}) collective-permute-start(s32[1,144,128]{2,1,0:T(8,128)S(1)} %get-tuple-element.38), channel_id=1, source_target_pairs={{0,4},{1,5},{2,6},{3,7},{4,0},{5,1},{6,2},{7,3},{8,12},{9,13},{10,... | collective-permute-start | bytes 221192 | tf_op jit(solution)/shard_map/ppermute | solution.py:44
  65.9 6.0 %collective-permute-start.13 = (s32[1,144,128]{2,1,0:T(8,128)S(1)}, s32[1,144,128]{2,1,0:T(8,128)S(1)}, u32[]{:S(2)}, u32[]{:S(2)}) collective-permute-start(s32[1,144,128]{2,1,0:T(8,128)S(1)} %get-tuple-element.38), channel_id=1, source_target_pairs={{0,8},{1,9},{2,10},{3,11},{4,12},{5,13},{6,14},{7,15},{8,0},{9,1},... | collective-permute-start | bytes 221192 | tf_op jit(solution)/shard_map/ppermute | solution.py:44
  67.5 6.2 %collective-permute-start.14 = (s32[1,144,128]{2,1,0:T(8,128)S(1)}, s32[1,144,128]{2,1,0:T(8,128)S(1)}, u32[]{:S(2)}, u32[]{:S(2)}) collective-permute-start(s32[1,144,128]{2,1,0:T(8,128)S(1)} %get-tuple-element.38), channel_id=1, source_target_pairs={{0,12},{1,13},{2,14},{3,15},{4,8},{5,9},{6,10},{7,11},{8,4},{9,5},... | collective-permute-start | bytes 221192 | tf_op jit(solution)/shard_map/ppermute | solution.py:44
  73.6 6.7 %collective-permute-start.15 = (s32[4,144,128]{2,1,0:T(8,128)S(1)}, s32[4,144,128]{2,1,0:T(8,128)S(1)}, u32[]{:S(2)}, u32[]{:S(2)}) collective-permute-start(s32[4,144,128]{2,1,0:T(8,128)S(1)} %constant_dynamic-update-slice_fusion.refs_0_), channel_id=1, source_target_pairs={{0,1},{1,0},{2,3},{3,2},{4,5},{5,4},{6,7},{7,6},{8,9},{9,8},{10,11... | collective-permute-start | bytes 884744 | tf_op jit(solution)/shard_map/ppermute | solution.py:44
  75.0 9.9 %collective-permute-start.16 = (s32[4,144,128]{2,1,0:T(8,128)S(1)}, s32[4,144,128]{2,1,0:T(8,128)S(1)}, u32[]{:S(2)}, u32[]{:S(2)}) collective-permute-start(s32[4,144,128]{2,1,0:T(8,128)S(1)} %constant_dynamic-update-slice_fusion.refs_0_), channel_id=1, source_target_pairs={{0,2},{1,3},{2,0},{3,1},{4,6},{5,7},{6,4},{7,5},{8,10},{9,11},{10,... | collective-permute-start | bytes 884744 | tf_op jit(solution)/shard_map/ppermute | solution.py:44
  76.5 8.3 %collective-permute-start.17 = (s32[4,144,128]{2,1,0:T(8,128)S(1)}, s32[4,144,128]{2,1,0:T(8,128)S(1)}, u32[]{:S(2)}, u32[]{:S(2)}) collective-permute-start(s32[4,144,128]{2,1,0:T(8,128)S(1)} %constant_dynamic-update-slice_fusion.refs_0_), channel_id=1, source_target_pairs={{0,3},{1,2},{2,1},{3,0},{4,7},{5,6},{6,5},{7,4},{8,11},{9,10},{10,... | collective-permute-start | bytes 884744 | tf_op jit(solution)/shard_map/ppermute | solution.py:44
  109.4 6.8 %collective-permute-start.18 = (s32[4,144,128]{2,1,0:T(8,128)S(1)}, s32[4,144,128]{2,1,0:T(8,128)S(1)}, u32[]{:S(2)}, u32[]{:S(2)}) collective-permute-start(s32[4,144,128]{2,1,0:T(8,128)S(1)} %get-tuple-element.40), channel_id=1, source_target_pairs={{0,1},{1,0},{2,3},{3,2},{4,5},{5,4},{6,7},{7,6},{8,9},{9,8},{10,11... | collective-permute-start | bytes 884744 | tf_op jit(solution)/shard_map/ppermute | solution.py:44
  110.4 8.5 %collective-permute-start.19 = (s32[4,144,128]{2,1,0:T(8,128)S(1)}, s32[4,144,128]{2,1,0:T(8,128)S(1)}, u32[]{:S(2)}, u32[]{:S(2)}) collective-permute-start(s32[4,144,128]{2,1,0:T(8,128)S(1)} %get-tuple-element.41), channel_id=1, source_target_pairs={{0,2},{1,3},{2,0},{3,1},{4,6},{5,7},{6,4},{7,5},{8,10},{9,11},{10,... | collective-permute-start | bytes 884744 | tf_op jit(solution)/shard_map/ppermute | solution.py:44
  111.5 8.9 %collective-permute-start.20 = (s32[4,144,128]{2,1,0:T(8,128)S(1)}, s32[4,144,128]{2,1,0:T(8,128)S(1)}, u32[]{:S(2)}, u32[]{:S(2)}) collective-permute-start(s32[4,144,128]{2,1,0:T(8,128)S(1)} %get-tuple-element.42), channel_id=1, source_target_pairs={{0,3},{1,2},{2,1},{3,0},{4,7},{5,6},{6,5},{7,4},{8,11},{9,10},{10,... | collective-permute-start | bytes 884744 | tf_op jit(solution)/shard_map/ppermute | solution.py:44
  131.2 5.9 %collective-permute-start.21 = (s32[1,144,128]{2,1,0:T(8,128)S(1)}, s32[1,144,128]{2,1,0:T(8,128)S(1)}, u32[]{:S(2)}, u32[]{:S(2)}) collective-permute-start(s32[1,144,128]{2,1,0:T(8,128)S(1)} %get-tuple-element.44), channel_id=1, source_target_pairs={{0,4},{1,5},{2,6},{3,7},{4,0},{5,1},{6,2},{7,3},{8,12},{9,13},{10,... | collective-permute-start | bytes 221192 | tf_op jit(solution)/shard_map/ppermute | solution.py:44
  131.3 5.8 %collective-permute-start.22 = (s32[1,144,128]{2,1,0:T(8,128)S(1)}, s32[1,144,128]{2,1,0:T(8,128)S(1)}, u32[]{:S(2)}, u32[]{:S(2)}) collective-permute-start(s32[1,144,128]{2,1,0:T(8,128)S(1)} %get-tuple-element.45), channel_id=1, source_target_pairs={{0,8},{1,9},{2,10},{3,11},{4,12},{5,13},{6,14},{7,15},{8,0},{9,1},... | collective-permute-start | bytes 221192 | tf_op jit(solution)/shard_map/ppermute | solution.py:44
  133.5 6.2 %collective-permute-start.23 = (s32[1,144,128]{2,1,0:T(8,128)S(1)}, s32[1,144,128]{2,1,0:T(8,128)S(1)}, u32[]{:S(2)}, u32[]{:S(2)}) collective-permute-start(s32[1,144,128]{2,1,0:T(8,128)S(1)} %get-tuple-element.46), channel_id=1, source_target_pairs={{0,12},{1,13},{2,14},{3,15},{4,8},{5,9},{6,10},{7,11},{8,4},{9,5},... | collective-permute-start | bytes 221192 | tf_op jit(solution)/shard_map/ppermute | solution.py:44
  140.2 4.5 %collective-permute-start.24 = (s32[1,144,128]{2,1,0:T(8,128)S(1)}, s32[1,144,128]{2,1,0:T(8,128)S(1)}, u32[]{:S(2)}, u32[]{:S(2)}) collective-permute-start(s32[1,144,128]{2,1,0:T(8,128)S(1)} %get-tuple-element.47), channel_id=1, source_target_pairs={{0,4},{1,5},{2,6},{3,7},{4,0},{5,1},{6,2},{7,3},{8,12},{9,13},{10,... | collective-permute-start | bytes 221192 | tf_op jit(solution)/shard_map/ppermute | solution.py:44
  140.3 5.3 %collective-permute-start.25 = (s32[1,144,128]{2,1,0:T(8,128)S(1)}, s32[1,144,128]{2,1,0:T(8,128)S(1)}, u32[]{:S(2)}, u32[]{:S(2)}) collective-permute-start(s32[1,144,128]{2,1,0:T(8,128)S(1)} %get-tuple-element.47), channel_id=1, source_target_pairs={{0,8},{1,9},{2,10},{3,11},{4,12},{5,13},{6,14},{7,15},{8,0},{9,1},... | collective-permute-start | bytes 221192 | tf_op jit(solution)/shard_map/ppermute | solution.py:44
  143.0 6.2 %collective-permute-start.26 = (s32[1,144,128]{2,1,0:T(8,128)S(1)}, s32[1,144,128]{2,1,0:T(8,128)S(1)}, u32[]{:S(2)}, u32[]{:S(2)}) collective-permute-start(s32[1,144,128]{2,1,0:T(8,128)S(1)} %get-tuple-element.47), channel_id=1, source_target_pairs={{0,12},{1,13},{2,14},{3,15},{4,8},{5,9},{6,10},{7,11},{8,4},{9,5},... | collective-permute-start | bytes 221192 | tf_op jit(solution)/shard_map/ppermute | solution.py:44
  149.2 7.2 %collective-permute-start.27 = (s32[4,144,128]{2,1,0:T(8,128)S(1)}, s32[4,144,128]{2,1,0:T(8,128)S(1)}, u32[]{:S(2)}, u32[]{:S(2)}) collective-permute-start(s32[4,144,128]{2,1,0:T(8,128)S(1)} %constant_dynamic-update-slice_fusion.4.refs_0_), channel_id=1, source_target_pairs={{0,1},{1,0},{2,3},{3,2},{4,5},{5,4},{6,7},{7,6},{8,9},{9,8},{10,11... | collective-permute-start | bytes 884744 | tf_op jit(solution)/shard_map/ppermute | solution.py:44
  150.2 10.7 %collective-permute-start.28 = (s32[4,144,128]{2,1,0:T(8,128)S(1)}, s32[4,144,128]{2,1,0:T(8,128)S(1)}, u32[]{:S(2)}, u32[]{:S(2)}) collective-permute-start(s32[4,144,128]{2,1,0:T(8,128)S(1)} %constant_dynamic-update-slice_fusion.4.refs_0_), channel_id=1, source_target_pairs={{0,2},{1,3},{2,0},{3,1},{4,6},{5,7},{6,4},{7,5},{8,10},{9,11},{10,... | collective-permute-start | bytes 884744 | tf_op jit(solution)/shard_map/ppermute | solution.py:44
  151.8 9.1 %collective-permute-start.29 = (s32[4,144,128]{2,1,0:T(8,128)S(1)}, s32[4,144,128]{2,1,0:T(8,128)S(1)}, u32[]{:S(2)}, u32[]{:S(2)}) collective-permute-start(s32[4,144,128]{2,1,0:T(8,128)S(1)} %constant_dynamic-update-slice_fusion.4.refs_0_), channel_id=1, source_target_pairs={{0,3},{1,2},{2,1},{3,0},{4,7},{5,6},{6,5},{7,4},{8,11},{9,10},{10,... | collective-permute-start | bytes 884744 | tf_op jit(solution)/shard_map/ppermute | solution.py:44
  167.2 4.0 %collective-permute-start.30 = (f32[72,128]{1,0:T(8,128)S(1)}, f32[72,128]{1,0:T(8,128)S(1)}, u32[]{:S(2)}, u32[]{:S(2)}) collective-permute-start(f32[72,128]{1,0:T(8,128)S(1)} %get-tuple-element.53), channel_id=1, source_target_pairs={{0,1},{1,0},{2,3},{3,2},{4,5},{5,4},{6,7},{7,6},{8,9},{9,8},{10,11... | collective-permute-start | bytes 110600 | tf_op jit(solution)/shard_map/ppermute | solution.py:44
  168.3 4.0 %collective-permute-start.31 = (f32[72,128]{1,0:T(8,128)S(1)}, f32[72,128]{1,0:T(8,128)S(1)}, u32[]{:S(2)}, u32[]{:S(2)}) collective-permute-start(f32[72,128]{1,0:T(8,128)S(1)} %get-tuple-element.54), channel_id=1, source_target_pairs={{0,2},{1,3},{2,0},{3,1},{4,6},{5,7},{6,4},{7,5},{8,10},{9,11},{10,... | collective-permute-start | bytes 110600 | tf_op jit(solution)/shard_map/ppermute | solution.py:44
  169.3 4.9 %collective-permute-start.32 = (f32[72,128]{1,0:T(8,128)S(1)}, f32[72,128]{1,0:T(8,128)S(1)}, u32[]{:S(2)}, u32[]{:S(2)}) collective-permute-start(f32[72,128]{1,0:T(8,128)S(1)} %get-tuple-element.55), channel_id=1, source_target_pairs={{0,3},{1,2},{2,1},{3,0},{4,7},{5,6},{6,5},{7,4},{8,11},{9,10},{10,... | collective-permute-start | bytes 110600 | tf_op jit(solution)/shard_map/ppermute | solution.py:44
  174.2 4.5 %collective-permute-start.33 = (f32[72,128]{1,0:T(8,128)S(1)}, f32[72,128]{1,0:T(8,128)S(1)}, u32[]{:S(2)}, u32[]{:S(2)}) collective-permute-start(f32[72,128]{1,0:T(8,128)S(1)} %add_add_fusion.1), channel_id=1, source_target_pairs={{0,4},{1,5},{2,6},{3,7},{4,0},{5,1},{6,2},{7,3},{8,12},{9,13},{10,... | collective-permute-start | bytes 110600 | tf_op jit(solution)/shard_map/ppermute | solution.py:44
  174.2 4.9 %collective-permute-start.34 = (f32[72,128]{1,0:T(8,128)S(1)}, f32[72,128]{1,0:T(8,128)S(1)}, u32[]{:S(2)}, u32[]{:S(2)}) collective-permute-start(f32[72,128]{1,0:T(8,128)S(1)} %add_add_fusion.1), channel_id=1, source_target_pairs={{0,8},{1,9},{2,10},{3,11},{4,12},{5,13},{6,14},{7,15},{8,0},{9,1},... | collective-permute-start | bytes 110600 | tf_op jit(solution)/shard_map/ppermute | solution.py:44
  176.2 5.8 %collective-permute-start.35 = (f32[72,128]{1,0:T(8,128)S(1)}, f32[72,128]{1,0:T(8,128)S(1)}, u32[]{:S(2)}, u32[]{:S(2)}) collective-permute-start(f32[72,128]{1,0:T(8,128)S(1)} %add_add_fusion.1), channel_id=1, source_target_pairs={{0,12},{1,13},{2,14},{3,15},{4,8},{5,9},{6,10},{7,11},{8,4},{9,5},... | collective-permute-start | bytes 110600 | tf_op jit(solution)/shard_map/ppermute | solution.py:44
  181.9 14.8 %collective-permute-start.36 = (f32[72,128]{1,0:T(8,128)S(1)}, f32[72,128]{1,0:T(8,128)S(1)}, u32[]{:S(2)}, u32[]{:S(2)}) collective-permute-start(f32[72,128]{1,0:T(8,128)S(1)} %add_add_fusion.refs_0_), channel_id=1, source_target_pairs={{0,1},{1,0},{2,3},{3,2},{4,5},{5,4},{6,7},{7,6},{8,9},{9,8},{10,11... | collective-permute-start | bytes 110600 | tf_op jit(solution)/shard_map/ppermute | solution.py:44
  183.7 13.0 %collective-permute-start.37 = (f32[72,128]{1,0:T(8,128)S(1)}, f32[72,128]{1,0:T(8,128)S(1)}, u32[]{:S(2)}, u32[]{:S(2)}) collective-permute-start(f32[72,128]{1,0:T(8,128)S(1)} %add_add_fusion.refs_0_), channel_id=1, source_target_pairs={{0,2},{1,3},{2,0},{3,1},{4,6},{5,7},{6,4},{7,5},{8,10},{9,11},{10,... | collective-permute-start | bytes 110600 | tf_op jit(solution)/shard_map/ppermute | solution.py:44
  184.1 12.7 %collective-permute-start.38 = (f32[72,128]{1,0:T(8,128)S(1)}, f32[72,128]{1,0:T(8,128)S(1)}, u32[]{:S(2)}, u32[]{:S(2)}) collective-permute-start(f32[72,128]{1,0:T(8,128)S(1)} %add_add_fusion.refs_0_), channel_id=1, source_target_pairs={{0,3},{1,2},{2,1},{3,0},{4,7},{5,6},{6,5},{7,4},{8,11},{9,10},{10,... | collective-permute-start | bytes 110600 | tf_op jit(solution)/shard_map/ppermute | solution.py:44
  198.0 1.2 collective-permute-start.39

commit v4 on v3

--- a/solution.py
+++ b/solution.py
@@ -10,15 +10,14 @@
 
 LANES = 128
 SUBLANES = 8
-BLOCK = 1024
 PANEL = 32
 PIECES = 2
 CODES = 128
 STEPS = 65535.0
 LEAST = 2.0**-90
-VMEM_LIMIT = 48 * 1024 * 1024
+VMEM_LIMIT = 40 * 1024 * 1024
 HIGHEST = lax.Precision.HIGHEST
-FACTOR_COST = pl.CostEstimate(flops=12_000_000_000, bytes_accessed=4 << 20, transcendentals=0)
+FACTOR_COST = pl.CostEstimate(flops=4_000_000_000, bytes_accessed=4 << 20, transcendentals=0)
 
 
 def stage_bits(groups):
@@ -69,13 +68,29 @@
     return parts[0]
 
 
-def sum_quarters(quarters, groups):
+def sum_quarters(quarters, groups, beside):
     stages = stage_bits(groups)
     spans = offsets(stages[0])
-    total = pair_sum([quarters[0]] + [exchange(part, groups, span) for part, span in zip(quarters[1:], spans[1:])])
+    steps = list(beside)
+    state = steps.pop(0)(None)
+    arrived = [exchange(part, groups, span) for part, span in zip(quarters[1:], spans[1:])]
+    arrived, state = lax.optimization_barrier((arrived, state))
+    total = pair_sum([quarters[0]] + arrived)
     for bits in stages[1:]:
-        total = pair_sum([total] + [exchange(total, groups, span) for span in offsets(bits)[1:]])
-    return [total] + [exchange(total, groups, span) for span in spans[1:]]
+        if len(steps) > 1:
+            state = steps.pop(0)(state)
+        arrived = [exchange(total, groups, span) for span in offsets(bits)[1:]]
+        arrived, state = lax.optimization_barrier((arrived, state))
+        total = pair_sum([total] + arrived)
+    for step in steps:
+        state = step(state)
+    return [total] + [exchange(total, groups, span) for span in spans[1:]], state
+
+
+TILES = 2
+FINE = 28
+NIBBLES = 4
+PACKED = TILES * LANES // 2 + SUBLANES
 
 
 def row_scales(peaks):
@@ -91,60 +106,68 @@
     return matrix
 
 
-def pack_tiles(tiles):
-    peaks = gather_columns([jnp.max(jnp.abs(tile), axis=1, keepdims=True) for tile in tiles])
-    codes, scales = row_scales(peaks)
+def pack_chunks(chunks):
+    peaks = [jnp.max(jnp.abs(chunk), axis=1, keepdims=True) for chunk in chunks]
+    codes, scales = row_scales(
+        gather_columns([peak[tile * LANES : (tile + 1) * LANES] for peak in peaks for tile in range(TILES)])
+    )
     factors = STEPS / scales
-    lines = codes.T
-    half = LANES // 2
+    lines = codes.T.astype(jnp.int32)
+    sub = lax.broadcasted_iota(jnp.int32, (SUBLANES, LANES), 0)
+    half = TILES * LANES // 2
     messages = []
-    for place, tile in enumerate(tiles):
-        value = jnp.round(tile * factors[:, place : place + 1]).astype(jnp.int32)
-        high = jnp.right_shift(value, 1)
-        low = jnp.bitwise_and(value, 1)
+    for place, chunk in enumerate(chunks):
+        factor = jnp.concatenate(
+            [factors[:, TILES * place + tile : TILES * place + tile + 1] for tile in range(TILES)], axis=0
+        )
+        scaled = chunk * factor
+        fine = FINE * SUBLANES
+        value = jnp.concatenate(
+            [jnp.round(scaled[:fine]).astype(jnp.int32), 2 * jnp.round(0.5 * scaled[fine:]).astype(jnp.int32)], axis=0
+        )
+        high = jnp.clip(jnp.right_shift(value, 1), -32768, 32767)
         words = jnp.bitwise_or(jnp.left_shift(high[:half], 16), jnp.bitwise_and(high[half:], 0xFFFF))
-        code = jnp.broadcast_to(lines[place : place + 1, :], (SUBLANES, LANES)).astype(jnp.int32)
-        extra = jnp.left_shift(code, 16)
-        for group in range(LANES // SUBLANES):
-            bits = low[group * SUBLANES : (group + 1) * SUBLANES]
+        first = jnp.broadcast_to(lines[TILES * place : TILES * place + 1], (SUBLANES, LANES))
+        second = jnp.broadcast_to(lines[TILES * place + 1 : TILES * place + 2], (SUBLANES, LANES))
+        code = jnp.where(sub < NIBBLES, first, second)
+        nibble = jnp.right_shift(code, NIBBLES * jnp.bitwise_and(sub, NIBBLES - 1))
+        extra = jnp.left_shift(nibble, FINE)
+        for group in range(FINE):
+            bits = jnp.bitwise_and(value[group * SUBLANES : (group + 1) * SUBLANES], 1)
             extra = jnp.bitwise_or(extra, jnp.left_shift(bits, group))
         messages.append(jnp.concatenate([words, extra], axis=0))
     return messages
 
 
-def unpack_tiles(messages):
-    half = LANES // 2
-    lines = [jnp.right_shift(message[half : half + 1], 16).astype(jnp.float32) for message in messages]
-    lines.append(jnp.zeros((LANES - len(messages), LANES), jnp.float32))
+def unpack_chunks(messages):
+    half = TILES * LANES // 2
+    lines = []
+    for message in messages:
+        nibble = jnp.bitwise_and(jnp.right_shift(message[half:], FINE), 15)
+        for tile in range(TILES):
+            code = jnp.left_shift(nibble[tile * NIBBLES + NIBBLES - 1 : (tile + 1) * NIBBLES], 28)
+            code = jnp.right_shift(code, 28 - NIBBLES * (NIBBLES - 1))
+            for place in range(NIBBLES - 1):
+                line = nibble[tile * NIBBLES + place : tile * NIBBLES + place + 1]
+                code = jnp.bitwise_or(code, jnp.left_shift(line, NIBBLES * place))
+            lines.append(code.astype(jnp.float32))
+    lines.append(jnp.zeros((LANES - len(lines), LANES), jnp.float32))
     scales = (jnp.exp2(jnp.concatenate(lines, axis=0) * (1.0 / CODES)) * (1.0 / STEPS)).T
 
-    def tile(place):
+    def make(place, tile):
         words, extra = messages[place][:half], messages[place][half:]
-        high = jnp.concatenate([jnp.right_shift(words, 16), jnp.right_shift(jnp.left_shift(words, 16), 16)], axis=0)
-        low = jnp.concatenate(
-            [jnp.bitwise_and(jnp.right_shift(extra, group), 1) for group in range(LANES // SUBLANES)], axis=0
-        )
-        value = jnp.bitwise_or(jnp.left_shift(high, 1), low)
-        return value.astype(jnp.float32) * scales[:, place : place + 1]
-
-    return [functools.partial(tile, place) for place in range(len(messages))]
-
-
-PACKED = LANES // 2 + SUBLANES
-
-
-def pack_chunks(chunks):
-    parts = chunks[0].shape[0] // LANES
-    messages = pack_tiles([chunk[part * LANES : (part + 1) * LANES] for chunk in chunks for part in range(parts)])
-    return [jnp.concatenate(messages[place * parts : (place + 1) * parts], axis=0) for place in range(len(chunks))]
-
-
-def unpack_chunks(messages):
-    parts = messages[0].shape[0] // PACKED
-    tiles = unpack_tiles(
-        [message[part * PACKED : (part + 1) * PACKED] for message in messages for part in range(parts)]
-    )
-    return [tiles[place * parts : (place + 1) * parts] for place in range(len(messages))]
+        high = jnp.right_shift(words if tile == 0 else jnp.left_shift(words, 16), 16)
+        low = [
+            jnp.bitwise_and(jnp.right_shift(extra, group), 1) if group < FINE else jnp.zeros_like(extra)
+            for group in range(tile * LANES // SUBLANES, (tile + 1) * LANES // SUBLANES)
+        ]
+        value = jnp.bitwise_or(jnp.left_shift(high, 1), jnp.concatenate(low, axis=0))
+        column = TILES * place + tile
+        return value.astype(jnp.float32) * scales[:, column : column + 1]
+
+    return [
+        [functools.partial(make, place, tile) for tile in range(TILES)] for place in range(len(messages))
+    ]
 
 
 def encode_kernel(place_ref, size_ref, start_ref, out_ref):
@@ -161,7 +184,7 @@
         encode_kernel,
         in_specs=[scalar, scalar, vmem],
         out_specs=vmem,
-        out_shape=jax.ShapeDtypeStruct((1, size // LANES * PACKED, width), jnp.int32),
+        out_shape=jax.ShapeDtypeStruct((1, PACKED, width), jnp.int32),
     )(place, sizes, start)
 
 
@@ -188,7 +211,7 @@
     width = chunks // parts
     vmem = pl.BlockSpec(memory_space=pltpu.VMEM)
     outs = [jax.ShapeDtypeStruct((width, rows, lanes), jnp.float32)]
-    outs += [jax.ShapeDtypeStruct((width, rows // LANES * PACKED, lanes), jnp.int32)] * max(parts - 1, 1)
+    outs += [jax.ShapeDtypeStruct((width, PACKED, lanes), jnp.int32)] * max(parts - 1, 1)
     return pl.pallas_call(
         functools.partial(combine_kernel, len(arrived), parts),
         in_specs=[vmem] * (1 + len(arrived)),
@@ -223,87 +246,61 @@
 
 
 def apply_kernel(order, normalise, scale, sources, place_ref, size_ref, rows_ref, *refs):
-    refs, outs, (full_ref, split_ref, work_ref) = refs[:sources], refs[sources:-3], refs[-3:]
-    step = pl.program_id(0)
+    refs, outs, (full_ref, work_ref, held_ref, sem) = refs[:sources], refs[sources:-4], refs[-4:]
     size, cap = full_ref.shape
-
-    @pl.when(step == 0)
-    def _():
-        load_all(order, place_ref, refs, full_ref)
-        value = full_ref[...]
-        if normalise:
-            start_factor(work_ref, rows_inner(value))
-            inverse_factor(work_ref, size, PANEL)
-            value = jnp.dot(
-                finish_factor(work_ref), value, precision=HIGHEST, preferred_element_type=jnp.float32
-            )
-        for piece, part in enumerate(split_pieces(value, PIECES)):
-            split_ref[pl.ds(piece * size, size), :] = part
-
-    rows = rows_ref[...]
-    image = lax.dot_general(
-        split_ref[...], rows, (((1,), (1,)), ((), ())), preferred_element_type=jnp.float32
-    )
+    copy = pltpu.make_async_copy(rows_ref, held_ref, sem)
+    copy.start()
+    load_all(order, place_ref, refs, full_ref)
+    value = full_ref[...]
+    if normalise:
+        start_factor(work_ref, rows_inner(value))
+        inverse_factor(work_ref, size, PANEL)
+        value = jnp.dot(finish_factor(work_ref), value, precision=HIGHEST, preferred_element_type=jnp.float32)
+    split = jnp.concatenate(split_pieces(value, PIECES), axis=0)
+    copy.wait()
+    image = rows_dot(split, held_ref[...])
     image = sum(image[piece * size : (piece + 1) * size] for piece in range(PIECES)) * scale
-    back = jnp.dot(
-        jnp.concatenate(split_pieces(image, PIECES), axis=0), rows, preferred_element_type=jnp.float32
-    )
+    split = jnp.concatenate(split_pieces(image, PIECES), axis=0)
+    back = jnp.dot(split, held_ref[...], preferred_element_type=jnp.float32)
     back = sum(back[piece * size : (piece + 1) * size] for piece in range(PIECES))
-
-    @pl.when(step == 0)
-    def _():
-        full_ref[...] = back
-
-    @pl.when(step > 0)
-    def _():
-        full_ref[...] += back
-
-    @pl.when(step == pl.num_programs(0) - 1)
-    def _():
-        live = lax.broadcasted_iota(jnp.int32, (1, cap), 1) < size_ref[0]
-        full_ref[...] = jnp.where(live, full_ref[...], 0.0)
-        if len(outs) == 1:
-            outs[0][...] = full_ref[...]
-            return
-        each, _, width = outs[0].shape
-        chunks = []
-        for offset in order:
-            first = pl.multiple_of(jnp.bitwise_xor(place_ref[0], offset) * width, width)
-            chunks.append(full_ref[:, pl.ds(first, width)])
-        for place in range(each):
-            outs[0][place] = chunks[place]
-        for place, message in enumerate(pack_chunks(chunks[each:])):
-            outs[1 + place // each][place % each] = message
-
-
-def apply_samples(genotypes, sizes, place, gathered, order, normalise, scale, groups):
+    live = lax.broadcasted_iota(jnp.int32, (1, cap), 1) < size_ref[0]
+    back = jnp.where(live, back, 0.0)
+    if len(outs) == 1:
+        outs[0][...] = back
+        return
+    full_ref[...] = back
+    each, _, width = outs[0].shape
+    chunks = []
+    for offset in order:
+        first = pl.multiple_of(jnp.bitwise_xor(place_ref[0], offset) * width, width)
+        chunks.append(full_ref[:, pl.ds(first, width)])
+    for place in range(each):
+        outs[0][place] = chunks[place]
+    for place, message in enumerate(pack_chunks(chunks[each:])):
+        outs[1 + place // each][place % each] = message
+
+
+def apply_samples(genotypes, sizes, place, gathered, order, normalise, scale):
     samples, cap = genotypes.shape
-    block = min(BLOCK, samples)
-    packed = len(gathered) > 1
-    if packed:
+    if len(gathered) > 1:
         each, rows, width = gathered[0].shape
-        size = rows // PACKED * LANES
+        size = TILES * LANES
         outs = [jax.ShapeDtypeStruct((each, size, width), jnp.float32)]
         outs += [jax.ShapeDtypeStruct((each, rows, width), jnp.int32)] * (len(gathered) - 1)
     else:
         size = gathered[0].shape[0]
         outs = [jax.ShapeDtypeStruct((size, cap), jnp.float32)]
-    scalar = pl.BlockSpec(memory_space=pltpu.SMEM)
-
-    def whole(value):
-        return pl.BlockSpec(value.shape, lambda step: (0,) * len(value.shape))
-
+    scalar, vmem = pl.BlockSpec(memory_space=pltpu.SMEM), pl.BlockSpec(memory_space=pltpu.VMEM)
     return pl.pallas_call(
         functools.partial(apply_kernel, order, normalise, scale, len(gathered)),
-        grid=(samples // block,),
-        in_specs=[scalar, scalar, pl.BlockSpec((block, cap), lambda step: (step, 0))]
-        + [whole(part) for part in gathered],
-        out_specs=[whole(out) for out in outs],
+        in_specs=[scalar, scalar, pl.BlockSpec(memory_space=pl.ANY)] + [vmem] * len(gathered),
+        out_specs=[vmem] * len(outs),
         out_shape=outs,
         scratch_shapes=[
             pltpu.VMEM((size, cap), jnp.float32),
-            pltpu.VMEM((PIECES * size, cap), jnp.bfloat16),
             pltpu.VMEM((size, 2 * size), jnp.float32),
+            pltpu.VMEM((samples, cap), jnp.bfloat16),
+            pltpu.SemaphoreType.DMA,
         ],
         compiler_params=pltpu.CompilerParams(vmem_limit_bytes=VMEM_LIMIT),
     )(place, sizes, genotypes, *gathered)
@@ -317,11 +314,11 @@
     return jnp.broadcast_to(tile[row : row + 1, :], (SUBLANES, LANES))
 
 
-def inverse_factor(work_ref, size, panel):
+def inverse_factor(work_ref, size, panel, first_top=0, last_top=None):
     tiles = 2 * size // LANES
     below = lax.broadcasted_iota(jnp.int32, (SUBLANES, LANES), 0)
     groups = panel // SUBLANES
-    for top in range(0, size, panel):
+    for top in range(first_top, size if last_top is None else last_top, panel):
         active = [
             tile
             for tile in range(tiles)
@@ -344,7 +341,6 @@
             for step in range(SUBLANES):
                 pivot = row_splat(columns[block][step], step)
                 root = lax.rsqrt(pivot)
-                root = root * (1.5 - 0.5 * pivot * root * root)
                 factor = {group: columns[group][step] * root for group in range(block, groups)}
                 for later in range(step + 1, SUBLANES):
                     weight = row_splat(factor[block], later)
@@ -367,10 +363,15 @@
         if rest < size:
             first, last = active[0] * LANES, (active[-1] + 1) * LANES
             lines = work_ref[top:rest, first:last]
-            weights = work_ref[top:rest, rest // LANES * LANES : size].T[rest % LANES :, :]
-            work_ref[rest:, first:last] -= jnp.dot(
-                weights, lines, precision=HIGHEST, preferred_element_type=jnp.float32
+            high, middle, low = split_pieces(work_ref[top:rest, rest // LANES * LANES : size], 3)
+            above, between, below_ = split_pieces(lines, 3)
+            update = lax.dot_general(
+                jnp.concatenate([high, high, high, middle, middle, low], axis=0),
+                jnp.concatenate([above, between, below_, above, between, above], axis=0),
+                (((0,), (0,)), ((), ())),
+                preferred_element_type=jnp.float32,
             )
+            work_ref[rest:, first:last] -= update[rest % LANES :]
 
 
 def start_factor(work_ref, inner):
@@ -388,10 +389,14 @@
     return jnp.where(row >= column, work_ref[:, size:], 0.0)
 
 
+def rows_dot(left, right):
+    return lax.dot_general(left, right, (((1,), (1,)), ((), ())), preferred_element_type=jnp.float32)
+
+
 def rows_inner(value):
-    return lax.dot_general(
-        value, value, (((1,), (1,)), ((), ())), precision=HIGHEST, preferred_element_type=jnp.float32
-    )
+    high, middle, low = split_pieces(value, 3)
+    mixed = rows_dot(high, middle) + rows_dot(high, low)
+    return rows_dot(high, high) + rows_dot(middle, middle) + (mixed + mixed.T)
 
 
 def fold_symmetric(value, folded_ref, height):
@@ -422,82 +427,70 @@
 
 
 def project_kernel(order, sources, quarter_ref, place_ref, rows_ref, *refs):
-    refs, (inner_ref, *outs), (full_ref, split_ref, cross_ref, folded_ref) = refs[:sources], refs[sources:-4], refs[-4:]
-    step = pl.program_id(0)
+    refs, (inner_ref, *outs), (full_ref, folded_ref, held_ref, sem) = refs[:sources], refs[sources:-4], refs[-4:]
     size = full_ref.shape[0]
-
-    @pl.when(step == 0)
-    def _():
-        load_all(order, place_ref, refs, full_ref)
-        image = full_ref[...]
-        inner_ref[...] = rows_inner(image)
-        for piece, part in enumerate(split_pieces(image, PIECES)):
-            split_ref[pl.ds(piece * size, size), :] = part
-        cross_ref[...] = jnp.zeros_like(cross_ref)
-
-    sampled = lax.dot_general(
-        split_ref[...], rows_ref[...], (((1,), (1,)), ((), ())), preferred_element_type=jnp.float32
-    )
+    copy = pltpu.make_async_copy(rows_ref, held_ref, sem)
+    copy.start()
+    load_all(order, place_ref, refs, full_ref)
+    image = full_ref[...]
+    inner_ref[...] = rows_inner(image)
+    split = jnp.concatenate(split_pieces(image, PIECES), axis=0)
+    copy.wait()
+    sampled = rows_dot(split, held_ref[...])
     sampled = sum(sampled[piece * size : (piece + 1) * size] for piece in range(PIECES))
-    cross_ref[...] += rows_inner(sampled)
-
-    @pl.when(step == pl.num_programs(0) - 1)
-    def _():
-        fold_symmetric(cross_ref[...], folded_ref, size)
-        for offset, out_ref in enumerate(outs):
-            out_ref[...] = folded_ref[jnp.bitwise_xor(quarter_ref[0], offset)]
+    high, low = split_pieces(sampled, PIECES)
+    mixed = rows_dot(high, low)
+    fold_symmetric(rows_dot(high, high) + (mixed + mixed.T), folded_ref, size)
+    for offset, out_ref in enumerate(outs):
+        out_ref[...] = folded_ref[jnp.bitwise_xor(quarter_ref[0], offset)]
 
 
 def project(genotypes, quarter, place, gathered, order, size):
     samples, cap = genotypes.shape
-    block = min(BLOCK, samples)
-    scalar = pl.BlockSpec(memory_space=pltpu.SMEM)
-
-    def whole(shape):
-        return pl.BlockSpec(shape, lambda step: (0,) * len(shape))
-
+    scalar, vmem = pl.BlockSpec(memory_space=pltpu.SMEM), pl.BlockSpec(memory_space=pltpu.VMEM)
     part = (size // 4 + SUBLANES, size // 2)
     outs = [(size, size)] + [part] * 4
     return pl.pallas_call(
         functools.partial(project_kernel, order, len(gathered)),
-        grid=(samples // block,),
-        in_specs=[scalar, scalar, pl.BlockSpec((block, cap), lambda step: (step, 0))]
-        + [whole(part.shape) for part in gathered],
-        out_specs=[whole(shape) for shape in outs],
+        in_specs=[scalar, scalar, pl.BlockSpec(memory_space=pl.ANY)] + [vmem] * len(gathered),
+        out_specs=[vmem] * len(outs),
         out_shape=[jax.ShapeDtypeStruct(shape, jnp.float32) for shape in outs],
         scratch_shapes=[
             pltpu.VMEM((size, cap), jnp.float32),
-            pltpu.VMEM((PIECES * size, cap), jnp.bfloat16),
-            pltpu.VMEM((size, size), jnp.float32),
             pltpu.VMEM((4,) + part, jnp.float32),
+            pltpu.VMEM((samples, cap), jnp.bfloat16),
+            pltpu.SemaphoreType.DMA,
         ],
         compiler_params=pltpu.CompilerParams(vmem_limit_bytes=VMEM_LIMIT),
     )(quarter, place, genotypes, *gathered)
 
 
-def second_kernel(gain, inner_ref, own_ref, out_ref, basis_ref, work_ref):
-    start_factor(work_ref, inner_ref[...])
-    inverse_factor(work_ref, work_ref.shape[0], PANEL)
-    factor = finish_factor(work_ref)
-    out_ref[...] = factor
-    own = jnp.dot(factor, own_ref[...], precision=HIGHEST, preferred_element_type=jnp.float32)
-    basis_ref[...] = own.T * gain
-
-
-def second_factor(inner, own, gain):
-    size, width = own.shape
-    return pl.pallas_call(
-        functools.partial(second_kernel, gain),
-        in_specs=[pl.BlockSpec(memory_space=pltpu.VMEM)] * 2,
-        out_specs=[pl.BlockSpec(memory_space=pltpu.VMEM)] * 2,
-        out_shape=[
-            jax.ShapeDtypeStruct((size, size), jnp.float32),
-            jax.ShapeDtypeStruct((width, size), jnp.float32),
-        ],
-        scratch_shapes=[pltpu.VMEM((size, 2 * size), jnp.float32)],
+def second_kernel(gain, first, last, *refs):
+    (source_ref, *own_ref), (work_ref, *basis_ref) = refs[: len(refs) // 2], refs[len(refs) // 2 :]
+    if first == 0:
+        start_factor(work_ref, source_ref[...])
+    else:
+        work_ref[...] = source_ref[...]
+    inverse_factor(work_ref, work_ref.shape[0], PANEL, first, last)
+    if own_ref:
+        factor = finish_factor(work_ref)
+        own = jnp.dot(factor, own_ref[0][...], precision=HIGHEST, preferred_element_type=jnp.float32)
+        basis_ref[0][...] = own.T * gain
+
+
+def second_factor(source, first, last, own=None, gain=1.0):
+    size = source.shape[0]
+    vmem = pl.BlockSpec(memory_space=pltpu.VMEM)
+    shapes = [(size, 2 * size)] + ([] if own is None else [own.shape[::-1]])
+    outs = pl.pallas_call(
+        functools.partial(second_kernel, gain, first, last),
+        in_specs=[vmem] * len(shapes),
+        out_specs=[vmem] * len(shapes),
+        out_shape=[jax.ShapeDtypeStruct(shape, jnp.float32) for shape in shapes],
         compiler_params=pltpu.CompilerParams(vmem_limit_bytes=VMEM_LIMIT),
         cost_estimate=FACTOR_COST,
-    )(inner, own)
+    )(source, *([] if own is None else [own]))
+    return outs[0] if own is None else outs
 
 
 def finish_kernel(scale, quarter_ref, factor_ref, *refs):
@@ -505,7 +498,7 @@
     for offset in range(4):
         folded_ref[jnp.bitwise_xor(quarter_ref[0], offset)] = parts[offset][...]
     cross = unfold_symmetric([folded_ref[place] for place in range(4)])
-    factor = factor_ref[...]
+    factor = finish_factor(factor_ref)
     half = jnp.dot(factor, cross, precision=HIGHEST, preferred_element_type=jnp.float32)
     result = scale * lax.dot_general(
         half, factor, (((1,), (1,)), ((), ())), precision=HIGHEST, preferred_element_type=jnp.float32
@@ -523,7 +516,7 @@
         in_specs=[pl.BlockSpec(memory_space=pltpu.SMEM)] + [vmem] * 5,
         out_specs=[vmem] * 2,
         out_shape=[
-            jax.ShapeDtypeStruct(factor.shape, jnp.float32),
+            jax.ShapeDtypeStruct((factor.shape[0],) * 2, jnp.float32),
             jax.ShapeDtypeStruct((SUBLANES, LANES), jnp.float32),
         ],
         scratch_shapes=[pltpu.VMEM((4,) + parts[0].shape, jnp.float32)],
@@ -553,14 +546,14 @@
     place = me.reshape(1).astype(jnp.int32)
     stages = stage_bits(groups)
     order = relative_order(stages)
-    packed = width == LANES
+    packed = width == LANES and size == TILES * LANES
 
     def gather(message):
         gathered = gather_chunks(message, groups)
         return gathered if packed else [to_natural(gathered, order, me)]
 
     def apply(message, normalise):
-        outs = apply_samples(dosages, sizes, place, gather(message), order, normalise, scale, groups)
+        outs = apply_samples(dosages, sizes, place, gather(message), order, normalise, scale)
         if not packed:
             outs = to_relative(outs[0], order, me, width, len(offsets(stages[0])))
         return reduce_chunks(outs[0], outs[1:], groups, packed)
@@ -574,8 +567,13 @@
     own, message = apply(message, True)
     quarter = jnp.bitwise_and(place, 3)
     inner, *quarters = project(dosages, quarter, place, gather(message), order, size)
-    quarters = sum_quarters(quarters, groups)
-    second, basis = second_factor(inner, own[0], math.sqrt(cap))
+    cuts = [0, size // 4 + size // 8, size - size // 4, size]
+    beside = [
+        lambda _: second_factor(inner, cuts[0], cuts[1]),
+        lambda work: second_factor(work, cuts[1], cuts[2]),
+        lambda work: second_factor(work, cuts[2], cuts[3], own[0], math.sqrt(cap)),
+    ]
+    quarters, (second, basis) = sum_quarters(quarters, groups, beside)
     rayleigh, trace = finish(quarter, second, quarters, scale)
     blocks = lax.axis_size("blk")
     total = trace

time: 205 us -> 174 us (0.85); the launches traced: 201 us -> 174 us
  Pallas kernels: 67.2 us -> 46 us
  waiting for transfers between devices: 77.4 us -> 68.8 us
  local copies, waits for them, and re-layouts: 0.57 us -> 2.76 us
    pallas_call x4, Pallas kernels: 13.4 us -> 3.71 us  [combine(): pl.pallas_call(functools.partial(combine_kernel, len(arrived), parts), in...]
    ppermute x39, waiting for transfers between devices: 76.2 us -> 67.6 us  [exchange(): lax.ppermute(value, 'smp', [(device, device ^ offset) for device in range...]
    pallas_call x2, Pallas kernels: 33.1 us -> 25.2 us  [apply_samples(): pl.pallas_call(functools.partial(apply_kernel, order, normalise, scale, l...]
    pallas_call x2 -> x4, Pallas kernels: 17.5 us -> 13.9 us  [the longest x3 8.65 us: second_factor(): pl.pallas_call(functools.partial(second_kernel, gain, first, last), in_sp...]
    unnamed x8 -> x10, local copies, waits for them, and re-layouts: 0.04 us -> 2.23 us
  transfers between devices with their start and end apart: 40 -> 40, of which waited for: 27 -> 25; matrix products, arithmetic and copies ran while one was open for 0% -> 0% of each run, Pallas kernels for 6% -> 5%
where the time goes in v4:
time: 174 us
  waiting for transfers between devices  68.8 us (40%)
  starting transfers between devices  52.2 us (30%)
  Pallas kernels  46 us (26%)
  local copies, waits for them, and re-layouts  2.76 us (2%)
  between operations  2.18 us (1%)
    ppermute x39, waiting for transfers between devices, exchange(): lax.ppermute(value, 'smp', [(device, device ^ offset) for device in range...  67.6 us
    ppermute x39, starting transfers between devices, exchange(): lax.ppermute(value, 'smp', [(device, device ^ offset) for device in range...  52.1 us
    pallas_call x2, Pallas kernels, apply_samples(): pl.pallas_call(functools.partial(apply_kernel, order, normalise, scale, l...  25.2 us
    pallas_call x3, Pallas kernels, second_factor(): pl.pallas_call(functools.partial(second_kernel, gain, first, last), in_sp...  8.65 us
    pallas_call x1, Pallas kernels, project(): pl.pallas_call(functools.partial(project_kernel, order, len(gathered)), i...  5.29 us
    pallas_call x4, Pallas kernels, combine(): pl.pallas_call(functools.partial(combine_kernel, len(arrived), parts), in...  3.71 us
  transfers between devices with their start and end apart: 40, of which 25 were waited for; matrix products, arithmetic and copies ran while one was open for 0% of the time, Pallas kernels for 5%

profile of v4, /device:TPU:0, one launch (start us, length us, event | category | flops | bytes accessed | tf_op | source)
XLA Modules:
  0.0 173.6 jit_solution(12641040113568958257)
XLA Ops:
  1.3 1.9 %shard_map.50 = s32[1,136,128]{2,1,0:T(8,128)} custom-call(s32[1]{0:T(128)} %bitcast.place_ref, s32[1]{0:T(128)S(6)} %copy.11.size_ref, f32[128,256]{1,0:T(8,128)} %bitcast.12), custom_call_target="tpu_custom_call" | custom-call | tf_op jit(solution)/shard_map/pallas_call | solution.py:183
  3.2 3.0 %collective-permute-start = (s32[1,136,128]{2,1,0:T(8,128)}, s32[1,136,128]{2,1,0:T(8,128)S(1)}, u32[]{:S(2)}, u32[]{:S(2)}) collective-permute-start(s32[1,136,128]{2,1,0:T(8,128)} %shard_map.50), channel_id=1, source_target_pairs={{0,4},{1,5},{2,6},{3,7},{4,0},{5,1},{6,2},{7,3},{8,12},{9,13},{10,... | collective-permute-start | bytes 208904 | tf_op jit(solution)/shard_map/ppermute | solution.py:43
  6.2 2.6 %collective-permute-start.1 = (s32[1,136,128]{2,1,0:T(8,128)}, s32[1,136,128]{2,1,0:T(8,128)S(1)}, u32[]{:S(2)}, u32[]{:S(2)}) collective-permute-start(s32[1,136,128]{2,1,0:T(8,128)} %shard_map.50), channel_id=1, source_target_pairs={{0,8},{1,9},{2,10},{3,11},{4,12},{5,13},{6,14},{7,15},{8,0},{9,1},... | collective-permute-start | bytes 208904 | tf_op jit(solution)/shard_map/ppermute | solution.py:43
  8.8 5.2 %collective-permute-done.1 = s32[1,136,128]{2,1,0:T(8,128)S(1)} collective-permute-done((s32[1,136,128]{2,1,0:T(8,128)}, s32[1,136,128]{2,1,0:T(8,128)S(1)}, u32[]{:S(2)}, u32[]{:S(2)}) %collective-permute-start.1) | collective-permute-done | bytes 69664 | tf_op jit(solution)/shard_map/ppermute | solution.py:43
  16.2 1.6 collective-permute-start.3
  17.7 1.5 collective-permute-start.4
  19.7 6.1 %collective-permute-done.3.refs_1_ = s32[4,136,128]{2,1,0:T(8,128)S(1)} collective-permute-done((s32[4,136,128]{2,1,0:T(8,128)S(1)}, s32[4,136,128]{2,1,0:T(8,128)S(1)}, u32[]{:S(2)}, u32[]{:S(2)}) %collective-permute-start.3) | collective-permute-done | bytes 278560 | tf_op jit(solution)/shard_map/ppermute | solution.py:43
  25.8 4.2 %collective-permute-done.4.refs_2_ = s32[4,136,128]{2,1,0:T(8,128)S(1)} collective-permute-done((s32[4,136,128]{2,1,0:T(8,128)S(1)}, s32[4,136,128]{2,1,0:T(8,128)S(1)}, u32[]{:S(2)}, u32[]{:S(2)}) %collective-permute-start.4) | collective-permute-done | bytes 278560 | tf_op jit(solution)/shard_map/ppermute | solution.py:43
  30.0 2.2 %copy-done = bf16[1,1024,2048]{2,1,0:T(8,128)(2,1)S(1)} copy-done((bf16[1,1024,2048]{2,1,0:T(8,128)(2,1)S(1)}, bf16[1,1024,2048]{2,1,0:T(8,128)(2,1)}, u32[]{:S(2)}) %copy-start) | copy-done | bytes 4194328
  32.2 7.4 %shard_map.51 = (f32[4,256,128]{2,1,0:T(8,128)S(1)}, s32[4,136,128]{2,1,0:T(8,128)S(1)}, s32[4,136,128]{2,1,0:T(8,128)S(1)}, s32[4,136,128]{2,1,0:T(8,128)S(1)}) custom-call(s32[1]{0:T(128)} %bitcast.place_ref, s32[1]{0:T(128)S(6)} %copy.11.size_ref, bf16[1024,2048]{1,0:T(8,128)(2,1)S(1)} %bitcast.8, s32[4,136,128]{2,1,0:T(8,128)S(1)} %pad_add_fusion.refs_0_, ...), custom_call_target="tpu_custom_call" | custom-call | tf_op jit(solution)/shard_map/pallas_call | solution.py:294
  39.6 1.3 collective-permute-start.6
  41.7 1.4 collective-permute-start.8
  43.1 4.7 %collective-permute-done.6.refs_0_ = s32[4,136,128]{2,1,0:T(8,128)S(1)} collective-permute-done((s32[4,136,128]{2,1,0:T(8,128)S(1)}, s32[4,136,128]{2,1,0:T(8,128)S(1)}, u32[]{:S(2)}, u32[]{:S(2)}) %collective-permute-start.6) | collective-permute-done | bytes 278560 | tf_op jit(solution)/shard_map/ppermute | solution.py:43
  47.8 4.1 %collective-permute-done.7.refs_1_ = s32[4,136,128]{2,1,0:T(8,128)S(1)} collective-permute-done((s32[4,136,128]{2,1,0:T(8,128)S(1)}, s32[4,136,128]{2,1,0:T(8,128)S(1)}, u32[]{:S(2)}, u32[]{:S(2)}) %collective-permute-start.7) | collective-permute-done | bytes 278560 | tf_op jit(solution)/shard_map/ppermute | solution.py:43
  53.0 3.4 %collective-permute-start.10 = (s32[1,136,128]{2,1,0:T(8,128)S(1)}, s32[1,136,128]{2,1,0:T(8,128)S(1)}, u32[]{:S(2)}, u32[]{:S(2)}) collective-permute-start(s32[1,136,128]{2,1,0:T(8,128)S(1)} %get-tuple-element.44), channel_id=1, source_target_pairs={{0,8},{1,9},{2,10},{3,11},{4,12},{5,13},{6,14},{7,15},{8,0},{9,1},... | collective-permute-start | bytes 208904 | tf_op jit(solution)/shard_map/ppermute | solution.py:43
  57.1 2.4 %collective-permute-done.10.refs_1_ = s32[1,136,128]{2,1,0:T(8,128)S(1)} collective-permute-done((s32[1,136,128]{2,1,0:T(8,128)S(1)}, s32[1,136,128]{2,1,0:T(8,128)S(1)}, u32[]{:S(2)}, u32[]{:S(2)}) %collective-permute-start.10) | collective-permute-done | bytes 69664 | tf_op jit(solution)/shard_map/ppermute | solution.py:43
  59.4 3.8 %collective-permute-done.11.refs_2_ = s32[1,136,128]{2,1,0:T(8,128)S(1)} collective-permute-done((s32[1,136,128]{2,1,0:T(8,128)S(1)}, s32[1,136,128]{2,1,0:T(8,128)S(1)}, u32[]{:S(2)}, u32[]{:S(2)}) %collective-permute-start.11) | collective-permute-done | bytes 69664 | tf_op jit(solution)/shard_map/ppermute | solution.py:43
  64.7 2.1 %collective-permute-start.13 = (s32[1,136,128]{2,1,0:T(8,128)S(1)}, s32[1,136,128]{2,1,0:T(8,128)S(1)}, u32[]{:S(2)}, u32[]{:S(2)}) collective-permute-start(s32[1,136,128]{2,1,0:T(8,128)S(1)} %get-tuple-element.46), channel_id=1, source_target_pairs={{0,8},{1,9},{2,10},{3,11},{4,12},{5,13},{6,14},{7,15},{8,0},{9,1},... | collective-permute-start | bytes 208904 | tf_op jit(solution)/shard_map/ppermute | solution.py:43
  66.8 1.8 %collective-permute-start.14 = (s32[1,136,128]{2,1,0:T(8,128)S(1)}, s32[1,136,128]{2,1,0:T(8,128)S(1)}, u32[]{:S(2)}, u32[]{:S(2)}) collective-permute-start(s32[1,136,128]{2,1,0:T(8,128)S(1)} %get-tuple-element.46), channel_id=1, source_target_pairs={{0,12},{1,13},{2,14},{3,15},{4,8},{5,9},{6,10},{7,11},{8,4},{9,5},... | collective-permute-start | bytes 208904 | tf_op jit(solution)/shard_map/ppermute | solution.py:43
  68.6 1.3 collective-permute-done.13
  69.9 3.0 %collective-permute-done.14 = s32[1,136,128]{2,1,0:T(8,128)S(1)} collective-permute-done((s32[1,136,128]{2,1,0:T(8,128)S(1)}, s32[1,136,128]{2,1,0:T(8,128)S(1)}, u32[]{:S(2)}, u32[]{:S(2)}) %collective-permute-start.14) | collective-permute-done | bytes 69664 | tf_op jit(solution)/shard_map/ppermute | solution.py:43
  74.0 1.5 collective-permute-start.16
  76.4 3.1 %collective-permute-done.15.refs_1_ = s32[4,136,128]{2,1,0:T(8,128)S(1)} collective-permute-done((s32[4,136,128]{2,1,0:T(8,128)S(1)}, s32[4,136,128]{2,1,0:T(8,128)S(1)}, u32[]{:S(2)}, u32[]{:S(2)}) %collective-permute-start.15) | collective-permute-done | bytes 278560 | tf_op jit(solution)/shard_map/ppermute | solution.py:43
  79.4 4.1 %collective-permute-done.16.refs_2_ = s32[4,136,128]{2,1,0:T(8,128)S(1)} collective-permute-done((s32[4,136,128]{2,1,0:T(8,128)S(1)}, s32[4,136,128]{2,1,0:T(8,128)S(1)}, u32[]{:S(2)}, u32[]{:S(2)}) %collective-permute-start.16) | collective-permute-done | bytes 278560 | tf_op jit(solution)/shard_map/ppermute | solution.py:43
  83.5 17.9 %shard_map.54 = (f32[4,256,128]{2,1,0:T(8,128)S(1)}, s32[4,136,128]{2,1,0:T(8,128)S(1)}, s32[4,136,128]{2,1,0:T(8,128)S(1)}, s32[4,136,128]{2,1,0:T(8,128)S(1)}) custom-call(s32[1]{0:T(128)} %bitcast.place_ref, s32[1]{0:T(128)S(6)} %copy.11.size_ref, bf16[1024,2048]{1,0:T(8,128)(2,1)S(1)} %bitcast.9, ...), custom_call_target="tpu_custom_call" | custom-call | tf_op jit(solution)/shard_map/pallas_call | solution.py:294
  103.5 1.5 collective-permute-start.20
  104.9 3.1 %collective-permute-done.18.refs_0_ = s32[4,136,128]{2,1,0:T(8,128)S(1)} collective-permute-done((s32[4,136,128]{2,1,0:T(8,128)S(1)}, s32[4,136,128]{2,1,0:T(8,128)S(1)}, u32[]{:S(2)}, u32[]{:S(2)}) %collective-permute-start.18) | collective-permute-done | bytes 278560 | tf_op jit(solution)/shard_map/ppermute | solution.py:43
  108.0 2.5 %collective-permute-done.19.refs_1_ = s32[4,136,128]{2,1,0:T(8,128)S(1)} collective-permute-done((s32[4,136,128]{2,1,0:T(8,128)S(1)}, s32[4,136,128]{2,1,0:T(8,128)S(1)}, u32[]{:S(2)}, u32[]{:S(2)}) %collective-permute-start.19) | collective-permute-done | bytes 278560 | tf_op jit(solution)/shard_map/ppermute | solution.py:43
  110.5 1.4 collective-permute-done.20.refs_2_
  113.1 2.5 %collective-permute-start.22 = (s32[1,136,128]{2,1,0:T(8,128)S(1)}, s32[1,136,128]{2,1,0:T(8,128)S(1)}, u32[]{:S(2)}, u32[]{:S(2)}) collective-permute-start(s32[1,136,128]{2,1,0:T(8,128)S(1)} %get-tuple-element.53), channel_id=1, source_target_pairs={{0,8},{1,9},{2,10},{3,11},{4,12},{5,13},{6,14},{7,15},{8,0},{9,1},... | collective-permute-start | bytes 208904 | tf_op jit(solution)/shard_map/ppermute | solution.py:43
  115.6 1.9 %collective-permute-start.23 = (s32[1,136,128]{2,1,0:T(8,128)S(1)}, s32[1,136,128]{2,1,0:T(8,128)S(1)}, u32[]{:S(2)}, u32[]{:S(2)}) collective-permute-start(s32[1,136,128]{2,1,0:T(8,128)S(1)} %get-tuple-element.54), channel_id=1, source_target_pairs={{0,12},{1,13},{2,14},{3,15},{4,8},{5,9},{6,10},{7,11},{8,4},{9,5},... | collective-permute-start | bytes 208904 | tf_op jit(solution)/shard_map/ppermute | solution.py:43
  117.5 1.4 collective-permute-done.21.refs_0_
  118.9 2.8 %collective-permute-done.23.refs_2_ = s32[1,136,128]{2,1,0:T(8,128)S(1)} collective-permute-done((s32[1,136,128]{2,1,0:T(8,128)S(1)}, s32[1,136,128]{2,1,0:T(8,128)S(1)}, u32[]{:S(2)}, u32[]{:S(2)}) %collective-permute-start.23) | collective-permute-done | bytes 69664 | tf_op jit(solution)/shard_map/ppermute | solution.py:43
  122.4 2.5 %collective-permute-start.25 = (s32[1,136,128]{2,1,0:T(8,128)S(1)}, s32[1,136,128]{2,1,0:T(8,128)S(1)}, u32[]{:S(2)}, u32[]{:S(2)}) collective-permute-start(s32[1,136,128]{2,1,0:T(8,128)S(1)} %get-tuple-element.55), channel_id=1, source_target_pairs={{0,8},{1,9},{2,10},{3,11},{4,12},{5,13},{6,14},{7,15},{8,0},{9,1},... | collective-permute-start | bytes 208904 | tf_op jit(solution)/shard_map/ppermute | solution.py:43
  124.8 1.9 %collective-permute-start.26 = (s32[1,136,128]{2,1,0:T(8,128)S(1)}, s32[1,136,128]{2,1,0:T(8,128)S(1)}, u32[]{:S(2)}, u32[]{:S(2)}) collective-permute-start(s32[1,136,128]{2,1,0:T(8,128)S(1)} %get-tuple-element.55), channel_id=1, source_target_pairs={{0,12},{1,13},{2,14},{3,15},{4,8},{5,9},{6,10},{7,11},{8,4},{9,5},... | collective-permute-start | bytes 208904 | tf_op jit(solution)/shard_map/ppermute | solution.py:43
  127.6 3.3 %collective-permute-done.26 = s32[1,136,128]{2,1,0:T(8,128)S(1)} collective-permute-done((s32[1,136,128]{2,1,0:T(8,128)S(1)}, s32[1,136,128]{2,1,0:T(8,128)S(1)}, u32[]{:S(2)}, u32[]{:S(2)}) %collective-permute-start.26) | collective-permute-done | bytes 69664 | tf_op jit(solution)/shard_map/ppermute | solution.py:43
  132.0 1.6 collective-permute-start.28
  134.4 3.8 %collective-permute-done.27.refs_1_ = s32[4,136,128]{2,1,0:T(8,128)S(1)} collective-permute-done((s32[4,136,128]{2,1,0:T(8,128)S(1)}, s32[4,136,128]{2,1,0:T(8,128)S(1)}, u32[]{:S(2)}, u32[]{:S(2)}) %collective-permute-start.27) | collective-permute-done | bytes 278560 | tf_op jit(solution)/shard_map/ppermute | solution.py:43
  138.2 4.1 %collective-permute-done.28.refs_2_ = s32[4,136,128]{2,1,0:T(8,128)S(1)} collective-permute-done((s32[4,136,128]{2,1,0:T(8,128)S(1)}, s32[4,136,128]{2,1,0:T(8,128)S(1)}, u32[]{:S(2)}, u32[]{:S(2)}) %collective-permute-start.28) | collective-permute-done | bytes 278560 | tf_op jit(solution)/shard_map/ppermute | solution.py:43
  142.3 5.3 %shard_map.57 = (f32[256,256]{1,0:T(8,128)S(1)}, f32[72,128]{1,0:T(8,128)S(1)}, f32[72,128]{1,0:T(8,128)S(1)}, f32[72,128]{1,0:T(8,128)S(1)}, f32[72,128]{1,0:T(8,128)S(1)}) custom-call(s32[1]{0:T(128)S(6)} %and.4.quarter_ref, s32[1]{0:T(128)} %bitcast.place_ref, bf16[1024,2048]{1,0:T(8,128)(2,1)S(1)} %bitcast.10, ...), custom_call_target="tpu_custom_call" | custom-call | tf_op jit(solution)/shard_map/pallas_call | solution.py:453
  149.7 1.5 collective-permute-start.32
  151.2 3.0 %shard_map.58.refs_0_ = f32[256,512]{1,0:T(8,128)S(1)} custom-call(f32[256,256]{1,0:T(8,128)S(1)} %get-tuple-element.60.refs_0_), custom_call_target="tpu_custom_call" | custom-call | flops 4000000000 | bytes 4194304 | tf_op jit(solution)/shard_map/pallas_call | solution.py:485
  154.6 2.0 %collective-permute-start.34 = (f32[72,128]{1,0:T(8,128)S(1)}, f32[72,128]{1,0:T(8,128)S(1)}, u32[]{:S(2)}, u32[]{:S(2)}) collective-permute-start(f32[72,128]{1,0:T(8,128)S(1)} %add_add_fusion.1), channel_id=1, source_target_pairs={{0,8},{1,9},{2,10},{3,11},{4,12},{5,13},{6,14},{7,15},{8,0},{9,1},... | collective-permute-start | bytes 110600 | tf_op jit(solution)/shard_map/ppermute | solution.py:43
  156.7 2.3 %collective-permute-start.35 = (f32[72,128]{1,0:T(8,128)S(1)}, f32[72,128]{1,0:T(8,128)S(1)}, u32[]{:S(2)}, u32[]{:S(2)}) collective-permute-start(f32[72,128]{1,0:T(8,128)S(1)} %add_add_fusion.1), channel_id=1, source_target_pairs={{0,12},{1,13},{2,14},{3,15},{4,8},{5,9},{6,10},{7,11},{8,4},{9,5},... | collective-permute-start | bytes 110600 | tf_op jit(solution)/shard_map/ppermute | solution.py:43
  159.0 2.9 %shard_map.59.refs_0_ = f32[256,512]{1,0:T(8,128)S(1)} custom-call(f32[256,512]{1,0:T(8,128)S(1)} %shard_map.58.refs_0_), custom_call_target="tpu_custom_call" | custom-call | flops 4000000000 | bytes 4194304 | tf_op jit(solution)/shard_map/pallas_call | solution.py:485
  162.4 1.3 collective-permute-start.36
  164.3 1.7 collective-permute-start.38
  166.0 2.8 %shard_map.60 = (f32[256,512]{1,0:T(8,128)S(1)}, f32[128,256]{1,0:T(8,128)}) custom-call(f32[256,512]{1,0:T(8,128)S(1)} %shard_map.59.refs_0_, f32[256,128]{1,0:T(8,128)S(1)} %bitcast.11), custom_call_target="tpu_custom_call" | custom-call | flops 4000000000 | bytes 4194304 | tf_op jit(solution)/shard_map/pallas_call | solution.py:485
  (62 shorter events, 23.1 us)
Async XLA Ops:
  3.2 5.6 %collective-permute-start = (s32[1,136,128]{2,1,0:T(8,128)}, s32[1,136,128]{2,1,0:T(8,128)S(1)}, u32[]{:S(2)}, u32[]{:S(2)}) collective-permute-start(s32[1,136,128]{2,1,0:T(8,128)} %shard_map.50), channel_id=1, source_target_pairs={{0,4},{1,5},{2,6},{3,7},{4,0},{5,1},{6,2},{7,3},{8,12},{9,13},{10,... | collective-permute-start | bytes 208904 | tf_op jit(solution)/shard_map/ppermute | solution.py:43
  6.2 7.8 %collective-permute-start.1 = (s32[1,136,128]{2,1,0:T(8,128)}, s32[1,136,128]{2,1,0:T(8,128)S(1)}, u32[]{:S(2)}, u32[]{:S(2)}) collective-permute-start(s32[1,136,128]{2,1,0:T(8,128)} %shard_map.50), channel_id=1, source_target_pairs={{0,8},{1,9},{2,10},{3,11},{4,12},{5,13},{6,14},{7,15},{8,0},{9,1},... | collective-permute-start | bytes 208904 | tf_op jit(solution)/shard_map/ppermute | solution.py:43
  8.8 6.4 %collective-permute-start.2 = (s32[1,136,128]{2,1,0:T(8,128)}, s32[1,136,128]{2,1,0:T(8,128)S(1)}, u32[]{:S(2)}, u32[]{:S(2)}) collective-permute-start(s32[1,136,128]{2,1,0:T(8,128)} %shard_map.50), channel_id=1, source_target_pairs={{0,12},{1,13},{2,14},{3,15},{4,8},{5,9},{6,10},{7,11},{8,4},{9,5},... | collective-permute-start | bytes 208904 | tf_op jit(solution)/shard_map/ppermute | solution.py:43
  16.2 9.6 %collective-permute-start.3 = (s32[4,136,128]{2,1,0:T(8,128)S(1)}, s32[4,136,128]{2,1,0:T(8,128)S(1)}, u32[]{:S(2)}, u32[]{:S(2)}) collective-permute-start(s32[4,136,128]{2,1,0:T(8,128)S(1)} %pad_add_fusion.refs_0_), channel_id=1, source_target_pairs={{0,1},{1,0},{2,3},{3,2},{4,5},{5,4},{6,7},{7,6},{8,9},{9,8},{10,11... | collective-permute-start | bytes 835592 | tf_op jit(solution)/shard_map/ppermute | solution.py:43
  17.7 12.3 %collective-permute-start.4 = (s32[4,136,128]{2,1,0:T(8,128)S(1)}, s32[4,136,128]{2,1,0:T(8,128)S(1)}, u32[]{:S(2)}, u32[]{:S(2)}) collective-permute-start(s32[4,136,128]{2,1,0:T(8,128)S(1)} %pad_add_fusion.refs_0_), channel_id=1, source_target_pairs={{0,2},{1,3},{2,0},{3,1},{4,6},{5,7},{6,4},{7,5},{8,10},{9,11},{10,... | collective-permute-start | bytes 835592 | tf_op jit(solution)/shard_map/ppermute | solution.py:43
  19.2 10.8 %collective-permute-start.5 = (s32[4,136,128]{2,1,0:T(8,128)S(1)}, s32[4,136,128]{2,1,0:T(8,128)S(1)}, u32[]{:S(2)}, u32[]{:S(2)}) collective-permute-start(s32[4,136,128]{2,1,0:T(8,128)S(1)} %pad_add_fusion.refs_0_), channel_id=1, source_target_pairs={{0,3},{1,2},{2,1},{3,0},{4,7},{5,6},{6,5},{7,4},{8,11},{9,10},{10,... | collective-permute-start | bytes 835592 | tf_op jit(solution)/shard_map/ppermute | solution.py:43
  30.0 2.2 %copy-start = (bf16[1,1024,2048]{2,1,0:T(8,128)(2,1)S(1)}, bf16[1,1024,2048]{2,1,0:T(8,128)(2,1)}, u32[]{:S(2)}) copy-start(bf16[1,1024,2048]{2,1,0:T(8,128)(2,1)} %param.3) | copy-start | bytes 12582916
  32.2 51.3 %copy-start.1 = (bf16[1,1024,2048]{2,1,0:T(8,128)(2,1)S(1)}, bf16[1,1024,2048]{2,1,0:T(8,128)(2,1)}, u32[]{:S(2)}) copy-start(bf16[1,1024,2048]{2,1,0:T(8,128)(2,1)} %param.3) | copy-start | bytes 12582916
  39.6 8.2 %collective-permute-start.6 = (s32[4,136,128]{2,1,0:T(8,128)S(1)}, s32[4,136,128]{2,1,0:T(8,128)S(1)}, u32[]{:S(2)}, u32[]{:S(2)}) collective-permute-start(s32[4,136,128]{2,1,0:T(8,128)S(1)} %get-tuple-element.39), channel_id=1, source_target_pairs={{0,1},{1,0},{2,3},{3,2},{4,5},{5,4},{6,7},{7,6},{8,9},{9,8},{10,11... | collective-permute-start | bytes 835592 | tf_op jit(solution)/shard_map/ppermute | solution.py:43
  40.9 11.1 %collective-permute-start.7 = (s32[4,136,128]{2,1,0:T(8,128)S(1)}, s32[4,136,128]{2,1,0:T(8,128)S(1)}, u32[]{:S(2)}, u32[]{:S(2)}) collective-permute-start(s32[4,136,128]{2,1,0:T(8,128)S(1)} %get-tuple-element.40), channel_id=1, source_target_pairs={{0,2},{1,3},{2,0},{3,1},{4,6},{5,7},{6,4},{7,5},{8,10},{9,11},{10,... | collective-permute-start | bytes 835592 | tf_op jit(solution)/shard_map/ppermute | solution.py:43
  41.7 10.2 %collective-permute-start.8 = (s32[4,136,128]{2,1,0:T(8,128)S(1)}, s32[4,136,128]{2,1,0:T(8,128)S(1)}, u32[]{:S(2)}, u32[]{:S(2)}) collective-permute-start(s32[4,136,128]{2,1,0:T(8,128)S(1)} %get-tuple-element.41), channel_id=1, source_target_pairs={{0,3},{1,2},{2,1},{3,0},{4,7},{5,6},{6,5},{7,4},{8,11},{9,10},{10,... | collective-permute-start | bytes 835592 | tf_op jit(solution)/shard_map/ppermute | solution.py:43
  53.0 6.5 %collective-permute-start.10 = (s32[1,136,128]{2,1,0:T(8,128)S(1)}, s32[1,136,128]{2,1,0:T(8,128)S(1)}, u32[]{:S(2)}, u32[]{:S(2)}) collective-permute-start(s32[1,136,128]{2,1,0:T(8,128)S(1)} %get-tuple-element.44), channel_id=1, source_target_pairs={{0,8},{1,9},{2,10},{3,11},{4,12},{5,13},{6,14},{7,15},{8,0},{9,1},... | collective-permute-start | bytes 208904 | tf_op jit(solution)/shard_map/ppermute | solution.py:43
  56.4 6.8 %collective-permute-start.11 = (s32[1,136,128]{2,1,0:T(8,128)S(1)}, s32[1,136,128]{2,1,0:T(8,128)S(1)}, u32[]{:S(2)}, u32[]{:S(2)}) collective-permute-start(s32[1,136,128]{2,1,0:T(8,128)S(1)} %get-tuple-element.45), channel_id=1, source_target_pairs={{0,12},{1,13},{2,14},{3,15},{4,8},{5,9},{6,10},{7,11},{8,4},{9,5},... | collective-permute-start | bytes 208904 | tf_op jit(solution)/shard_map/ppermute | solution.py:43
  57.0 6.3 %collective-permute-start.9 = (s32[1,136,128]{2,1,0:T(8,128)S(1)}, s32[1,136,128]{2,1,0:T(8,128)S(1)}, u32[]{:S(2)}, u32[]{:S(2)}) collective-permute-start(s32[1,136,128]{2,1,0:T(8,128)S(1)} %get-tuple-element.43), channel_id=1, source_target_pairs={{0,4},{1,5},{2,6},{3,7},{4,0},{5,1},{6,2},{7,3},{8,12},{9,13},{10,... | collective-permute-start | bytes 208904 | tf_op jit(solution)/shard_map/ppermute | solution.py:43
  64.2 4.4 %collective-permute-start.12 = (s32[1,136,128]{2,1,0:T(8,128)S(1)}, s32[1,136,128]{2,1,0:T(8,128)S(1)}, u32[]{:S(2)}, u32[]{:S(2)}) collective-permute-start(s32[1,136,128]{2,1,0:T(8,128)S(1)} %get-tuple-element.46), channel_id=1, source_target_pairs={{0,4},{1,5},{2,6},{3,7},{4,0},{5,1},{6,2},{7,3},{8,12},{9,13},{10,... | collective-permute-start | bytes 208904 | tf_op jit(solution)/shard_map/ppermute | solution.py:43
  64.7 5.2 %collective-permute-start.13 = (s32[1,136,128]{2,1,0:T(8,128)S(1)}, s32[1,136,128]{2,1,0:T(8,128)S(1)}, u32[]{:S(2)}, u32[]{:S(2)}) collective-permute-start(s32[1,136,128]{2,1,0:T(8,128)S(1)} %get-tuple-element.46), channel_id=1, source_target_pairs={{0,8},{1,9},{2,10},{3,11},{4,12},{5,13},{6,14},{7,15},{8,0},{9,1},... | collective-permute-start | bytes 208904 | tf_op jit(solution)/shard_map/ppermute | solution.py:43
  66.8 6.1 %collective-permute-start.14 = (s32[1,136,128]{2,1,0:T(8,128)S(1)}, s32[1,136,128]{2,1,0:T(8,128)S(1)}, u32[]{:S(2)}, u32[]{:S(2)}) collective-permute-start(s32[1,136,128]{2,1,0:T(8,128)S(1)} %get-tuple-element.46), channel_id=1, source_target_pairs={{0,12},{1,13},{2,14},{3,15},{4,8},{5,9},{6,10},{7,11},{8,4},{9,5},... | collective-permute-start | bytes 208904 | tf_op jit(solution)/shard_map/ppermute | solution.py:43
  72.9 6.5 %collective-permute-start.15 = (s32[4,136,128]{2,1,0:T(8,128)S(1)}, s32[4,136,128]{2,1,0:T(8,128)S(1)}, u32[]{:S(2)}, u32[]{:S(2)}) collective-permute-start(s32[4,136,128]{2,1,0:T(8,128)S(1)} %constant_dynamic-update-slice_fusion.refs_0_), channel_id=1, source_target_pairs={{0,1},{1,0},{2,3},{3,2},{4,5},{5,4},{6,7},{7,6},{8,9},{9,8},{10,11... | collective-permute-start | bytes 835592 | tf_op jit(solution)/shard_map/ppermute | solution.py:43
  74.0 9.5 %collective-permute-start.16 = (s32[4,136,128]{2,1,0:T(8,128)S(1)}, s32[4,136,128]{2,1,0:T(8,128)S(1)}, u32[]{:S(2)}, u32[]{:S(2)}) collective-permute-start(s32[4,136,128]{2,1,0:T(8,128)S(1)} %constant_dynamic-update-slice_fusion.refs_0_), channel_id=1, source_target_pairs={{0,2},{1,3},{2,0},{3,1},{4,6},{5,7},{6,4},{7,5},{8,10},{9,11},{10,... | collective-permute-start | bytes 835592 | tf_op jit(solution)/shard_map/ppermute | solution.py:43
  75.5 8.0 %collective-permute-start.17 = (s32[4,136,128]{2,1,0:T(8,128)S(1)}, s32[4,136,128]{2,1,0:T(8,128)S(1)}, u32[]{:S(2)}, u32[]{:S(2)}) collective-permute-start(s32[4,136,128]{2,1,0:T(8,128)S(1)} %constant_dynamic-update-slice_fusion.refs_0_), channel_id=1, source_target_pairs={{0,3},{1,2},{2,1},{3,0},{4,7},{5,6},{6,5},{7,4},{8,11},{9,10},{10,... | collective-permute-start | bytes 835592 | tf_op jit(solution)/shard_map/ppermute | solution.py:43
  101.4 6.6 %collective-permute-start.18 = (s32[4,136,128]{2,1,0:T(8,128)S(1)}, s32[4,136,128]{2,1,0:T(8,128)S(1)}, u32[]{:S(2)}, u32[]{:S(2)}) collective-permute-start(s32[4,136,128]{2,1,0:T(8,128)S(1)} %get-tuple-element.48), channel_id=1, source_target_pairs={{0,1},{1,0},{2,3},{3,2},{4,5},{5,4},{6,7},{7,6},{8,9},{9,8},{10,11... | collective-permute-start | bytes 835592 | tf_op jit(solution)/shard_map/ppermute | solution.py:43
  102.4 8.1 %collective-permute-start.19 = (s32[4,136,128]{2,1,0:T(8,128)S(1)}, s32[4,136,128]{2,1,0:T(8,128)S(1)}, u32[]{:S(2)}, u32[]{:S(2)}) collective-permute-start(s32[4,136,128]{2,1,0:T(8,128)S(1)} %get-tuple-element.49), channel_id=1, source_target_pairs={{0,2},{1,3},{2,0},{3,1},{4,6},{5,7},{6,4},{7,5},{8,10},{9,11},{10,... | collective-permute-start | bytes 835592 | tf_op jit(solution)/shard_map/ppermute | solution.py:43
  103.5 8.5 %collective-permute-start.20 = (s32[4,136,128]{2,1,0:T(8,128)S(1)}, s32[4,136,128]{2,1,0:T(8,128)S(1)}, u32[]{:S(2)}, u32[]{:S(2)}) collective-permute-start(s32[4,136,128]{2,1,0:T(8,128)S(1)} %get-tuple-element.50), channel_id=1, source_target_pairs={{0,3},{1,2},{2,1},{3,0},{4,7},{5,6},{6,5},{7,4},{8,11},{9,10},{10,... | collective-permute-start | bytes 835592 | tf_op jit(solution)/shard_map/ppermute | solution.py:43
  113.0 5.9 %collective-permute-start.21 = (s32[1,136,128]{2,1,0:T(8,128)S(1)}, s32[1,136,128]{2,1,0:T(8,128)S(1)}, u32[]{:S(2)}, u32[]{:S(2)}) collective-permute-start(s32[1,136,128]{2,1,0:T(8,128)S(1)} %get-tuple-element.52), channel_id=1, source_target_pairs={{0,4},{1,5},{2,6},{3,7},{4,0},{5,1},{6,2},{7,3},{8,12},{9,13},{10,... | collective-permute-start | bytes 208904 | tf_op jit(solution)/shard_map/ppermute | solution.py:43
  113.1 5.8 %collective-permute-start.22 = (s32[1,136,128]{2,1,0:T(8,128)S(1)}, s32[1,136,128]{2,1,0:T(8,128)S(1)}, u32[]{:S(2)}, u32[]{:S(2)}) collective-permute-start(s32[1,136,128]{2,1,0:T(8,128)S(1)} %get-tuple-element.53), channel_id=1, source_target_pairs={{0,8},{1,9},{2,10},{3,11},{4,12},{5,13},{6,14},{7,15},{8,0},{9,1},... | collective-permute-start | bytes 208904 | tf_op jit(solution)/shard_map/ppermute | solution.py:43
  115.6 6.1 %collective-permute-start.23 = (s32[1,136,128]{2,1,0:T(8,128)S(1)}, s32[1,136,128]{2,1,0:T(8,128)S(1)}, u32[]{:S(2)}, u32[]{:S(2)}) collective-permute-start(s32[1,136,128]{2,1,0:T(8,128)S(1)} %get-tuple-element.54), channel_id=1, source_target_pairs={{0,12},{1,13},{2,14},{3,15},{4,8},{5,9},{6,10},{7,11},{8,4},{9,5},... | collective-permute-start | bytes 208904 | tf_op jit(solution)/shard_map/ppermute | solution.py:43
  122.3 4.5 %collective-permute-start.24 = (s32[1,136,128]{2,1,0:T(8,128)S(1)}, s32[1,136,128]{2,1,0:T(8,128)S(1)}, u32[]{:S(2)}, u32[]{:S(2)}) collective-permute-start(s32[1,136,128]{2,1,0:T(8,128)S(1)} %get-tuple-element.55), channel_id=1, source_target_pairs={{0,4},{1,5},{2,6},{3,7},{4,0},{5,1},{6,2},{7,3},{8,12},{9,13},{10,... | collective-permute-start | bytes 208904 | tf_op jit(solution)/shard_map/ppermute | solution.py:43
  122.4 5.3 %collective-permute-start.25 = (s32[1,136,128]{2,1,0:T(8,128)S(1)}, s32[1,136,128]{2,1,0:T(8,128)S(1)}, u32[]{:S(2)}, u32[]{:S(2)}) collective-permute-start(s32[1,136,128]{2,1,0:T(8,128)S(1)} %get-tuple-element.55), channel_id=1, source_target_pairs={{0,8},{1,9},{2,10},{3,11},{4,12},{5,13},{6,14},{7,15},{8,0},{9,1},... | collective-permute-start | bytes 208904 | tf_op jit(solution)/shard_map/ppermute | solution.py:43
  124.8 6.1 %collective-permute-start.26 = (s32[1,136,128]{2,1,0:T(8,128)S(1)}, s32[1,136,128]{2,1,0:T(8,128)S(1)}, u32[]{:S(2)}, u32[]{:S(2)}) collective-permute-start(s32[1,136,128]{2,1,0:T(8,128)S(1)} %get-tuple-element.55), channel_id=1, source_target_pairs={{0,12},{1,13},{2,14},{3,15},{4,8},{5,9},{6,10},{7,11},{8,4},{9,5},... | collective-permute-start | bytes 208904 | tf_op jit(solution)/shard_map/ppermute | solution.py:43
  130.9 7.2 %collective-permute-start.27 = (s32[4,136,128]{2,1,0:T(8,128)S(1)}, s32[4,136,128]{2,1,0:T(8,128)S(1)}, u32[]{:S(2)}, u32[]{:S(2)}) collective-permute-start(s32[4,136,128]{2,1,0:T(8,128)S(1)} %constant_dynamic-update-slice_fusion.4.refs_0_), channel_id=1, source_target_pairs={{0,1},{1,0},{2,3},{3,2},{4,5},{5,4},{6,7},{7,6},{8,9},{9,8},{10,11... | collective-permute-start | bytes 835592 | tf_op jit(solution)/shard_map/ppermute | solution.py:43
  132.0 10.3 %collective-permute-start.28 = (s32[4,136,128]{2,1,0:T(8,128)S(1)}, s32[4,136,128]{2,1,0:T(8,128)S(1)}, u32[]{:S(2)}, u32[]{:S(2)}) collective-permute-start(s32[4,136,128]{2,1,0:T(8,128)S(1)} %constant_dynamic-update-slice_fusion.4.refs_0_), channel_id=1, source_target_pairs={{0,2},{1,3},{2,0},{3,1},{4,6},{5,7},{6,4},{7,5},{8,10},{9,11},{10,... | collective-permute-start | bytes 835592 | tf_op jit(solution)/shard_map/ppermute | solution.py:43
  133.5 8.8 %collective-permute-start.29 = (s32[4,136,128]{2,1,0:T(8,128)S(1)}, s32[4,136,128]{2,1,0:T(8,128)S(1)}, u32[]{:S(2)}, u32[]{:S(2)}) collective-permute-start(s32[4,136,128]{2,1,0:T(8,128)S(1)} %constant_dynamic-update-slice_fusion.4.refs_0_), channel_id=1, source_target_pairs={{0,3},{1,2},{2,1},{3,0},{4,7},{5,6},{6,5},{7,4},{8,11},{9,10},{10,... | collective-permute-start | bytes 835592 | tf_op jit(solution)/shard_map/ppermute | solution.py:43
  147.6 6.6 %collective-permute-start.30 = (f32[72,128]{1,0:T(8,128)S(1)}, f32[72,128]{1,0:T(8,128)S(1)}, u32[]{:S(2)}, u32[]{:S(2)}) collective-permute-start(f32[72,128]{1,0:T(8,128)S(1)} %get-tuple-element.57), channel_id=1, source_target_pairs={{0,1},{1,0},{2,3},{3,2},{4,5},{5,4},{6,7},{7,6},{8,9},{9,8},{10,11... | collective-permute-start | bytes 110600 | tf_op jit(solution)/shard_map/ppermute | solution.py:43
  148.6 5.6 %collective-permute-start.31 = (f32[72,128]{1,0:T(8,128)S(1)}, f32[72,128]{1,0:T(8,128)S(1)}, u32[]{:S(2)}, u32[]{:S(2)}) collective-permute-start(f32[72,128]{1,0:T(8,128)S(1)} %get-tuple-element.58), channel_id=1, source_target_pairs={{0,2},{1,3},{2,0},{3,1},{4,6},{5,7},{6,4},{7,5},{8,10},{9,11},{10,... | collective-permute-start | bytes 110600 | tf_op jit(solution)/shard_map/ppermute | solution.py:43
  149.7 4.9 %collective-permute-start.32 = (f32[72,128]{1,0:T(8,128)S(1)}, f32[72,128]{1,0:T(8,128)S(1)}, u32[]{:S(2)}, u32[]{:S(2)}) collective-permute-start(f32[72,128]{1,0:T(8,128)S(1)} %get-tuple-element.59), channel_id=1, source_target_pairs={{0,3},{1,2},{2,1},{3,0},{4,7},{5,6},{6,5},{7,4},{8,11},{9,10},{10,... | collective-permute-start | bytes 110600 | tf_op jit(solution)/shard_map/ppermute | solution.py:43
  154.6 7.3 %collective-permute-start.33 = (f32[72,128]{1,0:T(8,128)S(1)}, f32[72,128]{1,0:T(8,128)S(1)}, u32[]{:S(2)}, u32[]{:S(2)}) collective-permute-start(f32[72,128]{1,0:T(8,128)S(1)} %add_add_fusion.1), channel_id=1, source_target_pairs={{0,4},{1,5},{2,6},{3,7},{4,0},{5,1},{6,2},{7,3},{8,12},{9,13},{10,... | collective-permute-start | bytes 110600 | tf_op jit(solution)/shard_map/ppermute | solution.py:43
  154.6 7.3 %collective-permute-start.34 = (f32[72,128]{1,0:T(8,128)S(1)}, f32[72,128]{1,0:T(8,128)S(1)}, u32[]{:S(2)}, u32[]{:S(2)}) collective-permute-start(f32[72,128]{1,0:T(8,128)S(1)} %add_add_fusion.1), channel_id=1, source_target_pairs={{0,8},{1,9},{2,10},{3,11},{4,12},{5,13},{6,14},{7,15},{8,0},{9,1},... | collective-permute-start | bytes 110600 | tf_op jit(solution)/shard_map/ppermute | solution.py:43
  156.7 5.8 %collective-permute-start.35 = (f32[72,128]{1,0:T(8,128)S(1)}, f32[72,128]{1,0:T(8,128)S(1)}, u32[]{:S(2)}, u32[]{:S(2)}) collective-permute-start(f32[72,128]{1,0:T(8,128)S(1)} %add_add_fusion.1), channel_id=1, source_target_pairs={{0,12},{1,13},{2,14},{3,15},{4,8},{5,9},{6,10},{7,11},{8,4},{9,5},... | collective-permute-start | bytes 110600 | tf_op jit(solution)/shard_map/ppermute | solution.py:43
  162.4 6.3 %collective-permute-start.36 = (f32[72,128]{1,0:T(8,128)S(1)}, f32[72,128]{1,0:T(8,128)S(1)}, u32[]{:S(2)}, u32[]{:S(2)}) collective-permute-start(f32[72,128]{1,0:T(8,128)S(1)} %add_add_fusion.refs_0_), channel_id=1, source_target_pairs={{0,1},{1,0},{2,3},{3,2},{4,5},{5,4},{6,7},{7,6},{8,9},{9,8},{10,11... | collective-permute-start | bytes 110600 | tf_op jit(solution)/shard_map/ppermute | solution.py:43
  163.8 5.0 %collective-permute-start.37 = (f32[72,128]{1,0:T(8,128)S(1)}, f32[72,128]{1,0:T(8,128)S(1)}, u32[]{:S(2)}, u32[]{:S(2)}) collective-permute-start(f32[72,128]{1,0:T(8,128)S(1)} %add_add_fusion.refs_0_), channel_id=1, source_target_pairs={{0,2},{1,3},{2,0},{3,1},{4,6},{5,7},{6,4},{7,5},{8,10},{9,11},{10,... | collective-permute-start | bytes 110600 | tf_op jit(solution)/shard_map/ppermute | solution.py:43
  164.3 4.9 %collective-permute-start.38 = (f32[72,128]{1,0:T(8,128)S(1)}, f32[72,128]{1,0:T(8,128)S(1)}, u32[]{:S(2)}, u32[]{:S(2)}) collective-permute-start(f32[72,128]{1,0:T(8,128)S(1)} %add_add_fusion.refs_0_), channel_id=1, source_target_pairs={{0,3},{1,2},{2,1},{3,0},{4,7},{5,6},{6,5},{7,4},{8,11},{9,10},{10,... | collective-permute-start | bytes 110600 | tf_op jit(solution)/shard_map/ppermute | solution.py:43
  170.4 1.2 collective-permute-start.39

commit v5 on v4

--- a/solution.py
+++ b/solution.py
@@ -15,7 +15,8 @@
 CODES = 128
 STEPS = 65535.0
 LEAST = 2.0**-90
-VMEM_LIMIT = 40 * 1024 * 1024
+VMEM_LIMIT = 32 * 1024 * 1024
+VMEM_SMALL = 8 * 1024 * 1024
 HIGHEST = lax.Precision.HIGHEST
 FACTOR_COST = pl.CostEstimate(flops=4_000_000_000, bytes_accessed=4 << 20, transcendentals=0)
 
@@ -55,10 +56,31 @@
     return keep, sends[0] if packed else keep
 
 
+def stack_kernel(*refs):
+    first = 0
+    for ref in refs[:-1]:
+        refs[-1][first : first + ref.shape[0]] = ref[...]
+        first += ref.shape[0]
+
+
+def stack(parts):
+    if parts[0].dtype != jnp.int32:
+        return jnp.concatenate(parts, axis=0)
+    vmem = pl.BlockSpec(memory_space=pltpu.VMEM)
+    shape = (len(parts) * parts[0].shape[0],) + parts[0].shape[1:]
+    return pl.pallas_call(
+        stack_kernel,
+        in_specs=[vmem] * len(parts),
+        out_specs=vmem,
+        out_shape=jax.ShapeDtypeStruct(shape, parts[0].dtype),
+        compiler_params=pltpu.CompilerParams(vmem_limit_bytes=VMEM_SMALL),
+    )(*parts)
+
+
 def gather_chunks(message, groups):
     stages = stage_bits(groups)
     for bits in reversed(stages[1:]):
-        message = jnp.concatenate([message] + [exchange(message, groups, span) for span in offsets(bits)[1:]], axis=0)
+        message = stack([message] + [exchange(message, groups, span) for span in offsets(bits)[1:]])
     return [message] + [exchange(message, groups, span) for span in offsets(stages[0])[1:]]
 
 
@@ -217,7 +239,7 @@
         in_specs=[vmem] * (1 + len(arrived)),
         out_specs=[vmem] * len(outs),
         out_shape=outs,
-        compiler_params=pltpu.CompilerParams(vmem_limit_bytes=VMEM_LIMIT),
+        compiler_params=pltpu.CompilerParams(vmem_limit_bytes=VMEM_SMALL),
     )(keep, *arrived)
 
 
@@ -230,6 +252,25 @@
         if piece + 1 < pieces:
             rest = rest - part.astype(jnp.float32)
     return parts
+
+
+def hold_kernel(after_ref, rows_ref, out_ref, sem):
+    copy = pltpu.make_async_copy(rows_ref, out_ref, sem)
+    copy.start()
+    copy.wait()
+
+
+def hold(genotypes, after):
+    anywhere = pl.BlockSpec(memory_space=pl.ANY)
+    return pl.pallas_call(
+        hold_kernel,
+        in_specs=[anywhere, anywhere],
+        out_specs=pl.BlockSpec(memory_space=pltpu.VMEM),
+        out_shape=jax.ShapeDtypeStruct(genotypes.shape, genotypes.dtype),
+        scratch_shapes=[pltpu.SemaphoreType.DMA],
+        compiler_params=pltpu.CompilerParams(vmem_limit_bytes=VMEM_SMALL),
+        cost_estimate=FACTOR_COST,
+    )(after, genotypes)
 
 
 def load_all(order, place_ref, refs, full_ref):
@@ -246,10 +287,8 @@
 
 
 def apply_kernel(order, normalise, scale, sources, place_ref, size_ref, rows_ref, *refs):
-    refs, outs, (full_ref, work_ref, held_ref, sem) = refs[:sources], refs[sources:-4], refs[-4:]
+    refs, outs, (full_ref, work_ref) = refs[:sources], refs[sources:-2], refs[-2:]
     size, cap = full_ref.shape
-    copy = pltpu.make_async_copy(rows_ref, held_ref, sem)
-    copy.start()
     load_all(order, place_ref, refs, full_ref)
     value = full_ref[...]
     if normalise:
@@ -257,11 +296,10 @@
         inverse_factor(work_ref, size, PANEL)
         value = jnp.dot(finish_factor(work_ref), value, precision=HIGHEST, preferred_element_type=jnp.float32)
     split = jnp.concatenate(split_pieces(value, PIECES), axis=0)
-    copy.wait()
-    image = rows_dot(split, held_ref[...])
+    image = rows_dot(split, rows_ref[...])
     image = sum(image[piece * size : (piece + 1) * size] for piece in range(PIECES)) * scale
     split = jnp.concatenate(split_pieces(image, PIECES), axis=0)
-    back = jnp.dot(split, held_ref[...], preferred_element_type=jnp.float32)
+    back = jnp.dot(split, rows_ref[...], preferred_element_type=jnp.float32)
     back = sum(back[piece * size : (piece + 1) * size] for piece in range(PIECES))
     live = lax.broadcasted_iota(jnp.int32, (1, cap), 1) < size_ref[0]
     back = jnp.where(live, back, 0.0)
@@ -293,14 +331,12 @@
     scalar, vmem = pl.BlockSpec(memory_space=pltpu.SMEM), pl.BlockSpec(memory_space=pltpu.VMEM)
     return pl.pallas_call(
         functools.partial(apply_kernel, order, normalise, scale, len(gathered)),
-        in_specs=[scalar, scalar, pl.BlockSpec(memory_space=pl.ANY)] + [vmem] * len(gathered),
+        in_specs=[scalar, scalar, vmem] + [vmem] * len(gathered),
         out_specs=[vmem] * len(outs),
         out_shape=outs,
         scratch_shapes=[
             pltpu.VMEM((size, cap), jnp.float32),
             pltpu.VMEM((size, 2 * size), jnp.float32),
-            pltpu.VMEM((samples, cap), jnp.bfloat16),
-            pltpu.SemaphoreType.DMA,
         ],
         compiler_params=pltpu.CompilerParams(vmem_limit_bytes=VMEM_LIMIT),
     )(place, sizes, genotypes, *gathered)
@@ -427,16 +463,13 @@
 
 
 def project_kernel(order, sources, quarter_ref, place_ref, rows_ref, *refs):
-    refs, (inner_ref, *outs), (full_ref, folded_ref, held_ref, sem) = refs[:sources], refs[sources:-4], refs[-4:]
+    refs, (inner_ref, *outs), (full_ref, folded_ref) = refs[:sources], refs[sources:-2], refs[-2:]
     size = full_ref.shape[0]
-    copy = pltpu.make_async_copy(rows_ref, held_ref, sem)
-    copy.start()
     load_all(order, place_ref, refs, full_ref)
     image = full_ref[...]
     inner_ref[...] = rows_inner(image)
     split = jnp.concatenate(split_pieces(image, PIECES), axis=0)
-    copy.wait()
-    sampled = rows_dot(split, held_ref[...])
+    sampled = rows_dot(split, rows_ref[...])
     sampled = sum(sampled[piece * size : (piece + 1) * size] for piece in range(PIECES))
     high, low = split_pieces(sampled, PIECES)
     mixed = rows_dot(high, low)
@@ -452,67 +485,70 @@
     outs = [(size, size)] + [part] * 4
     return pl.pallas_call(
         functools.partial(project_kernel, order, len(gathered)),
-        in_specs=[scalar, scalar, pl.BlockSpec(memory_space=pl.ANY)] + [vmem] * len(gathered),
+        in_specs=[scalar, scalar, vmem] + [vmem] * len(gathered),
         out_specs=[vmem] * len(outs),
         out_shape=[jax.ShapeDtypeStruct(shape, jnp.float32) for shape in outs],
         scratch_shapes=[
             pltpu.VMEM((size, cap), jnp.float32),
             pltpu.VMEM((4,) + part, jnp.float32),
-            pltpu.VMEM((samples, cap), jnp.bfloat16),
-            pltpu.SemaphoreType.DMA,
         ],
         compiler_params=pltpu.CompilerParams(vmem_limit_bytes=VMEM_LIMIT),
     )(quarter, place, genotypes, *gathered)
 
 
-def second_kernel(gain, first, last, *refs):
-    (source_ref, *own_ref), (work_ref, *basis_ref) = refs[: len(refs) // 2], refs[len(refs) // 2 :]
+def second_kernel(first, last, source_ref, work_ref):
     if first == 0:
         start_factor(work_ref, source_ref[...])
     else:
         work_ref[...] = source_ref[...]
     inverse_factor(work_ref, work_ref.shape[0], PANEL, first, last)
-    if own_ref:
-        factor = finish_factor(work_ref)
-        own = jnp.dot(factor, own_ref[0][...], precision=HIGHEST, preferred_element_type=jnp.float32)
-        basis_ref[0][...] = own.T * gain
-
-
-def second_factor(source, first, last, own=None, gain=1.0):
+
+
+def second_factor(source, first, last):
     size = source.shape[0]
     vmem = pl.BlockSpec(memory_space=pltpu.VMEM)
-    shapes = [(size, 2 * size)] + ([] if own is None else [own.shape[::-1]])
-    outs = pl.pallas_call(
-        functools.partial(second_kernel, gain, first, last),
-        in_specs=[vmem] * len(shapes),
-        out_specs=[vmem] * len(shapes),
-        out_shape=[jax.ShapeDtypeStruct(shape, jnp.float32) for shape in shapes],
+    return pl.pallas_call(
+        functools.partial(second_kernel, first, last),
+        in_specs=[vmem],
+        out_specs=vmem,
+        out_shape=jax.ShapeDtypeStruct((size, 2 * size), jnp.float32),
         compiler_params=pltpu.CompilerParams(vmem_limit_bytes=VMEM_LIMIT),
         cost_estimate=FACTOR_COST,
-    )(source, *([] if own is None else [own]))
-    return outs[0] if own is None else outs
-
-
-def finish_kernel(scale, quarter_ref, factor_ref, *refs):
-    parts, (out_ref, trace_ref, folded_ref) = refs[:4], refs[4:]
+    )(source)
+
+
+def basis_kernel(gain, factor_ref, own_ref, out_ref):
+    own = jnp.dot(finish_factor(factor_ref), own_ref[...], precision=HIGHEST, preferred_element_type=jnp.float32)
+    out_ref[...] = own.T * gain
+
+
+def basis_rows(factor, own, gain):
+    vmem = pl.BlockSpec(memory_space=pltpu.VMEM)
+    return pl.pallas_call(
+        functools.partial(basis_kernel, gain),
+        in_specs=[vmem] * 2,
+        out_specs=vmem,
+        out_shape=jax.ShapeDtypeStruct(own.shape[::-1], jnp.float32),
+        compiler_params=pltpu.CompilerParams(vmem_limit_bytes=VMEM_SMALL),
+        cost_estimate=pl.CostEstimate(flops=1_000_000_000, bytes_accessed=1 << 20, transcendentals=0),
+    )(factor, own)
+
+
+def trace_kernel(scale, quarter_ref, factor_ref, *refs):
+    parts, (half_ref, trace_ref, folded_ref) = refs[:4], refs[4:]
     for offset in range(4):
         folded_ref[jnp.bitwise_xor(quarter_ref[0], offset)] = parts[offset][...]
     cross = unfold_symmetric([folded_ref[place] for place in range(4)])
     factor = finish_factor(factor_ref)
-    half = jnp.dot(factor, cross, precision=HIGHEST, preferred_element_type=jnp.float32)
-    result = scale * lax.dot_general(
-        half, factor, (((1,), (1,)), ((), ())), precision=HIGHEST, preferred_element_type=jnp.float32
-    )
-    out_ref[...] = result
-    row = lax.broadcasted_iota(jnp.int32, result.shape, 0)
-    column = lax.broadcasted_iota(jnp.int32, result.shape, 1)
-    trace_ref[...] = jnp.broadcast_to(jnp.sum(jnp.where(row == column, result, 0.0)), trace_ref.shape)
-
-
-def finish(quarter, factor, parts, scale):
+    half = scale * jnp.dot(factor, cross, precision=HIGHEST, preferred_element_type=jnp.float32)
+    half_ref[...] = half
+    trace_ref[...] = jnp.broadcast_to(jnp.sum(half * factor), trace_ref.shape)
+
+
+def trace_half(quarter, factor, parts, scale):
     vmem = pl.BlockSpec(memory_space=pltpu.VMEM)
     return pl.pallas_call(
-        functools.partial(finish_kernel, scale),
+        functools.partial(trace_kernel, scale),
         in_specs=[pl.BlockSpec(memory_space=pltpu.SMEM)] + [vmem] * 5,
         out_specs=[vmem] * 2,
         out_shape=[
@@ -520,8 +556,32 @@
             jax.ShapeDtypeStruct((SUBLANES, LANES), jnp.float32),
         ],
         scratch_shapes=[pltpu.VMEM((4,) + parts[0].shape, jnp.float32)],
-        compiler_params=pltpu.CompilerParams(vmem_limit_bytes=VMEM_LIMIT),
+        compiler_params=pltpu.CompilerParams(vmem_limit_bytes=VMEM_SMALL),
     )(quarter, factor, *parts)
+
+
+def finish_kernel(gain, half_ref, factor_ref, *refs):
+    traces, out_ref = refs[:-1], refs[-1]
+    total = sum(trace[:1, :1] for trace in traces)
+    whole = lax.dot_general(
+        half_ref[...],
+        finish_factor(factor_ref),
+        (((1,), (1,)), ((), ())),
+        precision=HIGHEST,
+        preferred_element_type=jnp.float32,
+    )
+    out_ref[...] = whole * (gain / total)
+
+
+def finish(half, factor, traces, gain):
+    vmem = pl.BlockSpec(memory_space=pltpu.VMEM)
+    return pl.pallas_call(
+        functools.partial(finish_kernel, gain),
+        in_specs=[vmem] * (2 + len(traces)),
+        out_specs=vmem,
+        out_shape=jax.ShapeDtypeStruct(half.shape, jnp.float32),
+        compiler_params=pltpu.CompilerParams(vmem_limit_bytes=VMEM_SMALL),
+    )(half, factor, *traces)
 
 
 def to_natural(gathered, order, me):
@@ -563,6 +623,7 @@
     else:
         row = me * width + lax.broadcasted_iota(jnp.int32, (width, size), 0)
         message = jnp.where(row < sizes[0], start[0], 0.0).T[None]
+    dosages = hold(dosages, message)
     _, message = apply(message, False)
     own, message = apply(message, True)
     quarter = jnp.bitwise_and(place, 3)
@@ -571,15 +632,17 @@
     beside = [
         lambda _: second_factor(inner, cuts[0], cuts[1]),
         lambda work: second_factor(work, cuts[1], cuts[2]),
-        lambda work: second_factor(work, cuts[2], cuts[3], own[0], math.sqrt(cap)),
+        lambda work: second_factor(work, cuts[2], cuts[3]),
     ]
-    quarters, (second, basis) = sum_quarters(quarters, groups, beside)
-    rayleigh, trace = finish(quarter, second, quarters, scale)
+    quarters, second = sum_quarters(quarters, groups, beside)
+    halfway, trace = trace_half(quarter, second, quarters, scale)
     blocks = lax.axis_size("blk")
-    total = trace
-    for shift in range(1, blocks):
-        total = total + lax.ppermute(trace, "blk", [(block, (block + shift) % blocks) for block in range(blocks)])
-    scaled = rayleigh * (genotypes.shape[0] * blocks * size / total[0, 0])
+    traces = [trace] + [
+        lax.ppermute(trace, "blk", [(block, (block + shift) % blocks) for block in range(blocks)])
+        for shift in range(1, blocks)
+    ]
+    basis = basis_rows(second, own[0], math.sqrt(cap))
+    scaled = finish(halfway, second, traces, float(genotypes.shape[0] * blocks * size))
     return basis[None], scaled[None]
 
 

time: 174 us -> 169 us (0.971)
  waiting for transfers between devices: 68.8 us -> 66.2 us
    pallas_call x4 -> x10, Pallas kernels: 9.88 us -> 10.8 us  [the longest x3 7.64 us: second_factor(): pl.pallas_call(functools.partial(second_kernel, first, last), in_specs=[v...]
  transfers between devices with their start and end apart: 40 -> 40, of which waited for: 25 -> 26; matrix products, arithmetic and copies ran while one was open for 0% -> 0% of each run, Pallas kernels for 5% -> 5%
where the time goes in v5:
time: 169 us
  waiting for transfers between devices  66.2 us (39%)
  starting transfers between devices  52.3 us (31%)
  Pallas kernels  45.4 us (27%)
  local copies, waits for them, and re-layouts  3.07 us (2%)
    ppermute x39, waiting for transfers between devices, exchange(): lax.ppermute(value, 'smp', [(device, device ^ offset) for device in range...  66.2 us
    ppermute x39, starting transfers between devices, exchange(): lax.ppermute(value, 'smp', [(device, device ^ offset) for device in range...  52.3 us
    pallas_call x2, Pallas kernels, apply_samples(): pl.pallas_call(functools.partial(apply_kernel, order, normalise, scale, l...  24 us
    pallas_call x3, Pallas kernels, second_factor(): pl.pallas_call(functools.partial(second_kernel, first, last), in_specs=[v...  7.64 us
    pallas_call x1, Pallas kernels, project(): pl.pallas_call(functools.partial(project_kernel, order, len(gathered)), i...  4.97 us
    pallas_call x4, Pallas kernels, combine(): pl.pallas_call(functools.partial(combine_kernel, len(arrived), parts), in...  3.71 us
  transfers between devices with their start and end apart: 40, of which 26 were waited for; matrix products, arithmetic and copies ran while one was open for 0% of the time, Pallas kernels for 5%

profile of v5, /device:TPU:0, one launch (start us, length us, event | category | flops | bytes accessed | tf_op | source)
XLA Modules:
  0.0 168.5 jit_solution(13363317796581131706)
XLA Ops:
  1.3 1.9 %shard_map.50.after_ref.refs_0_ = s32[1,136,128]{2,1,0:T(8,128)} custom-call(s32[1]{0:T(128)} %bitcast.place_ref, s32[1]{0:T(128)S(6)} %copy.5.size_ref, f32[128,256]{1,0:T(8,128)} %bitcast.9), custom_call_target="tpu_custom_call" | custom-call | tf_op jit(solution)/shard_map/pallas_call | solution.py:205
  3.2 3.0 %collective-permute-start = (s32[1,136,128]{2,1,0:T(8,128)}, s32[1,136,128]{2,1,0:T(8,128)S(1)}, u32[]{:S(2)}, u32[]{:S(2)}) collective-permute-start(s32[1,136,128]{2,1,0:T(8,128)} %shard_map.50.after_ref.refs_0_), channel_id=1, source_target_pairs={{0,4},{1,5},{2,6},{3,7},{4,0},{5,1},{6,2},{7,3},{8,12},{9,13},{10,... | collective-permute-start | bytes 208904 | tf_op jit(solution)/shard_map/ppermute | solution.py:44
  6.2 2.6 %collective-permute-start.1 = (s32[1,136,128]{2,1,0:T(8,128)}, s32[1,136,128]{2,1,0:T(8,128)S(1)}, u32[]{:S(2)}, u32[]{:S(2)}) collective-permute-start(s32[1,136,128]{2,1,0:T(8,128)} %shard_map.50.after_ref.refs_0_), channel_id=1, source_target_pairs={{0,8},{1,9},{2,10},{3,11},{4,12},{5,13},{6,14},{7,15},{8,0},{9,1},... | collective-permute-start | bytes 208904 | tf_op jit(solution)/shard_map/ppermute | solution.py:44
  8.8 5.2 %collective-permute-done.1.refs_2_ = s32[1,136,128]{2,1,0:T(8,128)S(1)} collective-permute-done((s32[1,136,128]{2,1,0:T(8,128)}, s32[1,136,128]{2,1,0:T(8,128)S(1)}, u32[]{:S(2)}, u32[]{:S(2)}) %collective-permute-start.1) | collective-permute-done | bytes 69664 | tf_op jit(solution)/shard_map/ppermute | solution.py:44
  16.1 1.6 collective-permute-start.3
  17.7 1.5 collective-permute-start.4
  19.7 2.2 %copy-done.1 = bf16[1,1024,2048]{2,1,0:T(8,128)(2,1)S(1)} copy-done((bf16[1,1024,2048]{2,1,0:T(8,128)(2,1)S(1)}, bf16[1,1024,2048]{2,1,0:T(8,128)(2,1)}, u32[]{:S(2)}) %copy-start.1) | copy-done | bytes 4194328
  22.2 3.6 %collective-permute-done.3.refs_1_ = s32[4,136,128]{2,1,0:T(8,128)S(1)} collective-permute-done((s32[4,136,128]{2,1,0:T(8,128)S(1)}, s32[4,136,128]{2,1,0:T(8,128)S(1)}, u32[]{:S(2)}, u32[]{:S(2)}) %collective-permute-start.3) | collective-permute-done | bytes 278560 | tf_op jit(solution)/shard_map/ppermute | solution.py:44
  25.8 4.2 %collective-permute-done.4.refs_2_ = s32[4,136,128]{2,1,0:T(8,128)S(1)} collective-permute-done((s32[4,136,128]{2,1,0:T(8,128)S(1)}, s32[4,136,128]{2,1,0:T(8,128)S(1)}, u32[]{:S(2)}, u32[]{:S(2)}) %collective-permute-start.4) | collective-permute-done | bytes 278560 | tf_op jit(solution)/shard_map/ppermute | solution.py:44
  30.0 6.6 %shard_map.53 = (f32[4,256,128]{2,1,0:T(8,128)S(1)}, s32[4,136,128]{2,1,0:T(8,128)S(1)}, s32[4,136,128]{2,1,0:T(8,128)S(1)}, s32[4,136,128]{2,1,0:T(8,128)S(1)}) custom-call(s32[1]{0:T(128)} %bitcast.place_ref, s32[1]{0:T(128)S(6)} %copy.5.size_ref, bf16[1024,2048]{1,0:T(8,128)(2,1)S(1)} %shard_map.51.rows_ref, s32[4,136,128]{2,1,0:T(8,128)S(1)} %shard_map.52.refs_0_, ...), custom_call_target="tpu_custom_call" | custom-call | tf_op jit(solution)/shard_map/pallas_call | solution.py:332
  38.7 1.4 collective-permute-start.8
  40.2 4.6 %collective-permute-done.6.refs_0_ = s32[4,136,128]{2,1,0:T(8,128)S(1)} collective-permute-done((s32[4,136,128]{2,1,0:T(8,128)S(1)}, s32[4,136,128]{2,1,0:T(8,128)S(1)}, u32[]{:S(2)}, u32[]{:S(2)}) %collective-permute-start.6) | collective-permute-done | bytes 278560 | tf_op jit(solution)/shard_map/ppermute | solution.py:44
  44.8 4.1 %collective-permute-done.7.refs_1_ = s32[4,136,128]{2,1,0:T(8,128)S(1)} collective-permute-done((s32[4,136,128]{2,1,0:T(8,128)S(1)}, s32[4,136,128]{2,1,0:T(8,128)S(1)}, u32[]{:S(2)}, u32[]{:S(2)}) %collective-permute-start.7) | collective-permute-done | bytes 278560 | tf_op jit(solution)/shard_map/ppermute | solution.py:44
  50.0 3.4 %collective-permute-start.10 = (s32[1,136,128]{2,1,0:T(8,128)S(1)}, s32[1,136,128]{2,1,0:T(8,128)S(1)}, u32[]{:S(2)}, u32[]{:S(2)}) collective-permute-start(s32[1,136,128]{2,1,0:T(8,128)S(1)} %get-tuple-element.42), channel_id=1, source_target_pairs={{0,8},{1,9},{2,10},{3,11},{4,12},{5,13},{6,14},{7,15},{8,0},{9,1},... | collective-permute-start | bytes 208904 | tf_op jit(solution)/shard_map/ppermute | solution.py:44
  54.1 2.4 %collective-permute-done.10.refs_1_ = s32[1,136,128]{2,1,0:T(8,128)S(1)} collective-permute-done((s32[1,136,128]{2,1,0:T(8,128)S(1)}, s32[1,136,128]{2,1,0:T(8,128)S(1)}, u32[]{:S(2)}, u32[]{:S(2)}) %collective-permute-start.10) | collective-permute-done | bytes 69664 | tf_op jit(solution)/shard_map/ppermute | solution.py:44
  56.5 3.8 %collective-permute-done.11.refs_2_ = s32[1,136,128]{2,1,0:T(8,128)S(1)} collective-permute-done((s32[1,136,128]{2,1,0:T(8,128)S(1)}, s32[1,136,128]{2,1,0:T(8,128)S(1)}, u32[]{:S(2)}, u32[]{:S(2)}) %collective-permute-start.11) | collective-permute-done | bytes 69664 | tf_op jit(solution)/shard_map/ppermute | solution.py:44
  61.7 2.1 %collective-permute-start.13 = (s32[1,136,128]{2,1,0:T(8,128)S(1)}, s32[1,136,128]{2,1,0:T(8,128)S(1)}, u32[]{:S(2)}, u32[]{:S(2)}) collective-permute-start(s32[1,136,128]{2,1,0:T(8,128)S(1)} %get-tuple-element.44.refs_0_), channel_id=1, source_target_pairs={{0,8},{1,9},{2,10},{3,11},{4,12},{5,13},{6,14},{7,15},{8,0},{9,1},... | collective-permute-start | bytes 208904 | tf_op jit(solution)/shard_map/ppermute | solution.py:44
  63.8 1.8 %collective-permute-start.14 = (s32[1,136,128]{2,1,0:T(8,128)S(1)}, s32[1,136,128]{2,1,0:T(8,128)S(1)}, u32[]{:S(2)}, u32[]{:S(2)}) collective-permute-start(s32[1,136,128]{2,1,0:T(8,128)S(1)} %get-tuple-element.44.refs_0_), channel_id=1, source_target_pairs={{0,12},{1,13},{2,14},{3,15},{4,8},{5,9},{6,10},{7,11},{8,4},{9,5},... | collective-permute-start | bytes 208904 | tf_op jit(solution)/shard_map/ppermute | solution.py:44
  66.9 3.0 %collective-permute-done.14.refs_3_ = s32[1,136,128]{2,1,0:T(8,128)S(1)} collective-permute-done((s32[1,136,128]{2,1,0:T(8,128)S(1)}, s32[1,136,128]{2,1,0:T(8,128)S(1)}, u32[]{:S(2)}, u32[]{:S(2)}) %collective-permute-start.14) | collective-permute-done | bytes 69664 | tf_op jit(solution)/shard_map/ppermute | solution.py:44
  71.1 1.5 collective-permute-start.16
  73.5 3.1 %collective-permute-done.15.refs_1_ = s32[4,136,128]{2,1,0:T(8,128)S(1)} collective-permute-done((s32[4,136,128]{2,1,0:T(8,128)S(1)}, s32[4,136,128]{2,1,0:T(8,128)S(1)}, u32[]{:S(2)}, u32[]{:S(2)}) %collective-permute-start.15) | collective-permute-done | bytes 278560 | tf_op jit(solution)/shard_map/ppermute | solution.py:44
  76.5 4.1 %collective-permute-done.16.refs_2_ = s32[4,136,128]{2,1,0:T(8,128)S(1)} collective-permute-done((s32[4,136,128]{2,1,0:T(8,128)S(1)}, s32[4,136,128]{2,1,0:T(8,128)S(1)}, u32[]{:S(2)}, u32[]{:S(2)}) %collective-permute-start.16) | collective-permute-done | bytes 278560 | tf_op jit(solution)/shard_map/ppermute | solution.py:44
  80.6 17.4 %shard_map.57 = (f32[4,256,128]{2,1,0:T(8,128)S(1)}, s32[4,136,128]{2,1,0:T(8,128)S(1)}, s32[4,136,128]{2,1,0:T(8,128)S(1)}, s32[4,136,128]{2,1,0:T(8,128)S(1)}) custom-call(s32[1]{0:T(128)} %bitcast.place_ref, s32[1]{0:T(128)S(6)} %copy.5.size_ref, bf16[1024,2048]{1,0:T(8,128)(2,1)S(1)} %shard_map.51.rows_ref, s32[4,136,128]{2,1,0:T(8,128)S(1)} %shard_map.56.refs_0_, ...), custom_call_target="tpu_custom_call" | custom-call | tf_op jit(solution)/shard_map/pallas_call | solution.py:332
  100.1 1.5 collective-permute-start.20
  101.6 3.1 %collective-permute-done.18.refs_0_ = s32[4,136,128]{2,1,0:T(8,128)S(1)} collective-permute-done((s32[4,136,128]{2,1,0:T(8,128)S(1)}, s32[4,136,128]{2,1,0:T(8,128)S(1)}, u32[]{:S(2)}, u32[]{:S(2)}) %collective-permute-start.18) | collective-permute-done | bytes 278560 | tf_op jit(solution)/shard_map/ppermute | solution.py:44
  104.6 2.5 %collective-permute-done.19.refs_1_ = s32[4,136,128]{2,1,0:T(8,128)S(1)} collective-permute-done((s32[4,136,128]{2,1,0:T(8,128)S(1)}, s32[4,136,128]{2,1,0:T(8,128)S(1)}, u32[]{:S(2)}, u32[]{:S(2)}) %collective-permute-start.19) | collective-permute-done | bytes 278560 | tf_op jit(solution)/shard_map/ppermute | solution.py:44
  107.1 1.4 collective-permute-done.20.refs_2_
  109.7 2.5 %collective-permute-start.22 = (s32[1,136,128]{2,1,0:T(8,128)S(1)}, s32[1,136,128]{2,1,0:T(8,128)S(1)}, u32[]{:S(2)}, u32[]{:S(2)}) collective-permute-start(s32[1,136,128]{2,1,0:T(8,128)S(1)} %get-tuple-element.51), channel_id=1, source_target_pairs={{0,8},{1,9},{2,10},{3,11},{4,12},{5,13},{6,14},{7,15},{8,0},{9,1},... | collective-permute-start | bytes 208904 | tf_op jit(solution)/shard_map/ppermute | solution.py:44
  112.2 1.9 %collective-permute-start.23 = (s32[1,136,128]{2,1,0:T(8,128)S(1)}, s32[1,136,128]{2,1,0:T(8,128)S(1)}, u32[]{:S(2)}, u32[]{:S(2)}) collective-permute-start(s32[1,136,128]{2,1,0:T(8,128)S(1)} %get-tuple-element.52), channel_id=1, source_target_pairs={{0,12},{1,13},{2,14},{3,15},{4,8},{5,9},{6,10},{7,11},{8,4},{9,5},... | collective-permute-start | bytes 208904 | tf_op jit(solution)/shard_map/ppermute | solution.py:44
  114.1 1.4 collective-permute-done.21.refs_0_
  115.5 2.8 %collective-permute-done.23.refs_2_ = s32[1,136,128]{2,1,0:T(8,128)S(1)} collective-permute-done((s32[1,136,128]{2,1,0:T(8,128)S(1)}, s32[1,136,128]{2,1,0:T(8,128)S(1)}, u32[]{:S(2)}, u32[]{:S(2)}) %collective-permute-start.23) | collective-permute-done | bytes 69664 | tf_op jit(solution)/shard_map/ppermute | solution.py:44
  119.0 2.5 %collective-permute-start.25 = (s32[1,136,128]{2,1,0:T(8,128)S(1)}, s32[1,136,128]{2,1,0:T(8,128)S(1)}, u32[]{:S(2)}, u32[]{:S(2)}) collective-permute-start(s32[1,136,128]{2,1,0:T(8,128)S(1)} %get-tuple-element.53.refs_0_), channel_id=1, source_target_pairs={{0,8},{1,9},{2,10},{3,11},{4,12},{5,13},{6,14},{7,15},{8,0},{9,1},... | collective-permute-start | bytes 208904 | tf_op jit(solution)/shard_map/ppermute | solution.py:44
  121.4 1.9 %collective-permute-start.26 = (s32[1,136,128]{2,1,0:T(8,128)S(1)}, s32[1,136,128]{2,1,0:T(8,128)S(1)}, u32[]{:S(2)}, u32[]{:S(2)}) collective-permute-start(s32[1,136,128]{2,1,0:T(8,128)S(1)} %get-tuple-element.53.refs_0_), channel_id=1, source_target_pairs={{0,12},{1,13},{2,14},{3,15},{4,8},{5,9},{6,10},{7,11},{8,4},{9,5},... | collective-permute-start | bytes 208904 | tf_op jit(solution)/shard_map/ppermute | solution.py:44
  124.3 3.3 %collective-permute-done.26.refs_3_ = s32[1,136,128]{2,1,0:T(8,128)S(1)} collective-permute-done((s32[1,136,128]{2,1,0:T(8,128)S(1)}, s32[1,136,128]{2,1,0:T(8,128)S(1)}, u32[]{:S(2)}, u32[]{:S(2)}) %collective-permute-start.26) | collective-permute-done | bytes 69664 | tf_op jit(solution)/shard_map/ppermute | solution.py:44
  128.7 1.5 collective-permute-start.28
  131.1 3.6 %collective-permute-done.27.refs_1_ = s32[4,136,128]{2,1,0:T(8,128)S(1)} collective-permute-done((s32[4,136,128]{2,1,0:T(8,128)S(1)}, s32[4,136,128]{2,1,0:T(8,128)S(1)}, u32[]{:S(2)}, u32[]{:S(2)}) %collective-permute-start.27) | collective-permute-done | bytes 278560 | tf_op jit(solution)/shard_map/ppermute | solution.py:44
  134.7 4.2 %collective-permute-done.28.refs_2_ = s32[4,136,128]{2,1,0:T(8,128)S(1)} collective-permute-done((s32[4,136,128]{2,1,0:T(8,128)S(1)}, s32[4,136,128]{2,1,0:T(8,128)S(1)}, u32[]{:S(2)}, u32[]{:S(2)}) %collective-permute-start.28) | collective-permute-done | bytes 278560 | tf_op jit(solution)/shard_map/ppermute | solution.py:44
  138.9 5.0 %shard_map.61 = (f32[256,256]{1,0:T(8,128)S(1)}, f32[72,128]{1,0:T(8,128)S(1)}, f32[72,128]{1,0:T(8,128)S(1)}, f32[72,128]{1,0:T(8,128)S(1)}, f32[72,128]{1,0:T(8,128)S(1)}) custom-call(s32[1]{0:T(128)S(6)} %and.4.quarter_ref, s32[1]{0:T(128)} %bitcast.place_ref, bf16[1024,2048]{1,0:T(8,128)(2,1)S(1)} %shard_map.51.rows_ref, ...), custom_call_target="tpu_custom_call" | custom-call | tf_op jit(solution)/shard_map/pallas_call | solution.py:486
  144.6 1.4 collective-permute-start.31
  146.1 1.3 collective-permute-start.32
  147.4 3.0 %shard_map.62.source_ref = f32[256,512]{1,0:T(8,128)S(1)} custom-call(f32[256,256]{1,0:T(8,128)S(1)} %get-tuple-element.58.source_ref), custom_call_target="tpu_custom_call" | custom-call | flops 4000000000 | bytes 4194304 | tf_op jit(solution)/shard_map/pallas_call | solution.py:510
  151.0 1.8 %collective-permute-start.34 = (f32[72,128]{1,0:T(8,128)S(1)}, f32[72,128]{1,0:T(8,128)S(1)}, u32[]{:S(2)}, u32[]{:S(2)}) collective-permute-start(f32[72,128]{1,0:T(8,128)S(1)} %add_add_fusion.1), channel_id=1, source_target_pairs={{0,8},{1,9},{2,10},{3,11},{4,12},{5,13},{6,14},{7,15},{8,0},{9,1},... | collective-permute-start | bytes 110600 | tf_op jit(solution)/shard_map/ppermute | solution.py:44
  152.8 2.6 %collective-permute-start.35 = (f32[72,128]{1,0:T(8,128)S(1)}, f32[72,128]{1,0:T(8,128)S(1)}, u32[]{:S(2)}, u32[]{:S(2)}) collective-permute-start(f32[72,128]{1,0:T(8,128)S(1)} %add_add_fusion.1), channel_id=1, source_target_pairs={{0,12},{1,13},{2,14},{3,15},{4,8},{5,9},{6,10},{7,11},{8,4},{9,5},... | collective-permute-start | bytes 110600 | tf_op jit(solution)/shard_map/ppermute | solution.py:44
  155.4 2.9 %shard_map.63.source_ref = f32[256,512]{1,0:T(8,128)S(1)} custom-call(f32[256,512]{1,0:T(8,128)S(1)} %shard_map.62.source_ref), custom_call_target="tpu_custom_call" | custom-call | flops 4000000000 | bytes 4194304 | tf_op jit(solution)/shard_map/pallas_call | solution.py:510
  158.6 1.5 collective-permute-start.36
  160.7 1.4 collective-permute-start.38
  162.2 1.8 %shard_map.64.factor_ref = f32[256,512]{1,0:T(8,128)S(1)} custom-call(f32[256,512]{1,0:T(8,128)S(1)} %shard_map.63.source_ref), custom_call_target="tpu_custom_call" | custom-call | flops 4000000000 | bytes 4194304 | tf_op jit(solution)/shard_map/pallas_call | solution.py:510
  164.1 1.5 collective-permute-done.38.refs_3_
  (56 shorter events, 23.7 us)
Async XLA Ops:
  3.2 5.6 %collective-permute-start = (s32[1,136,128]{2,1,0:T(8,128)}, s32[1,136,128]{2,1,0:T(8,128)S(1)}, u32[]{:S(2)}, u32[]{:S(2)}) collective-permute-start(s32[1,136,128]{2,1,0:T(8,128)} %shard_map.50.after_ref.refs_0_), channel_id=1, source_target_pairs={{0,4},{1,5},{2,6},{3,7},{4,0},{5,1},{6,2},{7,3},{8,12},{9,13},{10,... | collective-permute-start | bytes 208904 | tf_op jit(solution)/shard_map/ppermute | solution.py:44
  6.2 7.8 %collective-permute-start.1 = (s32[1,136,128]{2,1,0:T(8,128)}, s32[1,136,128]{2,1,0:T(8,128)S(1)}, u32[]{:S(2)}, u32[]{:S(2)}) collective-permute-start(s32[1,136,128]{2,1,0:T(8,128)} %shard_map.50.after_ref.refs_0_), channel_id=1, source_target_pairs={{0,8},{1,9},{2,10},{3,11},{4,12},{5,13},{6,14},{7,15},{8,0},{9,1},... | collective-permute-start | bytes 208904 | tf_op jit(solution)/shard_map/ppermute | solution.py:44
  8.8 6.4 %collective-permute-start.2 = (s32[1,136,128]{2,1,0:T(8,128)}, s32[1,136,128]{2,1,0:T(8,128)S(1)}, u32[]{:S(2)}, u32[]{:S(2)}) collective-permute-start(s32[1,136,128]{2,1,0:T(8,128)} %shard_map.50.after_ref.refs_0_), channel_id=1, source_target_pairs={{0,12},{1,13},{2,14},{3,15},{4,8},{5,9},{6,10},{7,11},{8,4},{9,5},... | collective-permute-start | bytes 208904 | tf_op jit(solution)/shard_map/ppermute | solution.py:44
  15.2 0.9 copy-start
  16.1 9.6 %collective-permute-start.3 = (s32[4,136,128]{2,1,0:T(8,128)S(1)}, s32[4,136,128]{2,1,0:T(8,128)S(1)}, u32[]{:S(2)}, u32[]{:S(2)}) collective-permute-start(s32[4,136,128]{2,1,0:T(8,128)S(1)} %shard_map.52.refs_0_), channel_id=1, source_target_pairs={{0,1},{1,0},{2,3},{3,2},{4,5},{5,4},{6,7},{7,6},{8,9},{9,8},{10,11... | collective-permute-start | bytes 835592 | tf_op jit(solution)/shard_map/ppermute | solution.py:44
  17.7 12.3 %collective-permute-start.4 = (s32[4,136,128]{2,1,0:T(8,128)S(1)}, s32[4,136,128]{2,1,0:T(8,128)S(1)}, u32[]{:S(2)}, u32[]{:S(2)}) collective-permute-start(s32[4,136,128]{2,1,0:T(8,128)S(1)} %shard_map.52.refs_0_), channel_id=1, source_target_pairs={{0,2},{1,3},{2,0},{3,1},{4,6},{5,7},{6,4},{7,5},{8,10},{9,11},{10,... | collective-permute-start | bytes 835592 | tf_op jit(solution)/shard_map/ppermute | solution.py:44
  19.2 10.8 %collective-permute-start.5 = (s32[4,136,128]{2,1,0:T(8,128)S(1)}, s32[4,136,128]{2,1,0:T(8,128)S(1)}, u32[]{:S(2)}, u32[]{:S(2)}) collective-permute-start(s32[4,136,128]{2,1,0:T(8,128)S(1)} %shard_map.52.refs_0_), channel_id=1, source_target_pairs={{0,3},{1,2},{2,1},{3,0},{4,7},{5,6},{6,5},{7,4},{8,11},{9,10},{10,... | collective-permute-start | bytes 835592 | tf_op jit(solution)/shard_map/ppermute | solution.py:44
  19.7 2.2 %copy-start.1 = (bf16[1,1024,2048]{2,1,0:T(8,128)(2,1)S(1)}, bf16[1,1024,2048]{2,1,0:T(8,128)(2,1)}, u32[]{:S(2)}) copy-start(bf16[1,1024,2048]{2,1,0:T(8,128)(2,1)} %param.3) | copy-start | bytes 12582916
  36.6 8.2 %collective-permute-start.6 = (s32[4,136,128]{2,1,0:T(8,128)S(1)}, s32[4,136,128]{2,1,0:T(8,128)S(1)}, u32[]{:S(2)}, u32[]{:S(2)}) collective-permute-start(s32[4,136,128]{2,1,0:T(8,128)S(1)} %get-tuple-element.37), channel_id=1, source_target_pairs={{0,1},{1,0},{2,3},{3,2},{4,5},{5,4},{6,7},{7,6},{8,9},{9,8},{10,11... | collective-permute-start | bytes 835592 | tf_op jit(solution)/shard_map/ppermute | solution.py:44
  37.9 11.1 %collective-permute-start.7 = (s32[4,136,128]{2,1,0:T(8,128)S(1)}, s32[4,136,128]{2,1,0:T(8,128)S(1)}, u32[]{:S(2)}, u32[]{:S(2)}) collective-permute-start(s32[4,136,128]{2,1,0:T(8,128)S(1)} %get-tuple-element.38), channel_id=1, source_target_pairs={{0,2},{1,3},{2,0},{3,1},{4,6},{5,7},{6,4},{7,5},{8,10},{9,11},{10,... | collective-permute-start | bytes 835592 | tf_op jit(solution)/shard_map/ppermute | solution.py:44
  38.7 10.2 %collective-permute-start.8 = (s32[4,136,128]{2,1,0:T(8,128)S(1)}, s32[4,136,128]{2,1,0:T(8,128)S(1)}, u32[]{:S(2)}, u32[]{:S(2)}) collective-permute-start(s32[4,136,128]{2,1,0:T(8,128)S(1)} %get-tuple-element.39), channel_id=1, source_target_pairs={{0,3},{1,2},{2,1},{3,0},{4,7},{5,6},{6,5},{7,4},{8,11},{9,10},{10,... | collective-permute-start | bytes 835592 | tf_op jit(solution)/shard_map/ppermute | solution.py:44
  50.0 6.4 %collective-permute-start.10 = (s32[1,136,128]{2,1,0:T(8,128)S(1)}, s32[1,136,128]{2,1,0:T(8,128)S(1)}, u32[]{:S(2)}, u32[]{:S(2)}) collective-permute-start(s32[1,136,128]{2,1,0:T(8,128)S(1)} %get-tuple-element.42), channel_id=1, source_target_pairs={{0,8},{1,9},{2,10},{3,11},{4,12},{5,13},{6,14},{7,15},{8,0},{9,1},... | collective-permute-start | bytes 208904 | tf_op jit(solution)/shard_map/ppermute | solution.py:44
  53.4 6.8 %collective-permute-start.11 = (s32[1,136,128]{2,1,0:T(8,128)S(1)}, s32[1,136,128]{2,1,0:T(8,128)S(1)}, u32[]{:S(2)}, u32[]{:S(2)}) collective-permute-start(s32[1,136,128]{2,1,0:T(8,128)S(1)} %get-tuple-element.43), channel_id=1, source_target_pairs={{0,12},{1,13},{2,14},{3,15},{4,8},{5,9},{6,10},{7,11},{8,4},{9,5},... | collective-permute-start | bytes 208904 | tf_op jit(solution)/shard_map/ppermute | solution.py:44
  54.0 6.3 %collective-permute-start.9 = (s32[1,136,128]{2,1,0:T(8,128)S(1)}, s32[1,136,128]{2,1,0:T(8,128)S(1)}, u32[]{:S(2)}, u32[]{:S(2)}) collective-permute-start(s32[1,136,128]{2,1,0:T(8,128)S(1)} %get-tuple-element.41), channel_id=1, source_target_pairs={{0,4},{1,5},{2,6},{3,7},{4,0},{5,1},{6,2},{7,3},{8,12},{9,13},{10,... | collective-permute-start | bytes 208904 | tf_op jit(solution)/shard_map/ppermute | solution.py:44
  61.3 4.4 %collective-permute-start.12 = (s32[1,136,128]{2,1,0:T(8,128)S(1)}, s32[1,136,128]{2,1,0:T(8,128)S(1)}, u32[]{:S(2)}, u32[]{:S(2)}) collective-permute-start(s32[1,136,128]{2,1,0:T(8,128)S(1)} %get-tuple-element.44.refs_0_), channel_id=1, source_target_pairs={{0,4},{1,5},{2,6},{3,7},{4,0},{5,1},{6,2},{7,3},{8,12},{9,13},{10,... | collective-permute-start | bytes 208904 | tf_op jit(solution)/shard_map/ppermute | solution.py:44
  61.7 5.2 %collective-permute-start.13 = (s32[1,136,128]{2,1,0:T(8,128)S(1)}, s32[1,136,128]{2,1,0:T(8,128)S(1)}, u32[]{:S(2)}, u32[]{:S(2)}) collective-permute-start(s32[1,136,128]{2,1,0:T(8,128)S(1)} %get-tuple-element.44.refs_0_), channel_id=1, source_target_pairs={{0,8},{1,9},{2,10},{3,11},{4,12},{5,13},{6,14},{7,15},{8,0},{9,1},... | collective-permute-start | bytes 208904 | tf_op jit(solution)/shard_map/ppermute | solution.py:44
  63.8 6.1 %collective-permute-start.14 = (s32[1,136,128]{2,1,0:T(8,128)S(1)}, s32[1,136,128]{2,1,0:T(8,128)S(1)}, u32[]{:S(2)}, u32[]{:S(2)}) collective-permute-start(s32[1,136,128]{2,1,0:T(8,128)S(1)} %get-tuple-element.44.refs_0_), channel_id=1, source_target_pairs={{0,12},{1,13},{2,14},{3,15},{4,8},{5,9},{6,10},{7,11},{8,4},{9,5},... | collective-permute-start | bytes 208904 | tf_op jit(solution)/shard_map/ppermute | solution.py:44
  69.9 6.6 %collective-permute-start.15 = (s32[4,136,128]{2,1,0:T(8,128)S(1)}, s32[4,136,128]{2,1,0:T(8,128)S(1)}, u32[]{:S(2)}, u32[]{:S(2)}) collective-permute-start(s32[4,136,128]{2,1,0:T(8,128)S(1)} %shard_map.56.refs_0_), channel_id=1, source_target_pairs={{0,1},{1,0},{2,3},{3,2},{4,5},{5,4},{6,7},{7,6},{8,9},{9,8},{10,11... | collective-permute-start | bytes 835592 | tf_op jit(solution)/shard_map/ppermute | solution.py:44
  71.1 9.5 %collective-permute-start.16 = (s32[4,136,128]{2,1,0:T(8,128)S(1)}, s32[4,136,128]{2,1,0:T(8,128)S(1)}, u32[]{:S(2)}, u32[]{:S(2)}) collective-permute-start(s32[4,136,128]{2,1,0:T(8,128)S(1)} %shard_map.56.refs_0_), channel_id=1, source_target_pairs={{0,2},{1,3},{2,0},{3,1},{4,6},{5,7},{6,4},{7,5},{8,10},{9,11},{10,... | collective-permute-start | bytes 835592 | tf_op jit(solution)/shard_map/ppermute | solution.py:44
  72.6 8.0 %collective-permute-start.17 = (s32[4,136,128]{2,1,0:T(8,128)S(1)}, s32[4,136,128]{2,1,0:T(8,128)S(1)}, u32[]{:S(2)}, u32[]{:S(2)}) collective-permute-start(s32[4,136,128]{2,1,0:T(8,128)S(1)} %shard_map.56.refs_0_), channel_id=1, source_target_pairs={{0,3},{1,2},{2,1},{3,0},{4,7},{5,6},{6,5},{7,4},{8,11},{9,10},{10,... | collective-permute-start | bytes 835592 | tf_op jit(solution)/shard_map/ppermute | solution.py:44
  98.0 6.6 %collective-permute-start.18 = (s32[4,136,128]{2,1,0:T(8,128)S(1)}, s32[4,136,128]{2,1,0:T(8,128)S(1)}, u32[]{:S(2)}, u32[]{:S(2)}) collective-permute-start(s32[4,136,128]{2,1,0:T(8,128)S(1)} %get-tuple-element.46), channel_id=1, source_target_pairs={{0,1},{1,0},{2,3},{3,2},{4,5},{5,4},{6,7},{7,6},{8,9},{9,8},{10,11... | collective-permute-start | bytes 835592 | tf_op jit(solution)/shard_map/ppermute | solution.py:44
  99.0 8.1 %collective-permute-start.19 = (s32[4,136,128]{2,1,0:T(8,128)S(1)}, s32[4,136,128]{2,1,0:T(8,128)S(1)}, u32[]{:S(2)}, u32[]{:S(2)}) collective-permute-start(s32[4,136,128]{2,1,0:T(8,128)S(1)} %get-tuple-element.47), channel_id=1, source_target_pairs={{0,2},{1,3},{2,0},{3,1},{4,6},{5,7},{6,4},{7,5},{8,10},{9,11},{10,... | collective-permute-start | bytes 835592 | tf_op jit(solution)/shard_map/ppermute | solution.py:44
  100.1 8.5 %collective-permute-start.20 = (s32[4,136,128]{2,1,0:T(8,128)S(1)}, s32[4,136,128]{2,1,0:T(8,128)S(1)}, u32[]{:S(2)}, u32[]{:S(2)}) collective-permute-start(s32[4,136,128]{2,1,0:T(8,128)S(1)} %get-tuple-element.48), channel_id=1, source_target_pairs={{0,3},{1,2},{2,1},{3,0},{4,7},{5,6},{6,5},{7,4},{8,11},{9,10},{10,... | collective-permute-start | bytes 835592 | tf_op jit(solution)/shard_map/ppermute | solution.py:44
  109.7 5.9 %collective-permute-start.21 = (s32[1,136,128]{2,1,0:T(8,128)S(1)}, s32[1,136,128]{2,1,0:T(8,128)S(1)}, u32[]{:S(2)}, u32[]{:S(2)}) collective-permute-start(s32[1,136,128]{2,1,0:T(8,128)S(1)} %get-tuple-element.50), channel_id=1, source_target_pairs={{0,4},{1,5},{2,6},{3,7},{4,0},{5,1},{6,2},{7,3},{8,12},{9,13},{10,... | collective-permute-start | bytes 208904 | tf_op jit(solution)/shard_map/ppermute | solution.py:44
  109.7 5.8 %collective-permute-start.22 = (s32[1,136,128]{2,1,0:T(8,128)S(1)}, s32[1,136,128]{2,1,0:T(8,128)S(1)}, u32[]{:S(2)}, u32[]{:S(2)}) collective-permute-start(s32[1,136,128]{2,1,0:T(8,128)S(1)} %get-tuple-element.51), channel_id=1, source_target_pairs={{0,8},{1,9},{2,10},{3,11},{4,12},{5,13},{6,14},{7,15},{8,0},{9,1},... | collective-permute-start | bytes 208904 | tf_op jit(solution)/shard_map/ppermute | solution.py:44
  112.2 6.1 %collective-permute-start.23 = (s32[1,136,128]{2,1,0:T(8,128)S(1)}, s32[1,136,128]{2,1,0:T(8,128)S(1)}, u32[]{:S(2)}, u32[]{:S(2)}) collective-permute-start(s32[1,136,128]{2,1,0:T(8,128)S(1)} %get-tuple-element.52), channel_id=1, source_target_pairs={{0,12},{1,13},{2,14},{3,15},{4,8},{5,9},{6,10},{7,11},{8,4},{9,5},... | collective-permute-start | bytes 208904 | tf_op jit(solution)/shard_map/ppermute | solution.py:44
  118.9 4.5 %collective-permute-start.24 = (s32[1,136,128]{2,1,0:T(8,128)S(1)}, s32[1,136,128]{2,1,0:T(8,128)S(1)}, u32[]{:S(2)}, u32[]{:S(2)}) collective-permute-start(s32[1,136,128]{2,1,0:T(8,128)S(1)} %get-tuple-element.53.refs_0_), channel_id=1, source_target_pairs={{0,4},{1,5},{2,6},{3,7},{4,0},{5,1},{6,2},{7,3},{8,12},{9,13},{10,... | collective-permute-start | bytes 208904 | tf_op jit(solution)/shard_map/ppermute | solution.py:44
  119.0 5.3 %collective-permute-start.25 = (s32[1,136,128]{2,1,0:T(8,128)S(1)}, s32[1,136,128]{2,1,0:T(8,128)S(1)}, u32[]{:S(2)}, u32[]{:S(2)}) collective-permute-start(s32[1,136,128]{2,1,0:T(8,128)S(1)} %get-tuple-element.53.refs_0_), channel_id=1, source_target_pairs={{0,8},{1,9},{2,10},{3,11},{4,12},{5,13},{6,14},{7,15},{8,0},{9,1},... | collective-permute-start | bytes 208904 | tf_op jit(solution)/shard_map/ppermute | solution.py:44
  121.4 6.1 %collective-permute-start.26 = (s32[1,136,128]{2,1,0:T(8,128)S(1)}, s32[1,136,128]{2,1,0:T(8,128)S(1)}, u32[]{:S(2)}, u32[]{:S(2)}) collective-permute-start(s32[1,136,128]{2,1,0:T(8,128)S(1)} %get-tuple-element.53.refs_0_), channel_id=1, source_target_pairs={{0,12},{1,13},{2,14},{3,15},{4,8},{5,9},{6,10},{7,11},{8,4},{9,5},... | collective-permute-start | bytes 208904 | tf_op jit(solution)/shard_map/ppermute | solution.py:44
  127.6 7.1 %collective-permute-start.27 = (s32[4,136,128]{2,1,0:T(8,128)S(1)}, s32[4,136,128]{2,1,0:T(8,128)S(1)}, u32[]{:S(2)}, u32[]{:S(2)}) collective-permute-start(s32[4,136,128]{2,1,0:T(8,128)S(1)} %shard_map.60.refs_0_), channel_id=1, source_target_pairs={{0,1},{1,0},{2,3},{3,2},{4,5},{5,4},{6,7},{7,6},{8,9},{9,8},{10,11... | collective-permute-start | bytes 835592 | tf_op jit(solution)/shard_map/ppermute | solution.py:44
  128.7 10.2 %collective-permute-start.28 = (s32[4,136,128]{2,1,0:T(8,128)S(1)}, s32[4,136,128]{2,1,0:T(8,128)S(1)}, u32[]{:S(2)}, u32[]{:S(2)}) collective-permute-start(s32[4,136,128]{2,1,0:T(8,128)S(1)} %shard_map.60.refs_0_), channel_id=1, source_target_pairs={{0,2},{1,3},{2,0},{3,1},{4,6},{5,7},{6,4},{7,5},{8,10},{9,11},{10,... | collective-permute-start | bytes 835592 | tf_op jit(solution)/shard_map/ppermute | solution.py:44
  130.2 8.6 %collective-permute-start.29 = (s32[4,136,128]{2,1,0:T(8,128)S(1)}, s32[4,136,128]{2,1,0:T(8,128)S(1)}, u32[]{:S(2)}, u32[]{:S(2)}) collective-permute-start(s32[4,136,128]{2,1,0:T(8,128)S(1)} %shard_map.60.refs_0_), channel_id=1, source_target_pairs={{0,3},{1,2},{2,1},{3,0},{4,7},{5,6},{6,5},{7,4},{8,11},{9,10},{10,... | collective-permute-start | bytes 835592 | tf_op jit(solution)/shard_map/ppermute | solution.py:44
  143.9 6.6 %collective-permute-start.30 = (f32[72,128]{1,0:T(8,128)S(1)}, f32[72,128]{1,0:T(8,128)S(1)}, u32[]{:S(2)}, u32[]{:S(2)}) collective-permute-start(f32[72,128]{1,0:T(8,128)S(1)} %get-tuple-element.55), channel_id=1, source_target_pairs={{0,1},{1,0},{2,3},{3,2},{4,5},{5,4},{6,7},{7,6},{8,9},{9,8},{10,11... | collective-permute-start | bytes 110600 | tf_op jit(solution)/shard_map/ppermute | solution.py:44
  144.6 5.8 %collective-permute-start.31 = (f32[72,128]{1,0:T(8,128)S(1)}, f32[72,128]{1,0:T(8,128)S(1)}, u32[]{:S(2)}, u32[]{:S(2)}) collective-permute-start(f32[72,128]{1,0:T(8,128)S(1)} %get-tuple-element.56), channel_id=1, source_target_pairs={{0,2},{1,3},{2,0},{3,1},{4,6},{5,7},{6,4},{7,5},{8,10},{9,11},{10,... | collective-permute-start | bytes 110600 | tf_op jit(solution)/shard_map/ppermute | solution.py:44
  146.1 4.9 %collective-permute-start.32 = (f32[72,128]{1,0:T(8,128)S(1)}, f32[72,128]{1,0:T(8,128)S(1)}, u32[]{:S(2)}, u32[]{:S(2)}) collective-permute-start(f32[72,128]{1,0:T(8,128)S(1)} %get-tuple-element.57), channel_id=1, source_target_pairs={{0,3},{1,2},{2,1},{3,0},{4,7},{5,6},{6,5},{7,4},{8,11},{9,10},{10,... | collective-permute-start | bytes 110600 | tf_op jit(solution)/shard_map/ppermute | solution.py:44
  150.9 7.3 %collective-permute-start.33 = (f32[72,128]{1,0:T(8,128)S(1)}, f32[72,128]{1,0:T(8,128)S(1)}, u32[]{:S(2)}, u32[]{:S(2)}) collective-permute-start(f32[72,128]{1,0:T(8,128)S(1)} %add_add_fusion.1), channel_id=1, source_target_pairs={{0,4},{1,5},{2,6},{3,7},{4,0},{5,1},{6,2},{7,3},{8,12},{9,13},{10,... | collective-permute-start | bytes 110600 | tf_op jit(solution)/shard_map/ppermute | solution.py:44
  151.0 7.3 %collective-permute-start.34 = (f32[72,128]{1,0:T(8,128)S(1)}, f32[72,128]{1,0:T(8,128)S(1)}, u32[]{:S(2)}, u32[]{:S(2)}) collective-permute-start(f32[72,128]{1,0:T(8,128)S(1)} %add_add_fusion.1), channel_id=1, source_target_pairs={{0,8},{1,9},{2,10},{3,11},{4,12},{5,13},{6,14},{7,15},{8,0},{9,1},... | collective-permute-start | bytes 110600 | tf_op jit(solution)/shard_map/ppermute | solution.py:44
  152.8 5.8 %collective-permute-start.35 = (f32[72,128]{1,0:T(8,128)S(1)}, f32[72,128]{1,0:T(8,128)S(1)}, u32[]{:S(2)}, u32[]{:S(2)}) collective-permute-start(f32[72,128]{1,0:T(8,128)S(1)} %add_add_fusion.1), channel_id=1, source_target_pairs={{0,12},{1,13},{2,14},{3,15},{4,8},{5,9},{6,10},{7,11},{8,4},{9,5},... | collective-permute-start | bytes 110600 | tf_op jit(solution)/shard_map/ppermute | solution.py:44
  158.6 5.3 %collective-permute-start.36 = (f32[72,128]{1,0:T(8,128)S(1)}, f32[72,128]{1,0:T(8,128)S(1)}, u32[]{:S(2)}, u32[]{:S(2)}) collective-permute-start(f32[72,128]{1,0:T(8,128)S(1)} %add_add_fusion.refs_0_), channel_id=1, source_target_pairs={{0,1},{1,0},{2,3},{3,2},{4,5},{5,4},{6,7},{7,6},{8,9},{9,8},{10,11... | collective-permute-start | bytes 110600 | tf_op jit(solution)/shard_map/ppermute | solution.py:44
  160.1 4.0 %collective-permute-start.37 = (f32[72,128]{1,0:T(8,128)S(1)}, f32[72,128]{1,0:T(8,128)S(1)}, u32[]{:S(2)}, u32[]{:S(2)}) collective-permute-start(f32[72,128]{1,0:T(8,128)S(1)} %add_add_fusion.refs_0_), channel_id=1, source_target_pairs={{0,2},{1,3},{2,0},{3,1},{4,6},{5,7},{6,4},{7,5},{8,10},{9,11},{10,... | collective-permute-start | bytes 110600 | tf_op jit(solution)/shard_map/ppermute | solution.py:44
  160.7 4.9 %collective-permute-start.38 = (f32[72,128]{1,0:T(8,128)S(1)}, f32[72,128]{1,0:T(8,128)S(1)}, u32[]{:S(2)}, u32[]{:S(2)}) collective-permute-start(f32[72,128]{1,0:T(8,128)S(1)} %add_add_fusion.refs_0_), channel_id=1, source_target_pairs={{0,3},{1,2},{2,1},{3,0},{4,7},{5,6},{6,5},{7,4},{8,11},{9,10},{10,... | collective-permute-start | bytes 110600 | tf_op jit(solution)/shard_map/ppermute | solution.py:44
  166.2 1.2 collective-permute-start.39

commit v6 on v5

--- a/solution.py
+++ b/solution.py
@@ -15,6 +15,9 @@
 CODES = 128
 STEPS = 65535.0
 LEAST = 2.0**-90
+FINER = 64.0
+WIDE_STEPS = 524287.0
+WIDE = 168
 VMEM_LIMIT = 32 * 1024 * 1024
 VMEM_SMALL = 8 * 1024 * 1024
 HIGHEST = lax.Precision.HIGHEST
@@ -449,31 +452,127 @@
         folded_ref[place, quarter:] = jnp.broadcast_to(diagonal, (SUBLANES, half))
 
 
-def unfold_symmetric(parts):
-    quarter = parts[0].shape[0] - SUBLANES
-    half = 2 * quarter
+def unfold_symmetric(folded, diagonal):
+    half = folded.shape[1]
     row = lax.broadcasted_iota(jnp.int32, (half, half), 0)
     column = lax.broadcasted_iota(jnp.int32, (half, half), 1)
-    left = jnp.concatenate([parts[0][:quarter], parts[1][:quarter]], axis=0)
-    both = jnp.concatenate([parts[2][:quarter], parts[3][:quarter]], axis=0)
+    left, both = folded[:half], folded[half:]
     turned = both.T
-    corner = jnp.where(row == column, parts[3][quarter : quarter + 1], jnp.where(row < column, both, turned))
+    corner = jnp.where(row == column, diagonal, jnp.where(row < column, both, turned))
     upper = jnp.concatenate([jnp.where(row >= column, both, turned), left.T], axis=1)
     return jnp.concatenate([upper, jnp.concatenate([left, corner], axis=1)], axis=0)
 
 
-def project_kernel(order, sources, quarter_ref, place_ref, rows_ref, *refs):
+def diagonal_of(value):
+    row = lax.broadcasted_iota(jnp.int32, value.shape, 0)
+    column = lax.broadcasted_iota(jnp.int32, value.shape, 1)
+    kept = jnp.where(row == column, value, 0.0)
+    return jnp.sum(kept, axis=0, keepdims=True), jnp.sum(kept, axis=1, keepdims=True)
+
+
+def fold_message(folded, diagonal):
+    size, half = folded.shape
+    row = lax.broadcasted_iota(jnp.int32, (size, 1), 0)
+    most = jnp.max(jnp.abs(diagonal), axis=1, keepdims=True)
+    peaks = jnp.max(jnp.abs(folded), axis=1, keepdims=True)
+    peaks = jnp.where(row == half, jnp.maximum(peaks, most), peaks)
+    codes, scales = row_scales(gather_columns([peaks[:half], peaks[half:]]))
+    factors = WIDE_STEPS / scales
+    lines = codes.T.astype(jnp.int32)
+    value = jnp.round(folded * jnp.concatenate([factors[:, :1], factors[:, 1:2]], axis=0)).astype(jnp.int32)
+    high = jnp.right_shift(value, NIBBLES)
+    rows = [jnp.bitwise_or(jnp.left_shift(high[:half], 16), jnp.bitwise_and(high[half:], 0xFFFF))]
+    for first in range(0, size, 8 * SUBLANES):
+        extra = jnp.zeros((SUBLANES, half), jnp.int32)
+        for group in range(8):
+            start = first + group * SUBLANES
+            extra = jnp.bitwise_or(
+                extra, jnp.left_shift(jnp.bitwise_and(value[start : start + SUBLANES], 15), NIBBLES * group)
+            )
+        rows.append(extra)
+    last = jnp.round(diagonal * (factors[:1, 1:2] * FINER)).astype(jnp.int32)
+    code = jnp.bitwise_or(jnp.bitwise_and(lines[0:1], 0xFFFF), jnp.left_shift(lines[1:2], 16))
+    sub = lax.broadcasted_iota(jnp.int32, (SUBLANES, half), 0)
+    rows.append(jnp.where(sub == 0, code, jnp.where(sub == 1, last, 0)))
+    return jnp.concatenate(rows, axis=0)
+
+
+def sum_folded(messages):
+    half = LANES
+    lines = []
+    for message in messages:
+        code = message[half + 32 : half + 33]
+        lines += [jnp.right_shift(jnp.left_shift(code, 16), 16), jnp.right_shift(code, 16)]
+    lines = [line.astype(jnp.float32) for line in lines]
+    lines.append(jnp.zeros((LANES - len(lines), LANES), jnp.float32))
+    scales = (jnp.exp2(jnp.concatenate(lines, axis=0) * (1.0 / CODES)) * (1.0 / WIDE_STEPS)).T
+    parts, diagonals = [], []
+    for place, message in enumerate(messages):
+        words = message[:half]
+        high = jnp.concatenate([jnp.right_shift(words, 16), jnp.right_shift(jnp.left_shift(words, 16), 16)], axis=0)
+        low = []
+        for tile in range(4):
+            extra = message[half + tile * SUBLANES : half + (tile + 1) * SUBLANES]
+            low += [jnp.bitwise_and(jnp.right_shift(extra, NIBBLES * group), 15) for group in range(8)]
+        value = jnp.bitwise_or(jnp.left_shift(high, NIBBLES), jnp.concatenate(low, axis=0))
+        scale = jnp.concatenate([scales[:, 2 * place : 2 * place + 1], scales[:, 2 * place + 1 : 2 * place + 2]], axis=0)
+        parts.append(value.astype(jnp.float32) * scale)
+        last = message[half + 33 : half + 34].astype(jnp.float32)
+        diagonals.append(last * (scales[:1, 2 * place + 1 : 2 * place + 2] * (1.0 / FINER)))
+    return pair_sum(parts), pair_sum(diagonals)
+
+
+def add_kernel(*refs):
+    refs[-1][...] = fold_message(*sum_folded([ref[...] for ref in refs[:-1]]))
+
+
+def add_messages(messages):
+    vmem = pl.BlockSpec(memory_space=pltpu.VMEM)
+    return pl.pallas_call(
+        add_kernel,
+        in_specs=[vmem] * len(messages),
+        out_specs=vmem,
+        out_shape=jax.ShapeDtypeStruct(messages[0].shape, messages[0].dtype),
+        compiler_params=pltpu.CompilerParams(vmem_limit_bytes=VMEM_SMALL),
+    )(*messages)
+
+
+def sum_messages(message, groups, beside):
+    stages = stage_bits(groups)
+    steps, state = list(beside), None
+    for depth, bits in enumerate(reversed(stages)):
+        if depth > 0:
+            message = add_messages(messages)
+        messages = [message] + [exchange(message, groups, span) for span in offsets(bits)[1:]]
+        if steps:
+            state = steps.pop(0)(state)
+        if depth + 1 < len(stages):
+            messages, state = lax.optimization_barrier((messages, state))
+    for step in steps:
+        state = step(state)
+    return messages, state
+
+
+def project_kernel(order, sources, coded, quarter_ref, place_ref, rows_ref, *refs):
     refs, (inner_ref, *outs), (full_ref, folded_ref) = refs[:sources], refs[sources:-2], refs[-2:]
     size = full_ref.shape[0]
     load_all(order, place_ref, refs, full_ref)
     image = full_ref[...]
-    inner_ref[...] = rows_inner(image)
+    inner = rows_inner(image)
+    inner_ref[...] = inner
     split = jnp.concatenate(split_pieces(image, PIECES), axis=0)
     sampled = rows_dot(split, rows_ref[...])
     sampled = sum(sampled[piece * size : (piece + 1) * size] for piece in range(PIECES))
     high, low = split_pieces(sampled, PIECES)
     mixed = rows_dot(high, low)
-    fold_symmetric(rows_dot(high, high) + (mixed + mixed.T), folded_ref, size)
+    cross = rows_dot(high, high) + (mixed + mixed.T)
+    across, down = diagonal_of(inner)
+    fold_symmetric(cross * (lax.rsqrt(down) * lax.rsqrt(across)), folded_ref, size)
+    if coded:
+        quarter = size // 4
+        folded = jnp.concatenate([folded_ref[place, :quarter] for place in range(4)], axis=0)
+        outs[0][...] = fold_message(folded, folded_ref[0, quarter : quarter + 1])
+        return
     for offset, out_ref in enumerate(outs):
         out_ref[...] = folded_ref[jnp.bitwise_xor(quarter_ref[0], offset)]
 
@@ -482,12 +581,17 @@
     samples, cap = genotypes.shape
     scalar, vmem = pl.BlockSpec(memory_space=pltpu.SMEM), pl.BlockSpec(memory_space=pltpu.VMEM)
     part = (size // 4 + SUBLANES, size // 2)
-    outs = [(size, size)] + [part] * 4
-    return pl.pallas_call(
-        functools.partial(project_kernel, order, len(gathered)),
+    coded = size == TILES * LANES
+    outs = [jax.ShapeDtypeStruct((size, size), jnp.float32)]
+    if coded:
+        outs += [jax.ShapeDtypeStruct((WIDE, LANES), jnp.int32)]
+    else:
+        outs += [jax.ShapeDtypeStruct(part, jnp.float32)] * 4
+    return pl.pallas_call(
+        functools.partial(project_kernel, order, len(gathered), coded),
         in_specs=[scalar, scalar, vmem] + [vmem] * len(gathered),
         out_specs=[vmem] * len(outs),
-        out_shape=[jax.ShapeDtypeStruct(shape, jnp.float32) for shape in outs],
+        out_shape=outs,
         scratch_shapes=[
             pltpu.VMEM((size, cap), jnp.float32),
             pltpu.VMEM((4,) + part, jnp.float32),
@@ -534,30 +638,37 @@
     )(factor, own)
 
 
-def trace_kernel(scale, quarter_ref, factor_ref, *refs):
-    parts, (half_ref, trace_ref, folded_ref) = refs[:4], refs[4:]
-    for offset in range(4):
-        folded_ref[jnp.bitwise_xor(quarter_ref[0], offset)] = parts[offset][...]
-    cross = unfold_symmetric([folded_ref[place] for place in range(4)])
+def trace_kernel(scale, quarter_ref, factor_ref, inner_ref, *refs):
+    parts, (half_ref, trace_ref, folded_ref) = refs[:-3], refs[-3:]
+    if parts[0].dtype == jnp.int32:
+        folded, diagonal = sum_folded([part[...] for part in parts])
+    else:
+        for offset in range(4):
+            folded_ref[jnp.bitwise_xor(quarter_ref[0], offset)] = parts[offset][...]
+        quarter = folded_ref.shape[1] - SUBLANES
+        folded = jnp.concatenate([folded_ref[place, :quarter] for place in range(4)], axis=0)
+        diagonal = folded_ref[3, quarter : quarter + 1]
+    across, down = diagonal_of(inner_ref[...])
+    cross = unfold_symmetric(folded, diagonal) * ((down * lax.rsqrt(down)) * (across * lax.rsqrt(across)))
     factor = finish_factor(factor_ref)
     half = scale * jnp.dot(factor, cross, precision=HIGHEST, preferred_element_type=jnp.float32)
     half_ref[...] = half
     trace_ref[...] = jnp.broadcast_to(jnp.sum(half * factor), trace_ref.shape)
 
 
-def trace_half(quarter, factor, parts, scale):
+def trace_half(quarter, factor, inner, parts, scale):
     vmem = pl.BlockSpec(memory_space=pltpu.VMEM)
     return pl.pallas_call(
         functools.partial(trace_kernel, scale),
-        in_specs=[pl.BlockSpec(memory_space=pltpu.SMEM)] + [vmem] * 5,
+        in_specs=[pl.BlockSpec(memory_space=pltpu.SMEM)] + [vmem] * (2 + len(parts)),
         out_specs=[vmem] * 2,
         out_shape=[
-            jax.ShapeDtypeStruct((factor.shape[0],) * 2, jnp.float32),
+            jax.ShapeDtypeStruct(inner.shape, jnp.float32),
             jax.ShapeDtypeStruct((SUBLANES, LANES), jnp.float32),
         ],
-        scratch_shapes=[pltpu.VMEM((4,) + parts[0].shape, jnp.float32)],
+        scratch_shapes=[pltpu.VMEM((4,) + parts[0].shape, parts[0].dtype)],
         compiler_params=pltpu.CompilerParams(vmem_limit_bytes=VMEM_SMALL),
-    )(quarter, factor, *parts)
+    )(quarter, factor, inner, *parts)
 
 
 def finish_kernel(gain, half_ref, factor_ref, *refs):
@@ -627,15 +738,20 @@
     _, message = apply(message, False)
     own, message = apply(message, True)
     quarter = jnp.bitwise_and(place, 3)
-    inner, *quarters = project(dosages, quarter, place, gather(message), order, size)
-    cuts = [0, size // 4 + size // 8, size - size // 4, size]
-    beside = [
-        lambda _: second_factor(inner, cuts[0], cuts[1]),
-        lambda work: second_factor(work, cuts[1], cuts[2]),
-        lambda work: second_factor(work, cuts[2], cuts[3]),
-    ]
-    quarters, second = sum_quarters(quarters, groups, beside)
-    halfway, trace = trace_half(quarter, second, quarters, scale)
+    inner, *parts = project(dosages, quarter, place, gather(message), order, size)
+    if len(parts) == 1:
+        cut = size // 2 + size // 8
+        beside = [lambda _: second_factor(inner, 0, cut), lambda work: second_factor(work, cut, size)]
+        parts, second = sum_messages(parts[0], groups, beside)
+    else:
+        cuts = [0, size // 4 + size // 8, size - size // 4, size]
+        beside = [
+            lambda _: second_factor(inner, cuts[0], cuts[1]),
+            lambda work: second_factor(work, cuts[1], cuts[2]),
+            lambda work: second_factor(work, cuts[2], cuts[3]),
+        ]
+        parts, second = sum_quarters(parts, groups, beside)
+    halfway, trace = trace_half(quarter, second, inner, parts, scale)
     blocks = lax.axis_size("blk")
     traces = [trace] + [
         lax.ppermute(trace, "blk", [(block, (block + shift) % blocks) for block in range(blocks)])

time: 169 us -> 165 us (0.976)
  starting transfers between devices: 52.3 us -> 48.8 us
  waiting for transfers between devices: 66.2 us -> 64.3 us
    ppermute x39 -> x36, starting transfers between devices: 52.3 us -> 48.7 us  [exchange(): lax.ppermute(value, 'smp', [(device, device ^ offset) for device in range...]
    ppermute x39 -> x36, waiting for transfers between devices: 66.2 us -> 64.2 us  [exchange(): lax.ppermute(value, 'smp', [(device, device ^ offset) for device in range...]
    pallas_call x1 -> x2, Pallas kernels: 4.97 us -> 5.93 us  [the longest x1 5.27 us: project(): pl.pallas_call(functools.partial(project_kernel, order, len(gathered), co...]
    pallas_call x3 -> x2, Pallas kernels: 7.64 us -> 7.66 us  [second_factor(): pl.pallas_call(functools.partial(second_kernel, first, last), in_specs=[v...]
  transfers between devices with their start and end apart: 40 -> 37, of which waited for: 26 -> 23; matrix products, arithmetic and copies ran while one was open for 0% -> 0% of each run, Pallas kernels for 5% -> 6%
where the time goes in v6:
time: 165 us; the launch traced here: 164 us
  waiting for transfers between devices  64.3 us (39%)
  starting transfers between devices  48.8 us (30%)
  Pallas kernels  46.9 us (28%)
  local copies, waits for them, and re-layouts  3.07 us (2%)
    ppermute x36, waiting for transfers between devices, exchange(): lax.ppermute(value, 'smp', [(device, device ^ offset) for device in range...  64.2 us
    ppermute x36, starting transfers between devices, exchange(): lax.ppermute(value, 'smp', [(device, device ^ offset) for device in range...  48.7 us
    pallas_call x2, Pallas kernels, apply_samples(): pl.pallas_call(functools.partial(apply_kernel, order, normalise, scale, l...  24 us
    pallas_call x2, Pallas kernels, second_factor(): pl.pallas_call(functools.partial(second_kernel, first, last), in_specs=[v...  7.66 us
    pallas_call x1, Pallas kernels, project(): pl.pallas_call(functools.partial(project_kernel, order, len(gathered), co...  5.27 us
    pallas_call x4, Pallas kernels, combine(): pl.pallas_call(functools.partial(combine_kernel, len(arrived), parts), in...  3.71 us
  transfers between devices with their start and end apart: 37, of which 23 were waited for; matrix products, arithmetic and copies ran while one was open for 0% of the time, Pallas kernels for 6%

profile of v6, /device:TPU:0, one launch (start us, length us, event | category | flops | bytes accessed | tf_op | source)
XLA Modules:
  0.0 164.5 jit_solution(4829536060177151990)
XLA Ops:
  1.3 1.9 %shard_map.50.after_ref.refs_0_ = s32[1,136,128]{2,1,0:T(8,128)} custom-call(s32[1]{0:T(128)} %bitcast.place_ref, s32[1]{0:T(128)S(6)} %copy.5.size_ref, f32[128,256]{1,0:T(8,128)} %bitcast.9), custom_call_target="tpu_custom_call" | custom-call | tf_op jit(solution)/shard_map/pallas_call | solution.py:208
  3.2 3.0 %collective-permute-start = (s32[1,136,128]{2,1,0:T(8,128)}, s32[1,136,128]{2,1,0:T(8,128)S(1)}, u32[]{:S(2)}, u32[]{:S(2)}) collective-permute-start(s32[1,136,128]{2,1,0:T(8,128)} %shard_map.50.after_ref.refs_0_), channel_id=1, source_target_pairs={{0,4},{1,5},{2,6},{3,7},{4,0},{5,1},{6,2},{7,3},{8,12},{9,13},{10,... | collective-permute-start | bytes 208904 | tf_op jit(solution)/shard_map/ppermute | solution.py:47
  6.2 2.6 %collective-permute-start.1 = (s32[1,136,128]{2,1,0:T(8,128)}, s32[1,136,128]{2,1,0:T(8,128)S(1)}, u32[]{:S(2)}, u32[]{:S(2)}) collective-permute-start(s32[1,136,128]{2,1,0:T(8,128)} %shard_map.50.after_ref.refs_0_), channel_id=1, source_target_pairs={{0,8},{1,9},{2,10},{3,11},{4,12},{5,13},{6,14},{7,15},{8,0},{9,1},... | collective-permute-start | bytes 208904 | tf_op jit(solution)/shard_map/ppermute | solution.py:47
  8.8 5.2 %collective-permute-done.1.refs_2_ = s32[1,136,128]{2,1,0:T(8,128)S(1)} collective-permute-done((s32[1,136,128]{2,1,0:T(8,128)}, s32[1,136,128]{2,1,0:T(8,128)S(1)}, u32[]{:S(2)}, u32[]{:S(2)}) %collective-permute-start.1) | collective-permute-done | bytes 69664 | tf_op jit(solution)/shard_map/ppermute | solution.py:47
  14.0 1.3 collective-permute-done.2.refs_3_
  16.1 1.6 collective-permute-start.3
  17.7 1.5 collective-permute-start.4
  19.7 2.2 %copy-done.1 = bf16[1,1024,2048]{2,1,0:T(8,128)(2,1)S(1)} copy-done((bf16[1,1024,2048]{2,1,0:T(8,128)(2,1)S(1)}, bf16[1,1024,2048]{2,1,0:T(8,128)(2,1)}, u32[]{:S(2)}) %copy-start.1) | copy-done | bytes 4194328
  22.2 3.6 %collective-permute-done.3.refs_1_ = s32[4,136,128]{2,1,0:T(8,128)S(1)} collective-permute-done((s32[4,136,128]{2,1,0:T(8,128)S(1)}, s32[4,136,128]{2,1,0:T(8,128)S(1)}, u32[]{:S(2)}, u32[]{:S(2)}) %collective-permute-start.3) | collective-permute-done | bytes 278560 | tf_op jit(solution)/shard_map/ppermute | solution.py:47
  25.8 4.2 %collective-permute-done.4.refs_2_ = s32[4,136,128]{2,1,0:T(8,128)S(1)} collective-permute-done((s32[4,136,128]{2,1,0:T(8,128)S(1)}, s32[4,136,128]{2,1,0:T(8,128)S(1)}, u32[]{:S(2)}, u32[]{:S(2)}) %collective-permute-start.4) | collective-permute-done | bytes 278560 | tf_op jit(solution)/shard_map/ppermute | solution.py:47
  30.0 6.6 %shard_map.53 = (f32[4,256,128]{2,1,0:T(8,128)S(1)}, s32[4,136,128]{2,1,0:T(8,128)S(1)}, s32[4,136,128]{2,1,0:T(8,128)S(1)}, s32[4,136,128]{2,1,0:T(8,128)S(1)}) custom-call(s32[1]{0:T(128)} %bitcast.place_ref, s32[1]{0:T(128)S(6)} %copy.5.size_ref, bf16[1024,2048]{1,0:T(8,128)(2,1)S(1)} %shard_map.51.rows_ref, s32[4,136,128]{2,1,0:T(8,128)S(1)} %shard_map.52.refs_0_, ...), custom_call_target="tpu_custom_call" | custom-call | tf_op jit(solution)/shard_map/pallas_call | solution.py:335
  36.6 1.3 collective-permute-start.6
  38.7 1.4 collective-permute-start.8
  40.2 4.6 %collective-permute-done.6.refs_0_ = s32[4,136,128]{2,1,0:T(8,128)S(1)} collective-permute-done((s32[4,136,128]{2,1,0:T(8,128)S(1)}, s32[4,136,128]{2,1,0:T(8,128)S(1)}, u32[]{:S(2)}, u32[]{:S(2)}) %collective-permute-start.6) | collective-permute-done | bytes 278560 | tf_op jit(solution)/shard_map/ppermute | solution.py:47
  44.8 4.1 %collective-permute-done.7.refs_1_ = s32[4,136,128]{2,1,0:T(8,128)S(1)} collective-permute-done((s32[4,136,128]{2,1,0:T(8,128)S(1)}, s32[4,136,128]{2,1,0:T(8,128)S(1)}, u32[]{:S(2)}, u32[]{:S(2)}) %collective-permute-start.7) | collective-permute-done | bytes 278560 | tf_op jit(solution)/shard_map/ppermute | solution.py:47
  50.0 3.4 %collective-permute-start.10 = (s32[1,136,128]{2,1,0:T(8,128)S(1)}, s32[1,136,128]{2,1,0:T(8,128)S(1)}, u32[]{:S(2)}, u32[]{:S(2)}) collective-permute-start(s32[1,136,128]{2,1,0:T(8,128)S(1)} %get-tuple-element.36), channel_id=1, source_target_pairs={{0,8},{1,9},{2,10},{3,11},{4,12},{5,13},{6,14},{7,15},{8,0},{9,1},... | collective-permute-start | bytes 208904 | tf_op jit(solution)/shard_map/ppermute | solution.py:47
  54.1 2.4 %collective-permute-done.10.refs_1_ = s32[1,136,128]{2,1,0:T(8,128)S(1)} collective-permute-done((s32[1,136,128]{2,1,0:T(8,128)S(1)}, s32[1,136,128]{2,1,0:T(8,128)S(1)}, u32[]{:S(2)}, u32[]{:S(2)}) %collective-permute-start.10) | collective-permute-done | bytes 69664 | tf_op jit(solution)/shard_map/ppermute | solution.py:47
  56.5 3.8 %collective-permute-done.11.refs_2_ = s32[1,136,128]{2,1,0:T(8,128)S(1)} collective-permute-done((s32[1,136,128]{2,1,0:T(8,128)S(1)}, s32[1,136,128]{2,1,0:T(8,128)S(1)}, u32[]{:S(2)}, u32[]{:S(2)}) %collective-permute-start.11) | collective-permute-done | bytes 69664 | tf_op jit(solution)/shard_map/ppermute | solution.py:47
  61.7 2.1 %collective-permute-start.13 = (s32[1,136,128]{2,1,0:T(8,128)S(1)}, s32[1,136,128]{2,1,0:T(8,128)S(1)}, u32[]{:S(2)}, u32[]{:S(2)}) collective-permute-start(s32[1,136,128]{2,1,0:T(8,128)S(1)} %get-tuple-element.38.refs_0_), channel_id=1, source_target_pairs={{0,8},{1,9},{2,10},{3,11},{4,12},{5,13},{6,14},{7,15},{8,0},{9,1},... | collective-permute-start | bytes 208904 | tf_op jit(solution)/shard_map/ppermute | solution.py:47
  63.8 1.8 %collective-permute-start.14 = (s32[1,136,128]{2,1,0:T(8,128)S(1)}, s32[1,136,128]{2,1,0:T(8,128)S(1)}, u32[]{:S(2)}, u32[]{:S(2)}) collective-permute-start(s32[1,136,128]{2,1,0:T(8,128)S(1)} %get-tuple-element.38.refs_0_), channel_id=1, source_target_pairs={{0,12},{1,13},{2,14},{3,15},{4,8},{5,9},{6,10},{7,11},{8,4},{9,5},... | collective-permute-start | bytes 208904 | tf_op jit(solution)/shard_map/ppermute | solution.py:47
  65.6 1.3 collective-permute-done.13.refs_2_
  66.9 3.0 %collective-permute-done.14.refs_3_ = s32[1,136,128]{2,1,0:T(8,128)S(1)} collective-permute-done((s32[1,136,128]{2,1,0:T(8,128)S(1)}, s32[1,136,128]{2,1,0:T(8,128)S(1)}, u32[]{:S(2)}, u32[]{:S(2)}) %collective-permute-start.14) | collective-permute-done | bytes 69664 | tf_op jit(solution)/shard_map/ppermute | solution.py:47
  69.9 1.2 collective-permute-start.15
  71.1 1.5 collective-permute-start.16
  73.5 3.1 %collective-permute-done.15.refs_1_ = s32[4,136,128]{2,1,0:T(8,128)S(1)} collective-permute-done((s32[4,136,128]{2,1,0:T(8,128)S(1)}, s32[4,136,128]{2,1,0:T(8,128)S(1)}, u32[]{:S(2)}, u32[]{:S(2)}) %collective-permute-start.15) | collective-permute-done | bytes 278560 | tf_op jit(solution)/shard_map/ppermute | solution.py:47
  76.5 4.1 %collective-permute-done.16.refs_2_ = s32[4,136,128]{2,1,0:T(8,128)S(1)} collective-permute-done((s32[4,136,128]{2,1,0:T(8,128)S(1)}, s32[4,136,128]{2,1,0:T(8,128)S(1)}, u32[]{:S(2)}, u32[]{:S(2)}) %collective-permute-start.16) | collective-permute-done | bytes 278560 | tf_op jit(solution)/shard_map/ppermute | solution.py:47
  80.6 17.4 %shard_map.57 = (f32[4,256,128]{2,1,0:T(8,128)S(1)}, s32[4,136,128]{2,1,0:T(8,128)S(1)}, s32[4,136,128]{2,1,0:T(8,128)S(1)}, s32[4,136,128]{2,1,0:T(8,128)S(1)}) custom-call(s32[1]{0:T(128)} %bitcast.place_ref, s32[1]{0:T(128)S(6)} %copy.5.size_ref, bf16[1024,2048]{1,0:T(8,128)(2,1)S(1)} %shard_map.51.rows_ref, s32[4,136,128]{2,1,0:T(8,128)S(1)} %shard_map.56.refs_0_, ...), custom_call_target="tpu_custom_call" | custom-call | tf_op jit(solution)/shard_map/pallas_call | solution.py:335
  100.1 1.5 collective-permute-start.20
  101.6 3.1 %collective-permute-done.18.refs_0_ = s32[4,136,128]{2,1,0:T(8,128)S(1)} collective-permute-done((s32[4,136,128]{2,1,0:T(8,128)S(1)}, s32[4,136,128]{2,1,0:T(8,128)S(1)}, u32[]{:S(2)}, u32[]{:S(2)}) %collective-permute-start.18) | collective-permute-done | bytes 278560 | tf_op jit(solution)/shard_map/ppermute | solution.py:47
  104.6 2.5 %collective-permute-done.19.refs_1_ = s32[4,136,128]{2,1,0:T(8,128)S(1)} collective-permute-done((s32[4,136,128]{2,1,0:T(8,128)S(1)}, s32[4,136,128]{2,1,0:T(8,128)S(1)}, u32[]{:S(2)}, u32[]{:S(2)}) %collective-permute-start.19) | collective-permute-done | bytes 278560 | tf_op jit(solution)/shard_map/ppermute | solution.py:47
  107.1 1.4 collective-permute-done.20.refs_2_
  109.7 2.5 %collective-permute-start.22 = (s32[1,136,128]{2,1,0:T(8,128)S(1)}, s32[1,136,128]{2,1,0:T(8,128)S(1)}, u32[]{:S(2)}, u32[]{:S(2)}) collective-permute-start(s32[1,136,128]{2,1,0:T(8,128)S(1)} %get-tuple-element.45), channel_id=1, source_target_pairs={{0,8},{1,9},{2,10},{3,11},{4,12},{5,13},{6,14},{7,15},{8,0},{9,1},... | collective-permute-start | bytes 208904 | tf_op jit(solution)/shard_map/ppermute | solution.py:47
  112.2 1.9 %collective-permute-start.23 = (s32[1,136,128]{2,1,0:T(8,128)S(1)}, s32[1,136,128]{2,1,0:T(8,128)S(1)}, u32[]{:S(2)}, u32[]{:S(2)}) collective-permute-start(s32[1,136,128]{2,1,0:T(8,128)S(1)} %get-tuple-element.46), channel_id=1, source_target_pairs={{0,12},{1,13},{2,14},{3,15},{4,8},{5,9},{6,10},{7,11},{8,4},{9,5},... | collective-permute-start | bytes 208904 | tf_op jit(solution)/shard_map/ppermute | solution.py:47
  114.1 1.4 collective-permute-done.21.refs_0_
  115.5 2.8 %collective-permute-done.23.refs_2_ = s32[1,136,128]{2,1,0:T(8,128)S(1)} collective-permute-done((s32[1,136,128]{2,1,0:T(8,128)S(1)}, s32[1,136,128]{2,1,0:T(8,128)S(1)}, u32[]{:S(2)}, u32[]{:S(2)}) %collective-permute-start.23) | collective-permute-done | bytes 69664 | tf_op jit(solution)/shard_map/ppermute | solution.py:47
  119.0 2.5 %collective-permute-start.25 = (s32[1,136,128]{2,1,0:T(8,128)S(1)}, s32[1,136,128]{2,1,0:T(8,128)S(1)}, u32[]{:S(2)}, u32[]{:S(2)}) collective-permute-start(s32[1,136,128]{2,1,0:T(8,128)S(1)} %get-tuple-element.47.refs_0_), channel_id=1, source_target_pairs={{0,8},{1,9},{2,10},{3,11},{4,12},{5,13},{6,14},{7,15},{8,0},{9,1},... | collective-permute-start | bytes 208904 | tf_op jit(solution)/shard_map/ppermute | solution.py:47
  121.4 1.9 %collective-permute-start.26 = (s32[1,136,128]{2,1,0:T(8,128)S(1)}, s32[1,136,128]{2,1,0:T(8,128)S(1)}, u32[]{:S(2)}, u32[]{:S(2)}) collective-permute-start(s32[1,136,128]{2,1,0:T(8,128)S(1)} %get-tuple-element.47.refs_0_), channel_id=1, source_target_pairs={{0,12},{1,13},{2,14},{3,15},{4,8},{5,9},{6,10},{7,11},{8,4},{9,5},... | collective-permute-start | bytes 208904 | tf_op jit(solution)/shard_map/ppermute | solution.py:47
  124.3 3.3 %collective-permute-done.26.refs_3_ = s32[1,136,128]{2,1,0:T(8,128)S(1)} collective-permute-done((s32[1,136,128]{2,1,0:T(8,128)S(1)}, s32[1,136,128]{2,1,0:T(8,128)S(1)}, u32[]{:S(2)}, u32[]{:S(2)}) %collective-permute-start.26) | collective-permute-done | bytes 69664 | tf_op jit(solution)/shard_map/ppermute | solution.py:47
  128.7 1.5 collective-permute-start.28
  131.1 3.1 %collective-permute-done.27.refs_1_ = s32[4,136,128]{2,1,0:T(8,128)S(1)} collective-permute-done((s32[4,136,128]{2,1,0:T(8,128)S(1)}, s32[4,136,128]{2,1,0:T(8,128)S(1)}, u32[]{:S(2)}, u32[]{:S(2)}) %collective-permute-start.27) | collective-permute-done | bytes 278560 | tf_op jit(solution)/shard_map/ppermute | solution.py:47
  134.2 4.0 %collective-permute-done.28.refs_2_ = s32[4,136,128]{2,1,0:T(8,128)S(1)} collective-permute-done((s32[4,136,128]{2,1,0:T(8,128)S(1)}, s32[4,136,128]{2,1,0:T(8,128)S(1)}, u32[]{:S(2)}, u32[]{:S(2)}) %collective-permute-start.28) | collective-permute-done | bytes 278560 | tf_op jit(solution)/shard_map/ppermute | solution.py:47
  138.2 5.3 %shard_map.61 = (f32[256,256]{1,0:T(8,128)S(1)}, s32[168,128]{1,0:T(8,128)S(1)}) custom-call(s32[1]{0:T(128)S(6)} %and.4.quarter_ref, s32[1]{0:T(128)} %bitcast.place_ref, bf16[1024,2048]{1,0:T(8,128)(2,1)S(1)} %shard_map.51.rows_ref, s32[4,136,128]{2,1,0:T(8,128)S(1)} %shard_map.60.refs_0_, s32[4,136,128]{2,1,0:T(8,128)S(1)} %collective-permute-done.27.refs_1_, ...), custom_call_target="tpu_custom_call" | custom-call | tf_op jit(solution)/shard_map/pallas_call | solution.py:590
  143.6 1.8 %collective-permute-start.31 = (s32[168,128]{1,0:T(8,128)S(1)}, s32[168,128]{1,0:T(8,128)S(1)}, u32[]{:S(2)}, u32[]{:S(2)}) collective-permute-start(s32[168,128]{1,0:T(8,128)S(1)} %get-tuple-element.52.refs_0_), channel_id=1, source_target_pairs={{0,8},{1,9},{2,10},{3,11},{4,12},{5,13},{6,14},{7,15},{8,0},{9,1},... | collective-permute-start | bytes 258056 | tf_op jit(solution)/shard_map/ppermute | solution.py:47
  145.4 2.6 %collective-permute-start.32 = (s32[168,128]{1,0:T(8,128)S(1)}, s32[168,128]{1,0:T(8,128)S(1)}, u32[]{:S(2)}, u32[]{:S(2)}) collective-permute-start(s32[168,128]{1,0:T(8,128)S(1)} %get-tuple-element.52.refs_0_), channel_id=1, source_target_pairs={{0,12},{1,13},{2,14},{3,15},{4,8},{5,9},{6,10},{7,11},{8,4},{9,5},... | collective-permute-start | bytes 258056 | tf_op jit(solution)/shard_map/ppermute | solution.py:47
  148.0 4.9 %shard_map.62.source_ref = f32[256,512]{1,0:T(8,128)S(1)} custom-call(f32[256,256]{1,0:T(8,128)S(1)} %get-tuple-element.49.source_ref.inner_ref), custom_call_target="tpu_custom_call" | custom-call | flops 4000000000 | bytes 4194304 | tf_op jit(solution)/shard_map/pallas_call | solution.py:614
  155.6 1.5 collective-permute-start.35
  157.1 2.8 %shard_map.63.factor_ref = f32[256,512]{1,0:T(8,128)S(1)} custom-call(f32[256,512]{1,0:T(8,128)S(1)} %shard_map.62.source_ref), custom_call_target="tpu_custom_call" | custom-call | flops 4000000000 | bytes 4194304 | tf_op jit(solution)/shard_map/pallas_call | solution.py:614
  163.3 1.1 shard_map.67
  (48 shorter events, 19.5 us)
Async XLA Ops:
  3.2 5.6 %collective-permute-start = (s32[1,136,128]{2,1,0:T(8,128)}, s32[1,136,128]{2,1,0:T(8,128)S(1)}, u32[]{:S(2)}, u32[]{:S(2)}) collective-permute-start(s32[1,136,128]{2,1,0:T(8,128)} %shard_map.50.after_ref.refs_0_), channel_id=1, source_target_pairs={{0,4},{1,5},{2,6},{3,7},{4,0},{5,1},{6,2},{7,3},{8,12},{9,13},{10,... | collective-permute-start | bytes 208904 | tf_op jit(solution)/shard_map/ppermute | solution.py:47
  6.2 7.8 %collective-permute-start.1 = (s32[1,136,128]{2,1,0:T(8,128)}, s32[1,136,128]{2,1,0:T(8,128)S(1)}, u32[]{:S(2)}, u32[]{:S(2)}) collective-permute-start(s32[1,136,128]{2,1,0:T(8,128)} %shard_map.50.after_ref.refs_0_), channel_id=1, source_target_pairs={{0,8},{1,9},{2,10},{3,11},{4,12},{5,13},{6,14},{7,15},{8,0},{9,1},... | collective-permute-start | bytes 208904 | tf_op jit(solution)/shard_map/ppermute | solution.py:47
  8.8 6.4 %collective-permute-start.2 = (s32[1,136,128]{2,1,0:T(8,128)}, s32[1,136,128]{2,1,0:T(8,128)S(1)}, u32[]{:S(2)}, u32[]{:S(2)}) collective-permute-start(s32[1,136,128]{2,1,0:T(8,128)} %shard_map.50.after_ref.refs_0_), channel_id=1, source_target_pairs={{0,12},{1,13},{2,14},{3,15},{4,8},{5,9},{6,10},{7,11},{8,4},{9,5},... | collective-permute-start | bytes 208904 | tf_op jit(solution)/shard_map/ppermute | solution.py:47
  15.2 0.9 copy-start
  16.1 9.6 %collective-permute-start.3 = (s32[4,136,128]{2,1,0:T(8,128)S(1)}, s32[4,136,128]{2,1,0:T(8,128)S(1)}, u32[]{:S(2)}, u32[]{:S(2)}) collective-permute-start(s32[4,136,128]{2,1,0:T(8,128)S(1)} %shard_map.52.refs_0_), channel_id=1, source_target_pairs={{0,1},{1,0},{2,3},{3,2},{4,5},{5,4},{6,7},{7,6},{8,9},{9,8},{10,11... | collective-permute-start | bytes 835592 | tf_op jit(solution)/shard_map/ppermute | solution.py:47
  17.7 12.3 %collective-permute-start.4 = (s32[4,136,128]{2,1,0:T(8,128)S(1)}, s32[4,136,128]{2,1,0:T(8,128)S(1)}, u32[]{:S(2)}, u32[]{:S(2)}) collective-permute-start(s32[4,136,128]{2,1,0:T(8,128)S(1)} %shard_map.52.refs_0_), channel_id=1, source_target_pairs={{0,2},{1,3},{2,0},{3,1},{4,6},{5,7},{6,4},{7,5},{8,10},{9,11},{10,... | collective-permute-start | bytes 835592 | tf_op jit(solution)/shard_map/ppermute | solution.py:47
  19.2 10.8 %collective-permute-start.5 = (s32[4,136,128]{2,1,0:T(8,128)S(1)}, s32[4,136,128]{2,1,0:T(8,128)S(1)}, u32[]{:S(2)}, u32[]{:S(2)}) collective-permute-start(s32[4,136,128]{2,1,0:T(8,128)S(1)} %shard_map.52.refs_0_), channel_id=1, source_target_pairs={{0,3},{1,2},{2,1},{3,0},{4,7},{5,6},{6,5},{7,4},{8,11},{9,10},{10,... | collective-permute-start | bytes 835592 | tf_op jit(solution)/shard_map/ppermute | solution.py:47
  19.7 2.2 %copy-start.1 = (bf16[1,1024,2048]{2,1,0:T(8,128)(2,1)S(1)}, bf16[1,1024,2048]{2,1,0:T(8,128)(2,1)}, u32[]{:S(2)}) copy-start(bf16[1,1024,2048]{2,1,0:T(8,128)(2,1)} %param.3) | copy-start | bytes 12582916
  36.6 8.2 %collective-permute-start.6 = (s32[4,136,128]{2,1,0:T(8,128)S(1)}, s32[4,136,128]{2,1,0:T(8,128)S(1)}, u32[]{:S(2)}, u32[]{:S(2)}) collective-permute-start(s32[4,136,128]{2,1,0:T(8,128)S(1)} %get-tuple-element.31), channel_id=1, source_target_pairs={{0,1},{1,0},{2,3},{3,2},{4,5},{5,4},{6,7},{7,6},{8,9},{9,8},{10,11... | collective-permute-start | bytes 835592 | tf_op jit(solution)/shard_map/ppermute | solution.py:47
  37.9 11.1 %collective-permute-start.7 = (s32[4,136,128]{2,1,0:T(8,128)S(1)}, s32[4,136,128]{2,1,0:T(8,128)S(1)}, u32[]{:S(2)}, u32[]{:S(2)}) collective-permute-start(s32[4,136,128]{2,1,0:T(8,128)S(1)} %get-tuple-element.32), channel_id=1, source_target_pairs={{0,2},{1,3},{2,0},{3,1},{4,6},{5,7},{6,4},{7,5},{8,10},{9,11},{10,... | collective-permute-start | bytes 835592 | tf_op jit(solution)/shard_map/ppermute | solution.py:47
  38.7 10.2 %collective-permute-start.8 = (s32[4,136,128]{2,1,0:T(8,128)S(1)}, s32[4,136,128]{2,1,0:T(8,128)S(1)}, u32[]{:S(2)}, u32[]{:S(2)}) collective-permute-start(s32[4,136,128]{2,1,0:T(8,128)S(1)} %get-tuple-element.33), channel_id=1, source_target_pairs={{0,3},{1,2},{2,1},{3,0},{4,7},{5,6},{6,5},{7,4},{8,11},{9,10},{10,... | collective-permute-start | bytes 835592 | tf_op jit(solution)/shard_map/ppermute | solution.py:47
  50.0 6.4 %collective-permute-start.10 = (s32[1,136,128]{2,1,0:T(8,128)S(1)}, s32[1,136,128]{2,1,0:T(8,128)S(1)}, u32[]{:S(2)}, u32[]{:S(2)}) collective-permute-start(s32[1,136,128]{2,1,0:T(8,128)S(1)} %get-tuple-element.36), channel_id=1, source_target_pairs={{0,8},{1,9},{2,10},{3,11},{4,12},{5,13},{6,14},{7,15},{8,0},{9,1},... | collective-permute-start | bytes 208904 | tf_op jit(solution)/shard_map/ppermute | solution.py:47
  53.4 6.8 %collective-permute-start.11 = (s32[1,136,128]{2,1,0:T(8,128)S(1)}, s32[1,136,128]{2,1,0:T(8,128)S(1)}, u32[]{:S(2)}, u32[]{:S(2)}) collective-permute-start(s32[1,136,128]{2,1,0:T(8,128)S(1)} %get-tuple-element.37), channel_id=1, source_target_pairs={{0,12},{1,13},{2,14},{3,15},{4,8},{5,9},{6,10},{7,11},{8,4},{9,5},... | collective-permute-start | bytes 208904 | tf_op jit(solution)/shard_map/ppermute | solution.py:47
  54.0 6.3 %collective-permute-start.9 = (s32[1,136,128]{2,1,0:T(8,128)S(1)}, s32[1,136,128]{2,1,0:T(8,128)S(1)}, u32[]{:S(2)}, u32[]{:S(2)}) collective-permute-start(s32[1,136,128]{2,1,0:T(8,128)S(1)} %get-tuple-element.35), channel_id=1, source_target_pairs={{0,4},{1,5},{2,6},{3,7},{4,0},{5,1},{6,2},{7,3},{8,12},{9,13},{10,... | collective-permute-start | bytes 208904 | tf_op jit(solution)/shard_map/ppermute | solution.py:47
  61.3 4.4 %collective-permute-start.12 = (s32[1,136,128]{2,1,0:T(8,128)S(1)}, s32[1,136,128]{2,1,0:T(8,128)S(1)}, u32[]{:S(2)}, u32[]{:S(2)}) collective-permute-start(s32[1,136,128]{2,1,0:T(8,128)S(1)} %get-tuple-element.38.refs_0_), channel_id=1, source_target_pairs={{0,4},{1,5},{2,6},{3,7},{4,0},{5,1},{6,2},{7,3},{8,12},{9,13},{10,... | collective-permute-start | bytes 208904 | tf_op jit(solution)/shard_map/ppermute | solution.py:47
  61.7 5.2 %collective-permute-start.13 = (s32[1,136,128]{2,1,0:T(8,128)S(1)}, s32[1,136,128]{2,1,0:T(8,128)S(1)}, u32[]{:S(2)}, u32[]{:S(2)}) collective-permute-start(s32[1,136,128]{2,1,0:T(8,128)S(1)} %get-tuple-element.38.refs_0_), channel_id=1, source_target_pairs={{0,8},{1,9},{2,10},{3,11},{4,12},{5,13},{6,14},{7,15},{8,0},{9,1},... | collective-permute-start | bytes 208904 | tf_op jit(solution)/shard_map/ppermute | solution.py:47
  63.8 6.1 %collective-permute-start.14 = (s32[1,136,128]{2,1,0:T(8,128)S(1)}, s32[1,136,128]{2,1,0:T(8,128)S(1)}, u32[]{:S(2)}, u32[]{:S(2)}) collective-permute-start(s32[1,136,128]{2,1,0:T(8,128)S(1)} %get-tuple-element.38.refs_0_), channel_id=1, source_target_pairs={{0,12},{1,13},{2,14},{3,15},{4,8},{5,9},{6,10},{7,11},{8,4},{9,5},... | collective-permute-start | bytes 208904 | tf_op jit(solution)/shard_map/ppermute | solution.py:47
  69.9 6.6 %collective-permute-start.15 = (s32[4,136,128]{2,1,0:T(8,128)S(1)}, s32[4,136,128]{2,1,0:T(8,128)S(1)}, u32[]{:S(2)}, u32[]{:S(2)}) collective-permute-start(s32[4,136,128]{2,1,0:T(8,128)S(1)} %shard_map.56.refs_0_), channel_id=1, source_target_pairs={{0,1},{1,0},{2,3},{3,2},{4,5},{5,4},{6,7},{7,6},{8,9},{9,8},{10,11... | collective-permute-start | bytes 835592 | tf_op jit(solution)/shard_map/ppermute | solution.py:47
  71.1 9.5 %collective-permute-start.16 = (s32[4,136,128]{2,1,0:T(8,128)S(1)}, s32[4,136,128]{2,1,0:T(8,128)S(1)}, u32[]{:S(2)}, u32[]{:S(2)}) collective-permute-start(s32[4,136,128]{2,1,0:T(8,128)S(1)} %shard_map.56.refs_0_), channel_id=1, source_target_pairs={{0,2},{1,3},{2,0},{3,1},{4,6},{5,7},{6,4},{7,5},{8,10},{9,11},{10,... | collective-permute-start | bytes 835592 | tf_op jit(solution)/shard_map/ppermute | solution.py:47
  72.6 8.0 %collective-permute-start.17 = (s32[4,136,128]{2,1,0:T(8,128)S(1)}, s32[4,136,128]{2,1,0:T(8,128)S(1)}, u32[]{:S(2)}, u32[]{:S(2)}) collective-permute-start(s32[4,136,128]{2,1,0:T(8,128)S(1)} %shard_map.56.refs_0_), channel_id=1, source_target_pairs={{0,3},{1,2},{2,1},{3,0},{4,7},{5,6},{6,5},{7,4},{8,11},{9,10},{10,... | collective-permute-start | bytes 835592 | tf_op jit(solution)/shard_map/ppermute | solution.py:47
  98.0 6.6 %collective-permute-start.18 = (s32[4,136,128]{2,1,0:T(8,128)S(1)}, s32[4,136,128]{2,1,0:T(8,128)S(1)}, u32[]{:S(2)}, u32[]{:S(2)}) collective-permute-start(s32[4,136,128]{2,1,0:T(8,128)S(1)} %get-tuple-element.40), channel_id=1, source_target_pairs={{0,1},{1,0},{2,3},{3,2},{4,5},{5,4},{6,7},{7,6},{8,9},{9,8},{10,11... | collective-permute-start | bytes 835592 | tf_op jit(solution)/shard_map/ppermute | solution.py:47
  99.0 8.1 %collective-permute-start.19 = (s32[4,136,128]{2,1,0:T(8,128)S(1)}, s32[4,136,128]{2,1,0:T(8,128)S(1)}, u32[]{:S(2)}, u32[]{:S(2)}) collective-permute-start(s32[4,136,128]{2,1,0:T(8,128)S(1)} %get-tuple-element.41), channel_id=1, source_target_pairs={{0,2},{1,3},{2,0},{3,1},{4,6},{5,7},{6,4},{7,5},{8,10},{9,11},{10,... | collective-permute-start | bytes 835592 | tf_op jit(solution)/shard_map/ppermute | solution.py:47
  100.1 8.5 %collective-permute-start.20 = (s32[4,136,128]{2,1,0:T(8,128)S(1)}, s32[4,136,128]{2,1,0:T(8,128)S(1)}, u32[]{:S(2)}, u32[]{:S(2)}) collective-permute-start(s32[4,136,128]{2,1,0:T(8,128)S(1)} %get-tuple-element.42), channel_id=1, source_target_pairs={{0,3},{1,2},{2,1},{3,0},{4,7},{5,6},{6,5},{7,4},{8,11},{9,10},{10,... | collective-permute-start | bytes 835592 | tf_op jit(solution)/shard_map/ppermute | solution.py:47
  109.7 5.9 %collective-permute-start.21 = (s32[1,136,128]{2,1,0:T(8,128)S(1)}, s32[1,136,128]{2,1,0:T(8,128)S(1)}, u32[]{:S(2)}, u32[]{:S(2)}) collective-permute-start(s32[1,136,128]{2,1,0:T(8,128)S(1)} %get-tuple-element.44), channel_id=1, source_target_pairs={{0,4},{1,5},{2,6},{3,7},{4,0},{5,1},{6,2},{7,3},{8,12},{9,13},{10,... | collective-permute-start | bytes 208904 | tf_op jit(solution)/shard_map/ppermute | solution.py:47
  109.7 5.8 %collective-permute-start.22 = (s32[1,136,128]{2,1,0:T(8,128)S(1)}, s32[1,136,128]{2,1,0:T(8,128)S(1)}, u32[]{:S(2)}, u32[]{:S(2)}) collective-permute-start(s32[1,136,128]{2,1,0:T(8,128)S(1)} %get-tuple-element.45), channel_id=1, source_target_pairs={{0,8},{1,9},{2,10},{3,11},{4,12},{5,13},{6,14},{7,15},{8,0},{9,1},... | collective-permute-start | bytes 208904 | tf_op jit(solution)/shard_map/ppermute | solution.py:47
  112.2 6.1 %collective-permute-start.23 = (s32[1,136,128]{2,1,0:T(8,128)S(1)}, s32[1,136,128]{2,1,0:T(8,128)S(1)}, u32[]{:S(2)}, u32[]{:S(2)}) collective-permute-start(s32[1,136,128]{2,1,0:T(8,128)S(1)} %get-tuple-element.46), channel_id=1, source_target_pairs={{0,12},{1,13},{2,14},{3,15},{4,8},{5,9},{6,10},{7,11},{8,4},{9,5},... | collective-permute-start | bytes 208904 | tf_op jit(solution)/shard_map/ppermute | solution.py:47
  118.9 4.5 %collective-permute-start.24 = (s32[1,136,128]{2,1,0:T(8,128)S(1)}, s32[1,136,128]{2,1,0:T(8,128)S(1)}, u32[]{:S(2)}, u32[]{:S(2)}) collective-permute-start(s32[1,136,128]{2,1,0:T(8,128)S(1)} %get-tuple-element.47.refs_0_), channel_id=1, source_target_pairs={{0,4},{1,5},{2,6},{3,7},{4,0},{5,1},{6,2},{7,3},{8,12},{9,13},{10,... | collective-permute-start | bytes 208904 | tf_op jit(solution)/shard_map/ppermute | solution.py:47
  119.0 5.3 %collective-permute-start.25 = (s32[1,136,128]{2,1,0:T(8,128)S(1)}, s32[1,136,128]{2,1,0:T(8,128)S(1)}, u32[]{:S(2)}, u32[]{:S(2)}) collective-permute-start(s32[1,136,128]{2,1,0:T(8,128)S(1)} %get-tuple-element.47.refs_0_), channel_id=1, source_target_pairs={{0,8},{1,9},{2,10},{3,11},{4,12},{5,13},{6,14},{7,15},{8,0},{9,1},... | collective-permute-start | bytes 208904 | tf_op jit(solution)/shard_map/ppermute | solution.py:47
  121.4 6.1 %collective-permute-start.26 = (s32[1,136,128]{2,1,0:T(8,128)S(1)}, s32[1,136,128]{2,1,0:T(8,128)S(1)}, u32[]{:S(2)}, u32[]{:S(2)}) collective-permute-start(s32[1,136,128]{2,1,0:T(8,128)S(1)} %get-tuple-element.47.refs_0_), channel_id=1, source_target_pairs={{0,12},{1,13},{2,14},{3,15},{4,8},{5,9},{6,10},{7,11},{8,4},{9,5},... | collective-permute-start | bytes 208904 | tf_op jit(solution)/shard_map/ppermute | solution.py:47
  127.6 6.6 %collective-permute-start.27 = (s32[4,136,128]{2,1,0:T(8,128)S(1)}, s32[4,136,128]{2,1,0:T(8,128)S(1)}, u32[]{:S(2)}, u32[]{:S(2)}) collective-permute-start(s32[4,136,128]{2,1,0:T(8,128)S(1)} %shard_map.60.refs_0_), channel_id=1, source_target_pairs={{0,1},{1,0},{2,3},{3,2},{4,5},{5,4},{6,7},{7,6},{8,9},{9,8},{10,11... | collective-permute-start | bytes 835592 | tf_op jit(solution)/shard_map/ppermute | solution.py:47
  128.7 9.5 %collective-permute-start.28 = (s32[4,136,128]{2,1,0:T(8,128)S(1)}, s32[4,136,128]{2,1,0:T(8,128)S(1)}, u32[]{:S(2)}, u32[]{:S(2)}) collective-permute-start(s32[4,136,128]{2,1,0:T(8,128)S(1)} %shard_map.60.refs_0_), channel_id=1, source_target_pairs={{0,2},{1,3},{2,0},{3,1},{4,6},{5,7},{6,4},{7,5},{8,10},{9,11},{10,... | collective-permute-start | bytes 835592 | tf_op jit(solution)/shard_map/ppermute | solution.py:47
  130.2 8.0 %collective-permute-start.29 = (s32[4,136,128]{2,1,0:T(8,128)S(1)}, s32[4,136,128]{2,1,0:T(8,128)S(1)}, u32[]{:S(2)}, u32[]{:S(2)}) collective-permute-start(s32[4,136,128]{2,1,0:T(8,128)S(1)} %shard_map.60.refs_0_), channel_id=1, source_target_pairs={{0,3},{1,2},{2,1},{3,0},{4,7},{5,6},{6,5},{7,4},{8,11},{9,10},{10,... | collective-permute-start | bytes 835592 | tf_op jit(solution)/shard_map/ppermute | solution.py:47
  143.5 9.4 %collective-permute-start.30 = (s32[168,128]{1,0:T(8,128)S(1)}, s32[168,128]{1,0:T(8,128)S(1)}, u32[]{:S(2)}, u32[]{:S(2)}) collective-permute-start(s32[168,128]{1,0:T(8,128)S(1)} %get-tuple-element.52.refs_0_), channel_id=1, source_target_pairs={{0,4},{1,5},{2,6},{3,7},{4,0},{5,1},{6,2},{7,3},{8,12},{9,13},{10,... | collective-permute-start | bytes 258056 | tf_op jit(solution)/shard_map/ppermute | solution.py:47
  143.6 9.3 %collective-permute-start.31 = (s32[168,128]{1,0:T(8,128)S(1)}, s32[168,128]{1,0:T(8,128)S(1)}, u32[]{:S(2)}, u32[]{:S(2)}) collective-permute-start(s32[168,128]{1,0:T(8,128)S(1)} %get-tuple-element.52.refs_0_), channel_id=1, source_target_pairs={{0,8},{1,9},{2,10},{3,11},{4,12},{5,13},{6,14},{7,15},{8,0},{9,1},... | collective-permute-start | bytes 258056 | tf_op jit(solution)/shard_map/ppermute | solution.py:47
  145.4 7.5 %collective-permute-start.32 = (s32[168,128]{1,0:T(8,128)S(1)}, s32[168,128]{1,0:T(8,128)S(1)}, u32[]{:S(2)}, u32[]{:S(2)}) collective-permute-start(s32[168,128]{1,0:T(8,128)S(1)} %get-tuple-element.52.refs_0_), channel_id=1, source_target_pairs={{0,12},{1,13},{2,14},{3,15},{4,8},{5,9},{6,10},{7,11},{8,4},{9,5},... | collective-permute-start | bytes 258056 | tf_op jit(solution)/shard_map/ppermute | solution.py:47
  153.6 6.3 %collective-permute-start.33 = (s32[168,128]{1,0:T(8,128)S(1)}, s32[168,128]{1,0:T(8,128)S(1)}, u32[]{:S(2)}, u32[]{:S(2)}) collective-permute-start(s32[168,128]{1,0:T(8,128)S(1)} %shard_map.65.refs_0_), channel_id=1, source_target_pairs={{0,1},{1,0},{2,3},{3,2},{4,5},{5,4},{6,7},{7,6},{8,9},{9,8},{10,11... | collective-permute-start | bytes 258056 | tf_op jit(solution)/shard_map/ppermute | solution.py:47
  154.6 5.3 %collective-permute-start.34 = (s32[168,128]{1,0:T(8,128)S(1)}, s32[168,128]{1,0:T(8,128)S(1)}, u32[]{:S(2)}, u32[]{:S(2)}) collective-permute-start(s32[168,128]{1,0:T(8,128)S(1)} %shard_map.65.refs_0_), channel_id=1, source_target_pairs={{0,2},{1,3},{2,0},{3,1},{4,6},{5,7},{6,4},{7,5},{8,10},{9,11},{10,... | collective-permute-start | bytes 258056 | tf_op jit(solution)/shard_map/ppermute | solution.py:47
  155.6 5.4 %collective-permute-start.35 = (s32[168,128]{1,0:T(8,128)S(1)}, s32[168,128]{1,0:T(8,128)S(1)}, u32[]{:S(2)}, u32[]{:S(2)}) collective-permute-start(s32[168,128]{1,0:T(8,128)S(1)} %shard_map.65.refs_0_), channel_id=1, source_target_pairs={{0,3},{1,2},{2,1},{3,0},{4,7},{5,6},{6,5},{7,4},{8,11},{9,10},{10,... | collective-permute-start | bytes 258056 | tf_op jit(solution)/shard_map/ppermute | solution.py:47
  162.1 1.2 collective-permute-start.36

commit v7 on v6

--- a/solution.py
+++ b/solution.py
@@ -740,7 +740,7 @@
     quarter = jnp.bitwise_and(place, 3)
     inner, *parts = project(dosages, quarter, place, gather(message), order, size)
     if len(parts) == 1:
-        cut = size // 2 + size // 8
+        cut = size // 2
         beside = [lambda _: second_factor(inner, 0, cut), lambda work: second_factor(work, cut, size)]
         parts, second = sum_messages(parts[0], groups, beside)
     else:

time: 165 us -> 164 us (level)
  no operation moved by 1% of the time
where the time goes in v7:
time: 164 us
  waiting for transfers between devices  63.3 us (39%)
  starting transfers between devices  48.8 us (30%)
  Pallas kernels  46.9 us (29%)
  local copies, waits for them, and re-layouts  3.07 us (2%)
    ppermute x36, waiting for transfers between devices, exchange(): lax.ppermute(value, 'smp', [(device, device ^ offset) for device in range...  63.3 us
    ppermute x36, starting transfers between devices, exchange(): lax.ppermute(value, 'smp', [(device, device ^ offset) for device in range...  48.7 us
    pallas_call x2, Pallas kernels, apply_samples(): pl.pallas_call(functools.partial(apply_kernel, order, normalise, scale, l...  24 us
    pallas_call x2, Pallas kernels, second_factor(): pl.pallas_call(functools.partial(second_kernel, first, last), in_specs=[v...  7.66 us
    pallas_call x1, Pallas kernels, project(): pl.pallas_call(functools.partial(project_kernel, order, len(gathered), co...  5.27 us
    pallas_call x4, Pallas kernels, combine(): pl.pallas_call(functools.partial(combine_kernel, len(arrived), parts), in...  3.71 us
  transfers between devices with their start and end apart: 37, of which 23 were waited for; matrix products, arithmetic and copies ran while one was open for 0% of the time, Pallas kernels for 6%

profile of v7, /device:TPU:0, one launch (start us, length us, event | category | flops | bytes accessed | tf_op | source)
XLA Modules:
  0.0 163.5 jit_solution(7314727980558331125)
XLA Ops:
  1.3 1.9 %shard_map.50.after_ref.refs_0_ = s32[1,136,128]{2,1,0:T(8,128)} custom-call(s32[1]{0:T(128)} %bitcast.place_ref, s32[1]{0:T(128)S(6)} %copy.5.size_ref, f32[128,256]{1,0:T(8,128)} %bitcast.9), custom_call_target="tpu_custom_call" | custom-call | tf_op jit(solution)/shard_map/pallas_call | solution.py:208
  3.2 3.0 %collective-permute-start = (s32[1,136,128]{2,1,0:T(8,128)}, s32[1,136,128]{2,1,0:T(8,128)S(1)}, u32[]{:S(2)}, u32[]{:S(2)}) collective-permute-start(s32[1,136,128]{2,1,0:T(8,128)} %shard_map.50.after_ref.refs_0_), channel_id=1, source_target_pairs={{0,4},{1,5},{2,6},{3,7},{4,0},{5,1},{6,2},{7,3},{8,12},{9,13},{10,... | collective-permute-start | bytes 208904 | tf_op jit(solution)/shard_map/ppermute | solution.py:47
  6.2 2.6 %collective-permute-start.1 = (s32[1,136,128]{2,1,0:T(8,128)}, s32[1,136,128]{2,1,0:T(8,128)S(1)}, u32[]{:S(2)}, u32[]{:S(2)}) collective-permute-start(s32[1,136,128]{2,1,0:T(8,128)} %shard_map.50.after_ref.refs_0_), channel_id=1, source_target_pairs={{0,8},{1,9},{2,10},{3,11},{4,12},{5,13},{6,14},{7,15},{8,0},{9,1},... | collective-permute-start | bytes 208904 | tf_op jit(solution)/shard_map/ppermute | solution.py:47
  8.8 5.2 %collective-permute-done.1.refs_2_ = s32[1,136,128]{2,1,0:T(8,128)S(1)} collective-permute-done((s32[1,136,128]{2,1,0:T(8,128)}, s32[1,136,128]{2,1,0:T(8,128)S(1)}, u32[]{:S(2)}, u32[]{:S(2)}) %collective-permute-start.1) | collective-permute-done | bytes 69664 | tf_op jit(solution)/shard_map/ppermute | solution.py:47
  14.0 1.3 collective-permute-done.2.refs_3_
  16.1 1.6 collective-permute-start.3
  17.7 1.5 collective-permute-start.4
  19.7 2.2 %copy-done.1 = bf16[1,1024,2048]{2,1,0:T(8,128)(2,1)S(1)} copy-done((bf16[1,1024,2048]{2,1,0:T(8,128)(2,1)S(1)}, bf16[1,1024,2048]{2,1,0:T(8,128)(2,1)}, u32[]{:S(2)}) %copy-start.1) | copy-done | bytes 4194328
  22.2 3.6 %collective-permute-done.3.refs_1_ = s32[4,136,128]{2,1,0:T(8,128)S(1)} collective-permute-done((s32[4,136,128]{2,1,0:T(8,128)S(1)}, s32[4,136,128]{2,1,0:T(8,128)S(1)}, u32[]{:S(2)}, u32[]{:S(2)}) %collective-permute-start.3) | collective-permute-done | bytes 278560 | tf_op jit(solution)/shard_map/ppermute | solution.py:47
  25.8 4.2 %collective-permute-done.4.refs_2_ = s32[4,136,128]{2,1,0:T(8,128)S(1)} collective-permute-done((s32[4,136,128]{2,1,0:T(8,128)S(1)}, s32[4,136,128]{2,1,0:T(8,128)S(1)}, u32[]{:S(2)}, u32[]{:S(2)}) %collective-permute-start.4) | collective-permute-done | bytes 278560 | tf_op jit(solution)/shard_map/ppermute | solution.py:47
  30.0 6.6 %shard_map.53 = (f32[4,256,128]{2,1,0:T(8,128)S(1)}, s32[4,136,128]{2,1,0:T(8,128)S(1)}, s32[4,136,128]{2,1,0:T(8,128)S(1)}, s32[4,136,128]{2,1,0:T(8,128)S(1)}) custom-call(s32[1]{0:T(128)} %bitcast.place_ref, s32[1]{0:T(128)S(6)} %copy.5.size_ref, bf16[1024,2048]{1,0:T(8,128)(2,1)S(1)} %shard_map.51.rows_ref, s32[4,136,128]{2,1,0:T(8,128)S(1)} %shard_map.52.refs_0_, ...), custom_call_target="tpu_custom_call" | custom-call | tf_op jit(solution)/shard_map/pallas_call | solution.py:335
  36.6 1.3 collective-permute-start.6
  38.7 1.4 collective-permute-start.8
  40.2 4.6 %collective-permute-done.6.refs_0_ = s32[4,136,128]{2,1,0:T(8,128)S(1)} collective-permute-done((s32[4,136,128]{2,1,0:T(8,128)S(1)}, s32[4,136,128]{2,1,0:T(8,128)S(1)}, u32[]{:S(2)}, u32[]{:S(2)}) %collective-permute-start.6) | collective-permute-done | bytes 278560 | tf_op jit(solution)/shard_map/ppermute | solution.py:47
  44.8 4.1 %collective-permute-done.7.refs_1_ = s32[4,136,128]{2,1,0:T(8,128)S(1)} collective-permute-done((s32[4,136,128]{2,1,0:T(8,128)S(1)}, s32[4,136,128]{2,1,0:T(8,128)S(1)}, u32[]{:S(2)}, u32[]{:S(2)}) %collective-permute-start.7) | collective-permute-done | bytes 278560 | tf_op jit(solution)/shard_map/ppermute | solution.py:47
  50.0 3.4 %collective-permute-start.10 = (s32[1,136,128]{2,1,0:T(8,128)S(1)}, s32[1,136,128]{2,1,0:T(8,128)S(1)}, u32[]{:S(2)}, u32[]{:S(2)}) collective-permute-start(s32[1,136,128]{2,1,0:T(8,128)S(1)} %get-tuple-element.36), channel_id=1, source_target_pairs={{0,8},{1,9},{2,10},{3,11},{4,12},{5,13},{6,14},{7,15},{8,0},{9,1},... | collective-permute-start | bytes 208904 | tf_op jit(solution)/shard_map/ppermute | solution.py:47
  54.1 2.4 %collective-permute-done.10.refs_1_ = s32[1,136,128]{2,1,0:T(8,128)S(1)} collective-permute-done((s32[1,136,128]{2,1,0:T(8,128)S(1)}, s32[1,136,128]{2,1,0:T(8,128)S(1)}, u32[]{:S(2)}, u32[]{:S(2)}) %collective-permute-start.10) | collective-permute-done | bytes 69664 | tf_op jit(solution)/shard_map/ppermute | solution.py:47
  56.5 3.8 %collective-permute-done.11.refs_2_ = s32[1,136,128]{2,1,0:T(8,128)S(1)} collective-permute-done((s32[1,136,128]{2,1,0:T(8,128)S(1)}, s32[1,136,128]{2,1,0:T(8,128)S(1)}, u32[]{:S(2)}, u32[]{:S(2)}) %collective-permute-start.11) | collective-permute-done | bytes 69664 | tf_op jit(solution)/shard_map/ppermute | solution.py:47
  61.7 2.1 %collective-permute-start.13 = (s32[1,136,128]{2,1,0:T(8,128)S(1)}, s32[1,136,128]{2,1,0:T(8,128)S(1)}, u32[]{:S(2)}, u32[]{:S(2)}) collective-permute-start(s32[1,136,128]{2,1,0:T(8,128)S(1)} %get-tuple-element.38.refs_0_), channel_id=1, source_target_pairs={{0,8},{1,9},{2,10},{3,11},{4,12},{5,13},{6,14},{7,15},{8,0},{9,1},... | collective-permute-start | bytes 208904 | tf_op jit(solution)/shard_map/ppermute | solution.py:47
  63.8 1.8 %collective-permute-start.14 = (s32[1,136,128]{2,1,0:T(8,128)S(1)}, s32[1,136,128]{2,1,0:T(8,128)S(1)}, u32[]{:S(2)}, u32[]{:S(2)}) collective-permute-start(s32[1,136,128]{2,1,0:T(8,128)S(1)} %get-tuple-element.38.refs_0_), channel_id=1, source_target_pairs={{0,12},{1,13},{2,14},{3,15},{4,8},{5,9},{6,10},{7,11},{8,4},{9,5},... | collective-permute-start | bytes 208904 | tf_op jit(solution)/shard_map/ppermute | solution.py:47
  65.6 1.3 collective-permute-done.13.refs_2_
  66.9 3.0 %collective-permute-done.14.refs_3_ = s32[1,136,128]{2,1,0:T(8,128)S(1)} collective-permute-done((s32[1,136,128]{2,1,0:T(8,128)S(1)}, s32[1,136,128]{2,1,0:T(8,128)S(1)}, u32[]{:S(2)}, u32[]{:S(2)}) %collective-permute-start.14) | collective-permute-done | bytes 69664 | tf_op jit(solution)/shard_map/ppermute | solution.py:47
  69.9 1.2 collective-permute-start.15
  71.1 1.5 collective-permute-start.16
  73.5 3.1 %collective-permute-done.15.refs_1_ = s32[4,136,128]{2,1,0:T(8,128)S(1)} collective-permute-done((s32[4,136,128]{2,1,0:T(8,128)S(1)}, s32[4,136,128]{2,1,0:T(8,128)S(1)}, u32[]{:S(2)}, u32[]{:S(2)}) %collective-permute-start.15) | collective-permute-done | bytes 278560 | tf_op jit(solution)/shard_map/ppermute | solution.py:47
  76.5 4.1 %collective-permute-done.16.refs_2_ = s32[4,136,128]{2,1,0:T(8,128)S(1)} collective-permute-done((s32[4,136,128]{2,1,0:T(8,128)S(1)}, s32[4,136,128]{2,1,0:T(8,128)S(1)}, u32[]{:S(2)}, u32[]{:S(2)}) %collective-permute-start.16) | collective-permute-done | bytes 278560 | tf_op jit(solution)/shard_map/ppermute | solution.py:47
  80.6 17.4 %shard_map.57 = (f32[4,256,128]{2,1,0:T(8,128)S(1)}, s32[4,136,128]{2,1,0:T(8,128)S(1)}, s32[4,136,128]{2,1,0:T(8,128)S(1)}, s32[4,136,128]{2,1,0:T(8,128)S(1)}) custom-call(s32[1]{0:T(128)} %bitcast.place_ref, s32[1]{0:T(128)S(6)} %copy.5.size_ref, bf16[1024,2048]{1,0:T(8,128)(2,1)S(1)} %shard_map.51.rows_ref, s32[4,136,128]{2,1,0:T(8,128)S(1)} %shard_map.56.refs_0_, ...), custom_call_target="tpu_custom_call" | custom-call | tf_op jit(solution)/shard_map/pallas_call | solution.py:335
  100.1 1.5 collective-permute-start.20
  101.6 3.1 %collective-permute-done.18.refs_0_ = s32[4,136,128]{2,1,0:T(8,128)S(1)} collective-permute-done((s32[4,136,128]{2,1,0:T(8,128)S(1)}, s32[4,136,128]{2,1,0:T(8,128)S(1)}, u32[]{:S(2)}, u32[]{:S(2)}) %collective-permute-start.18) | collective-permute-done | bytes 278560 | tf_op jit(solution)/shard_map/ppermute | solution.py:47
  104.6 2.5 %collective-permute-done.19.refs_1_ = s32[4,136,128]{2,1,0:T(8,128)S(1)} collective-permute-done((s32[4,136,128]{2,1,0:T(8,128)S(1)}, s32[4,136,128]{2,1,0:T(8,128)S(1)}, u32[]{:S(2)}, u32[]{:S(2)}) %collective-permute-start.19) | collective-permute-done | bytes 278560 | tf_op jit(solution)/shard_map/ppermute | solution.py:47
  107.1 1.4 collective-permute-done.20.refs_2_
  109.7 2.5 %collective-permute-start.22 = (s32[1,136,128]{2,1,0:T(8,128)S(1)}, s32[1,136,128]{2,1,0:T(8,128)S(1)}, u32[]{:S(2)}, u32[]{:S(2)}) collective-permute-start(s32[1,136,128]{2,1,0:T(8,128)S(1)} %get-tuple-element.45), channel_id=1, source_target_pairs={{0,8},{1,9},{2,10},{3,11},{4,12},{5,13},{6,14},{7,15},{8,0},{9,1},... | collective-permute-start | bytes 208904 | tf_op jit(solution)/shard_map/ppermute | solution.py:47
  112.2 1.9 %collective-permute-start.23 = (s32[1,136,128]{2,1,0:T(8,128)S(1)}, s32[1,136,128]{2,1,0:T(8,128)S(1)}, u32[]{:S(2)}, u32[]{:S(2)}) collective-permute-start(s32[1,136,128]{2,1,0:T(8,128)S(1)} %get-tuple-element.46), channel_id=1, source_target_pairs={{0,12},{1,13},{2,14},{3,15},{4,8},{5,9},{6,10},{7,11},{8,4},{9,5},... | collective-permute-start | bytes 208904 | tf_op jit(solution)/shard_map/ppermute | solution.py:47
  114.1 1.4 collective-permute-done.21.refs_0_
  115.5 2.8 %collective-permute-done.23.refs_2_ = s32[1,136,128]{2,1,0:T(8,128)S(1)} collective-permute-done((s32[1,136,128]{2,1,0:T(8,128)S(1)}, s32[1,136,128]{2,1,0:T(8,128)S(1)}, u32[]{:S(2)}, u32[]{:S(2)}) %collective-permute-start.23) | collective-permute-done | bytes 69664 | tf_op jit(solution)/shard_map/ppermute | solution.py:47
  119.0 2.5 %collective-permute-start.25 = (s32[1,136,128]{2,1,0:T(8,128)S(1)}, s32[1,136,128]{2,1,0:T(8,128)S(1)}, u32[]{:S(2)}, u32[]{:S(2)}) collective-permute-start(s32[1,136,128]{2,1,0:T(8,128)S(1)} %get-tuple-element.47.refs_0_), channel_id=1, source_target_pairs={{0,8},{1,9},{2,10},{3,11},{4,12},{5,13},{6,14},{7,15},{8,0},{9,1},... | collective-permute-start | bytes 208904 | tf_op jit(solution)/shard_map/ppermute | solution.py:47
  121.4 1.9 %collective-permute-start.26 = (s32[1,136,128]{2,1,0:T(8,128)S(1)}, s32[1,136,128]{2,1,0:T(8,128)S(1)}, u32[]{:S(2)}, u32[]{:S(2)}) collective-permute-start(s32[1,136,128]{2,1,0:T(8,128)S(1)} %get-tuple-element.47.refs_0_), channel_id=1, source_target_pairs={{0,12},{1,13},{2,14},{3,15},{4,8},{5,9},{6,10},{7,11},{8,4},{9,5},... | collective-permute-start | bytes 208904 | tf_op jit(solution)/shard_map/ppermute | solution.py:47
  124.3 3.3 %collective-permute-done.26.refs_3_ = s32[1,136,128]{2,1,0:T(8,128)S(1)} collective-permute-done((s32[1,136,128]{2,1,0:T(8,128)S(1)}, s32[1,136,128]{2,1,0:T(8,128)S(1)}, u32[]{:S(2)}, u32[]{:S(2)}) %collective-permute-start.26) | collective-permute-done | bytes 69664 | tf_op jit(solution)/shard_map/ppermute | solution.py:47
  128.7 1.5 collective-permute-start.28
  131.1 3.1 %collective-permute-done.27.refs_1_ = s32[4,136,128]{2,1,0:T(8,128)S(1)} collective-permute-done((s32[4,136,128]{2,1,0:T(8,128)S(1)}, s32[4,136,128]{2,1,0:T(8,128)S(1)}, u32[]{:S(2)}, u32[]{:S(2)}) %collective-permute-start.27) | collective-permute-done | bytes 278560 | tf_op jit(solution)/shard_map/ppermute | solution.py:47
  134.2 4.0 %collective-permute-done.28.refs_2_ = s32[4,136,128]{2,1,0:T(8,128)S(1)} collective-permute-done((s32[4,136,128]{2,1,0:T(8,128)S(1)}, s32[4,136,128]{2,1,0:T(8,128)S(1)}, u32[]{:S(2)}, u32[]{:S(2)}) %collective-permute-start.28) | collective-permute-done | bytes 278560 | tf_op jit(solution)/shard_map/ppermute | solution.py:47
  138.2 5.3 %shard_map.61 = (f32[256,256]{1,0:T(8,128)S(1)}, s32[168,128]{1,0:T(8,128)S(1)}) custom-call(s32[1]{0:T(128)S(6)} %and.4.quarter_ref, s32[1]{0:T(128)} %bitcast.place_ref, bf16[1024,2048]{1,0:T(8,128)(2,1)S(1)} %shard_map.51.rows_ref, s32[4,136,128]{2,1,0:T(8,128)S(1)} %shard_map.60.refs_0_, s32[4,136,128]{2,1,0:T(8,128)S(1)} %collective-permute-done.27.refs_1_, ...), custom_call_target="tpu_custom_call" | custom-call | tf_op jit(solution)/shard_map/pallas_call | solution.py:590
  143.6 1.8 %collective-permute-start.31 = (s32[168,128]{1,0:T(8,128)S(1)}, s32[168,128]{1,0:T(8,128)S(1)}, u32[]{:S(2)}, u32[]{:S(2)}) collective-permute-start(s32[168,128]{1,0:T(8,128)S(1)} %get-tuple-element.52.refs_0_), channel_id=1, source_target_pairs={{0,8},{1,9},{2,10},{3,11},{4,12},{5,13},{6,14},{7,15},{8,0},{9,1},... | collective-permute-start | bytes 258056 | tf_op jit(solution)/shard_map/ppermute | solution.py:47
  145.4 2.6 %collective-permute-start.32 = (s32[168,128]{1,0:T(8,128)S(1)}, s32[168,128]{1,0:T(8,128)S(1)}, u32[]{:S(2)}, u32[]{:S(2)}) collective-permute-start(s32[168,128]{1,0:T(8,128)S(1)} %get-tuple-element.52.refs_0_), channel_id=1, source_target_pairs={{0,12},{1,13},{2,14},{3,15},{4,8},{5,9},{6,10},{7,11},{8,4},{9,5},... | collective-permute-start | bytes 258056 | tf_op jit(solution)/shard_map/ppermute | solution.py:47
  148.0 4.0 %shard_map.62.source_ref = f32[256,512]{1,0:T(8,128)S(1)} custom-call(f32[256,256]{1,0:T(8,128)S(1)} %get-tuple-element.49.source_ref.inner_ref), custom_call_target="tpu_custom_call" | custom-call | flops 4000000000 | bytes 4194304 | tf_op jit(solution)/shard_map/pallas_call | solution.py:614
  152.6 1.4 collective-permute-start.33
  154.7 1.5 collective-permute-start.35
  156.2 3.7 %shard_map.63.factor_ref = f32[256,512]{1,0:T(8,128)S(1)} custom-call(f32[256,512]{1,0:T(8,128)S(1)} %shard_map.62.source_ref), custom_call_target="tpu_custom_call" | custom-call | flops 4000000000 | bytes 4194304 | tf_op jit(solution)/shard_map/pallas_call | solution.py:614
  (48 shorter events, 18.3 us)
Async XLA Ops:
  3.2 5.6 %collective-permute-start = (s32[1,136,128]{2,1,0:T(8,128)}, s32[1,136,128]{2,1,0:T(8,128)S(1)}, u32[]{:S(2)}, u32[]{:S(2)}) collective-permute-start(s32[1,136,128]{2,1,0:T(8,128)} %shard_map.50.after_ref.refs_0_), channel_id=1, source_target_pairs={{0,4},{1,5},{2,6},{3,7},{4,0},{5,1},{6,2},{7,3},{8,12},{9,13},{10,... | collective-permute-start | bytes 208904 | tf_op jit(solution)/shard_map/ppermute | solution.py:47
  6.2 7.8 %collective-permute-start.1 = (s32[1,136,128]{2,1,0:T(8,128)}, s32[1,136,128]{2,1,0:T(8,128)S(1)}, u32[]{:S(2)}, u32[]{:S(2)}) collective-permute-start(s32[1,136,128]{2,1,0:T(8,128)} %shard_map.50.after_ref.refs_0_), channel_id=1, source_target_pairs={{0,8},{1,9},{2,10},{3,11},{4,12},{5,13},{6,14},{7,15},{8,0},{9,1},... | collective-permute-start | bytes 208904 | tf_op jit(solution)/shard_map/ppermute | solution.py:47
  8.8 6.4 %collective-permute-start.2 = (s32[1,136,128]{2,1,0:T(8,128)}, s32[1,136,128]{2,1,0:T(8,128)S(1)}, u32[]{:S(2)}, u32[]{:S(2)}) collective-permute-start(s32[1,136,128]{2,1,0:T(8,128)} %shard_map.50.after_ref.refs_0_), channel_id=1, source_target_pairs={{0,12},{1,13},{2,14},{3,15},{4,8},{5,9},{6,10},{7,11},{8,4},{9,5},... | collective-permute-start | bytes 208904 | tf_op jit(solution)/shard_map/ppermute | solution.py:47
  15.2 0.9 copy-start
  16.1 9.6 %collective-permute-start.3 = (s32[4,136,128]{2,1,0:T(8,128)S(1)}, s32[4,136,128]{2,1,0:T(8,128)S(1)}, u32[]{:S(2)}, u32[]{:S(2)}) collective-permute-start(s32[4,136,128]{2,1,0:T(8,128)S(1)} %shard_map.52.refs_0_), channel_id=1, source_target_pairs={{0,1},{1,0},{2,3},{3,2},{4,5},{5,4},{6,7},{7,6},{8,9},{9,8},{10,11... | collective-permute-start | bytes 835592 | tf_op jit(solution)/shard_map/ppermute | solution.py:47
  17.7 12.3 %collective-permute-start.4 = (s32[4,136,128]{2,1,0:T(8,128)S(1)}, s32[4,136,128]{2,1,0:T(8,128)S(1)}, u32[]{:S(2)}, u32[]{:S(2)}) collective-permute-start(s32[4,136,128]{2,1,0:T(8,128)S(1)} %shard_map.52.refs_0_), channel_id=1, source_target_pairs={{0,2},{1,3},{2,0},{3,1},{4,6},{5,7},{6,4},{7,5},{8,10},{9,11},{10,... | collective-permute-start | bytes 835592 | tf_op jit(solution)/shard_map/ppermute | solution.py:47
  19.2 10.8 %collective-permute-start.5 = (s32[4,136,128]{2,1,0:T(8,128)S(1)}, s32[4,136,128]{2,1,0:T(8,128)S(1)}, u32[]{:S(2)}, u32[]{:S(2)}) collective-permute-start(s32[4,136,128]{2,1,0:T(8,128)S(1)} %shard_map.52.refs_0_), channel_id=1, source_target_pairs={{0,3},{1,2},{2,1},{3,0},{4,7},{5,6},{6,5},{7,4},{8,11},{9,10},{10,... | collective-permute-start | bytes 835592 | tf_op jit(solution)/shard_map/ppermute | solution.py:47
  19.7 2.2 %copy-start.1 = (bf16[1,1024,2048]{2,1,0:T(8,128)(2,1)S(1)}, bf16[1,1024,2048]{2,1,0:T(8,128)(2,1)}, u32[]{:S(2)}) copy-start(bf16[1,1024,2048]{2,1,0:T(8,128)(2,1)} %param.3) | copy-start | bytes 12582916
  36.6 8.2 %collective-permute-start.6 = (s32[4,136,128]{2,1,0:T(8,128)S(1)}, s32[4,136,128]{2,1,0:T(8,128)S(1)}, u32[]{:S(2)}, u32[]{:S(2)}) collective-permute-start(s32[4,136,128]{2,1,0:T(8,128)S(1)} %get-tuple-element.31), channel_id=1, source_target_pairs={{0,1},{1,0},{2,3},{3,2},{4,5},{5,4},{6,7},{7,6},{8,9},{9,8},{10,11... | collective-permute-start | bytes 835592 | tf_op jit(solution)/shard_map/ppermute | solution.py:47
  37.9 11.1 %collective-permute-start.7 = (s32[4,136,128]{2,1,0:T(8,128)S(1)}, s32[4,136,128]{2,1,0:T(8,128)S(1)}, u32[]{:S(2)}, u32[]{:S(2)}) collective-permute-start(s32[4,136,128]{2,1,0:T(8,128)S(1)} %get-tuple-element.32), channel_id=1, source_target_pairs={{0,2},{1,3},{2,0},{3,1},{4,6},{5,7},{6,4},{7,5},{8,10},{9,11},{10,... | collective-permute-start | bytes 835592 | tf_op jit(solution)/shard_map/ppermute | solution.py:47
  38.7 10.2 %collective-permute-start.8 = (s32[4,136,128]{2,1,0:T(8,128)S(1)}, s32[4,136,128]{2,1,0:T(8,128)S(1)}, u32[]{:S(2)}, u32[]{:S(2)}) collective-permute-start(s32[4,136,128]{2,1,0:T(8,128)S(1)} %get-tuple-element.33), channel_id=1, source_target_pairs={{0,3},{1,2},{2,1},{3,0},{4,7},{5,6},{6,5},{7,4},{8,11},{9,10},{10,... | collective-permute-start | bytes 835592 | tf_op jit(solution)/shard_map/ppermute | solution.py:47
  50.0 6.4 %collective-permute-start.10 = (s32[1,136,128]{2,1,0:T(8,128)S(1)}, s32[1,136,128]{2,1,0:T(8,128)S(1)}, u32[]{:S(2)}, u32[]{:S(2)}) collective-permute-start(s32[1,136,128]{2,1,0:T(8,128)S(1)} %get-tuple-element.36), channel_id=1, source_target_pairs={{0,8},{1,9},{2,10},{3,11},{4,12},{5,13},{6,14},{7,15},{8,0},{9,1},... | collective-permute-start | bytes 208904 | tf_op jit(solution)/shard_map/ppermute | solution.py:47
  53.4 6.8 %collective-permute-start.11 = (s32[1,136,128]{2,1,0:T(8,128)S(1)}, s32[1,136,128]{2,1,0:T(8,128)S(1)}, u32[]{:S(2)}, u32[]{:S(2)}) collective-permute-start(s32[1,136,128]{2,1,0:T(8,128)S(1)} %get-tuple-element.37), channel_id=1, source_target_pairs={{0,12},{1,13},{2,14},{3,15},{4,8},{5,9},{6,10},{7,11},{8,4},{9,5},... | collective-permute-start | bytes 208904 | tf_op jit(solution)/shard_map/ppermute | solution.py:47
  54.0 6.3 %collective-permute-start.9 = (s32[1,136,128]{2,1,0:T(8,128)S(1)}, s32[1,136,128]{2,1,0:T(8,128)S(1)}, u32[]{:S(2)}, u32[]{:S(2)}) collective-permute-start(s32[1,136,128]{2,1,0:T(8,128)S(1)} %get-tuple-element.35), channel_id=1, source_target_pairs={{0,4},{1,5},{2,6},{3,7},{4,0},{5,1},{6,2},{7,3},{8,12},{9,13},{10,... | collective-permute-start | bytes 208904 | tf_op jit(solution)/shard_map/ppermute | solution.py:47
  61.3 4.4 %collective-permute-start.12 = (s32[1,136,128]{2,1,0:T(8,128)S(1)}, s32[1,136,128]{2,1,0:T(8,128)S(1)}, u32[]{:S(2)}, u32[]{:S(2)}) collective-permute-start(s32[1,136,128]{2,1,0:T(8,128)S(1)} %get-tuple-element.38.refs_0_), channel_id=1, source_target_pairs={{0,4},{1,5},{2,6},{3,7},{4,0},{5,1},{6,2},{7,3},{8,12},{9,13},{10,... | collective-permute-start | bytes 208904 | tf_op jit(solution)/shard_map/ppermute | solution.py:47
  61.7 5.2 %collective-permute-start.13 = (s32[1,136,128]{2,1,0:T(8,128)S(1)}, s32[1,136,128]{2,1,0:T(8,128)S(1)}, u32[]{:S(2)}, u32[]{:S(2)}) collective-permute-start(s32[1,136,128]{2,1,0:T(8,128)S(1)} %get-tuple-element.38.refs_0_), channel_id=1, source_target_pairs={{0,8},{1,9},{2,10},{3,11},{4,12},{5,13},{6,14},{7,15},{8,0},{9,1},... | collective-permute-start | bytes 208904 | tf_op jit(solution)/shard_map/ppermute | solution.py:47
  63.8 6.1 %collective-permute-start.14 = (s32[1,136,128]{2,1,0:T(8,128)S(1)}, s32[1,136,128]{2,1,0:T(8,128)S(1)}, u32[]{:S(2)}, u32[]{:S(2)}) collective-permute-start(s32[1,136,128]{2,1,0:T(8,128)S(1)} %get-tuple-element.38.refs_0_), channel_id=1, source_target_pairs={{0,12},{1,13},{2,14},{3,15},{4,8},{5,9},{6,10},{7,11},{8,4},{9,5},... | collective-permute-start | bytes 208904 | tf_op jit(solution)/shard_map/ppermute | solution.py:47
  69.9 6.6 %collective-permute-start.15 = (s32[4,136,128]{2,1,0:T(8,128)S(1)}, s32[4,136,128]{2,1,0:T(8,128)S(1)}, u32[]{:S(2)}, u32[]{:S(2)}) collective-permute-start(s32[4,136,128]{2,1,0:T(8,128)S(1)} %shard_map.56.refs_0_), channel_id=1, source_target_pairs={{0,1},{1,0},{2,3},{3,2},{4,5},{5,4},{6,7},{7,6},{8,9},{9,8},{10,11... | collective-permute-start | bytes 835592 | tf_op jit(solution)/shard_map/ppermute | solution.py:47
  71.1 9.5 %collective-permute-start.16 = (s32[4,136,128]{2,1,0:T(8,128)S(1)}, s32[4,136,128]{2,1,0:T(8,128)S(1)}, u32[]{:S(2)}, u32[]{:S(2)}) collective-permute-start(s32[4,136,128]{2,1,0:T(8,128)S(1)} %shard_map.56.refs_0_), channel_id=1, source_target_pairs={{0,2},{1,3},{2,0},{3,1},{4,6},{5,7},{6,4},{7,5},{8,10},{9,11},{10,... | collective-permute-start | bytes 835592 | tf_op jit(solution)/shard_map/ppermute | solution.py:47
  72.6 8.0 %collective-permute-start.17 = (s32[4,136,128]{2,1,0:T(8,128)S(1)}, s32[4,136,128]{2,1,0:T(8,128)S(1)}, u32[]{:S(2)}, u32[]{:S(2)}) collective-permute-start(s32[4,136,128]{2,1,0:T(8,128)S(1)} %shard_map.56.refs_0_), channel_id=1, source_target_pairs={{0,3},{1,2},{2,1},{3,0},{4,7},{5,6},{6,5},{7,4},{8,11},{9,10},{10,... | collective-permute-start | bytes 835592 | tf_op jit(solution)/shard_map/ppermute | solution.py:47
  98.0 6.6 %collective-permute-start.18 = (s32[4,136,128]{2,1,0:T(8,128)S(1)}, s32[4,136,128]{2,1,0:T(8,128)S(1)}, u32[]{:S(2)}, u32[]{:S(2)}) collective-permute-start(s32[4,136,128]{2,1,0:T(8,128)S(1)} %get-tuple-element.40), channel_id=1, source_target_pairs={{0,1},{1,0},{2,3},{3,2},{4,5},{5,4},{6,7},{7,6},{8,9},{9,8},{10,11... | collective-permute-start | bytes 835592 | tf_op jit(solution)/shard_map/ppermute | solution.py:47
  99.0 8.1 %collective-permute-start.19 = (s32[4,136,128]{2,1,0:T(8,128)S(1)}, s32[4,136,128]{2,1,0:T(8,128)S(1)}, u32[]{:S(2)}, u32[]{:S(2)}) collective-permute-start(s32[4,136,128]{2,1,0:T(8,128)S(1)} %get-tuple-element.41), channel_id=1, source_target_pairs={{0,2},{1,3},{2,0},{3,1},{4,6},{5,7},{6,4},{7,5},{8,10},{9,11},{10,... | collective-permute-start | bytes 835592 | tf_op jit(solution)/shard_map/ppermute | solution.py:47
  100.1 8.5 %collective-permute-start.20 = (s32[4,136,128]{2,1,0:T(8,128)S(1)}, s32[4,136,128]{2,1,0:T(8,128)S(1)}, u32[]{:S(2)}, u32[]{:S(2)}) collective-permute-start(s32[4,136,128]{2,1,0:T(8,128)S(1)} %get-tuple-element.42), channel_id=1, source_target_pairs={{0,3},{1,2},{2,1},{3,0},{4,7},{5,6},{6,5},{7,4},{8,11},{9,10},{10,... | collective-permute-start | bytes 835592 | tf_op jit(solution)/shard_map/ppermute | solution.py:47
  109.7 5.9 %collective-permute-start.21 = (s32[1,136,128]{2,1,0:T(8,128)S(1)}, s32[1,136,128]{2,1,0:T(8,128)S(1)}, u32[]{:S(2)}, u32[]{:S(2)}) collective-permute-start(s32[1,136,128]{2,1,0:T(8,128)S(1)} %get-tuple-element.44), channel_id=1, source_target_pairs={{0,4},{1,5},{2,6},{3,7},{4,0},{5,1},{6,2},{7,3},{8,12},{9,13},{10,... | collective-permute-start | bytes 208904 | tf_op jit(solution)/shard_map/ppermute | solution.py:47
  109.7 5.8 %collective-permute-start.22 = (s32[1,136,128]{2,1,0:T(8,128)S(1)}, s32[1,136,128]{2,1,0:T(8,128)S(1)}, u32[]{:S(2)}, u32[]{:S(2)}) collective-permute-start(s32[1,136,128]{2,1,0:T(8,128)S(1)} %get-tuple-element.45), channel_id=1, source_target_pairs={{0,8},{1,9},{2,10},{3,11},{4,12},{5,13},{6,14},{7,15},{8,0},{9,1},... | collective-permute-start | bytes 208904 | tf_op jit(solution)/shard_map/ppermute | solution.py:47
  112.2 6.1 %collective-permute-start.23 = (s32[1,136,128]{2,1,0:T(8,128)S(1)}, s32[1,136,128]{2,1,0:T(8,128)S(1)}, u32[]{:S(2)}, u32[]{:S(2)}) collective-permute-start(s32[1,136,128]{2,1,0:T(8,128)S(1)} %get-tuple-element.46), channel_id=1, source_target_pairs={{0,12},{1,13},{2,14},{3,15},{4,8},{5,9},{6,10},{7,11},{8,4},{9,5},... | collective-permute-start | bytes 208904 | tf_op jit(solution)/shard_map/ppermute | solution.py:47
  118.9 4.5 %collective-permute-start.24 = (s32[1,136,128]{2,1,0:T(8,128)S(1)}, s32[1,136,128]{2,1,0:T(8,128)S(1)}, u32[]{:S(2)}, u32[]{:S(2)}) collective-permute-start(s32[1,136,128]{2,1,0:T(8,128)S(1)} %get-tuple-element.47.refs_0_), channel_id=1, source_target_pairs={{0,4},{1,5},{2,6},{3,7},{4,0},{5,1},{6,2},{7,3},{8,12},{9,13},{10,... | collective-permute-start | bytes 208904 | tf_op jit(solution)/shard_map/ppermute | solution.py:47
  119.0 5.3 %collective-permute-start.25 = (s32[1,136,128]{2,1,0:T(8,128)S(1)}, s32[1,136,128]{2,1,0:T(8,128)S(1)}, u32[]{:S(2)}, u32[]{:S(2)}) collective-permute-start(s32[1,136,128]{2,1,0:T(8,128)S(1)} %get-tuple-element.47.refs_0_), channel_id=1, source_target_pairs={{0,8},{1,9},{2,10},{3,11},{4,12},{5,13},{6,14},{7,15},{8,0},{9,1},... | collective-permute-start | bytes 208904 | tf_op jit(solution)/shard_map/ppermute | solution.py:47
  121.4 6.1 %collective-permute-start.26 = (s32[1,136,128]{2,1,0:T(8,128)S(1)}, s32[1,136,128]{2,1,0:T(8,128)S(1)}, u32[]{:S(2)}, u32[]{:S(2)}) collective-permute-start(s32[1,136,128]{2,1,0:T(8,128)S(1)} %get-tuple-element.47.refs_0_), channel_id=1, source_target_pairs={{0,12},{1,13},{2,14},{3,15},{4,8},{5,9},{6,10},{7,11},{8,4},{9,5},... | collective-permute-start | bytes 208904 | tf_op jit(solution)/shard_map/ppermute | solution.py:47
  127.6 6.6 %collective-permute-start.27 = (s32[4,136,128]{2,1,0:T(8,128)S(1)}, s32[4,136,128]{2,1,0:T(8,128)S(1)}, u32[]{:S(2)}, u32[]{:S(2)}) collective-permute-start(s32[4,136,128]{2,1,0:T(8,128)S(1)} %shard_map.60.refs_0_), channel_id=1, source_target_pairs={{0,1},{1,0},{2,3},{3,2},{4,5},{5,4},{6,7},{7,6},{8,9},{9,8},{10,11... | collective-permute-start | bytes 835592 | tf_op jit(solution)/shard_map/ppermute | solution.py:47
  128.7 9.5 %collective-permute-start.28 = (s32[4,136,128]{2,1,0:T(8,128)S(1)}, s32[4,136,128]{2,1,0:T(8,128)S(1)}, u32[]{:S(2)}, u32[]{:S(2)}) collective-permute-start(s32[4,136,128]{2,1,0:T(8,128)S(1)} %shard_map.60.refs_0_), channel_id=1, source_target_pairs={{0,2},{1,3},{2,0},{3,1},{4,6},{5,7},{6,4},{7,5},{8,10},{9,11},{10,... | collective-permute-start | bytes 835592 | tf_op jit(solution)/shard_map/ppermute | solution.py:47
  130.2 8.0 %collective-permute-start.29 = (s32[4,136,128]{2,1,0:T(8,128)S(1)}, s32[4,136,128]{2,1,0:T(8,128)S(1)}, u32[]{:S(2)}, u32[]{:S(2)}) collective-permute-start(s32[4,136,128]{2,1,0:T(8,128)S(1)} %shard_map.60.refs_0_), channel_id=1, source_target_pairs={{0,3},{1,2},{2,1},{3,0},{4,7},{5,6},{6,5},{7,4},{8,11},{9,10},{10,... | collective-permute-start | bytes 835592 | tf_op jit(solution)/shard_map/ppermute | solution.py:47
  143.5 8.4 %collective-permute-start.30 = (s32[168,128]{1,0:T(8,128)S(1)}, s32[168,128]{1,0:T(8,128)S(1)}, u32[]{:S(2)}, u32[]{:S(2)}) collective-permute-start(s32[168,128]{1,0:T(8,128)S(1)} %get-tuple-element.52.refs_0_), channel_id=1, source_target_pairs={{0,4},{1,5},{2,6},{3,7},{4,0},{5,1},{6,2},{7,3},{8,12},{9,13},{10,... | collective-permute-start | bytes 258056 | tf_op jit(solution)/shard_map/ppermute | solution.py:47
  143.6 8.4 %collective-permute-start.31 = (s32[168,128]{1,0:T(8,128)S(1)}, s32[168,128]{1,0:T(8,128)S(1)}, u32[]{:S(2)}, u32[]{:S(2)}) collective-permute-start(s32[168,128]{1,0:T(8,128)S(1)} %get-tuple-element.52.refs_0_), channel_id=1, source_target_pairs={{0,8},{1,9},{2,10},{3,11},{4,12},{5,13},{6,14},{7,15},{8,0},{9,1},... | collective-permute-start | bytes 258056 | tf_op jit(solution)/shard_map/ppermute | solution.py:47
  145.4 6.6 %collective-permute-start.32 = (s32[168,128]{1,0:T(8,128)S(1)}, s32[168,128]{1,0:T(8,128)S(1)}, u32[]{:S(2)}, u32[]{:S(2)}) collective-permute-start(s32[168,128]{1,0:T(8,128)S(1)} %get-tuple-element.52.refs_0_), channel_id=1, source_target_pairs={{0,12},{1,13},{2,14},{3,15},{4,8},{5,9},{6,10},{7,11},{8,4},{9,5},... | collective-permute-start | bytes 258056 | tf_op jit(solution)/shard_map/ppermute | solution.py:47
  152.6 7.3 %collective-permute-start.33 = (s32[168,128]{1,0:T(8,128)S(1)}, s32[168,128]{1,0:T(8,128)S(1)}, u32[]{:S(2)}, u32[]{:S(2)}) collective-permute-start(s32[168,128]{1,0:T(8,128)S(1)} %shard_map.65.refs_0_), channel_id=1, source_target_pairs={{0,1},{1,0},{2,3},{3,2},{4,5},{5,4},{6,7},{7,6},{8,9},{9,8},{10,11... | collective-permute-start | bytes 258056 | tf_op jit(solution)/shard_map/ppermute | solution.py:47
  154.0 5.9 %collective-permute-start.34 = (s32[168,128]{1,0:T(8,128)S(1)}, s32[168,128]{1,0:T(8,128)S(1)}, u32[]{:S(2)}, u32[]{:S(2)}) collective-permute-start(s32[168,128]{1,0:T(8,128)S(1)} %shard_map.65.refs_0_), channel_id=1, source_target_pairs={{0,2},{1,3},{2,0},{3,1},{4,6},{5,7},{6,4},{7,5},{8,10},{9,11},{10,... | collective-permute-start | bytes 258056 | tf_op jit(solution)/shard_map/ppermute | solution.py:47
  154.7 5.4 %collective-permute-start.35 = (s32[168,128]{1,0:T(8,128)S(1)}, s32[168,128]{1,0:T(8,128)S(1)}, u32[]{:S(2)}, u32[]{:S(2)}) collective-permute-start(s32[168,128]{1,0:T(8,128)S(1)} %shard_map.65.refs_0_), channel_id=1, source_target_pairs={{0,3},{1,2},{2,1},{3,0},{4,7},{5,6},{6,5},{7,4},{8,11},{9,10},{10,... | collective-permute-start | bytes 258056 | tf_op jit(solution)/shard_map/ppermute | solution.py:47
  161.2 1.2 collective-permute-start.36

commit v8 on v7

--- a/solution.py
+++ b/solution.py
@@ -297,7 +297,7 @@
     if normalise:
         start_factor(work_ref, rows_inner(value))
         inverse_factor(work_ref, size, PANEL)
-        value = jnp.dot(finish_factor(work_ref), value, precision=HIGHEST, preferred_element_type=jnp.float32)
+        value = wide_dot(finish_factor(work_ref), value)
     split = jnp.concatenate(split_pieces(value, PIECES), axis=0)
     image = rows_dot(split, rows_ref[...])
     image = sum(image[piece * size : (piece + 1) * size] for piece in range(PIECES)) * scale
@@ -432,6 +432,19 @@
     return lax.dot_general(left, right, (((1,), (1,)), ((), ())), preferred_element_type=jnp.float32)
 
 
+def wide_dot(left, right, across=False):
+    rows = left.shape[0]
+    pieces = split_pieces(left, 3)
+    total = None
+    for place, part in enumerate(split_pieces(right, 3)):
+        used = jnp.concatenate(pieces[: 3 - place], axis=0)
+        product = rows_dot(used, part) if across else jnp.dot(used, part, preferred_element_type=jnp.float32)
+        for piece in reversed(range(3 - place)):
+            term = product[piece * rows : (piece + 1) * rows]
+            total = term if total is None else total + term
+    return total
+
+
 def rows_inner(value):
     high, middle, low = split_pieces(value, 3)
     mixed = rows_dot(high, middle) + rows_dot(high, low)
@@ -622,7 +635,7 @@
 
 
 def basis_kernel(gain, factor_ref, own_ref, out_ref):
-    own = jnp.dot(finish_factor(factor_ref), own_ref[...], precision=HIGHEST, preferred_element_type=jnp.float32)
+    own = wide_dot(finish_factor(factor_ref), own_ref[...])
     out_ref[...] = own.T * gain
 
 
@@ -651,7 +664,7 @@
     across, down = diagonal_of(inner_ref[...])
     cross = unfold_symmetric(folded, diagonal) * ((down * lax.rsqrt(down)) * (across * lax.rsqrt(across)))
     factor = finish_factor(factor_ref)
-    half = scale * jnp.dot(factor, cross, precision=HIGHEST, preferred_element_type=jnp.float32)
+    half = scale * wide_dot(factor, cross)
     half_ref[...] = half
     trace_ref[...] = jnp.broadcast_to(jnp.sum(half * factor), trace_ref.shape)
 
@@ -674,13 +687,7 @@
 def finish_kernel(gain, half_ref, factor_ref, *refs):
     traces, out_ref = refs[:-1], refs[-1]
     total = sum(trace[:1, :1] for trace in traces)
-    whole = lax.dot_general(
-        half_ref[...],
-        finish_factor(factor_ref),
-        (((1,), (1,)), ((), ())),
-        precision=HIGHEST,
-        preferred_element_type=jnp.float32,
-    )
+    whole = wide_dot(half_ref[...], finish_factor(factor_ref), across=True)
     out_ref[...] = whole * (gain / total)
 
 

time: 164 us -> 163 us (level)
  transfers between devices with their start and end apart: 37 -> 37, of which waited for: 23 -> 22; matrix products, arithmetic and copies ran while one was open for 0% -> 0% of each run, Pallas kernels for 6% -> 6%
where the time goes in v8:
time: 163 us
  waiting for transfers between devices  63.4 us (39%)
  starting transfers between devices  48.8 us (30%)
  Pallas kernels  46.6 us (29%)
  local copies, waits for them, and re-layouts  3.07 us (2%)
    ppermute x36, waiting for transfers between devices, exchange(): lax.ppermute(value, 'smp', [(device, device ^ offset) for device in range...  63.3 us
    ppermute x36, starting transfers between devices, exchange(): lax.ppermute(value, 'smp', [(device, device ^ offset) for device in range...  48.7 us
    pallas_call x2, Pallas kernels, apply_samples(): pl.pallas_call(functools.partial(apply_kernel, order, normalise, scale, l...  23.9 us
    pallas_call x2, Pallas kernels, second_factor(): pl.pallas_call(functools.partial(second_kernel, first, last), in_specs=[v...  7.66 us
    pallas_call x1, Pallas kernels, project(): pl.pallas_call(functools.partial(project_kernel, order, len(gathered), co...  5.03 us
    pallas_call x4, Pallas kernels, combine(): pl.pallas_call(functools.partial(combine_kernel, len(arrived), parts), in...  3.71 us
  transfers between devices with their start and end apart: 37, of which 22 were waited for; matrix products, arithmetic and copies ran while one was open for 0% of the time, Pallas kernels for 6%

profile of v8, /device:TPU:0, one launch (start us, length us, event | category | flops | bytes accessed | tf_op | source)
XLA Modules:
  0.0 163.3 jit_solution(18034604868278048552)
XLA Ops:
  1.3 1.9 %shard_map.50.after_ref.refs_0_ = s32[1,136,128]{2,1,0:T(8,128)} custom-call(s32[1]{0:T(128)} %bitcast.place_ref, s32[1]{0:T(128)S(6)} %copy.5.size_ref, f32[128,256]{1,0:T(8,128)} %bitcast.9), custom_call_target="tpu_custom_call" | custom-call | tf_op jit(solution)/shard_map/pallas_call | solution.py:208
  3.2 3.0 %collective-permute-start = (s32[1,136,128]{2,1,0:T(8,128)}, s32[1,136,128]{2,1,0:T(8,128)S(1)}, u32[]{:S(2)}, u32[]{:S(2)}) collective-permute-start(s32[1,136,128]{2,1,0:T(8,128)} %shard_map.50.after_ref.refs_0_), channel_id=1, source_target_pairs={{0,4},{1,5},{2,6},{3,7},{4,0},{5,1},{6,2},{7,3},{8,12},{9,13},{10,... | collective-permute-start | bytes 208904 | tf_op jit(solution)/shard_map/ppermute | solution.py:47
  6.2 2.6 %collective-permute-start.1 = (s32[1,136,128]{2,1,0:T(8,128)}, s32[1,136,128]{2,1,0:T(8,128)S(1)}, u32[]{:S(2)}, u32[]{:S(2)}) collective-permute-start(s32[1,136,128]{2,1,0:T(8,128)} %shard_map.50.after_ref.refs_0_), channel_id=1, source_target_pairs={{0,8},{1,9},{2,10},{3,11},{4,12},{5,13},{6,14},{7,15},{8,0},{9,1},... | collective-permute-start | bytes 208904 | tf_op jit(solution)/shard_map/ppermute | solution.py:47
  8.8 5.2 %collective-permute-done.1.refs_2_ = s32[1,136,128]{2,1,0:T(8,128)S(1)} collective-permute-done((s32[1,136,128]{2,1,0:T(8,128)}, s32[1,136,128]{2,1,0:T(8,128)S(1)}, u32[]{:S(2)}, u32[]{:S(2)}) %collective-permute-start.1) | collective-permute-done | bytes 69664 | tf_op jit(solution)/shard_map/ppermute | solution.py:47
  14.0 1.3 collective-permute-done.2.refs_3_
  16.1 1.6 collective-permute-start.3
  17.7 1.5 collective-permute-start.4
  19.7 2.2 %copy-done.1 = bf16[1,1024,2048]{2,1,0:T(8,128)(2,1)S(1)} copy-done((bf16[1,1024,2048]{2,1,0:T(8,128)(2,1)S(1)}, bf16[1,1024,2048]{2,1,0:T(8,128)(2,1)}, u32[]{:S(2)}) %copy-start.1) | copy-done | bytes 4194328
  22.2 3.6 %collective-permute-done.3.refs_1_ = s32[4,136,128]{2,1,0:T(8,128)S(1)} collective-permute-done((s32[4,136,128]{2,1,0:T(8,128)S(1)}, s32[4,136,128]{2,1,0:T(8,128)S(1)}, u32[]{:S(2)}, u32[]{:S(2)}) %collective-permute-start.3) | collective-permute-done | bytes 278560 | tf_op jit(solution)/shard_map/ppermute | solution.py:47
  25.8 4.2 %collective-permute-done.4.refs_2_ = s32[4,136,128]{2,1,0:T(8,128)S(1)} collective-permute-done((s32[4,136,128]{2,1,0:T(8,128)S(1)}, s32[4,136,128]{2,1,0:T(8,128)S(1)}, u32[]{:S(2)}, u32[]{:S(2)}) %collective-permute-start.4) | collective-permute-done | bytes 278560 | tf_op jit(solution)/shard_map/ppermute | solution.py:47
  30.0 6.6 %shard_map.53 = (f32[4,256,128]{2,1,0:T(8,128)S(1)}, s32[4,136,128]{2,1,0:T(8,128)S(1)}, s32[4,136,128]{2,1,0:T(8,128)S(1)}, s32[4,136,128]{2,1,0:T(8,128)S(1)}) custom-call(s32[1]{0:T(128)} %bitcast.place_ref, s32[1]{0:T(128)S(6)} %copy.5.size_ref, bf16[1024,2048]{1,0:T(8,128)(2,1)S(1)} %shard_map.51.rows_ref, s32[4,136,128]{2,1,0:T(8,128)S(1)} %shard_map.52.refs_0_, ...), custom_call_target="tpu_custom_call" | custom-call | tf_op jit(solution)/shard_map/pallas_call | solution.py:335
  36.6 1.3 collective-permute-start.6
  38.7 1.4 collective-permute-start.8
  40.2 4.6 %collective-permute-done.6.refs_0_ = s32[4,136,128]{2,1,0:T(8,128)S(1)} collective-permute-done((s32[4,136,128]{2,1,0:T(8,128)S(1)}, s32[4,136,128]{2,1,0:T(8,128)S(1)}, u32[]{:S(2)}, u32[]{:S(2)}) %collective-permute-start.6) | collective-permute-done | bytes 278560 | tf_op jit(solution)/shard_map/ppermute | solution.py:47
  44.8 4.1 %collective-permute-done.7.refs_1_ = s32[4,136,128]{2,1,0:T(8,128)S(1)} collective-permute-done((s32[4,136,128]{2,1,0:T(8,128)S(1)}, s32[4,136,128]{2,1,0:T(8,128)S(1)}, u32[]{:S(2)}, u32[]{:S(2)}) %collective-permute-start.7) | collective-permute-done | bytes 278560 | tf_op jit(solution)/shard_map/ppermute | solution.py:47
  50.0 3.4 %collective-permute-start.10 = (s32[1,136,128]{2,1,0:T(8,128)S(1)}, s32[1,136,128]{2,1,0:T(8,128)S(1)}, u32[]{:S(2)}, u32[]{:S(2)}) collective-permute-start(s32[1,136,128]{2,1,0:T(8,128)S(1)} %get-tuple-element.36), channel_id=1, source_target_pairs={{0,8},{1,9},{2,10},{3,11},{4,12},{5,13},{6,14},{7,15},{8,0},{9,1},... | collective-permute-start | bytes 208904 | tf_op jit(solution)/shard_map/ppermute | solution.py:47
  54.1 2.4 %collective-permute-done.10.refs_1_ = s32[1,136,128]{2,1,0:T(8,128)S(1)} collective-permute-done((s32[1,136,128]{2,1,0:T(8,128)S(1)}, s32[1,136,128]{2,1,0:T(8,128)S(1)}, u32[]{:S(2)}, u32[]{:S(2)}) %collective-permute-start.10) | collective-permute-done | bytes 69664 | tf_op jit(solution)/shard_map/ppermute | solution.py:47
  56.5 3.8 %collective-permute-done.11.refs_2_ = s32[1,136,128]{2,1,0:T(8,128)S(1)} collective-permute-done((s32[1,136,128]{2,1,0:T(8,128)S(1)}, s32[1,136,128]{2,1,0:T(8,128)S(1)}, u32[]{:S(2)}, u32[]{:S(2)}) %collective-permute-start.11) | collective-permute-done | bytes 69664 | tf_op jit(solution)/shard_map/ppermute | solution.py:47
  61.7 2.1 %collective-permute-start.13 = (s32[1,136,128]{2,1,0:T(8,128)S(1)}, s32[1,136,128]{2,1,0:T(8,128)S(1)}, u32[]{:S(2)}, u32[]{:S(2)}) collective-permute-start(s32[1,136,128]{2,1,0:T(8,128)S(1)} %get-tuple-element.38.refs_0_), channel_id=1, source_target_pairs={{0,8},{1,9},{2,10},{3,11},{4,12},{5,13},{6,14},{7,15},{8,0},{9,1},... | collective-permute-start | bytes 208904 | tf_op jit(solution)/shard_map/ppermute | solution.py:47
  63.8 1.8 %collective-permute-start.14 = (s32[1,136,128]{2,1,0:T(8,128)S(1)}, s32[1,136,128]{2,1,0:T(8,128)S(1)}, u32[]{:S(2)}, u32[]{:S(2)}) collective-permute-start(s32[1,136,128]{2,1,0:T(8,128)S(1)} %get-tuple-element.38.refs_0_), channel_id=1, source_target_pairs={{0,12},{1,13},{2,14},{3,15},{4,8},{5,9},{6,10},{7,11},{8,4},{9,5},... | collective-permute-start | bytes 208904 | tf_op jit(solution)/shard_map/ppermute | solution.py:47
  65.6 1.3 collective-permute-done.13.refs_2_
  66.9 3.0 %collective-permute-done.14.refs_3_ = s32[1,136,128]{2,1,0:T(8,128)S(1)} collective-permute-done((s32[1,136,128]{2,1,0:T(8,128)S(1)}, s32[1,136,128]{2,1,0:T(8,128)S(1)}, u32[]{:S(2)}, u32[]{:S(2)}) %collective-permute-start.14) | collective-permute-done | bytes 69664 | tf_op jit(solution)/shard_map/ppermute | solution.py:47
  69.9 1.2 collective-permute-start.15
  71.1 1.5 collective-permute-start.16
  73.5 3.1 %collective-permute-done.15.refs_1_ = s32[4,136,128]{2,1,0:T(8,128)S(1)} collective-permute-done((s32[4,136,128]{2,1,0:T(8,128)S(1)}, s32[4,136,128]{2,1,0:T(8,128)S(1)}, u32[]{:S(2)}, u32[]{:S(2)}) %collective-permute-start.15) | collective-permute-done | bytes 278560 | tf_op jit(solution)/shard_map/ppermute | solution.py:47
  76.5 4.1 %collective-permute-done.16.refs_2_ = s32[4,136,128]{2,1,0:T(8,128)S(1)} collective-permute-done((s32[4,136,128]{2,1,0:T(8,128)S(1)}, s32[4,136,128]{2,1,0:T(8,128)S(1)}, u32[]{:S(2)}, u32[]{:S(2)}) %collective-permute-start.16) | collective-permute-done | bytes 278560 | tf_op jit(solution)/shard_map/ppermute | solution.py:47
  80.6 17.3 %shard_map.57 = (f32[4,256,128]{2,1,0:T(8,128)S(1)}, s32[4,136,128]{2,1,0:T(8,128)S(1)}, s32[4,136,128]{2,1,0:T(8,128)S(1)}, s32[4,136,128]{2,1,0:T(8,128)S(1)}) custom-call(s32[1]{0:T(128)} %bitcast.place_ref, s32[1]{0:T(128)S(6)} %copy.5.size_ref, bf16[1024,2048]{1,0:T(8,128)(2,1)S(1)} %shard_map.51.rows_ref, s32[4,136,128]{2,1,0:T(8,128)S(1)} %shard_map.56.refs_0_, ...), custom_call_target="tpu_custom_call" | custom-call | tf_op jit(solution)/shard_map/pallas_call | solution.py:335
  100.0 1.5 collective-permute-start.20
  101.4 3.1 %collective-permute-done.18.refs_0_ = s32[4,136,128]{2,1,0:T(8,128)S(1)} collective-permute-done((s32[4,136,128]{2,1,0:T(8,128)S(1)}, s32[4,136,128]{2,1,0:T(8,128)S(1)}, u32[]{:S(2)}, u32[]{:S(2)}) %collective-permute-start.18) | collective-permute-done | bytes 278560 | tf_op jit(solution)/shard_map/ppermute | solution.py:47
  104.5 2.5 %collective-permute-done.19.refs_1_ = s32[4,136,128]{2,1,0:T(8,128)S(1)} collective-permute-done((s32[4,136,128]{2,1,0:T(8,128)S(1)}, s32[4,136,128]{2,1,0:T(8,128)S(1)}, u32[]{:S(2)}, u32[]{:S(2)}) %collective-permute-start.19) | collective-permute-done | bytes 278560 | tf_op jit(solution)/shard_map/ppermute | solution.py:47
  107.0 1.4 collective-permute-done.20.refs_2_
  109.6 2.5 %collective-permute-start.22 = (s32[1,136,128]{2,1,0:T(8,128)S(1)}, s32[1,136,128]{2,1,0:T(8,128)S(1)}, u32[]{:S(2)}, u32[]{:S(2)}) collective-permute-start(s32[1,136,128]{2,1,0:T(8,128)S(1)} %get-tuple-element.45), channel_id=1, source_target_pairs={{0,8},{1,9},{2,10},{3,11},{4,12},{5,13},{6,14},{7,15},{8,0},{9,1},... | collective-permute-start | bytes 208904 | tf_op jit(solution)/shard_map/ppermute | solution.py:47
  112.1 1.9 %collective-permute-start.23 = (s32[1,136,128]{2,1,0:T(8,128)S(1)}, s32[1,136,128]{2,1,0:T(8,128)S(1)}, u32[]{:S(2)}, u32[]{:S(2)}) collective-permute-start(s32[1,136,128]{2,1,0:T(8,128)S(1)} %get-tuple-element.46), channel_id=1, source_target_pairs={{0,12},{1,13},{2,14},{3,15},{4,8},{5,9},{6,10},{7,11},{8,4},{9,5},... | collective-permute-start | bytes 208904 | tf_op jit(solution)/shard_map/ppermute | solution.py:47
  114.0 1.4 collective-permute-done.21.refs_0_
  115.4 2.8 %collective-permute-done.23.refs_2_ = s32[1,136,128]{2,1,0:T(8,128)S(1)} collective-permute-done((s32[1,136,128]{2,1,0:T(8,128)S(1)}, s32[1,136,128]{2,1,0:T(8,128)S(1)}, u32[]{:S(2)}, u32[]{:S(2)}) %collective-permute-start.23) | collective-permute-done | bytes 69664 | tf_op jit(solution)/shard_map/ppermute | solution.py:47
  118.9 2.5 %collective-permute-start.25 = (s32[1,136,128]{2,1,0:T(8,128)S(1)}, s32[1,136,128]{2,1,0:T(8,128)S(1)}, u32[]{:S(2)}, u32[]{:S(2)}) collective-permute-start(s32[1,136,128]{2,1,0:T(8,128)S(1)} %get-tuple-element.47.refs_0_), channel_id=1, source_target_pairs={{0,8},{1,9},{2,10},{3,11},{4,12},{5,13},{6,14},{7,15},{8,0},{9,1},... | collective-permute-start | bytes 208904 | tf_op jit(solution)/shard_map/ppermute | solution.py:47
  121.3 1.9 %collective-permute-start.26 = (s32[1,136,128]{2,1,0:T(8,128)S(1)}, s32[1,136,128]{2,1,0:T(8,128)S(1)}, u32[]{:S(2)}, u32[]{:S(2)}) collective-permute-start(s32[1,136,128]{2,1,0:T(8,128)S(1)} %get-tuple-element.47.refs_0_), channel_id=1, source_target_pairs={{0,12},{1,13},{2,14},{3,15},{4,8},{5,9},{6,10},{7,11},{8,4},{9,5},... | collective-permute-start | bytes 208904 | tf_op jit(solution)/shard_map/ppermute | solution.py:47
  124.1 3.3 %collective-permute-done.26.refs_3_ = s32[1,136,128]{2,1,0:T(8,128)S(1)} collective-permute-done((s32[1,136,128]{2,1,0:T(8,128)S(1)}, s32[1,136,128]{2,1,0:T(8,128)S(1)}, u32[]{:S(2)}, u32[]{:S(2)}) %collective-permute-start.26) | collective-permute-done | bytes 69664 | tf_op jit(solution)/shard_map/ppermute | solution.py:47
  128.6 1.5 collective-permute-start.28
  131.0 3.1 %collective-permute-done.27.refs_1_ = s32[4,136,128]{2,1,0:T(8,128)S(1)} collective-permute-done((s32[4,136,128]{2,1,0:T(8,128)S(1)}, s32[4,136,128]{2,1,0:T(8,128)S(1)}, u32[]{:S(2)}, u32[]{:S(2)}) %collective-permute-start.27) | collective-permute-done | bytes 278560 | tf_op jit(solution)/shard_map/ppermute | solution.py:47
  134.1 4.0 %collective-permute-done.28.refs_2_ = s32[4,136,128]{2,1,0:T(8,128)S(1)} collective-permute-done((s32[4,136,128]{2,1,0:T(8,128)S(1)}, s32[4,136,128]{2,1,0:T(8,128)S(1)}, u32[]{:S(2)}, u32[]{:S(2)}) %collective-permute-start.28) | collective-permute-done | bytes 278560 | tf_op jit(solution)/shard_map/ppermute | solution.py:47
  138.1 5.0 %shard_map.61 = (f32[256,256]{1,0:T(8,128)S(1)}, s32[168,128]{1,0:T(8,128)S(1)}) custom-call(s32[1]{0:T(128)S(6)} %and.4.quarter_ref, s32[1]{0:T(128)} %bitcast.place_ref, bf16[1024,2048]{1,0:T(8,128)(2,1)S(1)} %shard_map.51.rows_ref, s32[4,136,128]{2,1,0:T(8,128)S(1)} %shard_map.60.refs_0_, s32[4,136,128]{2,1,0:T(8,128)S(1)} %collective-permute-done.27.refs_1_, ...), custom_call_target="tpu_custom_call" | custom-call | tf_op jit(solution)/shard_map/pallas_call | solution.py:603
  143.2 1.8 %collective-permute-start.31 = (s32[168,128]{1,0:T(8,128)S(1)}, s32[168,128]{1,0:T(8,128)S(1)}, u32[]{:S(2)}, u32[]{:S(2)}) collective-permute-start(s32[168,128]{1,0:T(8,128)S(1)} %get-tuple-element.52.refs_0_), channel_id=1, source_target_pairs={{0,8},{1,9},{2,10},{3,11},{4,12},{5,13},{6,14},{7,15},{8,0},{9,1},... | collective-permute-start | bytes 258056 | tf_op jit(solution)/shard_map/ppermute | solution.py:47
  145.0 2.6 %collective-permute-start.32 = (s32[168,128]{1,0:T(8,128)S(1)}, s32[168,128]{1,0:T(8,128)S(1)}, u32[]{:S(2)}, u32[]{:S(2)}) collective-permute-start(s32[168,128]{1,0:T(8,128)S(1)} %get-tuple-element.52.refs_0_), channel_id=1, source_target_pairs={{0,12},{1,13},{2,14},{3,15},{4,8},{5,9},{6,10},{7,11},{8,4},{9,5},... | collective-permute-start | bytes 258056 | tf_op jit(solution)/shard_map/ppermute | solution.py:47
  147.6 4.0 %shard_map.62.source_ref = f32[256,512]{1,0:T(8,128)S(1)} custom-call(f32[256,256]{1,0:T(8,128)S(1)} %get-tuple-element.49.source_ref.inner_ref), custom_call_target="tpu_custom_call" | custom-call | flops 4000000000 | bytes 4194304 | tf_op jit(solution)/shard_map/pallas_call | solution.py:627
  152.3 1.4 collective-permute-start.33
  154.4 1.4 collective-permute-start.35
  155.8 3.7 %shard_map.63.factor_ref = f32[256,512]{1,0:T(8,128)S(1)} custom-call(f32[256,512]{1,0:T(8,128)S(1)} %shard_map.62.source_ref), custom_call_target="tpu_custom_call" | custom-call | flops 4000000000 | bytes 4194304 | tf_op jit(solution)/shard_map/pallas_call | solution.py:627
  (48 shorter events, 18.5 us)
Async XLA Ops:
  3.2 5.6 %collective-permute-start = (s32[1,136,128]{2,1,0:T(8,128)}, s32[1,136,128]{2,1,0:T(8,128)S(1)}, u32[]{:S(2)}, u32[]{:S(2)}) collective-permute-start(s32[1,136,128]{2,1,0:T(8,128)} %shard_map.50.after_ref.refs_0_), channel_id=1, source_target_pairs={{0,4},{1,5},{2,6},{3,7},{4,0},{5,1},{6,2},{7,3},{8,12},{9,13},{10,... | collective-permute-start | bytes 208904 | tf_op jit(solution)/shard_map/ppermute | solution.py:47
  6.2 7.8 %collective-permute-start.1 = (s32[1,136,128]{2,1,0:T(8,128)}, s32[1,136,128]{2,1,0:T(8,128)S(1)}, u32[]{:S(2)}, u32[]{:S(2)}) collective-permute-start(s32[1,136,128]{2,1,0:T(8,128)} %shard_map.50.after_ref.refs_0_), channel_id=1, source_target_pairs={{0,8},{1,9},{2,10},{3,11},{4,12},{5,13},{6,14},{7,15},{8,0},{9,1},... | collective-permute-start | bytes 208904 | tf_op jit(solution)/shard_map/ppermute | solution.py:47
  8.8 6.4 %collective-permute-start.2 = (s32[1,136,128]{2,1,0:T(8,128)}, s32[1,136,128]{2,1,0:T(8,128)S(1)}, u32[]{:S(2)}, u32[]{:S(2)}) collective-permute-start(s32[1,136,128]{2,1,0:T(8,128)} %shard_map.50.after_ref.refs_0_), channel_id=1, source_target_pairs={{0,12},{1,13},{2,14},{3,15},{4,8},{5,9},{6,10},{7,11},{8,4},{9,5},... | collective-permute-start | bytes 208904 | tf_op jit(solution)/shard_map/ppermute | solution.py:47
  15.2 0.9 copy-start
  16.1 9.6 %collective-permute-start.3 = (s32[4,136,128]{2,1,0:T(8,128)S(1)}, s32[4,136,128]{2,1,0:T(8,128)S(1)}, u32[]{:S(2)}, u32[]{:S(2)}) collective-permute-start(s32[4,136,128]{2,1,0:T(8,128)S(1)} %shard_map.52.refs_0_), channel_id=1, source_target_pairs={{0,1},{1,0},{2,3},{3,2},{4,5},{5,4},{6,7},{7,6},{8,9},{9,8},{10,11... | collective-permute-start | bytes 835592 | tf_op jit(solution)/shard_map/ppermute | solution.py:47
  17.7 12.3 %collective-permute-start.4 = (s32[4,136,128]{2,1,0:T(8,128)S(1)}, s32[4,136,128]{2,1,0:T(8,128)S(1)}, u32[]{:S(2)}, u32[]{:S(2)}) collective-permute-start(s32[4,136,128]{2,1,0:T(8,128)S(1)} %shard_map.52.refs_0_), channel_id=1, source_target_pairs={{0,2},{1,3},{2,0},{3,1},{4,6},{5,7},{6,4},{7,5},{8,10},{9,11},{10,... | collective-permute-start | bytes 835592 | tf_op jit(solution)/shard_map/ppermute | solution.py:47
  19.2 10.8 %collective-permute-start.5 = (s32[4,136,128]{2,1,0:T(8,128)S(1)}, s32[4,136,128]{2,1,0:T(8,128)S(1)}, u32[]{:S(2)}, u32[]{:S(2)}) collective-permute-start(s32[4,136,128]{2,1,0:T(8,128)S(1)} %shard_map.52.refs_0_), channel_id=1, source_target_pairs={{0,3},{1,2},{2,1},{3,0},{4,7},{5,6},{6,5},{7,4},{8,11},{9,10},{10,... | collective-permute-start | bytes 835592 | tf_op jit(solution)/shard_map/ppermute | solution.py:47
  19.7 2.2 %copy-start.1 = (bf16[1,1024,2048]{2,1,0:T(8,128)(2,1)S(1)}, bf16[1,1024,2048]{2,1,0:T(8,128)(2,1)}, u32[]{:S(2)}) copy-start(bf16[1,1024,2048]{2,1,0:T(8,128)(2,1)} %param.3) | copy-start | bytes 12582916
  36.6 8.2 %collective-permute-start.6 = (s32[4,136,128]{2,1,0:T(8,128)S(1)}, s32[4,136,128]{2,1,0:T(8,128)S(1)}, u32[]{:S(2)}, u32[]{:S(2)}) collective-permute-start(s32[4,136,128]{2,1,0:T(8,128)S(1)} %get-tuple-element.31), channel_id=1, source_target_pairs={{0,1},{1,0},{2,3},{3,2},{4,5},{5,4},{6,7},{7,6},{8,9},{9,8},{10,11... | collective-permute-start | bytes 835592 | tf_op jit(solution)/shard_map/ppermute | solution.py:47
  37.9 11.1 %collective-permute-start.7 = (s32[4,136,128]{2,1,0:T(8,128)S(1)}, s32[4,136,128]{2,1,0:T(8,128)S(1)}, u32[]{:S(2)}, u32[]{:S(2)}) collective-permute-start(s32[4,136,128]{2,1,0:T(8,128)S(1)} %get-tuple-element.32), channel_id=1, source_target_pairs={{0,2},{1,3},{2,0},{3,1},{4,6},{5,7},{6,4},{7,5},{8,10},{9,11},{10,... | collective-permute-start | bytes 835592 | tf_op jit(solution)/shard_map/ppermute | solution.py:47
  38.7 10.2 %collective-permute-start.8 = (s32[4,136,128]{2,1,0:T(8,128)S(1)}, s32[4,136,128]{2,1,0:T(8,128)S(1)}, u32[]{:S(2)}, u32[]{:S(2)}) collective-permute-start(s32[4,136,128]{2,1,0:T(8,128)S(1)} %get-tuple-element.33), channel_id=1, source_target_pairs={{0,3},{1,2},{2,1},{3,0},{4,7},{5,6},{6,5},{7,4},{8,11},{9,10},{10,... | collective-permute-start | bytes 835592 | tf_op jit(solution)/shard_map/ppermute | solution.py:47
  50.0 6.4 %collective-permute-start.10 = (s32[1,136,128]{2,1,0:T(8,128)S(1)}, s32[1,136,128]{2,1,0:T(8,128)S(1)}, u32[]{:S(2)}, u32[]{:S(2)}) collective-permute-start(s32[1,136,128]{2,1,0:T(8,128)S(1)} %get-tuple-element.36), channel_id=1, source_target_pairs={{0,8},{1,9},{2,10},{3,11},{4,12},{5,13},{6,14},{7,15},{8,0},{9,1},... | collective-permute-start | bytes 208904 | tf_op jit(solution)/shard_map/ppermute | solution.py:47
  53.4 6.8 %collective-permute-start.11 = (s32[1,136,128]{2,1,0:T(8,128)S(1)}, s32[1,136,128]{2,1,0:T(8,128)S(1)}, u32[]{:S(2)}, u32[]{:S(2)}) collective-permute-start(s32[1,136,128]{2,1,0:T(8,128)S(1)} %get-tuple-element.37), channel_id=1, source_target_pairs={{0,12},{1,13},{2,14},{3,15},{4,8},{5,9},{6,10},{7,11},{8,4},{9,5},... | collective-permute-start | bytes 208904 | tf_op jit(solution)/shard_map/ppermute | solution.py:47
  54.0 6.3 %collective-permute-start.9 = (s32[1,136,128]{2,1,0:T(8,128)S(1)}, s32[1,136,128]{2,1,0:T(8,128)S(1)}, u32[]{:S(2)}, u32[]{:S(2)}) collective-permute-start(s32[1,136,128]{2,1,0:T(8,128)S(1)} %get-tuple-element.35), channel_id=1, source_target_pairs={{0,4},{1,5},{2,6},{3,7},{4,0},{5,1},{6,2},{7,3},{8,12},{9,13},{10,... | collective-permute-start | bytes 208904 | tf_op jit(solution)/shard_map/ppermute | solution.py:47
  61.3 4.4 %collective-permute-start.12 = (s32[1,136,128]{2,1,0:T(8,128)S(1)}, s32[1,136,128]{2,1,0:T(8,128)S(1)}, u32[]{:S(2)}, u32[]{:S(2)}) collective-permute-start(s32[1,136,128]{2,1,0:T(8,128)S(1)} %get-tuple-element.38.refs_0_), channel_id=1, source_target_pairs={{0,4},{1,5},{2,6},{3,7},{4,0},{5,1},{6,2},{7,3},{8,12},{9,13},{10,... | collective-permute-start | bytes 208904 | tf_op jit(solution)/shard_map/ppermute | solution.py:47
  61.7 5.2 %collective-permute-start.13 = (s32[1,136,128]{2,1,0:T(8,128)S(1)}, s32[1,136,128]{2,1,0:T(8,128)S(1)}, u32[]{:S(2)}, u32[]{:S(2)}) collective-permute-start(s32[1,136,128]{2,1,0:T(8,128)S(1)} %get-tuple-element.38.refs_0_), channel_id=1, source_target_pairs={{0,8},{1,9},{2,10},{3,11},{4,12},{5,13},{6,14},{7,15},{8,0},{9,1},... | collective-permute-start | bytes 208904 | tf_op jit(solution)/shard_map/ppermute | solution.py:47
  63.8 6.1 %collective-permute-start.14 = (s32[1,136,128]{2,1,0:T(8,128)S(1)}, s32[1,136,128]{2,1,0:T(8,128)S(1)}, u32[]{:S(2)}, u32[]{:S(2)}) collective-permute-start(s32[1,136,128]{2,1,0:T(8,128)S(1)} %get-tuple-element.38.refs_0_), channel_id=1, source_target_pairs={{0,12},{1,13},{2,14},{3,15},{4,8},{5,9},{6,10},{7,11},{8,4},{9,5},... | collective-permute-start | bytes 208904 | tf_op jit(solution)/shard_map/ppermute | solution.py:47
  69.9 6.6 %collective-permute-start.15 = (s32[4,136,128]{2,1,0:T(8,128)S(1)}, s32[4,136,128]{2,1,0:T(8,128)S(1)}, u32[]{:S(2)}, u32[]{:S(2)}) collective-permute-start(s32[4,136,128]{2,1,0:T(8,128)S(1)} %shard_map.56.refs_0_), channel_id=1, source_target_pairs={{0,1},{1,0},{2,3},{3,2},{4,5},{5,4},{6,7},{7,6},{8,9},{9,8},{10,11... | collective-permute-start | bytes 835592 | tf_op jit(solution)/shard_map/ppermute | solution.py:47
  71.1 9.5 %collective-permute-start.16 = (s32[4,136,128]{2,1,0:T(8,128)S(1)}, s32[4,136,128]{2,1,0:T(8,128)S(1)}, u32[]{:S(2)}, u32[]{:S(2)}) collective-permute-start(s32[4,136,128]{2,1,0:T(8,128)S(1)} %shard_map.56.refs_0_), channel_id=1, source_target_pairs={{0,2},{1,3},{2,0},{3,1},{4,6},{5,7},{6,4},{7,5},{8,10},{9,11},{10,... | collective-permute-start | bytes 835592 | tf_op jit(solution)/shard_map/ppermute | solution.py:47
  72.6 8.0 %collective-permute-start.17 = (s32[4,136,128]{2,1,0:T(8,128)S(1)}, s32[4,136,128]{2,1,0:T(8,128)S(1)}, u32[]{:S(2)}, u32[]{:S(2)}) collective-permute-start(s32[4,136,128]{2,1,0:T(8,128)S(1)} %shard_map.56.refs_0_), channel_id=1, source_target_pairs={{0,3},{1,2},{2,1},{3,0},{4,7},{5,6},{6,5},{7,4},{8,11},{9,10},{10,... | collective-permute-start | bytes 835592 | tf_op jit(solution)/shard_map/ppermute | solution.py:47
  97.9 6.6 %collective-permute-start.18 = (s32[4,136,128]{2,1,0:T(8,128)S(1)}, s32[4,136,128]{2,1,0:T(8,128)S(1)}, u32[]{:S(2)}, u32[]{:S(2)}) collective-permute-start(s32[4,136,128]{2,1,0:T(8,128)S(1)} %get-tuple-element.40), channel_id=1, source_target_pairs={{0,1},{1,0},{2,3},{3,2},{4,5},{5,4},{6,7},{7,6},{8,9},{9,8},{10,11... | collective-permute-start | bytes 835592 | tf_op jit(solution)/shard_map/ppermute | solution.py:47
  98.9 8.1 %collective-permute-start.19 = (s32[4,136,128]{2,1,0:T(8,128)S(1)}, s32[4,136,128]{2,1,0:T(8,128)S(1)}, u32[]{:S(2)}, u32[]{:S(2)}) collective-permute-start(s32[4,136,128]{2,1,0:T(8,128)S(1)} %get-tuple-element.41), channel_id=1, source_target_pairs={{0,2},{1,3},{2,0},{3,1},{4,6},{5,7},{6,4},{7,5},{8,10},{9,11},{10,... | collective-permute-start | bytes 835592 | tf_op jit(solution)/shard_map/ppermute | solution.py:47
  100.0 8.5 %collective-permute-start.20 = (s32[4,136,128]{2,1,0:T(8,128)S(1)}, s32[4,136,128]{2,1,0:T(8,128)S(1)}, u32[]{:S(2)}, u32[]{:S(2)}) collective-permute-start(s32[4,136,128]{2,1,0:T(8,128)S(1)} %get-tuple-element.42), channel_id=1, source_target_pairs={{0,3},{1,2},{2,1},{3,0},{4,7},{5,6},{6,5},{7,4},{8,11},{9,10},{10,... | collective-permute-start | bytes 835592 | tf_op jit(solution)/shard_map/ppermute | solution.py:47
  109.5 5.9 %collective-permute-start.21 = (s32[1,136,128]{2,1,0:T(8,128)S(1)}, s32[1,136,128]{2,1,0:T(8,128)S(1)}, u32[]{:S(2)}, u32[]{:S(2)}) collective-permute-start(s32[1,136,128]{2,1,0:T(8,128)S(1)} %get-tuple-element.44), channel_id=1, source_target_pairs={{0,4},{1,5},{2,6},{3,7},{4,0},{5,1},{6,2},{7,3},{8,12},{9,13},{10,... | collective-permute-start | bytes 208904 | tf_op jit(solution)/shard_map/ppermute | solution.py:47
  109.6 5.8 %collective-permute-start.22 = (s32[1,136,128]{2,1,0:T(8,128)S(1)}, s32[1,136,128]{2,1,0:T(8,128)S(1)}, u32[]{:S(2)}, u32[]{:S(2)}) collective-permute-start(s32[1,136,128]{2,1,0:T(8,128)S(1)} %get-tuple-element.45), channel_id=1, source_target_pairs={{0,8},{1,9},{2,10},{3,11},{4,12},{5,13},{6,14},{7,15},{8,0},{9,1},... | collective-permute-start | bytes 208904 | tf_op jit(solution)/shard_map/ppermute | solution.py:47
  112.1 6.1 %collective-permute-start.23 = (s32[1,136,128]{2,1,0:T(8,128)S(1)}, s32[1,136,128]{2,1,0:T(8,128)S(1)}, u32[]{:S(2)}, u32[]{:S(2)}) collective-permute-start(s32[1,136,128]{2,1,0:T(8,128)S(1)} %get-tuple-element.46), channel_id=1, source_target_pairs={{0,12},{1,13},{2,14},{3,15},{4,8},{5,9},{6,10},{7,11},{8,4},{9,5},... | collective-permute-start | bytes 208904 | tf_op jit(solution)/shard_map/ppermute | solution.py:47
  118.8 4.5 %collective-permute-start.24 = (s32[1,136,128]{2,1,0:T(8,128)S(1)}, s32[1,136,128]{2,1,0:T(8,128)S(1)}, u32[]{:S(2)}, u32[]{:S(2)}) collective-permute-start(s32[1,136,128]{2,1,0:T(8,128)S(1)} %get-tuple-element.47.refs_0_), channel_id=1, source_target_pairs={{0,4},{1,5},{2,6},{3,7},{4,0},{5,1},{6,2},{7,3},{8,12},{9,13},{10,... | collective-permute-start | bytes 208904 | tf_op jit(solution)/shard_map/ppermute | solution.py:47
  118.9 5.3 %collective-permute-start.25 = (s32[1,136,128]{2,1,0:T(8,128)S(1)}, s32[1,136,128]{2,1,0:T(8,128)S(1)}, u32[]{:S(2)}, u32[]{:S(2)}) collective-permute-start(s32[1,136,128]{2,1,0:T(8,128)S(1)} %get-tuple-element.47.refs_0_), channel_id=1, source_target_pairs={{0,8},{1,9},{2,10},{3,11},{4,12},{5,13},{6,14},{7,15},{8,0},{9,1},... | collective-permute-start | bytes 208904 | tf_op jit(solution)/shard_map/ppermute | solution.py:47
  121.3 6.1 %collective-permute-start.26 = (s32[1,136,128]{2,1,0:T(8,128)S(1)}, s32[1,136,128]{2,1,0:T(8,128)S(1)}, u32[]{:S(2)}, u32[]{:S(2)}) collective-permute-start(s32[1,136,128]{2,1,0:T(8,128)S(1)} %get-tuple-element.47.refs_0_), channel_id=1, source_target_pairs={{0,12},{1,13},{2,14},{3,15},{4,8},{5,9},{6,10},{7,11},{8,4},{9,5},... | collective-permute-start | bytes 208904 | tf_op jit(solution)/shard_map/ppermute | solution.py:47
  127.5 6.6 %collective-permute-start.27 = (s32[4,136,128]{2,1,0:T(8,128)S(1)}, s32[4,136,128]{2,1,0:T(8,128)S(1)}, u32[]{:S(2)}, u32[]{:S(2)}) collective-permute-start(s32[4,136,128]{2,1,0:T(8,128)S(1)} %shard_map.60.refs_0_), channel_id=1, source_target_pairs={{0,1},{1,0},{2,3},{3,2},{4,5},{5,4},{6,7},{7,6},{8,9},{9,8},{10,11... | collective-permute-start | bytes 835592 | tf_op jit(solution)/shard_map/ppermute | solution.py:47
  128.6 9.5 %collective-permute-start.28 = (s32[4,136,128]{2,1,0:T(8,128)S(1)}, s32[4,136,128]{2,1,0:T(8,128)S(1)}, u32[]{:S(2)}, u32[]{:S(2)}) collective-permute-start(s32[4,136,128]{2,1,0:T(8,128)S(1)} %shard_map.60.refs_0_), channel_id=1, source_target_pairs={{0,2},{1,3},{2,0},{3,1},{4,6},{5,7},{6,4},{7,5},{8,10},{9,11},{10,... | collective-permute-start | bytes 835592 | tf_op jit(solution)/shard_map/ppermute | solution.py:47
  130.1 8.0 %collective-permute-start.29 = (s32[4,136,128]{2,1,0:T(8,128)S(1)}, s32[4,136,128]{2,1,0:T(8,128)S(1)}, u32[]{:S(2)}, u32[]{:S(2)}) collective-permute-start(s32[4,136,128]{2,1,0:T(8,128)S(1)} %shard_map.60.refs_0_), channel_id=1, source_target_pairs={{0,3},{1,2},{2,1},{3,0},{4,7},{5,6},{6,5},{7,4},{8,11},{9,10},{10,... | collective-permute-start | bytes 835592 | tf_op jit(solution)/shard_map/ppermute | solution.py:47
  143.2 8.4 %collective-permute-start.30 = (s32[168,128]{1,0:T(8,128)S(1)}, s32[168,128]{1,0:T(8,128)S(1)}, u32[]{:S(2)}, u32[]{:S(2)}) collective-permute-start(s32[168,128]{1,0:T(8,128)S(1)} %get-tuple-element.52.refs_0_), channel_id=1, source_target_pairs={{0,4},{1,5},{2,6},{3,7},{4,0},{5,1},{6,2},{7,3},{8,12},{9,13},{10,... | collective-permute-start | bytes 258056 | tf_op jit(solution)/shard_map/ppermute | solution.py:47
  143.2 8.4 %collective-permute-start.31 = (s32[168,128]{1,0:T(8,128)S(1)}, s32[168,128]{1,0:T(8,128)S(1)}, u32[]{:S(2)}, u32[]{:S(2)}) collective-permute-start(s32[168,128]{1,0:T(8,128)S(1)} %get-tuple-element.52.refs_0_), channel_id=1, source_target_pairs={{0,8},{1,9},{2,10},{3,11},{4,12},{5,13},{6,14},{7,15},{8,0},{9,1},... | collective-permute-start | bytes 258056 | tf_op jit(solution)/shard_map/ppermute | solution.py:47
  145.0 6.6 %collective-permute-start.32 = (s32[168,128]{1,0:T(8,128)S(1)}, s32[168,128]{1,0:T(8,128)S(1)}, u32[]{:S(2)}, u32[]{:S(2)}) collective-permute-start(s32[168,128]{1,0:T(8,128)S(1)} %get-tuple-element.52.refs_0_), channel_id=1, source_target_pairs={{0,12},{1,13},{2,14},{3,15},{4,8},{5,9},{6,10},{7,11},{8,4},{9,5},... | collective-permute-start | bytes 258056 | tf_op jit(solution)/shard_map/ppermute | solution.py:47
  152.3 7.3 %collective-permute-start.33 = (s32[168,128]{1,0:T(8,128)S(1)}, s32[168,128]{1,0:T(8,128)S(1)}, u32[]{:S(2)}, u32[]{:S(2)}) collective-permute-start(s32[168,128]{1,0:T(8,128)S(1)} %shard_map.65.refs_0_), channel_id=1, source_target_pairs={{0,1},{1,0},{2,3},{3,2},{4,5},{5,4},{6,7},{7,6},{8,9},{9,8},{10,11... | collective-permute-start | bytes 258056 | tf_op jit(solution)/shard_map/ppermute | solution.py:47
  153.7 5.9 %collective-permute-start.34 = (s32[168,128]{1,0:T(8,128)S(1)}, s32[168,128]{1,0:T(8,128)S(1)}, u32[]{:S(2)}, u32[]{:S(2)}) collective-permute-start(s32[168,128]{1,0:T(8,128)S(1)} %shard_map.65.refs_0_), channel_id=1, source_target_pairs={{0,2},{1,3},{2,0},{3,1},{4,6},{5,7},{6,4},{7,5},{8,10},{9,11},{10,... | collective-permute-start | bytes 258056 | tf_op jit(solution)/shard_map/ppermute | solution.py:47
  154.4 5.4 %collective-permute-start.35 = (s32[168,128]{1,0:T(8,128)S(1)}, s32[168,128]{1,0:T(8,128)S(1)}, u32[]{:S(2)}, u32[]{:S(2)}) collective-permute-start(s32[168,128]{1,0:T(8,128)S(1)} %shard_map.65.refs_0_), channel_id=1, source_target_pairs={{0,3},{1,2},{2,1},{3,0},{4,7},{5,6},{6,5},{7,4},{8,11},{9,10},{10,... | collective-permute-start | bytes 258056 | tf_op jit(solution)/shard_map/ppermute | solution.py:47
  160.9 1.2 collective-permute-start.36
